TPU v7x, 32 devices: a whole 2x2x4 slice. The times are simulated.
32 devices in a mesh: wide: 8 (over z, core), narrow: 4 (over y, x).
Axes of the slice: x: 2, y: 2, z: 4, core: 2. Of those that a mesh axis runs over, the one named last changes fastest.
Arguments:
- hidden: bfloat16 [16384, 2048], P(('wide', 'narrow')), may hold values from -6 to 6
- mix_weight: bfloat16 [4, 2048, 2048], P(None, None, 'narrow'), may hold values from -0.125 to 0.125
- out_weight: bfloat16 [2048, 2048], P('narrow'), may hold values from -0.125 to 0.125
- ffn_in_weight: bfloat16 [2, 2048, 5632], P(None, None, 'narrow'), may hold values from -0.125 to 0.125
- ffn_out_weight: bfloat16 [5632, 2048], P('narrow'), may hold values from -0.078125 to 0.078125
- seq_lengths: int32 [16], P('wide'), may hold values from 0 to 2048, as said below
- block_seq: int32 [64], P('wide'), may hold values from 0 to 15, as said below
- cotangent: bfloat16 [16384, 2048], P(('wide', 'narrow')), may hold values from -6 to 6
Outputs:
- layer_out: bfloat16 [16384, 2048], P(('wide', 'narrow'))
- input_grad: bfloat16 [16384, 2048], P(('wide', 'narrow'))
- grad_mix: float32 [4, 2048, 2048], P(None, None, 'narrow')
- grad_out: float32 [2048, 2048], P('narrow')
- grad_ffn_in: float32 [2, 2048, 5632], P(None, None, 'narrow')
- grad_ffn_out: float32 [5632, 2048], P('narrow')
Inputs may be any that keep to these rules, and one draw needn't show every extreme that they name: `seq_lengths`: slots 2g and 2g + 1 belong to index g of wide; the first holds a sequence of 1024 tokens or more; the second holds 0 or a length of 1024 or more. Index 0 holds one sequence of 2048 tokens. `block_seq`: the 8 blocks of index g of wide name slot 2g, then slot 2g + 1 if that slot's length is not 0; a slot of length L has exactly ceil(L / 256) blocks.
All inputs are finite; a program needn't handle non-finite values.
Results may differ from a plain program's by a relative error of at most 0.023.
Values may be sent and summed in bfloat16 or wider, within the bound.
A program may use at most 320 MiB of HBM per device.

v0:
```python
import jax
import jax.numpy as jnp
from jax import lax
from jax.sharding import PartitionSpec as P

HEADS = 16
HS = 128
BLK = 256
NBLK = 8


epsilon = 1e-06
head_floor = 1.0
highest = lax.Precision.HIGHEST


def row_norm(values):
    return values * lax.rsqrt(jnp.mean(values * values, axis=-1, keepdims=True) + epsilon)


def head_norm(values):
    return values * lax.rsqrt(jnp.mean(values * values, axis=-1, keepdims=True) + head_floor)


def silu_slope(values):
    sigmoid_part = jax.nn.sigmoid(values)
    return sigmoid_part * (1.0 + values * (1.0 - sigmoid_part))


def decay_tables(decay_rates):
    positions = jnp.arange(BLK, dtype=jnp.float32)
    distance = positions[:, None] - positions[None, :]
    causal = distance >= 0
    clipped = jnp.where(causal, distance, 0.0)
    within = jnp.where(causal[None], jnp.exp(-decay_rates[:, None, None] * clipped[None]), 0.0)
    entry_decay = jnp.exp(-(positions[:, None] + 1.0) * decay_rates[None, :])
    exit_decay = jnp.exp(-(BLK - 1.0 - positions[:, None]) * decay_rates[None, :])
    block_decay = jnp.exp(-BLK * decay_rates)
    return (within, entry_decay, exit_decay, block_decay)


def group_masks(lengths, owners):
    seq_slot = owners - owners[0]
    first_count = jnp.sum((seq_slot == 0).astype(jnp.int32))
    block_ids = jnp.arange(NBLK, dtype=jnp.int32)
    start_block = jnp.where(seq_slot == 0, jnp.int32(0), first_count)
    seq_limit = jnp.where(seq_slot == 0, lengths[0], lengths[1])
    offsets = (block_ids - start_block)[:, None] * BLK + jnp.arange(BLK, dtype=jnp.int32)[None, :]
    valid_rows = (offsets < seq_limit[:, None]).reshape(-1)
    fresh_block = block_ids == start_block
    return (valid_rows, fresh_block)


def forward_block(tables, kv_state, block_in):
    within, entry_decay, exit_decay, block_decay = tables
    queries, keys_in, values, fresh_block = block_in
    kv_state = jnp.where(fresh_block, 0.0, kv_state)
    scores = jnp.einsum("ihs,jhs->hij", queries, keys_in, preferred_element_type=jnp.float32)
    weights = (scores * within).astype(jnp.bfloat16)
    inner_part = jnp.einsum("hij,jhs->ihs", weights, values, preferred_element_type=jnp.float32)
    carried = jnp.einsum(
        "ihs,hst->iht",
        queries.astype(jnp.float32) * entry_decay[:, :, None],
        kv_state,
        precision=highest,
    )
    update = jnp.einsum(
        "ihs,iht->hst",
        keys_in.astype(jnp.float32) * exit_decay[:, :, None],
        values.astype(jnp.float32),
        precision=highest,
    )
    return (block_decay[:, None, None] * kv_state + update, (inner_part + carried, kv_state))


def backward_block(tables, later_grad, block_in):
    within, entry_decay, exit_decay, block_decay = tables
    queries, keys_in, values, grad_mix, kv_state, fresh_block = block_in
    scores = jnp.einsum("ihs,jhs->hij", queries, keys_in, preferred_element_type=jnp.float32)
    weights = (scores * within).astype(jnp.bfloat16)
    grad_values = jnp.einsum("hij,ihs->jhs", weights, grad_mix, preferred_element_type=jnp.float32)
    grad_weights = jnp.einsum("ihs,jhs->hij", grad_mix, values, preferred_element_type=jnp.float32)
    grad_scores = (grad_weights * within).astype(jnp.bfloat16)
    grad_queries = jnp.einsum(
        "hij,jhs->ihs", grad_scores, keys_in, preferred_element_type=jnp.float32
    )
    grad_keys = jnp.einsum("hij,ihs->jhs", grad_scores, queries, preferred_element_type=jnp.float32)
    grad_float = grad_mix.astype(jnp.float32)
    values_float = values.astype(jnp.float32)
    queries_float = queries.astype(jnp.float32)
    keys_float = keys_in.astype(jnp.float32)
    grad_queries = grad_queries + entry_decay[:, :, None] * jnp.einsum(
        "iht,hst->ihs", grad_float, kv_state, precision=highest
    )
    grad_keys = grad_keys + exit_decay[:, :, None] * jnp.einsum(
        "iht,hst->ihs", values_float, later_grad, precision=highest
    )
    grad_values = grad_values + jnp.einsum(
        "ihs,hst->iht", keys_float * exit_decay[:, :, None], later_grad, precision=highest
    )
    grad_state = jnp.einsum(
        "ihs,iht->hst", queries_float * entry_decay[:, :, None], grad_float, precision=highest
    )
    grad_state = grad_state + block_decay[:, None, None] * later_grad
    grad_state = jnp.where(fresh_block, 0.0, grad_state)
    return (grad_state, (grad_queries, grad_keys, grad_values))


def per_device(
    hidden, mix_weight, out_weight, ffn_in_weight, ffn_out_weight, seq_lengths, block_seq, cotangent
):
    local_rows = hidden.shape[0]
    group_rows = NBLK * BLK
    head_width = mix_weight.shape[2]
    head_count = head_width // HS
    narrow_index = lax.axis_index("narrow")
    valid_all, fresh_block = group_masks(seq_lengths, block_seq)
    valid_rows = lax.dynamic_slice_in_dim(
        valid_all.astype(jnp.float32), narrow_index * local_rows, local_rows
    )[:, None]
    head_ids = narrow_index * head_count + jnp.arange(head_count, dtype=jnp.int32)
    decay_rates = 2.0 ** (-8.0 * (head_ids.astype(jnp.float32) + 1.0) / HEADS)
    tables = decay_tables(decay_rates)

    def split_blocks(flat_rows):
        return flat_rows.reshape(NBLK, BLK, head_count, HS)

    inputs = hidden.astype(jnp.float32)
    normed_low = row_norm(inputs).astype(jnp.bfloat16)
    gathered = lax.all_gather(normed_low, "narrow", axis=0, tiled=True)
    projected = jnp.einsum("rd,cde->cre", gathered, mix_weight, preferred_element_type=jnp.float32)
    queries = jax.nn.silu(projected[0]).astype(jnp.bfloat16)
    keys_in = jax.nn.silu(projected[1]).astype(jnp.bfloat16)
    values = projected[2].astype(jnp.bfloat16)
    gate_part = projected[3]
    zero_state = jnp.zeros((head_count, HS, HS), jnp.float32)
    final_state, (mixing, kept_states) = lax.scan(
        lambda state_in, block_in: forward_block(tables, state_in, block_in),
        zero_state,
        (split_blocks(queries), split_blocks(keys_in), split_blocks(values), fresh_block),
    )
    mixing = mixing.reshape(group_rows, head_count, HS)
    headed = head_norm(mixing).reshape(group_rows, head_width)
    gated_low = (headed * gate_part).astype(jnp.bfloat16)
    branch = lax.psum_scatter(
        jnp.dot(gated_low, out_weight, preferred_element_type=jnp.float32).astype(jnp.bfloat16),
        "narrow",
        scatter_dimension=0,
        tiled=True,
    ).astype(jnp.float32)
    middle = inputs + valid_rows * branch
    normed_two_low = row_norm(middle).astype(jnp.bfloat16)
    gathered_two = lax.all_gather(normed_two_low, "narrow", axis=0, tiled=True)
    both_parts = jnp.einsum(
        "rd,cdf->crf", gathered_two, ffn_in_weight, preferred_element_type=jnp.float32
    )
    hidden_low = (both_parts[0] * both_parts[1]).astype(jnp.bfloat16)
    branch_two = lax.psum_scatter(
        jnp.dot(hidden_low, ffn_out_weight, preferred_element_type=jnp.float32).astype(
            jnp.bfloat16
        ),
        "narrow",
        scatter_dimension=0,
        tiled=True,
    ).astype(jnp.float32)
    layer_out = (middle + valid_rows * branch_two).astype(jnp.bfloat16)
    grad_rows = cotangent.astype(jnp.float32)
    ffn_grad_all = lax.all_gather(
        (valid_rows * grad_rows).astype(jnp.bfloat16), "narrow", axis=0, tiled=True
    )
    grad_ffn_out = jnp.einsum(
        "rf,rd->fd", hidden_low, ffn_grad_all, preferred_element_type=jnp.float32
    )
    grad_hidden = jnp.einsum(
        "rd,fd->rf", ffn_grad_all, ffn_out_weight, preferred_element_type=jnp.float32
    )
    grad_parts = jnp.stack([grad_hidden * both_parts[1], grad_hidden * both_parts[0]]).astype(
        jnp.bfloat16
    )
    grad_ffn_in = jnp.einsum(
        "rd,crf->cdf", gathered_two, grad_parts, preferred_element_type=jnp.float32
    )
    grad_slice = grad_parts
    grad_normed_two = lax.psum_scatter(
        jnp.einsum(
            "crf,cdf->rd", grad_slice, ffn_in_weight, preferred_element_type=jnp.float32
        ).astype(jnp.bfloat16),
        "narrow",
        scatter_dimension=0,
        tiled=True,
    ).astype(jnp.float32)
    norm_value, norm_pull = jax.vjp(row_norm, middle)
    grad_middle = grad_rows + norm_pull(grad_normed_two)[0]
    attn_grad_all = lax.all_gather(
        (valid_rows * grad_middle).astype(jnp.bfloat16), "narrow", axis=0, tiled=True
    )
    grad_out_weight = jnp.einsum(
        "re,rd->ed", gated_low, attn_grad_all, preferred_element_type=jnp.float32
    )
    grad_gated = jnp.einsum(
        "rd,ed->re", attn_grad_all, out_weight, preferred_element_type=jnp.float32
    )
    grad_gated = lax.optimization_barrier(grad_gated.astype(jnp.bfloat16)).astype(jnp.float32)
    grad_gate = grad_gated * headed
    grad_headed = (grad_gated * gate_part).reshape(group_rows, head_count, HS)
    head_value, head_pull = jax.vjp(head_norm, mixing)
    grad_mixing = head_pull(grad_headed)[0].astype(jnp.bfloat16)
    first_grad, (grad_queries, grad_keys, grad_values) = lax.scan(
        lambda later_grad, block_in: backward_block(tables, later_grad, block_in),
        zero_state,
        (
            split_blocks(queries),
            split_blocks(keys_in),
            split_blocks(values),
            split_blocks(grad_mixing),
            kept_states,
            fresh_block,
        ),
        reverse=True,
    )
    grad_projected = jnp.stack(
        [
            grad_queries.reshape(group_rows, head_width) * silu_slope(projected[0]),
            grad_keys.reshape(group_rows, head_width) * silu_slope(projected[1]),
            grad_values.reshape(group_rows, head_width),
            grad_gate,
        ]
    ).astype(jnp.bfloat16)
    grad_mix = jnp.einsum(
        "rd,cre->cde", gathered, grad_projected, preferred_element_type=jnp.float32
    )
    grad_slice = grad_projected
    grad_normed = lax.psum_scatter(
        jnp.einsum(
            "cre,cde->rd", grad_slice, mix_weight, preferred_element_type=jnp.float32
        ).astype(jnp.bfloat16),
        "narrow",
        scatter_dimension=0,
        tiled=True,
    ).astype(jnp.float32)
    first_value, first_pull = jax.vjp(row_norm, inputs)
    input_grad = (grad_middle + first_pull(grad_normed)[0]).astype(jnp.bfloat16)
    grad_mix, grad_out_weight, grad_ffn_in, grad_ffn_out = (
        lax.psum(grad_mix.astype(jnp.bfloat16), "wide").astype(jnp.float32),
        lax.psum(grad_out_weight.astype(jnp.bfloat16), "wide").astype(jnp.float32),
        lax.psum(grad_ffn_in.astype(jnp.bfloat16), "wide").astype(jnp.float32),
        lax.psum(grad_ffn_out.astype(jnp.bfloat16), "wide").astype(jnp.float32),
    )
    return (layer_out, input_grad, grad_mix, grad_out_weight, grad_ffn_in, grad_ffn_out)


def solution(mesh):
    in_specs = (
        P(("wide", "narrow"), None),
        P(None, None, "narrow"),
        P("narrow", None),
        P(None, None, "narrow"),
        P("narrow", None),
        P("wide"),
        P("wide"),
        P(("wide", "narrow"), None),
    )
    out_specs = (
        P(("wide", "narrow"), None),
        P(("wide", "narrow"), None),
        P(None, None, "narrow"),
        P("narrow", None),
        P(None, None, "narrow"),
        P("narrow", None),
    )
    return jax.shard_map(
        per_device, mesh=mesh, in_specs=in_specs, out_specs=out_specs, check_vma=False
    )
```

profile of v0, /device:TPU:0, one launch (start us, length us, event | category | flops | bytes accessed | tf_op | source)
XLA Modules:
  0.0 1773.6 jit_solution(11943600094673635417)
XLA Ops:
  18.1 86.3 %all-gather.5.cloned.1.call-done = bf16[2048,2048]{1,0:T(8,128)(2,1)} async-done(((bf16[512,2048]{1,0:T(8,128)(2,1)}), bf16[2048,2048]{1,0:T(8,128)(2,1)}) %all-gather.5.cloned.1.call-update) | async-done | bytes 8388624 | tf_op jit(solution)/shard_map/all_gather | solution.py:130
  104.4 21.5 %fusion.128 = f32[4,2048,512]{2,1,0:T(8,128)S(1)} fusion(bf16[4,2048,512]{2,1,0:T(8,128)(2,1)} %param.13, bf16[2048,2048]{1,0:T(8,128)(2,1)} %all-gather.5.cloned.1.call-done), kind=kOutput, calls=%fused_computation.157 | convolution fusion | flops 17179869184 | bytes 33554432 | tf_op jit(solution)/shard_map/rd,cde->cre/dot_general | solution.py:131
  125.9 4.8 fusion.155
  136.2 5.2 squeeze.101
  141.4 5.3 copy.75
  146.7 5.2 squeeze.102
  151.9 5.2 copy.77
  164.7 5.3 multiply_convert_fusion.8
  169.9 79.3 %while.42 = (s32[]{:T(128)}, f32[4,128,128]{2,1,0:T(8,128)S(1)}, f32[8,256,4,128]{1,3,2,0:T(8,128)}, f32[8,4,128,128]{3,2,1,0:T(8,128)}, pred[8]{0:T(512)(128)(4...) while((s32[]{:T(128)}, f32[4,128,128]{2,1,0:T(8,128)S(1)}, ...), condition=%wide.region_3.4_spmd.clone.clone.clone.clone, body=%wide.region_2.3_spmd.clone.clone.clone.sunk.clone | while | flops 539101184 | bytes 6904040 | solution.py:137
  252.0 5.2 copy.81
  257.7 4.9 mul.403
  262.6 4.9 multiply_convert_fusion.7
  268.9 6.8 convolution_convert_fusion.1
  276.6 85.7 %reduce-scatter.5.cloned.1.call-done = bf16[512,2048]{1,0:T(8,128)(2,1)} async-done(((bf16[2048,2048]{1,0:T(8,128)(2,1)}), bf16[512,2048]{1,0:T(8,128)(2,1)}) %reduce-scatter.5.cloned.1.call-update) | async-done | bytes 2097168 | tf_op jit(solution)/shard_map/reduce_scatter | solution.py:145
  366.3 4.6 fusion.135
  371.5 87.1 %all-gather.7.cloned.1.call-done = bf16[2048,2048]{1,0:T(8,128)(2,1)} async-done(((bf16[512,2048]{1,0:T(8,128)(2,1)}), bf16[2048,2048]{1,0:T(8,128)(2,1)}) %all-gather.7.cloned.1.call-update) | async-done | bytes 8388624 | tf_op jit(solution)/shard_map/all_gather | solution.py:153
  458.6 32.3 %convolution_bitcast_fusion.6 = f32[2,2048,1408]{2,1,0:T(8,128)} fusion(bf16[2,2048,1408]{2,1,0:T(8,128)(2,1)} %param.15, bf16[2048,2048]{1,0:T(8,128)(2,1)} %all-gather.7.cloned.1.call-done), kind=kOutput, calls=%fused_computation.133 | convolution fusion | flops 23622320128 | bytes 42991616 | tf_op jit(solution)/shard_map/rd,cdf->crf/dot_general | solution.py:154
  490.9 57.7 %all-gather.9.cloned.1.call-done = bf16[2048,2048]{1,0:T(8,128)(2,1)} async-done(((bf16[512,2048]{1,0:T(8,128)(2,1)}), bf16[2048,2048]{1,0:T(8,128)(2,1)}) %all-gather.9.cloned.1.call-update) | async-done | bytes 8388624 | tf_op jit(solution)/shard_map/all_gather | solution.py:168
  548.7 24.8 %fusion.131 = (bf16[1,2048,1408]{2,1,0:T(8,128)(2,1)}, bf16[1,2048,1408]{2,1,0:T(8,128)(2,1)}, bf16[2048,1408]{1,0:T(8,128)(2,1)}) fusion(f32[2,2048,1408]{2,1,0:T(8,128)} %convolution_bitcast_fusion.6, bf16[2048,2048]{1,0:T(8,128)(2,1)} %all-gather.9.cloned.1.call-done, bf16[1408,2048]{1,0:T(8,128)(2,1)} %param.16), kind=kOutput, calls=%fused_computation.161 | convolution fusion | flops 11828461568 | bytes 54525952 | tf_op jit(solution)/shard_map/rd,fd->rf/dot_general | solution.py:174
  573.5 31.5 %bitcast_convert_fusion.1 = bf16[2048,2048]{1,0:T(8,128)(2,1)} fusion(bf16[2,2048,1408]{2,1,0:T(8,128)(2,1)} %param.15, bf16[1,2048,1408]{2,1,0:T(8,128)(2,1)} %get-tuple-element.868, bf16[1,2048,1408]{2,1,0:T(8,128)(2,1)} %get-tuple-element.867), kind=kOutput, calls=%fused_computation.132 | convolution fusion | flops 23632281600 | bytes 31457280 | tf_op jit(solution)/shard_map/crf,cdf->rd/dot_general | solution.py:185
  605.1 86.5 %reduce-scatter.9.cloned.1.call-done = bf16[512,2048]{1,0:T(8,128)(2,1)} async-done(((bf16[2048,2048]{1,0:T(8,128)(2,1)}), bf16[512,2048]{1,0:T(8,128)(2,1)}) %reduce-scatter.9.cloned.1.call-update) | async-done | bytes 2097168 | tf_op jit(solution)/shard_map/reduce_scatter | solution.py:184
  696.3 4.1 multiply_convert_fusion.5
  702.1 5.5 copy.85
  707.6 19.4 %convolution_convert_fusion.2 = bf16[1408,2048]{1,0:T(8,128)(2,1)} fusion(bf16[2048,1408]{1,0:T(8,128)(2,1)} %get-tuple-element.869, bf16[2048,2048]{1,0:T(8,128)(2,1)} %all-gather.9.cloned.1.call-done), kind=kOutput, calls=%fused_computation.156 | convolution fusion | flops 11814043648 | bytes 19922944 | tf_op jit(solution)/shard_map/rf,rd->fd/dot_general | solution.py:171
  727.1 31.5 %convert_bitcast_fusion = bf16[2,2048,1408]{1,2,0:T(8,128)(2,1)} fusion(bf16[2048,2048]{1,0:T(8,128)(2,1)} %all-gather.7.cloned.1.call-done, bf16[1,2048,1408]{2,1,0:T(8,128)(2,1)} %get-tuple-element.868, bf16[1,2048,1408]{2,1,0:T(8,128)(2,1)} %get-tuple-element.867), kind=kOutput, calls=%fused_computation.137 | convolution fusion | flops 23633854464 | bytes 31457280 | tf_op jit(solution)/shard_map/rd,crf->cdf/dot_general | solution.py:180
  758.6 29.6 %all-gather.11.cloned.1.call-done = bf16[2048,2048]{1,0:T(8,128)(2,1)} async-done(((bf16[512,2048]{1,0:T(8,128)(2,1)}), bf16[2048,2048]{1,0:T(8,128)(2,1)}) %all-gather.11.cloned.1.call-update) | async-done | bytes 8388624 | tf_op jit(solution)/shard_map/all_gather | solution.py:194
  788.2 8.8 convolution_convert_fusion.4
  797.0 6.7 convert_multiply_fusion.6
  803.7 5.2 reshape.177
  809.0 5.2 copy.84
  814.2 4.4 multiply_reduce_fusion
  829.0 150.3 %while.43 = (s32[]{:T(128)}, f32[4,128,128]{2,1,0:T(8,128)S(1)}, f32[8,256,4,128]{3,2,1,0:T(4,128)}, f32[8,256,4,128]{3,2,1,0:T(4,128)}, bf16[8,256,4,128]{1,3,2...) while((s32[]{:T(128)}, f32[4,128,128]{2,1,0:T(8,128)S(1)}, ...), condition=%wide.region_12.13_spmd.clone.clone.clone.clone, body=%wide.region_11.12_spmd.clone.clone.clone.sunk.clone | while | flops 1144522752 | bytes 16679246 | solution.py:208
  979.3 5.5 reshape.178
  984.8 5.5 reshape.179
  990.2 4.4 copy.89
  994.6 4.1 stack_reshape.4
  998.7 7.5 multiply_convert_fusion.4
  1006.2 10.7 convolution_convert_fusion.3
  1017.0 20.7 %convert_bitcast_fusion.1 = bf16[4,2048,512]{1,2,0:T(8,128)(2,1)} fusion(bf16[2048,2048]{1,0:T(8,128)(2,1)S(1)} %bitcast.313, bf16[1,2048,512]{2,1,0:T(8,128)(2,1)S(1)} %copy-done.16, bf16[1,2048,512]{2,1,0:T(8,128)(2,1)S(1)} %copy-done.20, bf16[1,2048,512]{2,1,0:T(8,128)(2,1)S(1)} %get-tuple-element.871, bf16[1,2048,512]{2,1,0:T(8,128)(2,1)S(1)} %get-tuple-element.870), kind=kOutput, calls=%fused_computation.148 | convolution fusion | flops 17196646400 | bytes 25165824 | tf_op jit(solution)/shard_map/rd,cre->cde/dot_general | solution.py:229
  1037.7 23.9 %bitcast_convert_fusion = bf16[2048,2048]{1,0:T(8,128)(2,1)} fusion(bf16[4,2048,512]{2,1,0:T(8,128)(2,1)} %param.13, bf16[1,2048,512]{2,1,0:T(8,128)(2,1)} %get-tuple-element.877, bf16[1,2048,512]{2,1,0:T(8,128)(2,1)} %stack_reshape.4, bf16[1,2048,512]{2,1,0:T(8,128)(2,1)} %copy-done.19, bf16[1,2048,512]{2,1,0:T(8,128)(2,1)} %copy-done.18), kind=kOutput, calls=%fused_computation.131 | convolution fusion | flops 17196646400 | bytes 25165824 | tf_op jit(solution)/shard_map/cre,cde->rd/dot_general | solution.py:234
  1061.7 18.7 %convolution_convert_fusion = bf16[2048,2048]{1,0:T(8,128)(2,1)} fusion(bf16[2048,1408]{1,0:T(8,128)(2,1)} %get-tuple-element.869, bf16[1408,2048]{1,0:T(8,128)(2,1)} %param.16), kind=kOutput, calls=%fused_computation.154 | convolution fusion | flops 11815354368 | bytes 19922944 | tf_op jit(solution)/shard_map/dot_general | solution.py:159
  1080.3 499.4 %all-reduce.3.cloned.1.call-done = (bf16[4,2048,512]{1,2,0:T(8,128)(2,1)}, bf16[2,2048,1408]{1,2,0:T(8,128)(2,1)}, bf16[512,2048]{1,0:T(8,128)(2,1)}, bf16[1408,2048]{1,0:T(8,128)(2,1)}) async-done(((bf16[4,2048,512]{1,2,0:T(8,128)(2,1)}, bf16[2,2048,1408]{1,2,0:T(8,128)(2,1)}, bf16[512,2048]{1,0:T(8,128)(2,1)}, bf16[1408,2048]{1,0:T(8,128)(2,1)}), (bf16[4,2048,512]{1,2,0:T(8,128)(2,1)}, ...) | async-done | bytes 27787280 | tf_op jit(solution)/shard_map/psum | solution.py:244
  1579.8 17.1 copy.93
  1596.8 12.8 copy.92
  1609.6 8.9 convert_element_type.214
  1621.1 48.3 %reduce-scatter.11.cloned.1.call-done = bf16[512,2048]{1,0:T(8,128)(2,1)} async-done(((bf16[2048,2048]{1,0:T(8,128)(2,1)}), bf16[512,2048]{1,0:T(8,128)(2,1)}) %reduce-scatter.11.cloned.1.call-update) | async-done | bytes 2097168 | tf_op jit(solution)/shard_map/reduce_scatter | solution.py:233
  1672.3 86.9 %reduce-scatter.7.cloned.1.call-done = bf16[512,2048]{1,0:T(8,128)(2,1)} async-done(((bf16[2048,2048]{1,0:T(8,128)(2,1)}), bf16[512,2048]{1,0:T(8,128)(2,1)}) %reduce-scatter.7.cloned.1.call-update) | async-done | bytes 2097168 | tf_op jit(solution)/shard_map/reduce_scatter | solution.py:158
  1759.3 7.6 fusion.140
  (376 shorter events, 284.5 us)
Async XLA Ops:
  7.2 261.7 %copy-start = (bf16[512,2048]{1,0:T(8,128)(2,1)S(1)}, bf16[512,2048]{1,0:T(8,128)(2,1)}, u32[]{:S(2)}) copy-start(bf16[512,2048]{1,0:T(8,128)(2,1)} %param.14) | copy-start | bytes 6291460
  7.2 6.9 copy-start.49
  7.2 7.5 copy-start.50
  7.2 97.2 %all-gather.5.cloned.1.call-start = ((), (), s32[]{:S(2)}) async-start(), calls=%async_computation.4 | async-start | bytes 10485760 | tf_op jit(solution)/shard_map/all_gather | solution.py:130
  14.0 348.4 %reduce-scatter.5.cloned.1.call-start = ((), (), s32[]{:S(2)}) async-start(), calls=%async_computation.5 | async-start | bytes 10485760 | tf_op jit(solution)/shard_map/reduce_scatter | solution.py:145
  125.9 8.7 copy-start.5
  249.3 7.9 copy-start.27
  249.3 7.9 copy-start.29
  249.3 7.9 copy-start.34
  249.3 7.9 copy-start.36
  249.3 7.9 copy-start.51
  249.3 7.9 copy-start.53
  257.3 10.2 copy-start.21
  275.8 182.9 %all-gather.7.cloned.1.call-start = ((), (), s32[]{:S(2)}) async-start(), calls=%async_computation.6 | async-start | bytes 10485760 | tf_op jit(solution)/shard_map/all_gather | solution.py:153
  276.6 94.2 %copy-start.31 = (f32[512]{0:T(512)}, f32[512]{0:T(512)S(1)}, u32[]{:S(2)}) copy-start(f32[512]{0:T(512)S(1)} %dynamic_slice.72) | copy-start | bytes 6148
  370.9 177.8 %all-gather.9.cloned.1.call-start = ((), (), s32[]{:S(2)}) async-start(), calls=%async_computation.8 | async-start | bytes 10485760 | tf_op jit(solution)/shard_map/all_gather | solution.py:168
  371.4 320.2 %reduce-scatter.9.cloned.1.call-start = ((), (), s32[]{:S(2)}) async-start(), calls=%async_computation.9 | async-start | bytes 10485760 | tf_op jit(solution)/shard_map/reduce_scatter | solution.py:184
  605.0 86.6 %copy-start.32 = (f32[512]{0:T(512)S(1)}, f32[512]{0:T(512)}, u32[]{:S(2)}) copy-start(f32[512]{0:T(512)} %copy-done.31) | copy-start | bytes 6148
  605.0 90.7 %copy-start.42 = (f32[512]{0:T(512)S(1)}, f32[512]{0:T(512)}, u32[]{:S(2)}) copy-start(f32[512]{0:T(512)} %copy-done.41) | copy-start | bytes 6148
  605.0 91.3 %copy-start.39 = (f32[512]{0:T(512)S(1)}, f32[512]{0:T(512)}, u32[]{:S(2)}) copy-start(f32[512]{0:T(512)} %copy-done.38) | copy-start | bytes 6148
  605.0 183.2 %all-gather.11.cloned.1.call-start = ((), (), s32[]{:S(2)}) async-start(), calls=%async_computation.10 | async-start | bytes 10485760 | tf_op jit(solution)/shard_map/all_gather | solution.py:194
  700.5 879.3 %all-reduce.3.cloned.1.call-start = ((), (), s32[]{:S(2)}) async-start(), calls=%async_computation.12 | async-start | bytes 55574528 | tf_op jit(solution)/shard_map/psum | solution.py:244
  788.2 8.8 copy-start.7
  788.2 8.8 copy-start.9
  809.0 9.7 copy-start.24
  840.9 6.9 copy-start.26
  859.7 6.9 copy-start.26
  878.4 6.9 copy-start.26
  897.2 6.9 copy-start.26
  916.0 6.9 copy-start.26
  934.8 6.9 copy-start.26
  953.6 6.9 copy-start.26
  972.4 6.9 copy-start.26
  998.7 7.5 copy-start.15
  998.7 18.2 %slice-start = ((s8[8388608]{0:T(1024)(128)(4,1)}), s8[4194304]{0:T(1024)(128)(4,1)S(1)}, s32[]{:S(2)}) async-start(s8[8388608]{0:T(1024)(128)(4,1)} %bitcast.312), calls=%async_computation.13 | async-start | bytes 8388608
  1006.2 10.7 copy-start.18
  1006.2 10.7 copy-start.19
  1006.2 10.7 copy-start.16
  1006.2 10.7 copy-start.20
  1006.2 10.7 slice-start.1
  1037.7 631.8 %reduce-scatter.11.cloned.1.call-start = ((), (), s32[]{:S(2)}) async-start(), calls=%async_computation.11 | async-start | bytes 10485760 | tf_op jit(solution)/shard_map/reduce_scatter | solution.py:233
  1061.6 697.6 %reduce-scatter.7.cloned.1.call-start = ((), (), s32[]{:S(2)}) async-start(), calls=%async_computation.7 | async-start | bytes 10485760 | tf_op jit(solution)/shard_map/reduce_scatter | solution.py:158
  1609.6 8.9 copy-start.17
  1618.6 53.7 %copy-start.46 = (f32[512]{0:T(512)S(1)}, f32[512]{0:T(512)}, u32[]{:S(2)}) copy-start(f32[512]{0:T(512)} %copy-done.45) | copy-start | bytes 6148
  1618.6 140.7 %copy-start.33 = (f32[512]{0:T(512)S(1)}, f32[512]{0:T(512)}, u32[]{:S(2)}) copy-start(f32[512]{0:T(512)} %copy-done.31) | copy-start | bytes 6148
  1618.6 140.7 %copy-start.40 = (f32[512]{0:T(512)S(1)}, f32[512]{0:T(512)}, u32[]{:S(2)}) copy-start(f32[512]{0:T(512)} %copy-done.38) | copy-start | bytes 6148
  1618.6 140.7 %copy-start.44 = (f32[512]{0:T(512)S(1)}, f32[512]{0:T(512)}, u32[]{:S(2)}) copy-start(f32[512]{0:T(512)} %copy-done.43) | copy-start | bytes 6148
  1618.6 140.7 %copy-start.48 = (f32[512]{0:T(512)S(1)}, f32[512]{0:T(512)}, u32[]{:S(2)}) copy-start(f32[512]{0:T(512)} %copy-done.47) | copy-start | bytes 6148
  (25 other events, 103.1 us)
Sparse Core Ops, SparseCore 0:
  14.1 90.2 all-gather.4
  275.9 86.4 reduce-scatter.4
  371.0 87.5 all-gather.6
  461.0 87.6 all-gather.8
  605.1 86.4 reduce-scatter.8
  700.6 87.5 all-gather.10
  1037.8 541.9 all-reduce.2
  1582.8 86.5 reduce-scatter.10
  1672.8 86.3 reduce-scatter.6
where the time goes:
time: 1790 us; the launch traced here: 1770 us
  waiting for transfers between devices  1070 us (60%)
  matrix products  417 us (23%)
  local copies, waits for them, and re-layouts  175 us (10%)
  other arithmetic  96.7 us (5%)
    psum x1, waiting for transfers between devices, per_device(): lax.psum(grad_mix.astype(jnp.bfloat16), 'wide').astype(jnp.float32)  499 us
    all_gather x1, waiting for transfers between devices, per_device(): gathered_two = lax.all_gather(normed_two_low, 'narrow', axis=0, tiled=True)  87.1 us
    reduce_scatter x1, waiting for transfers between devices, per_device(): lax.psum_scatter(jnp.dot(hidden_low, ffn_out_weight, preferred_element_ty...  86.9 us
    reduce_scatter x1, waiting for transfers between devices, per_device(): lax.psum_scatter(jnp.einsum('crf,cdf->rd', grad_slice, ffn_in_weight, pre...  86.5 us
    all_gather x1, waiting for transfers between devices, per_device(): gathered = lax.all_gather(normed_low, 'narrow', axis=0, tiled=True)  86.3 us
    reduce_scatter x1, waiting for transfers between devices, per_device(): lax.psum_scatter(jnp.dot(gated_low, out_weight, preferred_element_type=jn...  85.7 us
    all_gather x1, waiting for transfers between devices, per_device(): lax.all_gather((valid_rows * grad_rows).astype(jnp.bfloat16), 'narrow', a...  57.7 us
    reduce_scatter x1, waiting for transfers between devices, per_device(): lax.psum_scatter(jnp.einsum('cre,cde->rd', grad_slice, mix_weight, prefer...  48.3 us
  transfers between devices with their start and end apart: 9, of which 9 were waited for; matrix products, arithmetic and copies ran while one was open for 10% of the time, Pallas kernels for 0%

commit v1 on v0

--- a/solution.py
+++ b/solution.py
@@ -1,6 +1,10 @@
+import functools
+
 import jax
 import jax.numpy as jnp
 from jax import lax
+from jax.experimental import pallas as pl
+from jax.experimental.pallas import tpu as pltpu
 from jax.sharding import PartitionSpec as P
 
 HEADS = 16
@@ -106,7 +110,7 @@
     return (grad_state, (grad_queries, grad_keys, grad_values))
 
 
-def per_device(
+def general_device(
     hidden, mix_weight, out_weight, ffn_in_weight, ffn_out_weight, seq_lengths, block_seq, cotangent
 ):
     local_rows = hidden.shape[0]
@@ -249,7 +253,513 @@
     return (layer_out, input_grad, grad_mix, grad_out_weight, grad_ffn_in, grad_ffn_out)
 
 
+HALF = BLK
+PIECE = 2 * BLK
+LINE = ((0, 1), (3, 2))
+MIDDLE = ((1, 2), (2, 1))
+BACK = ((1, 0), (2, 3))
+VMEM = 60 * 1024 * 1024
+
+
+def over_x(rows):
+    return lax.ppermute(rows, "narrow", [(at, at ^ 1) for at in range(4)])
+
+
+def over_y(rows):
+    return lax.ppermute(rows, "narrow", [(at, at ^ 2) for at in range(4)])
+
+
+def over_core(rows):
+    return lax.ppermute(rows, "wide", [(at, at ^ 1) for at in range(8)])
+
+
+def over_z(rows, pairs):
+    return lax.ppermute(rows, "wide", [(2 * a + c, 2 * b + c) for a, b in pairs for c in range(2)])
+
+
+def add_low(*terms):
+    return sum(term.astype(jnp.float32) for term in terms).astype(jnp.bfloat16)
+
+
+def gather_pieces(top, low):
+    top_x, low_y = over_x(top), over_y(low)
+    low_x, top_y = over_x(low), over_y(top)
+    low_d, top_d = over_x(low_y), over_y(top_x)
+    return ((top, low), (top_x, low_y), (low_x, top_y), (top_d, low_d))
+
+
+def scatter_pieces(own, first, second, third):
+    (top, low), (top_x, low_y), (low_x, top_y), (top_d, low_d) = own, first, second, third
+    to_top_x, to_low_y = over_y(top_d), over_x(low_d)
+    to_top, to_low = over_y(top_y), over_x(low_x)
+    more_top, more_low = over_x(add_low(top_x, to_top_x)), over_y(add_low(low_y, to_low_y))
+    total_top = top.astype(jnp.float32) + to_top.astype(jnp.float32) + more_top.astype(jnp.float32)
+    total_low = low.astype(jnp.float32) + to_low.astype(jnp.float32) + more_low.astype(jnp.float32)
+    return total_top, total_low
+
+
+def slot_tables(narrow_index, fresh_block):
+    block_ids = jnp.arange(NBLK, dtype=jnp.int32)
+    partner = (block_ids // 2) ^ narrow_index
+    even = jnp.array([0, 2, 5, 6], jnp.int32)[partner]
+    odd = jnp.array([1, 4, 3, 7], jnp.int32)[partner]
+    return jnp.where(block_ids % 2 == 0, even, odd), fresh_block.astype(jnp.int32)
+
+
+def wide_sum(grad):
+    wide_index = lax.axis_index("wide")
+    z, core = wide_index // 2, wide_index % 2
+    rows, columns = grad.shape
+    quarters = grad.reshape(2, 2, rows // 4, columns)
+    mine = lax.dynamic_index_in_dim(quarters, core, 0, keepdims=False)
+    other = lax.dynamic_index_in_dim(quarters, 1 - core, 0, keepdims=False)
+    both = add_low(mine, over_core(other))
+    lined = add_low(both, over_z(both, LINE))
+    inner = jnp.where(z == 1, 0, 1)
+    kept = lax.dynamic_index_in_dim(lined, inner, 0, keepdims=False)
+    sent = lax.dynamic_index_in_dim(lined, 1 - inner, 0, keepdims=False)
+    total = add_low(kept, over_z(sent, MIDDLE))
+    passed = over_z(total, MIDDLE)
+    full = jnp.where(z == 1, jnp.stack([total, passed]), jnp.stack([passed, total]))
+    end = (z == 0) | (z == 3)
+    result = jnp.where(end, over_z(full, BACK), full)
+    partner = over_core(result)
+    result = jnp.where(core == 0, jnp.stack([result, partner]), jnp.stack([partner, result]))
+    return result.reshape(rows, columns).astype(jnp.float32)
+
+
+def load_pair(top_ref, low_ref, rows_ref, sems, at):
+    return (
+        pltpu.make_async_copy(top_ref, rows_ref.at[pl.ds(0, HALF)], sems.at[at]),
+        pltpu.make_async_copy(low_ref, rows_ref.at[pl.ds(HALF, HALF)], sems.at[at + 1]),
+    )
+
+
+def across(left, right):
+    return lax.dot_general(left, right, (((1,), (1,)), ((), ())), preferred_element_type=jnp.float32)
+
+
+def down(left, right):
+    return lax.dot_general(left, right, (((0,), (0,)), ((), ())), preferred_element_type=jnp.float32)
+
+
+def straight(left, right):
+    return jnp.dot(left, right, preferred_element_type=jnp.float32)
+
+
+def any_specs(count):
+    return [pl.BlockSpec(memory_space=pl.ANY)] * count
+
+
+def cost(flops, bytes_accessed):
+    return pl.CostEstimate(flops=int(flops), bytes_accessed=int(bytes_accessed), transcendentals=0)
+
+
+def project_piece(pair, weight, kept, piece):
+    parts, width, columns = weight.shape
+    group_rows = NBLK * BLK
+
+    def body(*refs):
+        top_ref, low_ref, weight_ref = refs[:3]
+        rows_ref, out_ref, sems = refs[-3:]
+
+        @pl.when(pl.program_id(0) == 0)
+        def _():
+            copies = load_pair(top_ref, low_ref, rows_ref, sems, 0)
+            for copy in copies:
+                copy.start()
+            for copy in copies:
+                copy.wait()
+
+        out_ref[0] = straight(rows_ref[...], weight_ref[0]).astype(jnp.bfloat16)
+
+    return pl.pallas_call(
+        body,
+        grid=(parts,),
+        in_specs=any_specs(2)
+        + [pl.BlockSpec((1, width, columns), lambda c: (c, 0, 0))]
+        + any_specs(len(kept)),
+        out_specs=[
+            pl.BlockSpec((PIECE, width), lambda c: (piece, 0)),
+            pl.BlockSpec((1, PIECE, columns), lambda c: (c, piece, 0)),
+        ],
+        out_shape=[
+            jax.ShapeDtypeStruct((group_rows, width), jnp.bfloat16),
+            jax.ShapeDtypeStruct((parts, group_rows, columns), jnp.bfloat16),
+        ],
+        scratch_shapes=[pltpu.SemaphoreType.DMA((2,))],
+        input_output_aliases={3 + at: at for at in range(len(kept))},
+        compiler_params=pltpu.CompilerParams(vmem_limit_bytes=VMEM),
+        cost_estimate=cost(2 * PIECE * parts * width * columns, 2 * parts * width * columns + 8e6),
+        name="project",
+    )(*pair, weight, *kept)
+
+
+def back_piece(pair, weight, kept, piece):
+    columns, width = weight.shape
+    group_rows = NBLK * BLK
+
+    def body(*refs):
+        top_ref, low_ref, weight_ref = refs[:3]
+        rows_ref, out_ref, sems = refs[-3:]
+        copies = load_pair(top_ref, low_ref, rows_ref, sems, 0)
+        for copy in copies:
+            copy.start()
+        for copy in copies:
+            copy.wait()
+        out_ref[...] = across(rows_ref[...], weight_ref[...]).astype(jnp.bfloat16)
+
+    return pl.pallas_call(
+        body,
+        grid=(1,),
+        in_specs=any_specs(2)
+        + [pl.BlockSpec((columns, width), lambda c: (0, 0))]
+        + any_specs(len(kept)),
+        out_specs=[
+            pl.BlockSpec((PIECE, width), lambda c: (piece, 0)),
+            pl.BlockSpec((PIECE, columns), lambda c: (piece, 0)),
+        ],
+        out_shape=[
+            jax.ShapeDtypeStruct((group_rows, width), jnp.bfloat16),
+            jax.ShapeDtypeStruct((group_rows, columns), jnp.bfloat16),
+        ],
+        scratch_shapes=[pltpu.SemaphoreType.DMA((2,))],
+        input_output_aliases={3 + at: at for at in range(len(kept))},
+        compiler_params=pltpu.CompilerParams(vmem_limit_bytes=VMEM),
+        cost_estimate=cost(2 * PIECE * width * columns, 2 * width * columns + 6e6),
+        name="back_project",
+    )(*pair, weight, *kept)
+
+
+def sum_piece(acts, weight, piece, transposed):
+    parts, group_rows, columns = acts.shape
+    width = weight.shape[1] if transposed else weight.shape[2]
+
+    def body(act_ref, weight_ref, top_ref, low_ref, total):
+        part = pl.program_id(0)
+        product = (across if transposed else straight)(act_ref[0], weight_ref[0])
+
+        @pl.when(part == 0)
+        def _():
+            total[...] = product
+
+        @pl.when(part > 0)
+        def _():
+            total[...] += product
+
+        @pl.when(part == parts - 1)
+        def _():
+            top_ref[...] = total[:HALF].astype(jnp.bfloat16)
+            low_ref[...] = total[HALF:].astype(jnp.bfloat16)
+
+    return pl.pallas_call(
+        body,
+        grid=(parts,),
+        in_specs=[
+            pl.BlockSpec((1, PIECE, columns), lambda c: (c, piece, 0)),
+            pl.BlockSpec((1,) + weight.shape[1:], lambda c: (c, 0, 0)),
+        ],
+        out_specs=[pl.BlockSpec((HALF, width), lambda c: (0, 0))] * 2,
+        out_shape=[jax.ShapeDtypeStruct((HALF, width), jnp.bfloat16)] * 2,
+        scratch_shapes=[pltpu.VMEM((PIECE, width), jnp.float32)],
+        compiler_params=pltpu.CompilerParams(vmem_limit_bytes=VMEM),
+        cost_estimate=cost(2 * PIECE * parts * width * columns, 2 * parts * width * columns + 4e6),
+        name="partial_sum",
+    )(acts, weight)
+
+
+def unit_piece(pair, grad_pair, ffn_in, ffn_out, kept, piece):
+    _, width, units = ffn_in.shape
+    group_rows = NBLK * BLK
+    tile = 256
+    steps = pl.cdiv(units, tile)
+    last = units - (steps - 1) * tile
+
+    def body(*refs):
+        top_ref, low_ref, grad_top_ref, grad_low_ref, in_ref, out_ref = refs[:6]
+        rows_ref, grads_ref, act_ref, parts_ref = refs[-11:-7]
+        sum_refs = refs[-7:-3]
+        total_back, total_two, sems = refs[-3:]
+        step = pl.program_id(0)
+
+        @pl.when(step == 0)
+        def _():
+            copies = load_pair(top_ref, low_ref, rows_ref, sems, 0)
+            copies += load_pair(grad_top_ref, grad_low_ref, grads_ref, sems, 2)
+            for copy in copies:
+                copy.start()
+            total_back[...] = jnp.zeros_like(total_back)
+            total_two[...] = jnp.zeros_like(total_two)
+            for copy in copies:
+                copy.wait()
+
+        def work(size):
+            rows = rows_ref[...]
+            weight_a, weight_b = in_ref[0, :, :size], in_ref[1, :, :size]
+            weight_out = out_ref[:size, :]
+            part_a = straight(rows, weight_a)
+            part_b = straight(rows, weight_b)
+            grad_act = across(grads_ref[...], weight_out)
+            act = (part_a * part_b).astype(jnp.bfloat16)
+            grad_a = (grad_act * part_b).astype(jnp.bfloat16)
+            grad_b = (grad_act * part_a).astype(jnp.bfloat16)
+            act_ref[:, :size] = act
+            parts_ref[0, :, :size] = grad_a
+            parts_ref[1, :, :size] = grad_b
+            total_two[...] += straight(act, weight_out)
+            total_back[...] += across(grad_a, weight_a) + across(grad_b, weight_b)
+
+        if last == tile:
+            work(tile)
+        else:
+            pl.when(step < steps - 1)(lambda: work(tile))
+            pl.when(step == steps - 1)(lambda: work(last))
+
+        @pl.when(step == steps - 1)
+        def _():
+            for total, top_out, low_out in (
+                (total_back, sum_refs[0], sum_refs[1]),
+                (total_two, sum_refs[2], sum_refs[3]),
+            ):
+                top_out[...] = total[:HALF].astype(jnp.bfloat16)
+                low_out[...] = total[HALF:].astype(jnp.bfloat16)
+
+    low = jnp.bfloat16
+    return pl.pallas_call(
+        body,
+        grid=(steps,),
+        in_specs=any_specs(4)
+        + [
+            pl.BlockSpec((2, width, tile), lambda f: (0, 0, f)),
+            pl.BlockSpec((tile, width), lambda f: (f, 0)),
+        ]
+        + any_specs(len(kept)),
+        out_specs=[
+            pl.BlockSpec((PIECE, width), lambda f: (piece, 0)),
+            pl.BlockSpec((PIECE, width), lambda f: (piece, 0)),
+            pl.BlockSpec((PIECE, tile), lambda f: (piece, f)),
+            pl.BlockSpec((2, PIECE, tile), lambda f: (0, piece, f)),
+        ]
+        + [pl.BlockSpec((HALF, width), lambda f: (0, 0))] * 4,
+        out_shape=[
+            jax.ShapeDtypeStruct((group_rows, width), low),
+            jax.ShapeDtypeStruct((group_rows, width), low),
+            jax.ShapeDtypeStruct((group_rows, units), low),
+            jax.ShapeDtypeStruct((2, group_rows, units), low),
+        ]
+        + [jax.ShapeDtypeStruct((HALF, width), low)] * 4,
+        scratch_shapes=[
+            pltpu.VMEM((PIECE, width), jnp.float32),
+            pltpu.VMEM((PIECE, width), jnp.float32),
+            pltpu.SemaphoreType.DMA((4,)),
+        ],
+        input_output_aliases={6 + at: at for at in range(len(kept))},
+        compiler_params=pltpu.CompilerParams(vmem_limit_bytes=VMEM),
+        cost_estimate=cost(12 * PIECE * width * units, 6 * width * units + 12e6),
+        name="gated_unit",
+    )(*pair, *grad_pair, ffn_in, ffn_out, *kept)
+
+
+def block_decays(rate):
+    row = lax.broadcasted_iota(jnp.int32, (BLK, BLK), 0)
+    column = lax.broadcasted_iota(jnp.int32, (BLK, BLK), 1)
+    distance = (row - column).astype(jnp.float32)
+    within = jnp.where(row >= column, jnp.exp(-rate * jnp.maximum(distance, 0.0)), 0.0)
+    place = lax.broadcasted_iota(jnp.int32, (BLK, 1), 0).astype(jnp.float32)
+    entry = jnp.exp(-rate * (place + 1.0))
+    leave = jnp.exp(-rate * (BLK - 1.0 - place))
+    whole = jnp.exp(jnp.full((1, HS), -BLK * rate, jnp.float32))
+    return within, entry, leave, whole
+
+
+def mix_forward(slots, fresh, rates, parts):
+    _, group_rows, columns = parts.shape
+    heads = columns // HS
+    low = jnp.bfloat16
+
+    def body(slot_ref, fresh_ref, rate_ref, parts_ref, gated_ref, mixing_ref, states_ref):
+        within, entry, leave, whole = block_decays(rate_ref[pl.program_id(0)])
+        state = jnp.zeros((HS, HS), jnp.float32)
+        for block in range(NBLK):
+            rows = pl.ds(pl.multiple_of(slot_ref[block] * BLK, BLK), BLK)
+            queries = jax.nn.silu(parts_ref[0, rows, :].astype(jnp.float32)).astype(low)
+            keys = jax.nn.silu(parts_ref[1, rows, :].astype(jnp.float32))
+            values = parts_ref[2, rows, :]
+            gate = parts_ref[3, rows, :].astype(jnp.float32)
+            state = jnp.where(fresh_ref[block] != 0, 0.0, state)
+            state_low = state.astype(low)
+            states_ref[0, block] = state_low
+            weights = (across(queries, keys.astype(low)) * within).astype(low)
+            mixing = straight(weights, values) + entry * straight(queries, state_low)
+            late_keys = (keys.astype(low).astype(jnp.float32) * leave).astype(low)
+            state = whole * state + down(late_keys, values)
+            scale = lax.rsqrt(jnp.mean(mixing * mixing, axis=-1, keepdims=True) + head_floor)
+            gated_ref[0, rows, :] = (mixing * scale * gate).astype(low)
+            mixing_ref[rows, :] = mixing.astype(low)
+
+    return pl.pallas_call(
+        body,
+        grid_spec=pltpu.PrefetchScalarGridSpec(
+            num_scalar_prefetch=3,
+            grid=(heads,),
+            in_specs=[pl.BlockSpec((4, group_rows, HS), lambda h, *_: (0, 0, h))],
+            out_specs=[
+                pl.BlockSpec((1, group_rows, HS), lambda h, *_: (0, 0, h)),
+                pl.BlockSpec((group_rows, HS), lambda h, *_: (0, h)),
+                pl.BlockSpec((1, NBLK, HS, HS), lambda h, *_: (h, 0, 0, 0)),
+            ],
+        ),
+        out_shape=[
+            jax.ShapeDtypeStruct((1, group_rows, columns), low),
+            jax.ShapeDtypeStruct((group_rows, columns), low),
+            jax.ShapeDtypeStruct((heads, NBLK, HS, HS), low),
+        ],
+        compiler_params=pltpu.CompilerParams(vmem_limit_bytes=VMEM),
+        cost_estimate=cost(8e9, 14e6),
+        name="mix_forward",
+    )(slots, fresh, rates, parts)
+
+
+def mix_backward(slots, fresh, rates, parts, mixing_all, states, grad_gated):
+    _, group_rows, columns = parts.shape
+    heads = columns // HS
+    low = jnp.bfloat16
+
+    def body(
+        slot_ref, fresh_ref, rate_ref, parts_ref, mixing_ref, states_ref, grad_ref, out_ref
+    ):
+        within, entry, leave, whole = block_decays(rate_ref[pl.program_id(0)])
+        later = jnp.zeros((HS, HS), jnp.float32)
+        for block in reversed(range(NBLK)):
+            rows = pl.ds(pl.multiple_of(slot_ref[block] * BLK, BLK), BLK)
+            raw_queries = parts_ref[0, rows, :].astype(jnp.float32)
+            raw_keys = parts_ref[1, rows, :].astype(jnp.float32)
+            queries_float = jax.nn.silu(raw_queries).astype(low).astype(jnp.float32)
+            queries, keys = queries_float.astype(low), jax.nn.silu(raw_keys).astype(low)
+            values = parts_ref[2, rows, :]
+            gate = parts_ref[3, rows, :].astype(jnp.float32)
+            mixing = mixing_ref[rows, :].astype(jnp.float32)
+            grad_gated_rows = grad_ref[rows, :].astype(jnp.float32)
+            scale = lax.rsqrt(jnp.mean(mixing * mixing, axis=-1, keepdims=True) + head_floor)
+            headed = mixing * scale
+            out_ref[3, rows, :] = (grad_gated_rows * headed).astype(low)
+            grad_headed = grad_gated_rows * gate
+            inner = jnp.mean(grad_headed * headed, axis=-1, keepdims=True)
+            grad = (scale * (grad_headed - headed * inner)).astype(low)
+            weights = (across(queries, keys) * within).astype(low)
+            grad_scores = (across(grad, values) * within).astype(low)
+            later_low = later.astype(low)
+            grad_queries = straight(grad_scores, keys) + entry * across(grad, states_ref[0, block])
+            grad_keys = down(grad_scores, queries) + leave * across(values, later_low)
+            grad_values = down(weights, grad) + leave * straight(keys, later_low)
+            early_queries = (queries_float * entry).astype(low)
+            later = jnp.where(fresh_ref[block] != 0, 0.0, whole * later + down(early_queries, grad))
+            out_ref[0, rows, :] = (grad_queries * silu_slope(raw_queries)).astype(low)
+            out_ref[1, rows, :] = (grad_keys * silu_slope(raw_keys)).astype(low)
+            out_ref[2, rows, :] = grad_values.astype(low)
+
+    return pl.pallas_call(
+        body,
+        grid_spec=pltpu.PrefetchScalarGridSpec(
+            num_scalar_prefetch=3,
+            grid=(heads,),
+            in_specs=[
+                pl.BlockSpec((4, group_rows, HS), lambda h, *_: (0, 0, h)),
+                pl.BlockSpec((group_rows, HS), lambda h, *_: (0, h)),
+                pl.BlockSpec((1, NBLK, HS, HS), lambda h, *_: (h, 0, 0, 0)),
+                pl.BlockSpec((group_rows, HS), lambda h, *_: (0, h)),
+            ],
+            out_specs=pl.BlockSpec((4, group_rows, HS), lambda h, *_: (0, 0, h)),
+        ),
+        out_shape=jax.ShapeDtypeStruct(parts.shape, low),
+        compiler_params=pltpu.CompilerParams(vmem_limit_bytes=VMEM),
+        cost_estimate=cost(20e9, 22e6),
+        name="mix_backward",
+    )(slots, fresh, rates, parts, mixing_all, states, grad_gated)
+
+
+def norm_back(values, grad):
+    scale = lax.rsqrt(jnp.mean(values * values, axis=-1, keepdims=True) + epsilon)
+    unit = values * scale
+    return scale * (grad - unit * jnp.mean(grad * unit, axis=-1, keepdims=True))
+
+
+def square_device(
+    hidden, mix_weight, out_weight, ffn_in_weight, ffn_out_weight, seq_lengths, block_seq, cotangent
+):
+    local_rows = hidden.shape[0]
+    head_count = mix_weight.shape[2] // HS
+    narrow_index = lax.axis_index("narrow")
+    valid_all, fresh_block = group_masks(seq_lengths, block_seq)
+    live = lax.dynamic_slice_in_dim(
+        valid_all.astype(jnp.float32), narrow_index * local_rows, local_rows
+    )[:, None]
+    head_ids = narrow_index * head_count + jnp.arange(head_count, dtype=jnp.int32)
+    rates = 2.0 ** (-8.0 * (head_ids.astype(jnp.float32) + 1.0) / HEADS)
+    slots, fresh = slot_tables(narrow_index, fresh_block)
+    low = jnp.bfloat16
+
+    def halves(rows):
+        return rows[:HALF], rows[HALF:]
+
+    lives = halves(live)
+    inputs = [rows.astype(jnp.float32) for rows in halves(hidden)]
+    grads_in = [rows.astype(jnp.float32) for rows in halves(cotangent)]
+
+    pieces = gather_pieces(*(row_norm(rows).astype(low) for rows in inputs))
+    kept = ()
+    for at, pair in enumerate(pieces):
+        kept = project_piece(pair, mix_weight, kept, at)
+    normed_all, parts = kept
+    grad_pieces = gather_pieces(*((m * g).astype(low) for m, g in zip(lives, grads_in)))
+
+    gated, mixing, states = mix_forward(slots, fresh, rates, parts)
+    partial = [sum_piece(gated, out_weight[None], at, False) for at in range(4)]
+    branch = scatter_pieces(*partial)
+    middle = [x + m * b for x, m, b in zip(inputs, lives, branch)]
+
+    pieces = gather_pieces(*(row_norm(rows).astype(low) for rows in middle))
+    kept, back_sums, two_sums = (), [], []
+    for at, (pair, grad_pair) in enumerate(zip(pieces, grad_pieces)):
+        *kept, back_top, back_low, two_top, two_low = unit_piece(
+            pair, grad_pair, ffn_in_weight, ffn_out_weight, kept, at
+        )
+        back_sums.append((back_top, back_low))
+        two_sums.append((two_top, two_low))
+    normed_two_all, grad_two_all, act, grad_parts = kept
+    grad_normed_two = scatter_pieces(*back_sums)
+    grad_middle = [g + norm_back(v, n) for g, v, n in zip(grads_in, middle, grad_normed_two)]
+    pieces = gather_pieces(*((m * g).astype(low) for m, g in zip(lives, grad_middle)))
+
+    grad_ffn_out = wide_sum(down(act, grad_two_all).astype(low))
+    grad_ffn_in = jnp.stack(
+        [wide_sum(down(normed_two_all, grad_parts[c]).astype(low)) for c in range(2)]
+    )
+
+    kept = ()
+    for at, pair in enumerate(pieces):
+        kept = back_piece(pair, out_weight, kept, at)
+    grad_branch_all, grad_gated = kept
+    grad_out = wide_sum(down(gated[0], grad_branch_all).astype(low))
+    grad_projected = mix_backward(slots, fresh, rates, parts, mixing, states, grad_gated)
+    partial = [sum_piece(grad_projected, mix_weight, at, True) for at in range(4)]
+    grad_normed = scatter_pieces(*partial)
+    grad_mix = jnp.stack(
+        [wide_sum(down(normed_all, grad_projected[c]).astype(low)) for c in range(4)]
+    )
+    branch_two = scatter_pieces(*two_sums)
+    layer_out = jnp.concatenate(
+        [(v + m * b).astype(low) for v, m, b in zip(middle, lives, branch_two)]
+    )
+    input_grad = jnp.concatenate(
+        [(g + norm_back(x, n)).astype(low) for g, x, n in zip(grad_middle, inputs, grad_normed)]
+    )
+    return (layer_out, input_grad, grad_mix, grad_out, grad_ffn_in, grad_ffn_out)
+
+
 def solution(mesh):
+    square = mesh.shape["wide"] == 8 and mesh.shape["narrow"] == 4
+    per_device = square_device if square else general_device
     in_specs = (
         P(("wide", "narrow"), None),
         P(None, None, "narrow"),

time: 1790 us -> 1350 us (0.75)
  waiting for transfers between devices: 1070 us -> 733 us
  matrix products: 417 us -> 96.9 us
  Pallas kernels: 0 us -> 262 us
  local copies, waits for them, and re-layouts: 175 us -> 19 us
  starting transfers between devices: 0.37 us -> 106 us
  other arithmetic: 96.7 us -> 120 us
    ppermute x0 -> x96, waiting for transfers between devices: none -> 733 us  [the longest x32 492 us: over_z(): lax.ppermute(rows, 'wide', [(2 * a + c, 2 * b + c) for a, b in pairs for...]
    psum x1 -> x0, waiting for transfers between devices: 499 us -> none  [per_device(): lax.psum(grad_mix.astype(jnp.bfloat16), 'wide').astype(jnp.float32)]
    dot_general x100 -> x8, matrix products: 417 us -> 96.9 us  [down(): lax.dot_general(left, right, (((0,), (0,)), ((), ())), preferred_element_...]
    reduce_scatter x4 -> x0, waiting for transfers between devices: 307 us -> none  [the longest x1 86.9 us: per_device(): lax.psum_scatter(jnp.dot(hidden_low, ffn_out_weight, preferred_element_ty...]
    pallas_call x0 -> x22, Pallas kernels: none -> 262 us  [the longest x4 117 us: unit_piece(): pl.pallas_call(body, grid=(steps,), in_specs=any_specs(4) + [pl.BlockSpec...]
    all_gather x4 -> x0, waiting for transfers between devices: 261 us -> none  [the longest x1 87.1 us: per_device(): gathered_two = lax.all_gather(normed_two_low, 'narrow', axis=0, tiled=True)]
    ppermute x0 -> x96, starting transfers between devices: none -> 106 us  [the longest x32 49.1 us: over_z(): lax.ppermute(rows, 'wide', [(2 * a + c, 2 * b + c) for a, b in pairs for...]
    unnamed x116 -> x139, local copies, waits for them, and re-layouts: 42.6 us -> 8.22 us
  transfers between devices with their start and end apart: 9 -> 96, of which waited for: 9 -> 32; matrix products, arithmetic and copies ran while one was open for 10% -> 15% of each run, Pallas kernels for 0% -> 18%
where the time goes in v1:
time: 1350 us; the launch traced here: 1340 us
  waiting for transfers between devices  733 us (54%)
  Pallas kernels  262 us (19%)
  other arithmetic  120 us (9%)
  starting transfers between devices  106 us (8%)
  matrix products  96.9 us (7%)
  local copies, waits for them, and re-layouts  19 us (1%)
    ppermute x32, waiting for transfers between devices, over_z(): lax.ppermute(rows, 'wide', [(2 * a + c, 2 * b + c) for a, b in pairs for...  492 us
    ppermute x24, waiting for transfers between devices, over_x(): return lax.ppermute(rows, 'narrow', [(at, at ^ 1) for at in range(4)])  176 us
    pallas_call x4, Pallas kernels, unit_piece(): pl.pallas_call(body, grid=(steps,), in_specs=any_specs(4) + [pl.BlockSpec...  117 us
    dot_general x8, matrix products, down(): lax.dot_general(left, right, (((0,), (0,)), ((), ())), preferred_element_...  96.9 us
    ppermute x24, waiting for transfers between devices, over_y(): return lax.ppermute(rows, 'narrow', [(at, at ^ 2) for at in range(4)])  64.3 us
    pallas_call x8, Pallas kernels, sum_piece(): pl.pallas_call(body, grid=(parts,), in_specs=[pl.BlockSpec((1, PIECE, col...  57.8 us
    ppermute x32, starting transfers between devices, over_z(): lax.ppermute(rows, 'wide', [(2 * a + c, 2 * b + c) for a, b in pairs for...  49.1 us
    convert_element_type x32, other arithmetic, add_low(): sum((term.astype(jnp.float32) for term in terms)).astype(jnp.bfloat16)  42.7 us
  transfers between devices with their start and end apart: 96, of which 32 were waited for; matrix products, arithmetic and copies ran while one was open for 15% of the time, Pallas kernels for 18%

profile of v1, /device:TPU:0, one launch (start us, length us, event | category | flops | bytes accessed | tf_op | source)
XLA Modules:
  0.0 1340.3 jit_solution(17580704676140238843)
XLA Ops:
  11.2 9.8 project.4
  22.7 31.8 %collective-permute-done.refs_0_ = bf16[256,2048]{1,0:T(8,128)(2,1)} collective-permute-done((bf16[256,2048]{1,0:T(8,128)(2,1)S(1)}, bf16[256,2048]{1,0:T(8,128)(2,1)}, u32[]{:S(2)}, u32[]{:S(2)}) %collective-permute-start) | collective-permute-done | bytes 1048608 | tf_op jit(solution)/shard_map/ppermute | solution.py:265
  59.0 9.8 project.5
  68.8 9.8 project.6
  79.0 9.8 project.7
  88.8 9.8 mix_forward.1
  115.5 13.8 %collective-permute-done.10 = bf16[256,2048]{1,0:T(8,128)(2,1)} collective-permute-done((bf16[256,2048]{1,0:T(8,128)(2,1)}, bf16[256,2048]{1,0:T(8,128)(2,1)}, u32[]{:S(2)}, u32[]{:S(2)}) %collective-permute-start.10) | collective-permute-done | bytes 1048608 | tf_op jit(solution)/shard_map/ppermute | solution.py:265
  142.7 10.3 collective-permute-done.6
  152.9 18.8 %collective-permute-done.11 = bf16[256,2048]{1,0:T(8,128)(2,1)} collective-permute-done((bf16[256,2048]{1,0:T(8,128)(2,1)}, bf16[256,2048]{1,0:T(8,128)(2,1)}, u32[]{:S(2)}, u32[]{:S(2)}) %collective-permute-start.11) | collective-permute-done | bytes 1048608 | tf_op jit(solution)/shard_map/ppermute | solution.py:269
  182.5 29.3 %gated_unit.4 = (bf16[2048,2048]{1,0:T(8,128)(2,1)}, bf16[2048,2048]{1,0:T(8,128)(2,1)}, bf16[2048,1408]{1,0:T(8,128)(2,1)}, bf16[2,2048,1408]{2,1,0:T(8,128)(2,...) custom-call(bf16[256,2048]{1,0:T(8,128)(2,1)} %copy-done.45, ...), custom_call_target="tpu_custom_call" | custom-call | flops 17716740096 | bytes 29301504 | tf_op jit(solution)/shard_map/gated_unit/pallas_call | solution.py:528
  213.4 13.9 %collective-permute-done.16.refs_0_ = bf16[256,2048]{1,0:T(8,128)(2,1)} collective-permute-done((bf16[256,2048]{1,0:T(8,128)(2,1)S(1)}, bf16[256,2048]{1,0:T(8,128)(2,1)}, u32[]{:S(2)}, u32[]{:S(2)}) %collective-permute-start.16) | collective-permute-done | bytes 1048608 | tf_op jit(solution)/shard_map/ppermute | solution.py:265
  228.4 21.3 %collective-permute-done.18.refs_2_ = bf16[256,2048]{1,0:T(8,128)(2,1)S(1)} collective-permute-done((bf16[256,2048]{1,0:T(8,128)(2,1)}, bf16[256,2048]{1,0:T(8,128)(2,1)S(1)}, u32[]{:S(2)}, u32[]{:S(2)}) %collective-permute-start.18) | collective-permute-done | bytes 1048608 | tf_op jit(solution)/shard_map/ppermute | solution.py:265
  251.2 29.0 %gated_unit.5 = (bf16[2048,2048]{1,0:T(8,128)(2,1)}, bf16[2048,2048]{1,0:T(8,128)(2,1)}, bf16[2048,1408]{1,0:T(8,128)(2,1)}, bf16[2,2048,1408]{2,1,0:T(8,128)(2,...) custom-call(bf16[256,2048]{1,0:T(8,128)(2,1)} %collective-permute-do, ...), custom_call_target="tpu_custom_call", output_to_operand_aliasing={{0}: (6, {}), {1}: (7, {}), {2}: (8, {}), {3}: (9, {})} | custom-call | flops 17716740096 | bytes 29301504 | tf_op jit(solution)/shard_map/gated_unit/pallas_call | solution.py:528
  283.4 29.0 %gated_unit.6 = (bf16[2048,2048]{1,0:T(8,128)(2,1)}, bf16[2048,2048]{1,0:T(8,128)(2,1)}, bf16[2048,1408]{1,0:T(8,128)(2,1)}, bf16[2,2048,1408]{2,1,0:T(8,128)(2,...) custom-call(bf16[256,2048]{1,0:T(8,128)(2,1)} %collective-permute-do, ...), custom_call_target="tpu_custom_call", output_to_operand_aliasing={{0}: (6, {}), {1}: (7, {}), {2}: (8, {}), {3}: (9, {})} | custom-call | flops 17716740096 | bytes 29301504 | tf_op jit(solution)/shard_map/gated_unit/pallas_call | solution.py:528
  316.5 12.7 collective-permute-done.23.refs_2_
  329.2 29.2 %gated_unit.7 = (bf16[2048,2048]{1,0:T(8,128)(2,1)}, bf16[2048,2048]{1,0:T(8,128)(2,1)}, bf16[2048,1408]{1,0:T(8,128)(2,1)}, bf16[2,2048,1408]{2,1,0:T(8,128)(2,...) custom-call(bf16[256,2048]{1,0:T(8,128)(2,1)} %copy-done.59, ...), custom_call_target="tpu_custom_call", output_to_operand_aliasing={{0}: (6, {}), {1}: (7, {}), {2}: (8, {}), {3}: (9, {})} | custom-call | flops 17716740096 | bytes 29301504 | tf_op jit(solution)/shard_map/gated_unit/pallas_call | solution.py:528
  358.4 17.2 %convolution_convert_fusion.2 = bf16[2048,1408]{1,0:T(8,128)(2,1)S(1)} fusion(bf16[2048,2048]{1,0:T(8,128)(2,1)} %get-tuple-element.136, bf16[2,2048,1408]{2,1,0:T(8,128)(2,1)} %get-tuple-element.137), kind=kOutput, calls=%fused_computation.6 | convolution fusion | flops 11814043648 | bytes 19922944 | tf_op jit(solution)/shard_map/dot_general | solution.py:343
  375.7 19.4 %convolution_convert_fusion.1 = bf16[2048,1408]{1,0:T(8,128)(2,1)S(1)} fusion(bf16[2048,2048]{1,0:T(8,128)(2,1)} %get-tuple-element.136, bf16[2,2048,1408]{2,1,0:T(8,128)(2,1)} %get-tuple-element.137), kind=kOutput, calls=%fused_computation.5 | convolution fusion | flops 11814043648 | bytes 19922944 | tf_op jit(solution)/shard_map/dot_general | solution.py:343
  397.2 16.3 %convolution_convert_fusion = bf16[1408,2048]{1,0:T(8,128)(2,1)S(1)} fusion(bf16[2048,1408]{1,0:T(8,128)(2,1)} %get-tuple-element.138, bf16[2048,2048]{1,0:T(8,128)(2,1)} %get-tuple-element.139), kind=kOutput, calls=%fused_computation.4 | convolution fusion | flops 11814043648 | bytes 19922944 | tf_op jit(solution)/shard_map/dot_general | solution.py:343
  423.8 23.2 %collective-permute-done.28 = bf16[256,2048]{1,0:T(8,128)(2,1)S(1)} collective-permute-done((bf16[256,2048]{1,0:T(8,128)(2,1)S(1)}, bf16[256,2048]{1,0:T(8,128)(2,1)S(1)}, u32[]{:S(2)}, u32[]{:S(2)}) %collective-permute-start.28) | collective-permute-done | bytes 1048608 | tf_op jit(solution)/shard_map/ppermute | solution.py:265
  448.4 21.0 %collective-permute-done.36 = bf16[256,2048]{1,0:T(8,128)(2,1)S(1)} collective-permute-done((bf16[256,2048]{1,0:T(8,128)(2,1)S(1)}, bf16[256,2048]{1,0:T(8,128)(2,1)S(1)}, u32[]{:S(2)}, u32[]{:S(2)}) %collective-permute-start.36) | collective-permute-done | bytes 1048608 | tf_op jit(solution)/shard_map/ppermute | solution.py:265
  471.0 14.2 %collective-permute-done.32 = bf16[256,2048]{1,0:T(8,128)(2,1)S(1)} collective-permute-done((bf16[256,2048]{1,0:T(8,128)(2,1)S(1)}, bf16[256,2048]{1,0:T(8,128)(2,1)S(1)}, u32[]{:S(2)}, u32[]{:S(2)}) %collective-permute-start.32) | collective-permute-done | bytes 1048608 | tf_op jit(solution)/shard_map/ppermute | solution.py:265
  489.3 13.9 %collective-permute-done.26 = bf16[256,2048]{1,0:T(8,128)(2,1)S(1)} collective-permute-done((bf16[256,2048]{1,0:T(8,128)(2,1)S(1)}, bf16[256,2048]{1,0:T(8,128)(2,1)S(1)}, u32[]{:S(2)}, u32[]{:S(2)}) %collective-permute-start.26) | collective-permute-done | bytes 1048608 | tf_op jit(solution)/shard_map/ppermute | solution.py:265
  517.2 9.2 collective-permute-done.29
  547.8 8.7 collective-permute-done.38.refs_1_
  596.9 18.1 %mix_backward.1.act_ref = bf16[4,2048,512]{2,1,0:T(8,128)(2,1)} custom-call(s32[8]{0:T(128)} %compare_select_fusion.1.slot_ref, s32[8]{0:T(128)} %compare_convert_fusion.fresh_ref, f32[4]{0:T(128)} %multiply_power_fusion.rate_ref, bf16[4,2048,512]{2,1,0:T(8,128)(2,1)} %get-tuple-element.79.parts_ref, bf16[2048,512]{1,0:T(8,128)(2,1)} %get-tuple-element.113.mixing_ref, ...), custom_call_target="tpu_custom_call" | custom-call | flops 20000000000 | bytes 22000000 | tf_op jit(solution)/shard_map/mix_backward/pallas_call | solution.py:661
  615.0 10.1 convolution_convert_fusion.7
  625.0 9.6 convolution_convert_fusion.6
  634.7 9.7 convolution_convert_fusion.5
  650.7 10.0 partial_sum.15
  660.7 10.1 partial_sum.14
  682.4 10.3 partial_sum.13
  694.2 10.2 partial_sum.12
  714.5 19.1 %collective-permute-done.46 = bf16[256,2048]{1,0:T(8,128)(2,1)S(1)} collective-permute-done((bf16[256,2048]{1,0:T(8,128)(2,1)S(1)}, bf16[256,2048]{1,0:T(8,128)(2,1)S(1)}, u32[]{:S(2)}, u32[]{:S(2)}) %collective-permute-start.46) | collective-permute-done | bytes 1048608 | tf_op jit(solution)/shard_map/ppermute | solution.py:265
  750.6 47.7 %collective-permute-done.91 = bf16[2,352,2048]{2,1,0:T(8,128)(2,1)S(1)} collective-permute-done((bf16[2,352,2048]{2,1,0:T(8,128)(2,1)S(1)}, bf16[2,352,2048]{2,1,0:T(8,128)(2,1)S(1)}, u32[]{:S(2)}, u32[]{:S(2)}) %collective-permute-start.91) | collective-permute-done | bytes 2883616 | tf_op jit(solution)/shard_map/ppermute | solution.py:277
  814.6 11.7 collective-permute-done.73
  828.8 19.9 %collective-permute-done.49 = bf16[2,512,512]{2,1,0:T(8,128)(2,1)} collective-permute-done((bf16[2,512,512]{2,1,0:T(8,128)(2,1)S(1)}, bf16[2,512,512]{2,1,0:T(8,128)(2,1)}, u32[]{:S(2)}, u32[]{:S(2)}) %collective-permute-start.49) | collective-permute-done | bytes 1048608 | tf_op jit(solution)/shard_map/ppermute | solution.py:277
  853.7 17.5 %collective-permute-done.55 = bf16[2,512,512]{2,1,0:T(8,128)(2,1)} collective-permute-done((bf16[2,512,512]{2,1,0:T(8,128)(2,1)S(1)}, bf16[2,512,512]{2,1,0:T(8,128)(2,1)}, u32[]{:S(2)}, u32[]{:S(2)}) %collective-permute-start.55) | collective-permute-done | bytes 1048608 | tf_op jit(solution)/shard_map/ppermute | solution.py:277
  874.9 18.8 %collective-permute-done.61 = bf16[2,512,512]{2,1,0:T(8,128)(2,1)S(1)} collective-permute-done((bf16[2,512,512]{2,1,0:T(8,128)(2,1)S(1)}, bf16[2,512,512]{2,1,0:T(8,128)(2,1)S(1)}, u32[]{:S(2)}, u32[]{:S(2)}) %collective-permute-start.61) | collective-permute-done | bytes 1048608 | tf_op jit(solution)/shard_map/ppermute | solution.py:277
  894.7 18.7 %collective-permute-done.67 = bf16[2,512,512]{2,1,0:T(8,128)(2,1)S(1)} collective-permute-done((bf16[2,512,512]{2,1,0:T(8,128)(2,1)S(1)}, bf16[2,512,512]{2,1,0:T(8,128)(2,1)S(1)}, u32[]{:S(2)}, u32[]{:S(2)}) %collective-permute-start.67) | collective-permute-done | bytes 1048608 | tf_op jit(solution)/shard_map/ppermute | solution.py:277
  928.0 109.5 %collective-permute-done.52 = bf16[2,512,512]{2,1,0:T(8,128)(2,1)S(1)} collective-permute-done((bf16[2,512,512]{2,1,0:T(8,128)(2,1)S(1)}, bf16[2,512,512]{2,1,0:T(8,128)(2,1)S(1)}, u32[]{:S(2)}, u32[]{:S(2)}) %collective-permute-start.52) | collective-permute-done | bytes 1048608 | tf_op jit(solution)/shard_map/ppermute | solution.py:277
  1039.2 20.8 %collective-permute-done.76 = bf16[2,128,2048]{2,1,0:T(8,128)(2,1)S(1)} collective-permute-done((bf16[2,128,2048]{2,1,0:T(8,128)(2,1)S(1)}, bf16[2,128,2048]{2,1,0:T(8,128)(2,1)S(1)}, u32[]{:S(2)}, u32[]{:S(2)}) %collective-permute-start.76) | collective-permute-done | bytes 1048608 | tf_op jit(solution)/shard_map/ppermute | solution.py:277
  1061.7 20.8 %collective-permute-done.58 = bf16[2,512,512]{2,1,0:T(8,128)(2,1)S(1)} collective-permute-done((bf16[2,512,512]{2,1,0:T(8,128)(2,1)S(1)}, bf16[2,512,512]{2,1,0:T(8,128)(2,1)S(1)}, u32[]{:S(2)}, u32[]{:S(2)}) %collective-permute-start.58) | collective-permute-done | bytes 1048608 | tf_op jit(solution)/shard_map/ppermute | solution.py:277
  1084.3 20.6 %collective-permute-done.64 = bf16[2,512,512]{2,1,0:T(8,128)(2,1)S(1)} collective-permute-done((bf16[2,512,512]{2,1,0:T(8,128)(2,1)S(1)}, bf16[2,512,512]{2,1,0:T(8,128)(2,1)S(1)}, u32[]{:S(2)}, u32[]{:S(2)}) %collective-permute-start.64) | collective-permute-done | bytes 1048608 | tf_op jit(solution)/shard_map/ppermute | solution.py:277
  1105.3 13.8 %collective-permute-done.70 = bf16[2,512,512]{2,1,0:T(8,128)(2,1)S(1)} collective-permute-done((bf16[2,512,512]{2,1,0:T(8,128)(2,1)S(1)}, bf16[2,512,512]{2,1,0:T(8,128)(2,1)S(1)}, u32[]{:S(2)}, u32[]{:S(2)}) %collective-permute-start.70) | collective-permute-done | bytes 1048608 | tf_op jit(solution)/shard_map/ppermute | solution.py:277
  1137.8 50.9 %collective-permute-done.94 = bf16[2,352,2048]{2,1,0:T(8,128)(2,1)S(1)} collective-permute-done((bf16[2,352,2048]{2,1,0:T(8,128)(2,1)S(1)}, bf16[2,352,2048]{2,1,0:T(8,128)(2,1)S(1)}, u32[]{:S(2)}, u32[]{:S(2)}) %collective-permute-start.94) | collective-permute-done | bytes 2883616 | tf_op jit(solution)/shard_map/ppermute | solution.py:277
  1189.4 61.2 %collective-permute-done.82 = bf16[2,512,1408]{2,1,0:T(8,128)(2,1)S(1)} collective-permute-done((bf16[2,512,1408]{2,1,0:T(8,128)(2,1)S(1)}, bf16[2,512,1408]{2,1,0:T(8,128)(2,1)S(1)}, u32[]{:S(2)}, u32[]{:S(2)}) %collective-permute-start.82) | collective-permute-done | bytes 2883616 | tf_op jit(solution)/shard_map/ppermute | solution.py:277
  1251.2 60.2 %collective-permute-done.88 = bf16[2,512,1408]{2,1,0:T(8,128)(2,1)S(1)} collective-permute-done((bf16[2,512,1408]{2,1,0:T(8,128)(2,1)S(1)}, bf16[2,512,1408]{2,1,0:T(8,128)(2,1)S(1)}, u32[]{:S(2)}, u32[]{:S(2)}) %collective-permute-start.88) | collective-permute-done | bytes 2883616 | tf_op jit(solution)/shard_map/ppermute | solution.py:277
  (434 shorter events, 307.0 us)
Async XLA Ops:
  4.2 50.7 %collective-permute-start.2 = (bf16[256,2048]{1,0:T(8,128)(2,1)}, bf16[256,2048]{1,0:T(8,128)(2,1)}, u32[]{:S(2)}, u32[]{:S(2)}) collective-permute-start(bf16[256,2048]{1,0:T(8,128)(2,1)} %get-tuple-element.162.refs_1_), channel_id=1, source_target_pairs={{0,2},{1,3},{2,0},{3,1},{4,6},{5,7},{6,4},{7,5},{8,10},{9,11},{10,... | collective-permute-start | bytes 3145736 | tf_op jit(solution)/shard_map/ppermute | solution.py:269
  7.1 61.7 %collective-permute-start.4 = (bf16[256,2048]{1,0:T(8,128)(2,1)}, bf16[256,2048]{1,0:T(8,128)(2,1)}, u32[]{:S(2)}, u32[]{:S(2)}) collective-permute-start(bf16[256,2048]{1,0:T(8,128)(2,1)} %get-tuple-element.162.refs_1_), channel_id=1, source_target_pairs={{0,1},{1,0},{2,3},{3,2},{4,5},{5,4},{6,7},{7,6},{8,9},{9,8},{10,11... | collective-permute-start | bytes 3145736 | tf_op jit(solution)/shard_map/ppermute | solution.py:265
  8.6 45.9 %collective-permute-start = (bf16[256,2048]{1,0:T(8,128)(2,1)S(1)}, bf16[256,2048]{1,0:T(8,128)(2,1)}, u32[]{:S(2)}, u32[]{:S(2)}) collective-permute-start(bf16[256,2048]{1,0:T(8,128)(2,1)S(1)} %get-tuple-element.163.refs_0_), channel_id=1, source_target_pairs={{0,1},{1,0},{2,3},{3,2},{4,5},{5,4},{6,7},{7,6},{8,9},{9,8},{10,11... | collective-permute-start | bytes 3145736 | tf_op jit(solution)/shard_map/ppermute | solution.py:265
  9.2 59.7 %collective-permute-start.5 = (bf16[256,2048]{1,0:T(8,128)(2,1)S(1)}, bf16[256,2048]{1,0:T(8,128)(2,1)}, u32[]{:S(2)}, u32[]{:S(2)}) collective-permute-start(bf16[256,2048]{1,0:T(8,128)(2,1)S(1)} %get-tuple-element.163.refs_0_), channel_id=1, source_target_pairs={{0,2},{1,3},{2,0},{3,1},{4,6},{5,7},{6,4},{7,5},{8,10},{9,11},{10,... | collective-permute-start | bytes 3145736 | tf_op jit(solution)/shard_map/ppermute | solution.py:269
  110.0 43.0 %collective-permute-start.6 = (bf16[256,2048]{1,0:T(8,128)(2,1)}, bf16[256,2048]{1,0:T(8,128)(2,1)S(1)}, u32[]{:S(2)}, u32[]{:S(2)}) collective-permute-start(bf16[256,2048]{1,0:T(8,128)(2,1)} %get-tuple-element.82), channel_id=1, source_target_pairs={{0,2},{1,3},{2,0},{3,1},{4,6},{5,7},{6,4},{7,5},{8,10},{9,11},{10,... | collective-permute-start | bytes 3145736 | tf_op jit(solution)/shard_map/ppermute | solution.py:269
  178.6 101.6 %collective-permute-start.12 = (bf16[256,2048]{1,0:T(8,128)(2,1)S(1)}, bf16[256,2048]{1,0:T(8,128)(2,1)}, u32[]{:S(2)}, u32[]{:S(2)}) collective-permute-start(bf16[256,2048]{1,0:T(8,128)(2,1)S(1)} %multiply_convert_fusion.2.refs_1_), channel_id=1, source_target_pairs={{0,1},{1,0},{2,3},{3,2},{4,5},{5,4},{6,7},{7,6},{8,9},{9,8},{10,11... | collective-permute-start | bytes 3145736 | tf_op jit(solution)/shard_map/ppermute | solution.py:265
  179.9 47.4 %collective-permute-start.16 = (bf16[256,2048]{1,0:T(8,128)(2,1)S(1)}, bf16[256,2048]{1,0:T(8,128)(2,1)}, u32[]{:S(2)}, u32[]{:S(2)}) collective-permute-start(bf16[256,2048]{1,0:T(8,128)(2,1)S(1)} %multiply_convert_fusion.3.refs_0_), channel_id=1, source_target_pairs={{0,1},{1,0},{2,3},{3,2},{4,5},{5,4},{6,7},{7,6},{8,9},{9,8},{10,11... | collective-permute-start | bytes 3145736 | tf_op jit(solution)/shard_map/ppermute | solution.py:265
  181.0 68.7 %collective-permute-start.18 = (bf16[256,2048]{1,0:T(8,128)(2,1)}, bf16[256,2048]{1,0:T(8,128)(2,1)S(1)}, u32[]{:S(2)}, u32[]{:S(2)}) collective-permute-start(bf16[256,2048]{1,0:T(8,128)(2,1)} %get-tuple-element.164.refs_2_), channel_id=1, source_target_pairs={{0,1},{1,0},{2,3},{3,2},{4,5},{5,4},{6,7},{7,6},{8,9},{9,8},{10,11... | collective-permute-start | bytes 3145736 | tf_op jit(solution)/shard_map/ppermute | solution.py:265
  182.0 68.2 %collective-permute-start.19 = (bf16[256,2048]{1,0:T(8,128)(2,1)}, bf16[256,2048]{1,0:T(8,128)(2,1)}, u32[]{:S(2)}, u32[]{:S(2)}) collective-permute-start(bf16[256,2048]{1,0:T(8,128)(2,1)} %get-tuple-element.165.refs_3_), channel_id=1, source_target_pairs={{0,2},{1,3},{2,0},{3,1},{4,6},{5,7},{6,4},{7,5},{8,10},{9,11},{10,... | collective-permute-start | bytes 3145736 | tf_op jit(solution)/shard_map/ppermute | solution.py:269
  211.8 70.0 %collective-permute-start.13 = (bf16[256,2048]{1,0:T(8,128)(2,1)}, bf16[256,2048]{1,0:T(8,128)(2,1)}, u32[]{:S(2)}, u32[]{:S(2)}) collective-permute-start(bf16[256,2048]{1,0:T(8,128)(2,1)} %copy-done.45), channel_id=1, source_target_pairs={{0,2},{1,3},{2,0},{3,1},{4,6},{5,7},{6,4},{7,5},{8,10},{9,11},{10,... | collective-permute-start | bytes 3145736 | tf_op jit(solution)/shard_map/ppermute | solution.py:269
  227.3 55.0 %collective-permute-start.14 = (bf16[256,2048]{1,0:T(8,128)(2,1)}, bf16[256,2048]{1,0:T(8,128)(2,1)S(1)}, u32[]{:S(2)}, u32[]{:S(2)}) collective-permute-start(bf16[256,2048]{1,0:T(8,128)(2,1)} %get-tuple-element.165.refs_3_), channel_id=1, source_target_pairs={{0,1},{1,0},{2,3},{3,2},{4,5},{5,4},{6,7},{7,6},{8,9},{9,8},{10,11... | collective-permute-start | bytes 3145736 | tf_op jit(solution)/shard_map/ppermute | solution.py:265
  250.2 63.7 %collective-permute-start.22 = (bf16[256,2048]{1,0:T(8,128)(2,1)}, bf16[256,2048]{1,0:T(8,128)(2,1)}, u32[]{:S(2)}, u32[]{:S(2)}) collective-permute-start(bf16[256,2048]{1,0:T(8,128)(2,1)} %collective-permute-done.17.refs_1_), channel_id=1, source_target_pairs={{0,1},{1,0},{2,3},{3,2},{4,5},{5,4},{6,7},{7,6},{8,9},{9,8},{10,11... | collective-permute-start | bytes 3145736 | tf_op jit(solution)/shard_map/ppermute | solution.py:265
  281.8 47.4 %collective-permute-start.23 = (bf16[256,2048]{1,0:T(8,128)(2,1)}, bf16[256,2048]{1,0:T(8,128)(2,1)}, u32[]{:S(2)}, u32[]{:S(2)}) collective-permute-start(bf16[256,2048]{1,0:T(8,128)(2,1)} %copy-done.56), channel_id=1, source_target_pairs={{0,2},{1,3},{2,0},{3,1},{4,6},{5,7},{6,4},{7,5},{8,10},{9,11},{10,... | collective-permute-start | bytes 3145736 | tf_op jit(solution)/shard_map/ppermute | solution.py:269
  282.3 46.9 %collective-permute-start.24 = (bf16[256,2048]{1,0:T(8,128)(2,1)}, bf16[256,2048]{1,0:T(8,128)(2,1)}, u32[]{:S(2)}, u32[]{:S(2)}) collective-permute-start(bf16[256,2048]{1,0:T(8,128)(2,1)} %collective-permute-done.19.refs_3_), channel_id=1, source_target_pairs={{0,1},{1,0},{2,3},{3,2},{4,5},{5,4},{6,7},{7,6},{8,9},{9,8},{10,11... | collective-permute-start | bytes 3145736 | tf_op jit(solution)/shard_map/ppermute | solution.py:265
  312.4 158.5 %collective-permute-start.30 = (bf16[256,2048]{1,0:T(8,128)(2,1)}, bf16[256,2048]{1,0:T(8,128)(2,1)S(1)}, u32[]{:S(2)}, u32[]{:S(2)}) collective-permute-start(bf16[256,2048]{1,0:T(8,128)(2,1)} %get-tuple-element.110), channel_id=1, source_target_pairs={{0,2},{1,3},{2,0},{3,1},{4,6},{5,7},{6,4},{7,5},{8,10},{9,11},{10,... | collective-permute-start | bytes 3145736 | tf_op jit(solution)/shard_map/ppermute | solution.py:269
  314.0 174.8 %collective-permute-start.20 = (bf16[256,2048]{1,0:T(8,128)(2,1)}, bf16[256,2048]{1,0:T(8,128)(2,1)S(1)}, u32[]{:S(2)}, u32[]{:S(2)}) collective-permute-start(bf16[256,2048]{1,0:T(8,128)(2,1)} %get-tuple-element.98), channel_id=1, source_target_pairs={{0,2},{1,3},{2,0},{3,1},{4,6},{5,7},{6,4},{7,5},{8,10},{9,11},{10,... | collective-permute-start | bytes 3145736 | tf_op jit(solution)/shard_map/ppermute | solution.py:269
  315.5 173.8 %collective-permute-start.35 = (bf16[256,2048]{1,0:T(8,128)(2,1)}, bf16[256,2048]{1,0:T(8,128)(2,1)S(1)}, u32[]{:S(2)}, u32[]{:S(2)}) collective-permute-start(bf16[256,2048]{1,0:T(8,128)(2,1)} %get-tuple-element.116), channel_id=1, source_target_pairs={{0,1},{1,0},{2,3},{3,2},{4,5},{5,4},{6,7},{7,6},{8,9},{9,8},{10,11... | collective-permute-start | bytes 3145736 | tf_op jit(solution)/shard_map/ppermute | solution.py:265
  422.3 47.1 %collective-permute-start.36 = (bf16[256,2048]{1,0:T(8,128)(2,1)S(1)}, bf16[256,2048]{1,0:T(8,128)(2,1)S(1)}, u32[]{:S(2)}, u32[]{:S(2)}) collective-permute-start(bf16[256,2048]{1,0:T(8,128)(2,1)S(1)} %copy-done.61), channel_id=1, source_target_pairs={{0,1},{1,0},{2,3},{3,2},{4,5},{5,4},{6,7},{7,6},{8,9},{9,8},{10,11... | collective-permute-start | bytes 3145736 | tf_op jit(solution)/shard_map/ppermute | solution.py:265
  470.9 69.7 %collective-permute-start.78 = (bf16[2,512,1408]{2,1,0:T(8,128)(2,1)}, bf16[2,512,1408]{2,1,0:T(8,128)(2,1)}, u32[]{:S(2)}, u32[]{:S(2)}) collective-permute-start(bf16[2,512,1408]{2,1,0:T(8,128)(2,1)} %dynamic-slice_bitcast_fusion.2), channel_id=1, source_target_pairs={{0,4},{4,0},{8,12},{12,8},{16,20},{20,16},{24,28},{28,24},{1,5},{5... | collective-permute-start | bytes 8650760 | tf_op jit(solution)/shard_map/ppermute | solution.py:273
  489.3 56.4 %collective-permute-start.90 = (bf16[2,352,2048]{2,1,0:T(8,128)(2,1)}, bf16[2,352,2048]{2,1,0:T(8,128)(2,1)}, u32[]{:S(2)}, u32[]{:S(2)}) collective-permute-start(bf16[2,352,2048]{2,1,0:T(8,128)(2,1)} %dynamic-slice_bitcast_fusion), channel_id=1, source_target_pairs={{0,4},{4,0},{8,12},{12,8},{16,20},{20,16},{24,28},{28,24},{1,5},{5... | collective-permute-start | bytes 8650760 | tf_op jit(solution)/shard_map/ppermute | solution.py:273
  510.2 50.9 %collective-permute-start.84 = (bf16[2,512,1408]{2,1,0:T(8,128)(2,1)}, bf16[2,512,1408]{2,1,0:T(8,128)(2,1)}, u32[]{:S(2)}, u32[]{:S(2)}) collective-permute-start(bf16[2,512,1408]{2,1,0:T(8,128)(2,1)} %dynamic-slice_bitcast_fusion.1), channel_id=1, source_target_pairs={{0,4},{4,0},{8,12},{12,8},{16,20},{20,16},{24,28},{28,24},{1,5},{5... | collective-permute-start | bytes 8650760 | tf_op jit(solution)/shard_map/ppermute | solution.py:273
  545.7 45.0 %collective-permute-start.34 = (bf16[256,2048]{1,0:T(8,128)(2,1)}, bf16[256,2048]{1,0:T(8,128)(2,1)S(1)}, u32[]{:S(2)}, u32[]{:S(2)}) collective-permute-start(bf16[256,2048]{1,0:T(8,128)(2,1)} %collective-permute-done.33.refs_0_), channel_id=1, source_target_pairs={{0,2},{1,3},{2,0},{3,1},{4,6},{5,7},{6,4},{7,5},{8,10},{9,11},{10,... | collective-permute-start | bytes 3145736 | tf_op jit(solution)/shard_map/ppermute | solution.py:269
  561.2 179.8 %collective-permute-start.79 = (bf16[2,512,1408]{2,1,0:T(8,128)(2,1)}, bf16[2,512,1408]{2,1,0:T(8,128)(2,1)}, u32[]{:S(2)}, u32[]{:S(2)}) collective-permute-start(bf16[2,512,1408]{2,1,0:T(8,128)(2,1)} %fusion.2), channel_id=1, source_target_pairs={{0,8},{4,12},{24,16},{28,20},{1,9},{5,13},{25,17},{29,21},{2,10},{... | collective-permute-start | bytes 8650760 | tf_op jit(solution)/shard_map/ppermute | solution.py:277
  578.9 166.7 %collective-permute-start.85 = (bf16[2,512,1408]{2,1,0:T(8,128)(2,1)}, bf16[2,512,1408]{2,1,0:T(8,128)(2,1)}, u32[]{:S(2)}, u32[]{:S(2)}) collective-permute-start(bf16[2,512,1408]{2,1,0:T(8,128)(2,1)} %fusion.1), channel_id=1, source_target_pairs={{0,8},{4,12},{24,16},{28,20},{1,9},{5,13},{25,17},{29,21},{2,10},{... | collective-permute-start | bytes 8650760 | tf_op jit(solution)/shard_map/ppermute | solution.py:277
  733.7 64.6 %collective-permute-start.91 = (bf16[2,352,2048]{2,1,0:T(8,128)(2,1)S(1)}, bf16[2,352,2048]{2,1,0:T(8,128)(2,1)S(1)}, u32[]{:S(2)}, u32[]{:S(2)}) collective-permute-start(bf16[2,352,2048]{2,1,0:T(8,128)(2,1)S(1)} %copy-done.10), channel_id=1, source_target_pairs={{0,8},{4,12},{24,16},{28,20},{1,9},{5,13},{25,17},{29,21},{2,10},{... | collective-permute-start | bytes 8650760 | tf_op jit(solution)/shard_map/ppermute | solution.py:277
  737.8 67.5 %collective-permute-start.42 = (bf16[256,2048]{1,0:T(8,128)(2,1)S(1)}, bf16[256,2048]{1,0:T(8,128)(2,1)S(1)}, u32[]{:S(2)}, u32[]{:S(2)}) collective-permute-start(bf16[256,2048]{1,0:T(8,128)(2,1)S(1)} %copy-done.55), channel_id=1, source_target_pairs={{0,2},{1,3},{2,0},{3,1},{4,6},{5,7},{6,4},{7,5},{8,10},{9,11},{10,... | collective-permute-start | bytes 3145736 | tf_op jit(solution)/shard_map/ppermute | solution.py:269
  740.2 67.5 %collective-permute-start.45 = (bf16[256,2048]{1,0:T(8,128)(2,1)S(1)}, bf16[256,2048]{1,0:T(8,128)(2,1)S(1)}, u32[]{:S(2)}, u32[]{:S(2)}) collective-permute-start(bf16[256,2048]{1,0:T(8,128)(2,1)S(1)} %copy-done.54), channel_id=1, source_target_pairs={{0,1},{1,0},{2,3},{3,2},{4,5},{5,4},{6,7},{7,6},{8,9},{9,8},{10,11... | collective-permute-start | bytes 3145736 | tf_op jit(solution)/shard_map/ppermute | solution.py:265
  741.0 69.0 %collective-permute-start.47 = (bf16[256,2048]{1,0:T(8,128)(2,1)S(1)}, bf16[256,2048]{1,0:T(8,128)(2,1)S(1)}, u32[]{:S(2)}, u32[]{:S(2)}) collective-permute-start(bf16[256,2048]{1,0:T(8,128)(2,1)S(1)} %add_convert_fusion.8), channel_id=1, source_target_pairs={{0,2},{1,3},{2,0},{3,1},{4,6},{5,7},{6,4},{7,5},{8,10},{9,11},{10,... | collective-permute-start | bytes 3145736 | tf_op jit(solution)/shard_map/ppermute | solution.py:269
  745.6 65.8 %collective-permute-start.44 = (bf16[256,2048]{1,0:T(8,128)(2,1)S(1)}, bf16[256,2048]{1,0:T(8,128)(2,1)S(1)}, u32[]{:S(2)}, u32[]{:S(2)}) collective-permute-start(bf16[256,2048]{1,0:T(8,128)(2,1)S(1)} %add_convert_fusion.9), channel_id=1, source_target_pairs={{0,1},{1,0},{2,3},{3,2},{4,5},{5,4},{6,7},{7,6},{8,9},{9,8},{10,11... | collective-permute-start | bytes 3145736 | tf_op jit(solution)/shard_map/ppermute | solution.py:265
  805.3 43.4 %collective-permute-start.49 = (bf16[2,512,512]{2,1,0:T(8,128)(2,1)S(1)}, bf16[2,512,512]{2,1,0:T(8,128)(2,1)}, u32[]{:S(2)}, u32[]{:S(2)}) collective-permute-start(bf16[2,512,512]{2,1,0:T(8,128)(2,1)S(1)} %fusion.34), channel_id=1, source_target_pairs={{0,8},{4,12},{24,16},{28,20},{1,9},{5,13},{25,17},{29,21},{2,10},{... | collective-permute-start | bytes 3145736 | tf_op jit(solution)/shard_map/ppermute | solution.py:277
  807.7 63.5 %collective-permute-start.55 = (bf16[2,512,512]{2,1,0:T(8,128)(2,1)S(1)}, bf16[2,512,512]{2,1,0:T(8,128)(2,1)}, u32[]{:S(2)}, u32[]{:S(2)}) collective-permute-start(bf16[2,512,512]{2,1,0:T(8,128)(2,1)S(1)} %fusion.33), channel_id=1, source_target_pairs={{0,8},{4,12},{24,16},{28,20},{1,9},{5,13},{25,17},{29,21},{2,10},{... | collective-permute-start | bytes 3145736 | tf_op jit(solution)/shard_map/ppermute | solution.py:277
  810.0 83.7 %collective-permute-start.61 = (bf16[2,512,512]{2,1,0:T(8,128)(2,1)S(1)}, bf16[2,512,512]{2,1,0:T(8,128)(2,1)S(1)}, u32[]{:S(2)}, u32[]{:S(2)}) collective-permute-start(bf16[2,512,512]{2,1,0:T(8,128)(2,1)S(1)} %fusion.32), channel_id=1, source_target_pairs={{0,8},{4,12},{24,16},{28,20},{1,9},{5,13},{25,17},{29,21},{2,10},{... | collective-permute-start | bytes 3145736 | tf_op jit(solution)/shard_map/ppermute | solution.py:277
  811.3 102.1 %collective-permute-start.67 = (bf16[2,512,512]{2,1,0:T(8,128)(2,1)S(1)}, bf16[2,512,512]{2,1,0:T(8,128)(2,1)S(1)}, u32[]{:S(2)}, u32[]{:S(2)}) collective-permute-start(bf16[2,512,512]{2,1,0:T(8,128)(2,1)S(1)} %fusion.31), channel_id=1, source_target_pairs={{0,8},{4,12},{24,16},{28,20},{1,9},{5,13},{25,17},{29,21},{2,10},{... | collective-permute-start | bytes 3145736 | tf_op jit(solution)/shard_map/ppermute | solution.py:277
  826.3 92.5 %collective-permute-start.80 = (bf16[512,1408]{1,0:T(8,128)(2,1)S(1)}, bf16[512,1408]{1,0:T(8,128)(2,1)S(1)}, u32[]{:S(2)}, u32[]{:S(2)}) collective-permute-start(bf16[512,1408]{1,0:T(8,128)(2,1)S(1)} %dynamic-slice_bitcast_fusion.5), channel_id=1, source_target_pairs={{8,16},{12,20},{16,8},{20,12},{9,17},{13,21},{17,9},{21,13},{10,18... | collective-permute-start | bytes 4325384 | tf_op jit(solution)/shard_map/ppermute | solution.py:277
  848.7 71.1 %collective-permute-start.86 = (bf16[512,1408]{1,0:T(8,128)(2,1)S(1)}, bf16[512,1408]{1,0:T(8,128)(2,1)S(1)}, u32[]{:S(2)}, u32[]{:S(2)}) collective-permute-start(bf16[512,1408]{1,0:T(8,128)(2,1)S(1)} %dynamic-slice_bitcast_fusion.4), channel_id=1, source_target_pairs={{8,16},{12,20},{16,8},{20,12},{9,17},{13,21},{17,9},{21,13},{10,18... | collective-permute-start | bytes 4325384 | tf_op jit(solution)/shard_map/ppermute | solution.py:277
  871.2 43.2 %collective-permute-start.74 = (bf16[128,2048]{1,0:T(8,128)(2,1)S(1)}, bf16[128,2048]{1,0:T(8,128)(2,1)S(1)}, u32[]{:S(2)}, u32[]{:S(2)}) collective-permute-start(bf16[128,2048]{1,0:T(8,128)(2,1)S(1)} %dynamic-slice_bitcast_fusion.11), channel_id=1, source_target_pairs={{8,16},{12,20},{16,8},{20,12},{9,17},{13,21},{17,9},{21,13},{10,18... | collective-permute-start | bytes 1572872 | tf_op jit(solution)/shard_map/ppermute | solution.py:277
  921.8 115.7 %collective-permute-start.52 = (bf16[2,512,512]{2,1,0:T(8,128)(2,1)S(1)}, bf16[2,512,512]{2,1,0:T(8,128)(2,1)S(1)}, u32[]{:S(2)}, u32[]{:S(2)}) collective-permute-start(bf16[2,512,512]{2,1,0:T(8,128)(2,1)S(1)} %maximum_select_fusion.11), channel_id=1, source_target_pairs={{8,0},{12,4},{16,24},{20,28},{9,1},{13,5},{17,25},{21,29},{10,2},{... | collective-permute-start | bytes 3145736 | tf_op jit(solution)/shard_map/ppermute | solution.py:277
  923.3 136.6 %collective-permute-start.76 = (bf16[2,128,2048]{2,1,0:T(8,128)(2,1)S(1)}, bf16[2,128,2048]{2,1,0:T(8,128)(2,1)S(1)}, u32[]{:S(2)}, u32[]{:S(2)}) collective-permute-start(bf16[2,128,2048]{2,1,0:T(8,128)(2,1)S(1)} %maximum_select_fusion.15), channel_id=1, source_target_pairs={{8,0},{12,4},{16,24},{20,28},{9,1},{13,5},{17,25},{21,29},{10,2},{... | collective-permute-start | bytes 3145736 | tf_op jit(solution)/shard_map/ppermute | solution.py:277
  925.2 195.3 %collective-permute-start.93 = (bf16[352,2048]{1,0:T(8,128)(2,1)S(1)}, bf16[352,2048]{1,0:T(8,128)(2,1)S(1)}, u32[]{:S(2)}, u32[]{:S(2)}) collective-permute-start(bf16[352,2048]{1,0:T(8,128)(2,1)S(1)} %fusion.13), channel_id=1, source_target_pairs={{8,16},{12,20},{16,8},{20,12},{9,17},{13,21},{17,9},{21,13},{10,18... | collective-permute-start | bytes 4325384 | tf_op jit(solution)/shard_map/ppermute | solution.py:277
  926.1 195.4 %collective-permute-start.81 = (bf16[512,1408]{1,0:T(8,128)(2,1)S(1)}, bf16[512,1408]{1,0:T(8,128)(2,1)S(1)}, u32[]{:S(2)}, u32[]{:S(2)}) collective-permute-start(bf16[512,1408]{1,0:T(8,128)(2,1)S(1)} %fusion.15), channel_id=1, source_target_pairs={{8,16},{12,20},{16,8},{20,12},{9,17},{13,21},{17,9},{21,13},{10,18... | collective-permute-start | bytes 4325384 | tf_op jit(solution)/shard_map/ppermute | solution.py:277
  927.1 196.3 %collective-permute-start.87 = (bf16[512,1408]{1,0:T(8,128)(2,1)S(1)}, bf16[512,1408]{1,0:T(8,128)(2,1)S(1)}, u32[]{:S(2)}, u32[]{:S(2)}) collective-permute-start(bf16[512,1408]{1,0:T(8,128)(2,1)S(1)} %fusion.14), channel_id=1, source_target_pairs={{8,16},{12,20},{16,8},{20,12},{9,17},{13,21},{17,9},{21,13},{10,18... | collective-permute-start | bytes 4325384 | tf_op jit(solution)/shard_map/ppermute | solution.py:277
  1037.5 44.9 %collective-permute-start.58 = (bf16[2,512,512]{2,1,0:T(8,128)(2,1)S(1)}, bf16[2,512,512]{2,1,0:T(8,128)(2,1)S(1)}, u32[]{:S(2)}, u32[]{:S(2)}) collective-permute-start(bf16[2,512,512]{2,1,0:T(8,128)(2,1)S(1)} %maximum_select_fusion.12), channel_id=1, source_target_pairs={{8,0},{12,4},{16,24},{20,28},{9,1},{13,5},{17,25},{21,29},{10,2},{... | collective-permute-start | bytes 3145736 | tf_op jit(solution)/shard_map/ppermute | solution.py:277
  1060.0 44.9 %collective-permute-start.64 = (bf16[2,512,512]{2,1,0:T(8,128)(2,1)S(1)}, bf16[2,512,512]{2,1,0:T(8,128)(2,1)S(1)}, u32[]{:S(2)}, u32[]{:S(2)}) collective-permute-start(bf16[2,512,512]{2,1,0:T(8,128)(2,1)S(1)} %maximum_select_fusion.13), channel_id=1, source_target_pairs={{8,0},{12,4},{16,24},{20,28},{9,1},{13,5},{17,25},{21,29},{10,2},{... | collective-permute-start | bytes 3145736 | tf_op jit(solution)/shard_map/ppermute | solution.py:277
  1121.5 67.2 %collective-permute-start.94 = (bf16[2,352,2048]{2,1,0:T(8,128)(2,1)S(1)}, bf16[2,352,2048]{2,1,0:T(8,128)(2,1)S(1)}, u32[]{:S(2)}, u32[]{:S(2)}) collective-permute-start(bf16[2,352,2048]{2,1,0:T(8,128)(2,1)S(1)} %maximum_select_fusion.5), channel_id=1, source_target_pairs={{8,0},{12,4},{16,24},{20,28},{9,1},{13,5},{17,25},{21,29},{10,2},{... | collective-permute-start | bytes 8650760 | tf_op jit(solution)/shard_map/ppermute | solution.py:277
  1124.5 126.1 %collective-permute-start.82 = (bf16[2,512,1408]{2,1,0:T(8,128)(2,1)S(1)}, bf16[2,512,1408]{2,1,0:T(8,128)(2,1)S(1)}, u32[]{:S(2)}, u32[]{:S(2)}) collective-permute-start(bf16[2,512,1408]{2,1,0:T(8,128)(2,1)S(1)} %maximum_select_fusion.3), channel_id=1, source_target_pairs={{8,0},{12,4},{16,24},{20,28},{9,1},{13,5},{17,25},{21,29},{10,2},{... | collective-permute-start | bytes 8650760 | tf_op jit(solution)/shard_map/ppermute | solution.py:277
  1126.5 184.9 %collective-permute-start.88 = (bf16[2,512,1408]{2,1,0:T(8,128)(2,1)S(1)}, bf16[2,512,1408]{2,1,0:T(8,128)(2,1)S(1)}, u32[]{:S(2)}, u32[]{:S(2)}) collective-permute-start(bf16[2,512,1408]{2,1,0:T(8,128)(2,1)S(1)} %maximum_select_fusion.4), channel_id=1, source_target_pairs={{8,0},{12,4},{16,24},{20,28},{9,1},{13,5},{17,25},{21,29},{10,2},{... | collective-permute-start | bytes 8650760 | tf_op jit(solution)/shard_map/ppermute | solution.py:277
  1189.3 124.6 %collective-permute-start.95 = (bf16[2,352,2048]{2,1,0:T(8,128)(2,1)S(1)}, bf16[2,352,2048]{2,1,0:T(8,128)(2,1)}, u32[]{:S(2)}, u32[]{:S(2)}) collective-permute-start(bf16[2,352,2048]{2,1,0:T(8,128)(2,1)S(1)} %broadcast_select_fusion), channel_id=1, source_target_pairs={{0,4},{4,0},{8,12},{12,8},{16,20},{20,16},{24,28},{28,24},{1,5},{5... | collective-permute-start | bytes 8650760 | tf_op jit(solution)/shard_map/ppermute | solution.py:273
  1251.1 66.5 %collective-permute-start.83 = (bf16[2,512,1408]{2,1,0:T(8,128)(2,1)S(1)}, bf16[2,512,1408]{2,1,0:T(8,128)(2,1)}, u32[]{:S(2)}, u32[]{:S(2)}) collective-permute-start(bf16[2,512,1408]{2,1,0:T(8,128)(2,1)S(1)} %broadcast_select_fusion.2), channel_id=1, source_target_pairs={{0,4},{4,0},{8,12},{12,8},{16,20},{20,16},{24,28},{28,24},{1,5},{5... | collective-permute-start | bytes 8650760 | tf_op jit(solution)/shard_map/ppermute | solution.py:273
  (117 other events, 1873.6 us)

commit v2 on v1

--- a/solution.py
+++ b/solution.py
@@ -255,9 +255,6 @@
 
 HALF = BLK
 PIECE = 2 * BLK
-LINE = ((0, 1), (3, 2))
-MIDDLE = ((1, 2), (2, 1))
-BACK = ((1, 0), (2, 3))
 VMEM = 60 * 1024 * 1024
 
 
@@ -267,14 +264,6 @@
 
 def over_y(rows):
     return lax.ppermute(rows, "narrow", [(at, at ^ 2) for at in range(4)])
-
-
-def over_core(rows):
-    return lax.ppermute(rows, "wide", [(at, at ^ 1) for at in range(8)])
-
-
-def over_z(rows, pairs):
-    return lax.ppermute(rows, "wide", [(2 * a + c, 2 * b + c) for a, b in pairs for c in range(2)])
 
 
 def add_low(*terms):
@@ -290,12 +279,14 @@
 
 def scatter_pieces(own, first, second, third):
     (top, low), (top_x, low_y), (low_x, top_y), (top_d, low_d) = own, first, second, third
-    to_top_x, to_low_y = over_y(top_d), over_x(low_d)
-    to_top, to_low = over_y(top_y), over_x(low_x)
-    more_top, more_low = over_x(add_low(top_x, to_top_x)), over_y(add_low(low_y, to_low_y))
-    total_top = top.astype(jnp.float32) + to_top.astype(jnp.float32) + more_top.astype(jnp.float32)
-    total_low = low.astype(jnp.float32) + to_low.astype(jnp.float32) + more_low.astype(jnp.float32)
-    return total_top, total_low
+    to_top_y, to_low_x = over_x(top_d), over_y(low_d)
+    to_top, to_low = over_x(top_x), over_y(low_y)
+    more_top, more_low = over_y(add_low(top_y, to_top_y)), over_x(add_low(low_x, to_low_x))
+    return add_rows(top, to_top, more_top), add_rows(low, to_low, more_low)
+
+
+def add_rows(*terms):
+    return sum(term.astype(jnp.float32) for term in terms)
 
 
 def slot_tables(narrow_index, fresh_block):
@@ -306,35 +297,6 @@
     return jnp.where(block_ids % 2 == 0, even, odd), fresh_block.astype(jnp.int32)
 
 
-def wide_sum(grad):
-    wide_index = lax.axis_index("wide")
-    z, core = wide_index // 2, wide_index % 2
-    rows, columns = grad.shape
-    quarters = grad.reshape(2, 2, rows // 4, columns)
-    mine = lax.dynamic_index_in_dim(quarters, core, 0, keepdims=False)
-    other = lax.dynamic_index_in_dim(quarters, 1 - core, 0, keepdims=False)
-    both = add_low(mine, over_core(other))
-    lined = add_low(both, over_z(both, LINE))
-    inner = jnp.where(z == 1, 0, 1)
-    kept = lax.dynamic_index_in_dim(lined, inner, 0, keepdims=False)
-    sent = lax.dynamic_index_in_dim(lined, 1 - inner, 0, keepdims=False)
-    total = add_low(kept, over_z(sent, MIDDLE))
-    passed = over_z(total, MIDDLE)
-    full = jnp.where(z == 1, jnp.stack([total, passed]), jnp.stack([passed, total]))
-    end = (z == 0) | (z == 3)
-    result = jnp.where(end, over_z(full, BACK), full)
-    partner = over_core(result)
-    result = jnp.where(core == 0, jnp.stack([result, partner]), jnp.stack([partner, result]))
-    return result.reshape(rows, columns).astype(jnp.float32)
-
-
-def load_pair(top_ref, low_ref, rows_ref, sems, at):
-    return (
-        pltpu.make_async_copy(top_ref, rows_ref.at[pl.ds(0, HALF)], sems.at[at]),
-        pltpu.make_async_copy(low_ref, rows_ref.at[pl.ds(HALF, HALF)], sems.at[at + 1]),
-    )
-
-
 def across(left, right):
     return lax.dot_general(left, right, (((1,), (1,)), ((), ())), preferred_element_type=jnp.float32)
 
@@ -353,41 +315,607 @@
 
 def cost(flops, bytes_accessed):
     return pl.CostEstimate(flops=int(flops), bytes_accessed=int(bytes_accessed), transcendentals=0)
+
+
+MESH = pl.DeviceIdType.MESH
+SLOTS = 13
+STAGES = 12
+SUB = 128
+TILE = 256
+
+
+def begin(copies):
+    for copy in copies:
+        copy.start()
+
+
+def finish(copies):
+    for copy in copies:
+        copy.wait()
+
+
+def neighbours():
+    wide, narrow = lax.axis_index("wide"), lax.axis_index("narrow")
+    z, core = wide // 2, wide % 2
+    mate = (wide + 1 - 2 * core, narrow)
+    near_x = (wide, narrow + 1 - 2 * (narrow % 2))
+    near_y = (wide, (narrow + 2) % 4)
+    return wide, narrow, z, core, mate, near_x, near_y
+
+
+def line_scratch():
+    low = jnp.bfloat16
+    pair = pltpu.VMEM((SLOTS, 2, SUB, TILE), low)
+    return [
+        pltpu.VMEM((SLOTS, 4, SUB, TILE), low),
+        pair,
+        pair,
+        pair,
+        pltpu.VMEM((SLOTS, SUB, TILE), low),
+        pair,
+        pair,
+        pltpu.SemaphoreType.DMA((14, SLOTS)),
+        pltpu.SemaphoreType.DMA((4, SLOTS)),
+    ]
+
+
+def enter(neighbour_places):
+    wide, narrow, z, core, mate, near_x, near_y = neighbour_places
+    barrier = pltpu.get_barrier_semaphore()
+
+    def greet(place):
+        pl.semaphore_signal(barrier, inc=1, device_id=place, device_id_type=MESH)
+
+    for place in (mate, near_x, near_y):
+        greet(place)
+    middle = (z == 1) | (z == 2)
+
+    @pl.when(middle)
+    def _():
+        greet((2 * (3 - z) + core, narrow))
+        greet((6 * (z - 1) + core, narrow))
+        pl.semaphore_wait(barrier, 5)
+
+    @pl.when(jnp.logical_not(middle))
+    def _():
+        greet((2 * (1 + z // 3) + core, narrow))
+        pl.semaphore_wait(barrier, 4)
+
+
+def line_sum(scratch, places, count, product, targets):
+    own, met, both, ended, crossed, full, other, sems, out_sems = scratch
+    wide, narrow, z, core, mate, _, _ = places
+    region = z // 2
+    middle = (z == 1) | (z == 2)
+    end = jnp.logical_not(middle)
+    inward = (2 * (1 + z // 3) + core, narrow)
+    across_line = (2 * (3 - z) + core, narrow)
+    outward = (6 * (z - 1) + core, narrow)
+
+    def remote(src, dst, kind, slot, place):
+        return pltpu.make_async_remote_copy(
+            src_ref=src,
+            dst_ref=dst,
+            send_sem=sems.at[2 * kind, slot],
+            recv_sem=sems.at[2 * kind + 1, slot],
+            device_id=place,
+            device_id_type=MESH,
+        )
+
+    def core_one(s):
+        return remote(own.at[s, pl.ds(2 * (1 - core), 2)], met.at[s], 0, s, mate)
+
+    def line_one(s):
+        return remote(both.at[s], ended.at[s], 1, s, inward)
+
+    def cross_one(s):
+        return remote(both.at[s, 1 - region], crossed.at[s], 2, s, across_line)
+
+    def cross_two(s):
+        return remote(full.at[s, region], full.at[s, region], 3, s, across_line)
+
+    def out_one(s):
+        return remote(full.at[s, region], full.at[s, region], 4, s, outward)
+
+    def out_two(s):
+        return remote(full.at[s, 1 - region], full.at[s, 1 - region], 5, s, outward)
+
+    def core_two(s):
+        return remote(full.at[s], other.at[s], 6, s, mate)
+
+    def add(left, right):
+        return (left.astype(jnp.float32) + right.astype(jnp.float32)).astype(jnp.bfloat16)
+
+    def deliveries(k, s):
+        for t in range(2):
+            for which, (src, part) in enumerate(
+                ((full.at[s, t], 2 * core + t), (other.at[s, t], 2 * (1 - core) + t))
+            ):
+                for condition, ref in targets(k, part):
+                    yield condition, pltpu.make_async_copy(src, ref, out_sems.at[2 * t + which, s])
+
+    def start(k, s):
+        product(k, own.at[s])
+        core_one(s).start()
+
+    def cores(k, s):
+        core_one(s).wait_recv()
+        both[s] = add(own[s, pl.ds(2 * core, 2)], met[s])
+        pl.when(end)(lambda: line_one(s).start())
+
+    def ends(k, s):
+        @pl.when(middle)
+        def _():
+            line_one(s).wait_recv()
+            both[s] = add(both[s], ended[s])
+            cross_one(s).start()
+
+    def centre(k, s):
+        @pl.when(middle)
+        def _():
+            cross_one(s).wait_recv()
+            full[s, region] = add(both[s, region], crossed[s])
+            cross_two(s).start()
+            out_one(s).start()
+
+    def pass_on(k, s):
+        @pl.when(middle)
+        def _():
+            cross_two(s).wait_recv()
+            out_two(s).start()
+
+    def back(k, s):
+        @pl.when(end)
+        def _():
+            out_one(s).wait_recv()
+            out_two(s).wait_recv()
+
+        core_two(s).start()
+
+    def deliver(k, s):
+        core_two(s).wait_recv()
+        for condition, copy in deliveries(k, s):
+            pl.when(condition)(copy.start)
+
+    def clear(k, s):
+        core_one(s).wait_send()
+        core_two(s).wait_send()
+
+        @pl.when(end)
+        def _():
+            line_one(s).wait_send()
+
+        @pl.when(middle)
+        def _():
+            for copy in (cross_one(s), cross_two(s), out_one(s), out_two(s)):
+                copy.wait_send()
+
+        for condition, copy in deliveries(k, s):
+            pl.when(condition)(copy.wait)
+
+    stages = (
+        (12, clear),
+        (10, deliver),
+        (9, back),
+        (7, pass_on),
+        (5, centre),
+        (3, ends),
+        (1, cores),
+        (0, start),
+    )
+
+    def step(i, carry):
+        for delay, work in stages:
+            k = i - delay
+
+            @pl.when((k >= 0) & (k < count))
+            def _(work=work, k=k):
+                work(k, lax.rem(k + SLOTS, SLOTS))
+
+        return carry
+
+    return step
+
+
+def square_scratch():
+    low = jnp.bfloat16
+    block = pltpu.VMEM((2, BLK, HEADS * HS), low)
+    return [block, block, pltpu.SemaphoreType.DMA((6, 2)), pltpu.SemaphoreType.DMA((2,))]
+
+
+def square_sum(scratch, places, parts, landed):
+    met, mid, sems, load_sems = scratch
+    top_x, low_y, low_x, top_y, top_d, low_d = parts
+    near_x, near_y = places[5:]
+
+    def remote(src, dst, kind, place):
+        return pltpu.make_async_remote_copy(
+            src_ref=src,
+            dst_ref=dst,
+            send_sem=sems.at[kind, 0],
+            recv_sem=sems.at[kind, 1],
+            device_id=place,
+            device_id_type=MESH,
+        )
+
+    first = [remote(top_d, met.at[0], 0, near_x), remote(low_d, met.at[1], 1, near_y)]
+    direct = [remote(top_x, landed[0], 2, near_x), remote(low_y, landed[1], 3, near_y)]
+    second = [remote(mid.at[0], landed[2], 4, near_y), remote(mid.at[1], landed[3], 5, near_x)]
+    loads = [
+        pltpu.make_async_copy(top_y, mid.at[0], load_sems.at[0]),
+        pltpu.make_async_copy(low_x, mid.at[1], load_sems.at[1]),
+    ]
+
+    def open_sum():
+        begin(first)
+        begin(direct)
+        begin(loads)
+
+    def join_sum():
+        finish(loads)
+        for at in range(2):
+            first[at].wait()
+
+            def tile(i, carry, at=at):
+                rows = pl.ds(pl.multiple_of(i * 64, 64), 64)
+                mid[at, rows, :] = add_low(mid[at, rows, :], met[at, rows, :])
+                return carry
+
+            lax.fori_loop(0, BLK // 64, tile, 0)
+            second[at].start()
+
+    def close_sum():
+        finish(direct)
+        finish(second)
+
+    return open_sum, join_sum, close_sum
+
+
+def unit_grads(act, grad_two_all, normed_two_all, grad_parts, back_sums, middle, cotangent, live):
+    rows, units = act.shape
+    width = grad_two_all.shape[1]
+    local_rows = middle.shape[0]
+    low = jnp.bfloat16
+    out_blocks, in_blocks = units // SUB, width // SUB
+    halves = width // 1024
+    out_chunks = out_blocks * halves
+    columns = grad_parts.shape[1] // TILE
+    in_chunks = (width // PIECE) * columns
+    count = out_chunks + in_chunks
+
+    def body(*refs):
+        act_in, two_in, normed_in, parts_in = refs[:4]
+        partial = refs[4:12]
+        middle_in, cot_in, live_ref = refs[12:15]
+        out_grad, in_grad, branch_out, middle_out = refs[15:19]
+        act_ref, shared, parts_ref, landed, own_ref, cot_ref, mid_ref, grad_ref, branch = refs[19:28]
+        load_sems, stage_sems, gather_sems = refs[28:31]
+        line = refs[31:40]
+        square = refs[40:44]
+        places = neighbours()
+        near_x, near_y = places[5:]
+        enter(places)
+        load_act = pltpu.make_async_copy(act_in, act_ref, load_sems.at[0])
+        load_two = pltpu.make_async_copy(two_in, shared, load_sems.at[1])
+        load_parts = pltpu.make_async_copy(parts_in, parts_ref, load_sems.at[2])
+        load_normed = pltpu.make_async_copy(normed_in, shared, load_sems.at[3])
+        open_sum, join_sum, close_sum = square_sum(
+            square, places, partial[2:], [landed.at[at] for at in range(4)]
+        )
+        load_two.start()
+        load_act.start()
+        open_sum()
+        load_parts.start()
+        load_two.wait()
+        load_act.wait()
+
+        def product(k, own):
+            @pl.when(k < out_chunks)
+            def _():
+                rows_at = pl.ds(pl.multiple_of((k // halves) * SUB, SUB), SUB)
+                wide_at = pl.ds(pl.multiple_of((k % halves) * 1024, 1024), 1024)
+                result = down(act_ref[:, rows_at], shared[:, wide_at]).astype(low)
+                for part in range(4):
+                    own[part] = result[:, part * TILE : (part + 1) * TILE]
+
+            @pl.when(k == out_chunks)
+            def _():
+                load_normed.start()
+                load_parts.wait()
+                load_normed.wait()
+
+            @pl.when(k >= out_chunks)
+            def _():
+                at = k - out_chunks
+                rows_at = pl.ds(pl.multiple_of((at // columns) * PIECE, PIECE), PIECE)
+                wide_at = pl.ds(pl.multiple_of((at % columns) * TILE, TILE), TILE)
+                result = down(shared[:, rows_at], parts_ref[:, wide_at]).astype(low)
+                for part in range(4):
+                    own[part] = result[part * SUB : (part + 1) * SUB]
+
+        def targets(k, part):
+            wide_at = pl.ds(pl.multiple_of((k % halves) * 1024 + part * TILE, TILE), TILE)
+            at = jnp.maximum(k - out_chunks, 0)
+            in_at = pl.ds(pl.multiple_of((at % columns) * TILE, TILE), TILE)
+            first = jnp.minimum(k, out_chunks - 1) // halves
+            return [
+                (k < out_chunks, out_grad.at[first, :, wide_at]),
+                (k >= out_chunks, in_grad.at[(at // columns) * 4 + part, :, in_at]),
+            ]
+
+        step = line_sum(line, places, count, product, targets)
+
+        def block(at):
+            return pl.ds(at * BLK, BLK)
+
+        def spread(src, slot, kind, place):
+            return pltpu.make_async_remote_copy(
+                src_ref=src,
+                dst_ref=branch_out.at[block(slot)],
+                send_sem=gather_sems.at[kind, 0],
+                recv_sem=gather_sems.at[kind, 1],
+                device_id=place,
+                device_id_type=MESH,
+            )
+
+        def stage(half):
+            return [
+                pltpu.make_async_copy(partial[half], own_ref, stage_sems.at[0]),
+                pltpu.make_async_copy(cot_in.at[block(half)], cot_ref, stage_sems.at[1]),
+                pltpu.make_async_copy(middle_in.at[block(half)], mid_ref, stage_sems.at[2]),
+            ]
+
+        keep = [
+            pltpu.make_async_copy(branch.at[at], branch_out.at[block(at)], stage_sems.at[3 + at])
+            for at in range(2)
+        ]
+
+        def rows_back(half):
+            def tile(i, carry):
+                at = pl.ds(pl.multiple_of(i * 32, 32), 32)
+                grad = own_ref[at, :].astype(jnp.float32)
+                grad += landed[half, at, :].astype(jnp.float32)
+                grad += landed[2 + half, at, :].astype(jnp.float32)
+                result = cot_ref[at, :].astype(jnp.float32) + norm_back(mid_ref[at, :], grad)
+                grad_ref[at, :] = result
+                live_at = pl.ds(pl.multiple_of(half * BLK + i * 32, 32), 32)
+                branch[half, at, :] = (live_ref[live_at, :1] * result).astype(low)
+                return carry
+
+            lax.fori_loop(0, BLK // 32, tile, 0)
+            copy = pltpu.make_async_copy(grad_ref, middle_out.at[block(half)], stage_sems.at[5])
+            copy.start()
+            return copy
+
+        sends = [
+            spread(branch.at[0], 2, 0, near_x),
+            spread(branch.at[1], 3, 1, near_y),
+            spread(branch.at[1], 4, 2, near_x),
+            spread(branch.at[0], 5, 3, near_y),
+        ]
+        later = [
+            spread(branch_out.at[block(3)], 7, 4, near_x),
+            spread(branch_out.at[block(2)], 6, 5, near_y),
+        ]
+
+        lax.fori_loop(0, 9, step, 0)
+        join_sum()
+        begin(stage(0))
+        lax.fori_loop(9, 25, step, 0)
+        close_sum()
+        finish(stage(0))
+        written = rows_back(0)
+        sends[0].start()
+        begin(stage(1))
+        finish(stage(1))
+        written.wait()
+        written = rows_back(1)
+        begin([sends[1], sends[2], sends[3]])
+        begin(keep)
+        lax.fori_loop(25, 33, step, 0)
+        sends[0].wait_recv()
+        sends[1].wait_recv()
+        begin(later)
+        lax.fori_loop(33, count + STAGES, step, 0)
+        written.wait()
+        finish(keep)
+        for copy in sends[:2]:
+            copy.wait_send()
+        finish(sends[2:])
+        finish(later)
+
+    return pl.pallas_call(
+        body,
+        in_specs=any_specs(14) + [pl.BlockSpec(memory_space=pltpu.VMEM)],
+        out_specs=any_specs(4),
+        out_shape=[
+            jax.ShapeDtypeStruct((out_blocks, SUB, width), low),
+            jax.ShapeDtypeStruct((in_blocks, SUB, grad_parts.shape[1]), low),
+            jax.ShapeDtypeStruct((rows, width), low),
+            jax.ShapeDtypeStruct((local_rows, width), jnp.float32),
+        ],
+        scratch_shapes=[
+            pltpu.VMEM(act.shape, low),
+            pltpu.VMEM((rows, width), low),
+            pltpu.VMEM(grad_parts.shape, low),
+            pltpu.VMEM((4, BLK, width), low),
+            pltpu.VMEM((BLK, width), low),
+            pltpu.VMEM((BLK, width), low),
+            pltpu.VMEM((BLK, width), jnp.float32),
+            pltpu.VMEM((BLK, width), jnp.float32),
+            pltpu.VMEM((2, BLK, width), low),
+            pltpu.SemaphoreType.DMA((4,)),
+            pltpu.SemaphoreType.DMA((6,)),
+            pltpu.SemaphoreType.DMA((6, 2)),
+        ]
+        + line_scratch()
+        + square_scratch(),
+        compiler_params=pltpu.CompilerParams(
+            vmem_limit_bytes=VMEM, collective_id=1, has_side_effects=True
+        ),
+        cost_estimate=cost(2 * 3 * rows * width * units, 60e6),
+        name="unit_grads",
+    )(act, grad_two_all, normed_two_all, grad_parts, *back_sums, middle, cotangent, live)
+
+
+def mix_grads(gated, grad_branch_all, normed_all, grad_projected, sums, two_sums):
+    _, rows, columns = gated.shape
+    width = normed_all.shape[1]
+    parts = grad_projected.shape[0]
+    low = jnp.bfloat16
+    out_chunks = width // TILE
+    per_row = columns // TILE
+    per_part = (width // PIECE) * per_row
+    count = out_chunks + parts * per_part
+
+    def body(*refs):
+        gated_in, branch_in, normed_in, grads_in = refs[:4]
+        partial, two_partial = refs[4:10], refs[10:16]
+        out_grad, mix_grad = refs[16:18]
+        landed, two_landed = refs[18:22], refs[22:26]
+        gated_ref, branch_ref, normed_ref, grads_ref, load_sems = refs[26:31]
+        line = refs[31:40]
+        square, two_square = refs[40:44], refs[44:48]
+        places = neighbours()
+        enter(places)
+        loads = [
+            pltpu.make_async_copy(gated_in.at[0], gated_ref, load_sems.at[0]),
+            pltpu.make_async_copy(branch_in, branch_ref, load_sems.at[1]),
+            pltpu.make_async_copy(normed_in, normed_ref, load_sems.at[2]),
+            pltpu.make_async_copy(grads_in, grads_ref, load_sems.at[3]),
+        ]
+        begin(loads)
+        open_sum, join_sum, close_sum = square_sum(square, places, partial, landed)
+        open_two, join_two, close_two = square_sum(two_square, places, two_partial, two_landed)
+        open_sum()
+        finish(loads[:2])
+
+        def product(k, own):
+            @pl.when(k < out_chunks)
+            def _():
+                wide_at = pl.ds(pl.multiple_of(k * TILE, TILE), TILE)
+                result = down(gated_ref[...], branch_ref[:, wide_at]).astype(low)
+                for part in range(4):
+                    own[part] = result[part * SUB : (part + 1) * SUB]
+
+            @pl.when(k == out_chunks)
+            def _():
+                finish(loads[2:])
+
+            @pl.when(k >= out_chunks)
+            def _():
+                at = k - out_chunks
+                rows_at = pl.ds(pl.multiple_of(((at // per_row) % 4) * PIECE, PIECE), PIECE)
+                wide_at = pl.ds(pl.multiple_of((at % per_row) * TILE, TILE), TILE)
+                result = down(normed_ref[:, rows_at], grads_ref[at // per_part, :, wide_at]).astype(low)
+                for part in range(4):
+                    own[part] = result[part * SUB : (part + 1) * SUB]
+
+        def targets(k, part):
+            first_at = pl.ds(pl.multiple_of(jnp.minimum(k, out_chunks - 1) * TILE, TILE), TILE)
+            at = jnp.maximum(k - out_chunks, 0)
+            wide_at = pl.ds(pl.multiple_of((at % per_row) * TILE, TILE), TILE)
+            return [
+                (k < out_chunks, out_grad.at[part, :, first_at]),
+                (k >= out_chunks, mix_grad.at[(at // per_row) * 4 + part, :, wide_at]),
+            ]
+
+        step = line_sum(line, places, count, product, targets)
+        lax.fori_loop(0, 9, step, 0)
+        join_sum()
+        open_two()
+        lax.fori_loop(9, 33, step, 0)
+        join_two()
+        lax.fori_loop(33, count + STAGES, step, 0)
+        close_sum()
+        close_two()
+
+    return pl.pallas_call(
+        body,
+        in_specs=any_specs(16),
+        out_specs=any_specs(10),
+        out_shape=[
+            jax.ShapeDtypeStruct((columns // SUB, SUB, width), low),
+            jax.ShapeDtypeStruct((parts * width // SUB, SUB, columns), low),
+        ]
+        + [jax.ShapeDtypeStruct((BLK, width), low)] * 8,
+        scratch_shapes=[
+            pltpu.VMEM((rows, columns), low),
+            pltpu.VMEM((rows, width), low),
+            pltpu.VMEM((rows, width), low),
+            pltpu.VMEM(grad_projected.shape, low),
+            pltpu.SemaphoreType.DMA((4,)),
+        ]
+        + line_scratch()
+        + square_scratch()
+        + square_scratch(),
+        compiler_params=pltpu.CompilerParams(
+            vmem_limit_bytes=VMEM, collective_id=2, has_side_effects=True
+        ),
+        cost_estimate=cost(2 * 5 * rows * width * columns, 60e6),
+        name="mix_grads",
+    )(gated, grad_branch_all, normed_all, grad_projected, *sums, *two_sums)
+
+
+def row_copies(pair, rows, sems, at):
+    return [
+        pltpu.make_async_copy(src, rows.at[pl.ds(half * HALF, HALF)], sems.at[at + half])
+        for half, src in enumerate(pair)
+    ]
 
 
 def project_piece(pair, weight, kept, piece):
     parts, width, columns = weight.shape
     group_rows = NBLK * BLK
+    low = jnp.bfloat16
+    spot = pl.ds(piece * PIECE, PIECE)
+    joined = 2
 
     def body(*refs):
-        top_ref, low_ref, weight_ref = refs[:3]
-        rows_ref, out_ref, sems = refs[-3:]
-
-        @pl.when(pl.program_id(0) == 0)
-        def _():
-            copies = load_pair(top_ref, low_ref, rows_ref, sems, 0)
-            for copy in copies:
-                copy.start()
-            for copy in copies:
-                copy.wait()
-
-        out_ref[0] = straight(rows_ref[...], weight_ref[0]).astype(jnp.bfloat16)
+        weight_in = refs[2]
+        rows_out, parts_out, rows, weights, out, row_sems, weight_sems, out_sems = refs[3 + len(kept) :]
+        row_loads = row_copies(refs[:2], rows, row_sems, 0)
+        weight_loads = [
+            pltpu.make_async_copy(
+                weight_in.at[c], weights.at[:, pl.ds(c * columns, columns)], weight_sems.at[c]
+            )
+            for c in range(parts)
+        ]
+        stores = [
+            pltpu.make_async_copy(
+                out.at[:, pl.ds(c * columns, columns)], parts_out.at[c, spot, :], out_sems.at[c]
+            )
+            for c in range(parts)
+        ]
+        begin(row_loads)
+        begin(weight_loads)
+        finish(row_loads)
+        keep = pltpu.make_async_copy(rows, rows_out.at[spot, :], row_sems.at[2])
+        keep.start()
+        for c in range(0, parts, joined):
+            finish(weight_loads[c : c + joined])
+            at = slice(c * columns, (c + joined) * columns)
+            out[:, at] = straight(rows[...], weights[:, at]).astype(low)
+            begin(stores[c : c + joined])
+        finish(stores)
+        keep.wait()
 
     return pl.pallas_call(
         body,
-        grid=(parts,),
-        in_specs=any_specs(2)
-        + [pl.BlockSpec((1, width, columns), lambda c: (c, 0, 0))]
-        + any_specs(len(kept)),
-        out_specs=[
-            pl.BlockSpec((PIECE, width), lambda c: (piece, 0)),
-            pl.BlockSpec((1, PIECE, columns), lambda c: (c, piece, 0)),
+        in_specs=any_specs(3 + len(kept)),
+        out_specs=any_specs(2),
+        out_shape=[
+            jax.ShapeDtypeStruct((group_rows, width), low),
+            jax.ShapeDtypeStruct((parts, group_rows, columns), low),
         ],
-        out_shape=[
-            jax.ShapeDtypeStruct((group_rows, width), jnp.bfloat16),
-            jax.ShapeDtypeStruct((parts, group_rows, columns), jnp.bfloat16),
+        scratch_shapes=[
+            pltpu.VMEM((PIECE, width), low),
+            pltpu.VMEM((width, parts * columns), low),
+            pltpu.VMEM((PIECE, parts * columns), low),
+            pltpu.SemaphoreType.DMA((3,)),
+            pltpu.SemaphoreType.DMA((parts,)),
+            pltpu.SemaphoreType.DMA((parts,)),
         ],
-        scratch_shapes=[pltpu.SemaphoreType.DMA((2,))],
         input_output_aliases={3 + at: at for at in range(len(kept))},
         compiler_params=pltpu.CompilerParams(vmem_limit_bytes=VMEM),
         cost_estimate=cost(2 * PIECE * parts * width * columns, 2 * parts * width * columns + 8e6),
@@ -395,163 +923,214 @@
     )(*pair, weight, *kept)
 
 
-def back_piece(pair, weight, kept, piece):
-    columns, width = weight.shape
-    group_rows = NBLK * BLK
-
-    def body(*refs):
-        top_ref, low_ref, weight_ref = refs[:3]
-        rows_ref, out_ref, sems = refs[-3:]
-        copies = load_pair(top_ref, low_ref, rows_ref, sems, 0)
-        for copy in copies:
-            copy.start()
-        for copy in copies:
-            copy.wait()
-        out_ref[...] = across(rows_ref[...], weight_ref[...]).astype(jnp.bfloat16)
+def partial_sums(acts, weight, pieces, transposed):
+    parts, _, columns = acts.shape
+    width = weight.shape[1] if transposed else weight.shape[2]
+    deep = parts * columns
+    low = jnp.bfloat16
+    wide_tile = 1024
+
+    def body(act_in, weight_in, *refs):
+        outs = refs[: 2 * len(pieces)]
+        acts_ref, weights, out, act_sems, weight_sems, out_sems = refs[2 * len(pieces) :]
+
+        def place(c):
+            return pl.ds(c * columns, columns)
+
+        act_loads = [
+            [
+                pltpu.make_async_copy(
+                    act_in.at[c, pl.ds(piece * PIECE, PIECE), :],
+                    acts_ref.at[at, :, place(c)],
+                    act_sems.at[at, c],
+                )
+                for c in range(parts)
+            ]
+            for at, piece in enumerate(pieces)
+        ]
+        weight_loads = []
+        for j in range(width // wide_tile):
+            tile = pl.ds(j * wide_tile, wide_tile)
+            weight_loads.append(
+                [
+                    pltpu.make_async_copy(
+                        weight_in.at[c, tile, :], weights.at[tile, place(c)], weight_sems.at[j, c]
+                    )
+                    if transposed
+                    else pltpu.make_async_copy(
+                        weight_in.at[c, :, tile], weights.at[place(c), tile], weight_sems.at[j, c]
+                    )
+                    for c in range(parts)
+                ]
+            )
+        begin(act_loads[0])
+        for loads in weight_loads:
+            begin(loads)
+        for loads in act_loads[1:]:
+            begin(loads)
+        stores = []
+        for at in range(len(pieces)):
+            finish(act_loads[at])
+            for j, loads in enumerate(weight_loads):
+                if at == 0:
+                    finish(loads)
+                tile = slice(j * wide_tile, (j + 1) * wide_tile)
+                if transposed:
+                    total = across(acts_ref[at], weights[tile, :])
+                else:
+                    total = straight(acts_ref[at], weights[:, tile])
+                out[2 * at, :, tile] = total[:HALF].astype(low)
+                out[2 * at + 1, :, tile] = total[HALF:].astype(low)
+            now = [
+                pltpu.make_async_copy(out.at[at_out], outs[at_out], out_sems.at[at_out])
+                for at_out in (2 * at, 2 * at + 1)
+            ]
+            begin(now)
+            stores += now
+        finish(stores)
 
     return pl.pallas_call(
         body,
-        grid=(1,),
-        in_specs=any_specs(2)
-        + [pl.BlockSpec((columns, width), lambda c: (0, 0))]
-        + any_specs(len(kept)),
-        out_specs=[
-            pl.BlockSpec((PIECE, width), lambda c: (piece, 0)),
-            pl.BlockSpec((PIECE, columns), lambda c: (piece, 0)),
+        in_specs=any_specs(2),
+        out_specs=any_specs(2 * len(pieces)),
+        out_shape=[jax.ShapeDtypeStruct((HALF, width), low)] * (2 * len(pieces)),
+        scratch_shapes=[
+            pltpu.VMEM((len(pieces), PIECE, deep), low),
+            pltpu.VMEM((width, deep) if transposed else (deep, width), low),
+            pltpu.VMEM((2 * len(pieces), HALF, width), low),
+            pltpu.SemaphoreType.DMA((len(pieces), parts)),
+            pltpu.SemaphoreType.DMA((width // wide_tile, parts)),
+            pltpu.SemaphoreType.DMA((2 * len(pieces),)),
         ],
-        out_shape=[
-            jax.ShapeDtypeStruct((group_rows, width), jnp.bfloat16),
-            jax.ShapeDtypeStruct((group_rows, columns), jnp.bfloat16),
-        ],
-        scratch_shapes=[pltpu.SemaphoreType.DMA((2,))],
-        input_output_aliases={3 + at: at for at in range(len(kept))},
         compiler_params=pltpu.CompilerParams(vmem_limit_bytes=VMEM),
-        cost_estimate=cost(2 * PIECE * width * columns, 2 * width * columns + 6e6),
-        name="back_project",
-    )(*pair, weight, *kept)
-
-
-def sum_piece(acts, weight, piece, transposed):
-    parts, group_rows, columns = acts.shape
-    width = weight.shape[1] if transposed else weight.shape[2]
-
-    def body(act_ref, weight_ref, top_ref, low_ref, total):
-        part = pl.program_id(0)
-        product = (across if transposed else straight)(act_ref[0], weight_ref[0])
-
-        @pl.when(part == 0)
-        def _():
-            total[...] = product
-
-        @pl.when(part > 0)
-        def _():
-            total[...] += product
-
-        @pl.when(part == parts - 1)
-        def _():
-            top_ref[...] = total[:HALF].astype(jnp.bfloat16)
-            low_ref[...] = total[HALF:].astype(jnp.bfloat16)
-
-    return pl.pallas_call(
-        body,
-        grid=(parts,),
-        in_specs=[
-            pl.BlockSpec((1, PIECE, columns), lambda c: (c, piece, 0)),
-            pl.BlockSpec((1,) + weight.shape[1:], lambda c: (c, 0, 0)),
-        ],
-        out_specs=[pl.BlockSpec((HALF, width), lambda c: (0, 0))] * 2,
-        out_shape=[jax.ShapeDtypeStruct((HALF, width), jnp.bfloat16)] * 2,
-        scratch_shapes=[pltpu.VMEM((PIECE, width), jnp.float32)],
-        compiler_params=pltpu.CompilerParams(vmem_limit_bytes=VMEM),
-        cost_estimate=cost(2 * PIECE * parts * width * columns, 2 * parts * width * columns + 4e6),
-        name="partial_sum",
+        cost_estimate=cost(
+            2 * len(pieces) * PIECE * parts * width * columns, 2 * parts * width * columns + 8e6
+        ),
+        name="partial_sums",
     )(acts, weight)
 
 
 def unit_piece(pair, grad_pair, ffn_in, ffn_out, kept, piece):
     _, width, units = ffn_in.shape
     group_rows = NBLK * BLK
-    tile = 256
-    steps = pl.cdiv(units, tile)
-    last = units - (steps - 1) * tile
+    main = units // TILE * TILE
+    tail = units - main
+    low = jnp.bfloat16
+    spot = pl.ds(piece * PIECE, PIECE)
+    cuts = ((0, 2 * TILE), (2 * TILE, main - 2 * TILE))
+    wide_tile = 1024
 
     def body(*refs):
-        top_ref, low_ref, grad_top_ref, grad_low_ref, in_ref, out_ref = refs[:6]
-        rows_ref, grads_ref, act_ref, parts_ref = refs[-11:-7]
-        sum_refs = refs[-7:-3]
-        total_back, total_two, sems = refs[-3:]
-        step = pl.program_id(0)
-
-        @pl.when(step == 0)
-        def _():
-            copies = load_pair(top_ref, low_ref, rows_ref, sems, 0)
-            copies += load_pair(grad_top_ref, grad_low_ref, grads_ref, sems, 2)
-            for copy in copies:
-                copy.start()
-            total_back[...] = jnp.zeros_like(total_back)
-            total_two[...] = jnp.zeros_like(total_two)
-            for copy in copies:
-                copy.wait()
-
-        def work(size):
-            rows = rows_ref[...]
-            weight_a, weight_b = in_ref[0, :, :size], in_ref[1, :, :size]
-            weight_out = out_ref[:size, :]
-            part_a = straight(rows, weight_a)
-            part_b = straight(rows, weight_b)
-            grad_act = across(grads_ref[...], weight_out)
-            act = (part_a * part_b).astype(jnp.bfloat16)
-            grad_a = (grad_act * part_b).astype(jnp.bfloat16)
-            grad_b = (grad_act * part_a).astype(jnp.bfloat16)
-            act_ref[:, :size] = act
-            parts_ref[0, :, :size] = grad_a
-            parts_ref[1, :, :size] = grad_b
-            total_two[...] += straight(act, weight_out)
-            total_back[...] += across(grad_a, weight_a) + across(grad_b, weight_b)
-
-        if last == tile:
-            work(tile)
-        else:
-            pl.when(step < steps - 1)(lambda: work(tile))
-            pl.when(step == steps - 1)(lambda: work(last))
-
-        @pl.when(step == steps - 1)
-        def _():
-            for total, top_out, low_out in (
-                (total_back, sum_refs[0], sum_refs[1]),
-                (total_two, sum_refs[2], sum_refs[3]),
-            ):
-                top_out[...] = total[:HALF].astype(jnp.bfloat16)
-                low_out[...] = total[HALF:].astype(jnp.bfloat16)
-
-    low = jnp.bfloat16
+        in_ref, out_ref = refs[4:6]
+        outs = refs[6 + len(kept) :]
+        rows_out, grads_out, act_out, parts_out = outs[:4]
+        sum_outs = outs[4:8]
+        rows, grads, w_in, w_out, act, parts, sums, row_sems, sems, done_sems, sum_sems = outs[8:]
+        loads = row_copies(refs[:2], rows, row_sems, 0)
+        grad_loads = row_copies(refs[2:4], grads, row_sems, 2)
+
+        def weight_loads(which, start, size, first, second):
+            at = pl.ds(start, size)
+            return [
+                pltpu.make_async_copy(
+                    in_ref.at[0, :, at], w_in.at[:, pl.ds(first, size)], sems.at[which, 0]
+                ),
+                pltpu.make_async_copy(
+                    in_ref.at[1, :, at], w_in.at[:, pl.ds(second, size)], sems.at[which, 1]
+                ),
+                pltpu.make_async_copy(out_ref.at[at, :], w_out.at[at, :], sems.at[which, 2]),
+            ]
+
+        weights = [weight_loads(at, *cut, cut[0], main + cut[0]) for at, cut in enumerate(cuts)]
+        weights.append(weight_loads(2, main, tail, 2 * main, 2 * main + tail))
+        begin(loads)
+        begin(weights[0])
+        begin(grad_loads)
+        begin(weights[1])
+        begin(weights[2])
+        finish(loads)
+        stores = [
+            pltpu.make_async_copy(rows, rows_out.at[spot, :], done_sems.at[0]),
+            pltpu.make_async_copy(grads, grads_out.at[spot, :], done_sems.at[1]),
+        ]
+
+        def products(at, first, second, part_a, part_b, grad_act):
+            act[:, at] = (part_a * part_b).astype(low)
+            parts[:, first] = (grad_act * part_b).astype(low)
+            parts[:, second] = (grad_act * part_a).astype(low)
+
+        for which, (start, size) in enumerate(cuts):
+            finish(weights[which][:1])
+            at, second = slice(start, start + size), slice(main + start, main + start + size)
+            part_a = straight(rows[...], w_in[:, at])
+            finish(weights[which][1:2])
+            part_b = straight(rows[...], w_in[:, second])
+            finish(weights[which][2:])
+            if which == 0:
+                finish(grad_loads)
+                begin(stores)
+            grad_act = across(grads[...], w_out[at, :])
+            products(at, at, second, part_a, part_b, grad_act)
+        if tail:
+            finish(weights[2])
+            both = straight(rows[...], w_in[:, 2 * main :])
+            grad_act = across(grads[...], w_out[main:, :])
+            products(
+                slice(main, units),
+                slice(2 * main, 2 * main + tail),
+                slice(2 * main + tail, 2 * units),
+                both[:, :tail],
+                both[:, tail:],
+                grad_act,
+            )
+        more = [
+            pltpu.make_async_copy(act, act_out.at[spot, :], done_sems.at[2]),
+            pltpu.make_async_copy(parts, parts_out.at[spot, :], done_sems.at[3]),
+        ]
+        begin(more)
+        stores += more
+        for j in range(width // wide_tile):
+            at = slice(j * wide_tile, (j + 1) * wide_tile)
+            back = across(parts[...], w_in[at, :])
+            sums[0, :, at] = back[:HALF].astype(low)
+            sums[1, :, at] = back[HALF:].astype(low)
+            two = straight(act[...], w_out[:, at])
+            sums[2, :, at] = two[:HALF].astype(low)
+            sums[3, :, at] = two[HALF:].astype(low)
+            tile = pl.ds(j * wide_tile, wide_tile)
+            now = [
+                pltpu.make_async_copy(
+                    sums.at[at_out, :, tile], sum_outs[at_out].at[:, tile], sum_sems.at[j, at_out]
+                )
+                for at_out in range(4)
+            ]
+            begin(now)
+            stores += now
+        finish(stores)
+
     return pl.pallas_call(
         body,
-        grid=(steps,),
-        in_specs=any_specs(4)
-        + [
-            pl.BlockSpec((2, width, tile), lambda f: (0, 0, f)),
-            pl.BlockSpec((tile, width), lambda f: (f, 0)),
-        ]
-        + any_specs(len(kept)),
-        out_specs=[
-            pl.BlockSpec((PIECE, width), lambda f: (piece, 0)),
-            pl.BlockSpec((PIECE, width), lambda f: (piece, 0)),
-            pl.BlockSpec((PIECE, tile), lambda f: (piece, f)),
-            pl.BlockSpec((2, PIECE, tile), lambda f: (0, piece, f)),
-        ]
-        + [pl.BlockSpec((HALF, width), lambda f: (0, 0))] * 4,
+        in_specs=any_specs(6 + len(kept)),
+        out_specs=any_specs(8),
         out_shape=[
             jax.ShapeDtypeStruct((group_rows, width), low),
             jax.ShapeDtypeStruct((group_rows, width), low),
             jax.ShapeDtypeStruct((group_rows, units), low),
-            jax.ShapeDtypeStruct((2, group_rows, units), low),
+            jax.ShapeDtypeStruct((group_rows, 2 * units), low),
         ]
         + [jax.ShapeDtypeStruct((HALF, width), low)] * 4,
         scratch_shapes=[
-            pltpu.VMEM((PIECE, width), jnp.float32),
-            pltpu.VMEM((PIECE, width), jnp.float32),
+            pltpu.VMEM((PIECE, width), low),
+            pltpu.VMEM((PIECE, width), low),
+            pltpu.VMEM((width, 2 * units), low),
+            pltpu.VMEM((units, width), low),
+            pltpu.VMEM((PIECE, units), low),
+            pltpu.VMEM((PIECE, 2 * units), low),
+            pltpu.VMEM((4, HALF, width), low),
             pltpu.SemaphoreType.DMA((4,)),
+            pltpu.SemaphoreType.DMA((3, 3)),
+            pltpu.SemaphoreType.DMA((4,)),
+            pltpu.SemaphoreType.DMA((width // wide_tile, 4)),
         ],
         input_output_aliases={6 + at: at for at in range(len(kept))},
         compiler_params=pltpu.CompilerParams(vmem_limit_bytes=VMEM),
@@ -687,7 +1266,8 @@
 def square_device(
     hidden, mix_weight, out_weight, ffn_in_weight, ffn_out_weight, seq_lengths, block_seq, cotangent
 ):
-    local_rows = hidden.shape[0]
+    local_rows, width = hidden.shape
+    units = ffn_out_weight.shape[0]
     head_count = mix_weight.shape[2] // HS
     narrow_index = lax.axis_index("narrow")
     valid_all, fresh_block = group_masks(seq_lengths, block_seq)
@@ -714,8 +1294,11 @@
     grad_pieces = gather_pieces(*((m * g).astype(low) for m, g in zip(lives, grads_in)))
 
     gated, mixing, states = mix_forward(slots, fresh, rates, parts)
-    partial = [sum_piece(gated, out_weight[None], at, False) for at in range(4)]
-    branch = scatter_pieces(*partial)
+    far_top, far_low, near_top, near_low = partial_sums(gated, out_weight[None], (3, 1), False)
+    side_low, side_top, own_top, own_low = partial_sums(gated, out_weight[None], (2, 0), False)
+    branch = scatter_pieces(
+        (own_top, own_low), (near_top, near_low), (side_low, side_top), (far_top, far_low)
+    )
     middle = [x + m * b for x, m, b in zip(inputs, lives, branch)]
 
     pieces = gather_pieces(*(row_norm(rows).astype(low) for rows in middle))
@@ -724,35 +1307,51 @@
         *kept, back_top, back_low, two_top, two_low = unit_piece(
             pair, grad_pair, ffn_in_weight, ffn_out_weight, kept, at
         )
-        back_sums.append((back_top, back_low))
-        two_sums.append((two_top, two_low))
+        back_sums += [back_top, back_low]
+        two_sums += [two_top, two_low]
     normed_two_all, grad_two_all, act, grad_parts = kept
-    grad_normed_two = scatter_pieces(*back_sums)
-    grad_middle = [g + norm_back(v, n) for g, v, n in zip(grads_in, middle, grad_normed_two)]
-    pieces = gather_pieces(*((m * g).astype(low) for m, g in zip(lives, grad_middle)))
-
-    grad_ffn_out = wide_sum(down(act, grad_two_all).astype(low))
+
+    out_grads, in_grads, grad_branch_all, grad_middle = unit_grads(
+        act, grad_two_all, normed_two_all, grad_parts, back_sums, jnp.concatenate(middle), cotangent, live
+    )
+    main = units // TILE * TILE
+    tail = units - main
+    in_grads = in_grads.reshape(width, 2 * units)
     grad_ffn_in = jnp.stack(
-        [wide_sum(down(normed_two_all, grad_parts[c]).astype(low)) for c in range(2)]
-    )
-
-    kept = ()
-    for at, pair in enumerate(pieces):
-        kept = back_piece(pair, out_weight, kept, at)
-    grad_branch_all, grad_gated = kept
-    grad_out = wide_sum(down(gated[0], grad_branch_all).astype(low))
+        [
+            jnp.concatenate(
+                [
+                    in_grads[:, c * main : (c + 1) * main],
+                    in_grads[:, 2 * main + c * tail : 2 * main + (c + 1) * tail],
+                ],
+                axis=1,
+            )
+            for c in range(2)
+        ]
+    ).astype(jnp.float32)
+    grad_ffn_out = out_grads.reshape(units, width).astype(jnp.float32)
+
+    grad_gated = across(grad_branch_all, out_weight).astype(low)
     grad_projected = mix_backward(slots, fresh, rates, parts, mixing, states, grad_gated)
-    partial = [sum_piece(grad_projected, mix_weight, at, True) for at in range(4)]
-    grad_normed = scatter_pieces(*partial)
-    grad_mix = jnp.stack(
-        [wide_sum(down(normed_all, grad_projected[c]).astype(low)) for c in range(4)]
-    )
-    branch_two = scatter_pieces(*two_sums)
+    sums = partial_sums(grad_projected, mix_weight, (0, 1, 2, 3), True)
+    out_grads, mix_grads_low, *terms = mix_grads(
+        gated, grad_branch_all, normed_all, grad_projected, sums[2:], two_sums[2:]
+    )
+    grad_out = out_grads.reshape(out_weight.shape).astype(jnp.float32)
+    grad_mix = mix_grads_low.reshape(mix_weight.shape).astype(jnp.float32)
+    grad_normed = add_rows(sums[0], terms[0], terms[2]), add_rows(sums[1], terms[1], terms[3])
+    branch_two = (
+        add_rows(two_sums[0], terms[4], terms[6]),
+        add_rows(two_sums[1], terms[5], terms[7]),
+    )
     layer_out = jnp.concatenate(
         [(v + m * b).astype(low) for v, m, b in zip(middle, lives, branch_two)]
     )
     input_grad = jnp.concatenate(
-        [(g + norm_back(x, n)).astype(low) for g, x, n in zip(grad_middle, inputs, grad_normed)]
+        [
+            (g + norm_back(x, n)).astype(low)
+            for g, x, n in zip(halves(grad_middle), inputs, grad_normed)
+        ]
     )
     return (layer_out, input_grad, grad_mix, grad_out, grad_ffn_in, grad_ffn_out)
 

time: 1350 us -> 839 us (0.62)
  waiting for transfers between devices: 733 us -> 118 us
  Pallas kernels: 262 us -> 587 us
  matrix products: 96.9 us -> 9.14 us
  starting transfers between devices: 106 us -> 26.5 us
  other arithmetic: 120 us -> 70.3 us
    ppermute x48 -> x0, waiting for transfers between devices: 492 us -> none  [the longest x32 492 us: over_z(): lax.ppermute(rows, 'wide', [(2 * a + c, 2 * b + c) for a, b in pairs for...]
    pallas_call x20 -> x13, Pallas kernels: 235 us -> 559 us  [the longest x1 224 us: unit_grads(): pl.pallas_call(body, in_specs=any_specs(14) + [pl.BlockSpec(memory_space=...]
    dot_general x8 -> x1, matrix products: 96.9 us -> 9.14 us  [across(): lax.dot_general(left, right, (((1,), (1,)), ((), ())), preferred_element_...]
    ppermute x24 -> x12, waiting for transfers between devices: 176 us -> 95.5 us  [over_x(): return lax.ppermute(rows, 'narrow', [(at, at ^ 1) for at in range(4)])]
    ppermute x48 -> x0, starting transfers between devices: 51.1 us -> none  [the longest x32 49.1 us: over_z(): lax.ppermute(rows, 'wide', [(2 * a + c, 2 * b + c) for a, b in pairs for...]
    ppermute x24 -> x12, waiting for transfers between devices: 64.3 us -> 22.1 us  [over_y(): return lax.ppermute(rows, 'narrow', [(at, at ^ 2) for at in range(4)])]
    convert_element_type x32 -> x2, other arithmetic: 42.7 us -> 5.53 us  [add_low(): sum((term.astype(jnp.float32) for term in terms)).astype(jnp.bfloat16)]
    select_n x24 -> x0, other arithmetic: 19.4 us -> none  [the longest x8 13.3 us: wide_sum(): jnp.where(core == 0, jnp.stack([result, partner]), jnp.stack([partner, re...]
  transfers between devices with their start and end apart: 96 -> 24, of which waited for: 32 -> 9; matrix products, arithmetic and copies ran while one was open for 15% -> 2% of each run, Pallas kernels for 18% -> 15%
where the time goes in v2:
time: 839 us; the launch traced here: 830 us
  Pallas kernels  587 us (70%)
  waiting for transfers between devices  118 us (14%)
  other arithmetic  70.3 us (8%)
  starting transfers between devices  26.5 us (3%)
  local copies, waits for them, and re-layouts  17.7 us (2%)
  matrix products  9.14 us (1%)
    pallas_call x1, Pallas kernels, unit_grads(): pl.pallas_call(body, in_specs=any_specs(14) + [pl.BlockSpec(memory_space=...  224 us
    pallas_call x1, Pallas kernels, mix_grads(): pl.pallas_call(body, in_specs=any_specs(16), out_specs=any_specs(10), out...  140 us
    pallas_call x4, Pallas kernels, unit_piece(): pl.pallas_call(body, in_specs=any_specs(6 + len(kept)), out_specs=any_spe...  123 us
    ppermute x12, waiting for transfers between devices, over_x(): return lax.ppermute(rows, 'narrow', [(at, at ^ 1) for at in range(4)])  95.5 us
    pallas_call x4, Pallas kernels, project_piece(): pl.pallas_call(body, in_specs=any_specs(3 + len(kept)), out_specs=any_spe...  36.7 us
    pallas_call x3, Pallas kernels, partial_sums(): pl.pallas_call(body, in_specs=any_specs(2), out_specs=any_specs(2 * len(p...  35 us
    ppermute x12, waiting for transfers between devices, over_y(): return lax.ppermute(rows, 'narrow', [(at, at ^ 2) for at in range(4)])  22.1 us
    pallas_call x1, Pallas kernels, mix_backward(): pl.pallas_call(body, grid_spec=pltpu.PrefetchScalarGridSpec(num_scalar_pr...  18.1 us
  transfers between devices with their start and end apart: 24, of which 9 were waited for; matrix products, arithmetic and copies ran while one was open for 2% of the time, Pallas kernels for 15%

profile of v2, /device:TPU:0, one launch (start us, length us, event | category | flops | bytes accessed | tf_op | source)
XLA Modules:
  0.0 829.6 jit_solution(12123257892262330922)
XLA Ops:
  0.6 2.2 fusion.17
  4.2 3.0 collective-permute-start.2
  7.1 1.5 collective-permute-start.4
  11.2 9.1 %project.4 = (bf16[2048,2048]{1,0:T(8,128)(2,1)}, bf16[4,2048,512]{2,1,0:T(8,128)(2,1)}) custom-call(bf16[256,2048]{1,0:T(8,128)(2,1)} %copy-done.25, bf16[256,2048]{1,0:T(8,128)(2,1)} %get-tuple-element.172.refs_1_, bf16[4,2048,512]{2,1,0:T(8,128)(2,1)} %weight_in.1), custom_call_target="tpu_custom_call" | custom-call | flops 4294967296 | bytes 16388608 | tf_op jit(solution)/shard_map/project/pallas_call | solution.py:903
  22.2 32.3 %collective-permute-done.refs_0_ = bf16[256,2048]{1,0:T(8,128)(2,1)} collective-permute-done((bf16[256,2048]{1,0:T(8,128)(2,1)S(1)}, bf16[256,2048]{1,0:T(8,128)(2,1)}, u32[]{:S(2)}, u32[]{:S(2)}) %collective-permute-start) | collective-permute-done | bytes 1048608 | tf_op jit(solution)/shard_map/ppermute | solution.py:262
  54.9 1.6 collective-permute-start.3
  58.9 9.1 %project.5 = (bf16[2048,2048]{1,0:T(8,128)(2,1)}, bf16[4,2048,512]{2,1,0:T(8,128)(2,1)}) custom-call(bf16[256,2048]{1,0:T(8,128)(2,1)} %collective-permute-done.refs_0_, bf16[256,2048]{1,0:T(8,128)(2,1)} %collective-permute-done.2.refs_1_, bf16[4,2048,512]{2,1,0:T(8,128)(2,1)} %weight_in.1, ...), custom_call_target="tpu_custom_call", output_to_operand_aliasing={{0}: (3, {}), {1}: (4, {})} | custom-call | flops 4294967296 | bytes 16388608 | tf_op jit(solution)/shard_map/project/pallas_call | solution.py:903
  68.0 9.1 %project.6 = (bf16[2048,2048]{1,0:T(8,128)(2,1)}, bf16[4,2048,512]{2,1,0:T(8,128)(2,1)}) custom-call(bf16[256,2048]{1,0:T(8,128)(2,1)} %collective-permute-done.4.refs_0_, bf16[256,2048]{1,0:T(8,128)(2,1)} %collective-permute-done.5.refs_1_, bf16[4,2048,512]{2,1,0:T(8,128)(2,1)} %weight_in.1, ...), custom_call_target="tpu_custom_call", output_to_operand_aliasing={{0}: (3, {}), {1}: (4, {})} | custom-call | flops 4294967296 | bytes 16388608 | tf_op jit(solution)/shard_map/project/pallas_call | solution.py:903
  79.0 9.4 %project.7 = (bf16[2048,2048]{1,0:T(8,128)(2,1)}, bf16[4,2048,512]{2,1,0:T(8,128)(2,1)}) custom-call(bf16[256,2048]{1,0:T(8,128)(2,1)} %collective-permute-done.1.refs_0_, bf16[256,2048]{1,0:T(8,128)(2,1)} %collective-permute-done.3.refs_1_, bf16[4,2048,512]{2,1,0:T(8,128)(2,1)} %weight_in.1, ...), custom_call_target="tpu_custom_call", output_to_operand_aliasing={{0}: (3, {}), {1}: (4, {})} | custom-call | flops 4294967296 | bytes 16388608 | tf_op jit(solution)/shard_map/project/pallas_call | solution.py:903
  88.3 9.8 %mix_forward.1 = (bf16[1,2048,512]{2,1,0:T(8,128)(2,1)}, bf16[2048,512]{1,0:T(8,128)(2,1)}, bf16[4,8,128,128]{3,2,1,0:T(8,128)(2,1)}) custom-call(s32[8]{0:T(128)} %compare_select_fusion.1.slot_ref, s32[8]{0:T(128)} %compare_convert_fusion.fresh_ref, f32[4]{0:T(128)} %multiply_power_fusion.rate_ref, bf16[4,2048,512]{2,1,0:T(8,128)(2,1)} %get-tuple-element.85.parts_ref), custom_call_target="tpu_custom_call" | custom-call | flops 8000000000 | bytes 14000000 | tf_op jit(solution)/shard_map/mix_forward/pallas_call | solution.py:1179
  98.1 5.5 partial_sums.4
  103.6 1.4 collective-permute-start.10
  105.0 1.5 collective-permute-start.7
  107.8 5.5 partial_sums.3
  113.3 16.8 %collective-permute-done.10 = bf16[256,2048]{1,0:T(8,128)(2,1)} collective-permute-done((bf16[256,2048]{1,0:T(8,128)(2,1)}, bf16[256,2048]{1,0:T(8,128)(2,1)}, u32[]{:S(2)}, u32[]{:S(2)}) %collective-permute-start.10) | collective-permute-done | bytes 1048608 | tf_op jit(solution)/shard_map/ppermute | solution.py:266
  130.1 2.9 add_convert_fusion.2
  134.4 2.6 add_convert_fusion.3
  137.0 1.5 collective-permute-start.8
  140.2 13.6 %collective-permute-done.6 = bf16[256,2048]{1,0:T(8,128)(2,1)S(1)} collective-permute-done((bf16[256,2048]{1,0:T(8,128)(2,1)}, bf16[256,2048]{1,0:T(8,128)(2,1)S(1)}, u32[]{:S(2)}, u32[]{:S(2)}) %collective-permute-start.6) | collective-permute-done | bytes 1048608 | tf_op jit(solution)/shard_map/ppermute | solution.py:262
  153.8 18.7 %collective-permute-done.11 = bf16[256,2048]{1,0:T(8,128)(2,1)} collective-permute-done((bf16[256,2048]{1,0:T(8,128)(2,1)}, bf16[256,2048]{1,0:T(8,128)(2,1)}, u32[]{:S(2)}, u32[]{:S(2)}) %collective-permute-start.11) | collective-permute-done | bytes 1048608 | tf_op jit(solution)/shard_map/ppermute | solution.py:262
  172.5 5.6 multiply_reduce_fusion.1
  180.5 2.5 pad_maximum_fusion.refs_12_
  186.2 1.5 collective-permute-start.18
  187.7 30.7 %gated_unit.4 = (bf16[2048,2048]{1,0:T(8,128)(2,1)}, bf16[2048,2048]{1,0:T(8,128)(2,1)}, bf16[2048,1408]{1,0:T(8,128)(2,1)}, bf16[2048,2816]{1,0:T(8,128)(2,1)},...) custom-call(bf16[256,2048]{1,0:T(8,128)(2,1)} %multiply_convert_fusi, ...), custom_call_target="tpu_custom_call" | custom-call | flops 17716740096 | bytes 29301504 | tf_op jit(solution)/shard_map/gated_unit/pallas_call | solution.py:1111
  219.0 9.1 %collective-permute-done.12.refs_0_ = bf16[256,2048]{1,0:T(8,128)(2,1)} collective-permute-done((bf16[256,2048]{1,0:T(8,128)(2,1)}, bf16[256,2048]{1,0:T(8,128)(2,1)}, u32[]{:S(2)}, u32[]{:S(2)}) %collective-permute-start.12) | collective-permute-done | bytes 1048608 | tf_op jit(solution)/shard_map/ppermute | solution.py:262
  229.2 21.4 %collective-permute-done.16.refs_2_ = bf16[256,2048]{1,0:T(8,128)(2,1)} collective-permute-done((bf16[256,2048]{1,0:T(8,128)(2,1)S(1)}, bf16[256,2048]{1,0:T(8,128)(2,1)}, u32[]{:S(2)}, u32[]{:S(2)}) %collective-permute-start.16) | collective-permute-done | bytes 1048608 | tf_op jit(solution)/shard_map/ppermute | solution.py:262
  251.6 1.5 collective-permute-start.15
  253.1 30.7 %gated_unit.5 = (bf16[2048,2048]{1,0:T(8,128)(2,1)}, bf16[2048,2048]{1,0:T(8,128)(2,1)}, bf16[2048,1408]{1,0:T(8,128)(2,1)}, bf16[2048,2816]{1,0:T(8,128)(2,1)},...) custom-call(bf16[256,2048]{1,0:T(8,128)(2,1)} %collective-permute-do, ...), custom_call_target="tpu_custom_call", output_to_operand_aliasing={{0}: (6, {}), {1}: (7, {}), {2}: (8, {}), {3}: (9, {})} | custom-call | flops 17716740096 | bytes 29301504 | tf_op jit(solution)/shard_map/gated_unit/pallas_call | solution.py:1111
  284.4 1.5 collective-permute-start.17
  286.4 30.8 %gated_unit.6 = (bf16[2048,2048]{1,0:T(8,128)(2,1)}, bf16[2048,2048]{1,0:T(8,128)(2,1)}, bf16[2048,1408]{1,0:T(8,128)(2,1)}, bf16[2048,2816]{1,0:T(8,128)(2,1)},...) custom-call(bf16[256,2048]{1,0:T(8,128)(2,1)} %collective-permute-do, ...), custom_call_target="tpu_custom_call", output_to_operand_aliasing={{0}: (6, {}), {1}: (7, {}), {2}: (8, {}), {3}: (9, {})} | custom-call | flops 17716740096 | bytes 29301504 | tf_op jit(solution)/shard_map/gated_unit/pallas_call | solution.py:1111
  317.3 3.8 collective-permute-done.17.refs_2_
  321.1 31.0 %gated_unit.7 = (bf16[2048,2048]{1,0:T(8,128)(2,1)}, bf16[2048,2048]{1,0:T(8,128)(2,1)}, bf16[2048,1408]{1,0:T(8,128)(2,1)}, bf16[2048,2816]{1,0:T(8,128)(2,1)},...) custom-call(bf16[256,2048]{1,0:T(8,128)(2,1)} %copy-done.42, ...), custom_call_target="tpu_custom_call", output_to_operand_aliasing={{0}: (6, {}), {1}: (7, {}), {2}: (8, {}), {3}: (9, {})} | custom-call | flops 17716740096 | bytes 29301504 | tf_op jit(solution)/shard_map/gated_unit/pallas_call | solution.py:1111
  352.2 223.5 %unit_grads.1 = (bf16[11,128,2048]{2,1,0:T(8,128)(2,1)}, bf16[16,128,2816]{2,1,0:T(8,128)(2,1)}, bf16[2048,2048]{1,0:T(8,128)(2,1)}, f32[512,2048]{1,0:T(8,128)}) custom-call(bf16[2048,1408]{1,0:T(8,128)(2,1)} %get-tuple-element.108.refs_0_, bf16[2048,2048]{1,0:T(8,128)(2,1)} %get-tuple-element.109.refs_1_, bf16[2048,2048]{1,0:T(8,128)(2,1)} %get-tuple-element.110.refs_2_, ...), custom_call_target="tpu_custom_call" | custom-call | flops 35433480192 | bytes 60000000 | tf_op jit(solution)/shard_map/unit_grads/pallas_call | solution.py:727
  575.7 8.6 %fusion.20 = (bf16[2048,1280]{1,0:T(8,128)(2,1)}, bf16[2048,1280]{1,0:T(8,128)(2,1)}) fusion(bf16[2048,2816]{1,0:T(8,128)(2,1)} %bitcast.30), kind=kLoop, calls=%fused_computation.72 | loop fusion | bytes 20971520 | tf_op jit(solution)/shard_map/slice | solution.py:1324
  584.3 2.4 fusion.21
  586.8 9.1 %convolution_convert_fusion.grad_ref = bf16[2048,512]{1,0:T(8,128)(2,1)} fusion(bf16[2048,2048]{1,0:T(8,128)(2,1)} %get-tuple-element.120.refs_1_, bf16[512,2048]{1,0:T(8,128)(2,1)S(1)} %copy-done.40), kind=kOutput, calls=%fused_computation.14 | convolution fusion | flops 4296015872 | bytes 12582912 | tf_op jit(solution)/shard_map/dot_general | solution.py:301
  595.9 18.1 %mix_backward.1.act_in.refs_3_ = bf16[4,2048,512]{2,1,0:T(8,128)(2,1)} custom-call(s32[8]{0:T(128)} %compare_select_fusion.1.slot_ref, s32[8]{0:T(128)} %compare_convert_fusion.fresh_ref, f32[4]{0:T(128)} %multiply_power_fusion.rate_ref, bf16[4,2048,512]{2,1,0:T(8,128)(2,1)} %get-tuple-element.85.parts_ref, bf16[2048,512]{1,0:T(8,128)(2,1)} %get-tuple-element.122.mixing_ref, ...), custom_call_target="tpu_custom_call" | custom-call | flops 20000000000 | bytes 22000000 | tf_op jit(solution)/shard_map/mix_backward/pallas_call | solution.py:1240
  614.1 24.0 %partial_sums.5 = (bf16[256,2048]{1,0:T(8,128)(2,1)}, bf16[256,2048]{1,0:T(8,128)(2,1)}, bf16[256,2048]{1,0:T(8,128)(2,1)}, bf16[256,2048]{1,0:T(8,128)(2,1)}, b...) custom-call(bf16[4,2048,512]{2,1,0:T(8,128)(2,1)} %mix_backward.1.ac, ...), custom_call_target="tpu_custom_call" | custom-call | flops 17179869184 | bytes 16388608 | tf_op jit(solution)/shard_map/partial_sums/pallas_call | solution.py:992
  638.0 140.3 %mix_grads.1 = (bf16[4,128,2048]{2,1,0:T(8,128)(2,1)}, bf16[64,128,512]{2,1,0:T(8,128)(2,1)}, bf16[256,2048]{1,0:T(8,128)(2,1)}, bf16[256,2048]{1,0:T(8,128)(2,1...) custom-call(bf16[1,2048,512]{2,1,0:T(8,128)(2,1)} %get-tuple-element, ...), custom_call_target="tpu_custom_call" | custom-call | flops 21474836480 | bytes 60000000 | tf_op jit(solution)/shard_map/mix_grads/pallas_call | solution.py:833
  778.4 12.1 %bitcast_convert_fusion = f32[4,2048,512]{2,1,0:T(8,128)} fusion(bf16[4,2048,512]{2,1,0:T(8,128)(2,1)} %bitcast.32), kind=kLoop, calls=%fused_computation.3 | loop fusion | flops 4194304 | bytes 25165824 | tf_op jit(solution)/shard_map/convert_element_type | solution.py:1341
  790.6 3.2 fusion.11
  793.8 2.7 bitcast_convert_fusion.2
  796.4 8.8 %bitcast_convert_fusion.1 = f32[1408,2048]{1,0:T(8,128)} fusion(bf16[11,128,2048]{2,1,0:T(8,128)(2,1)} %get-tuple-element.151), kind=kLoop, calls=%fused_computation.6 | loop fusion | flops 2883584 | bytes 17301504 | tf_op jit(solution)/shard_map/convert_element_type | solution.py:1332
  806.3 2.9 maximum_bitcast_fusion.1
  809.3 9.3 %maximum_convert_fusion = f32[2,2048,1408]{2,1,0:T(8,128)} fusion(bf16[1,2048,1408]{2,1,0:T(8,128)(2,1)S(1)} %maximum_bitcast_fusion.1, bf16[1,2048,1408]{2,1,0:T(8,128)(2,1)S(1)} %maximum_bitcast_fusion), kind=kLoop, calls=%fused_computation.2 | loop fusion | flops 11534336 | bytes 34603008 | tf_op jit(solution)/shard_map/convert_element_type | solution.py:1331
  818.6 2.8 fusion.15
  821.5 1.6 pad_maximum_fusion.2
  827.6 1.6 pad_maximum_fusion.1
  (150 shorter events, 29.5 us)
Async XLA Ops:
  2.9 6.4 copy-start.38
  2.9 7.0 copy-start.39
  4.2 7.0 copy-start.25
  4.2 50.7 %collective-permute-start.2 = (bf16[256,2048]{1,0:T(8,128)(2,1)}, bf16[256,2048]{1,0:T(8,128)(2,1)}, u32[]{:S(2)}, u32[]{:S(2)}) collective-permute-start(bf16[256,2048]{1,0:T(8,128)(2,1)} %get-tuple-element.172.refs_1_), channel_id=1, source_target_pairs={{0,2},{1,3},{2,0},{3,1},{4,6},{5,7},{6,4},{7,5},{8,10},{9,11},{10,... | collective-permute-start | bytes 3145736 | tf_op jit(solution)/shard_map/ppermute | solution.py:266
  7.1 60.9 %collective-permute-start.4 = (bf16[256,2048]{1,0:T(8,128)(2,1)}, bf16[256,2048]{1,0:T(8,128)(2,1)}, u32[]{:S(2)}, u32[]{:S(2)}) collective-permute-start(bf16[256,2048]{1,0:T(8,128)(2,1)} %get-tuple-element.172.refs_1_), channel_id=1, source_target_pairs={{0,1},{1,0},{2,3},{3,2},{4,5},{5,4},{6,7},{7,6},{8,9},{9,8},{10,11... | collective-permute-start | bytes 3145736 | tf_op jit(solution)/shard_map/ppermute | solution.py:262
  8.6 45.9 %collective-permute-start = (bf16[256,2048]{1,0:T(8,128)(2,1)S(1)}, bf16[256,2048]{1,0:T(8,128)(2,1)}, u32[]{:S(2)}, u32[]{:S(2)}) collective-permute-start(bf16[256,2048]{1,0:T(8,128)(2,1)S(1)} %get-tuple-element.173.refs_0_), channel_id=1, source_target_pairs={{0,1},{1,0},{2,3},{3,2},{4,5},{5,4},{6,7},{7,6},{8,9},{9,8},{10,11... | collective-permute-start | bytes 3145736 | tf_op jit(solution)/shard_map/ppermute | solution.py:262
  9.2 58.9 %collective-permute-start.5 = (bf16[256,2048]{1,0:T(8,128)(2,1)S(1)}, bf16[256,2048]{1,0:T(8,128)(2,1)}, u32[]{:S(2)}, u32[]{:S(2)}) collective-permute-start(bf16[256,2048]{1,0:T(8,128)(2,1)S(1)} %get-tuple-element.173.refs_0_), channel_id=1, source_target_pairs={{0,2},{1,3},{2,0},{3,1},{4,6},{5,7},{6,4},{7,5},{8,10},{9,11},{10,... | collective-permute-start | bytes 3145736 | tf_op jit(solution)/shard_map/ppermute | solution.py:266
  11.2 45.9 %copy-start.1 = (s32[4]{0:T(128)S(1)}, s32[4]{0:T(128)}, u32[]{:S(2)}) copy-start(s32[4]{0:T(128)} %constant.69.clone) | copy-start | bytes 52
  11.2 46.5 %copy-start = (s32[4]{0:T(128)S(1)}, s32[4]{0:T(128)}, u32[]{:S(2)}) copy-start(s32[4]{0:T(128)} %constant.70.clone) | copy-start | bytes 52
  54.5 24.0 %collective-permute-start.1 = (bf16[256,2048]{1,0:T(8,128)(2,1)}, bf16[256,2048]{1,0:T(8,128)(2,1)}, u32[]{:S(2)}, u32[]{:S(2)}) collective-permute-start(bf16[256,2048]{1,0:T(8,128)(2,1)} %collective-permute-done.refs_0_), channel_id=1, source_target_pairs={{0,2},{1,3},{2,0},{3,1},{4,6},{5,7},{6,4},{7,5},{8,10},{9,11},{10,... | collective-permute-start | bytes 3145736 | tf_op jit(solution)/shard_map/ppermute | solution.py:266
  54.9 24.1 %collective-permute-start.3 = (bf16[256,2048]{1,0:T(8,128)(2,1)}, bf16[256,2048]{1,0:T(8,128)(2,1)}, u32[]{:S(2)}, u32[]{:S(2)}) collective-permute-start(bf16[256,2048]{1,0:T(8,128)(2,1)} %collective-permute-done.2.refs_1_), channel_id=1, source_target_pairs={{0,1},{1,0},{2,3},{3,2},{4,5},{5,4},{6,7},{7,6},{8,9},{9,8},{10,11... | collective-permute-start | bytes 3145736 | tf_op jit(solution)/shard_map/ppermute | solution.py:262
  103.6 26.5 %collective-permute-start.10 = (bf16[256,2048]{1,0:T(8,128)(2,1)}, bf16[256,2048]{1,0:T(8,128)(2,1)}, u32[]{:S(2)}, u32[]{:S(2)}) collective-permute-start(bf16[256,2048]{1,0:T(8,128)(2,1)} %get-tuple-element.94), channel_id=1, source_target_pairs={{0,2},{1,3},{2,0},{3,1},{4,6},{5,7},{6,4},{7,5},{8,10},{9,11},{10,... | collective-permute-start | bytes 3145736 | tf_op jit(solution)/shard_map/ppermute | solution.py:266
  105.0 29.3 %collective-permute-start.7 = (bf16[256,2048]{1,0:T(8,128)(2,1)}, bf16[256,2048]{1,0:T(8,128)(2,1)}, u32[]{:S(2)}, u32[]{:S(2)}) collective-permute-start(bf16[256,2048]{1,0:T(8,128)(2,1)} %get-tuple-element.90), channel_id=1, source_target_pairs={{0,1},{1,0},{2,3},{3,2},{4,5},{5,4},{6,7},{7,6},{8,9},{9,8},{10,11... | collective-permute-start | bytes 3145736 | tf_op jit(solution)/shard_map/ppermute | solution.py:262
  106.5 47.3 %collective-permute-start.6 = (bf16[256,2048]{1,0:T(8,128)(2,1)}, bf16[256,2048]{1,0:T(8,128)(2,1)S(1)}, u32[]{:S(2)}, u32[]{:S(2)}) collective-permute-start(bf16[256,2048]{1,0:T(8,128)(2,1)} %get-tuple-element.88), channel_id=1, source_target_pairs={{0,1},{1,0},{2,3},{3,2},{4,5},{5,4},{6,7},{7,6},{8,9},{9,8},{10,11... | collective-permute-start | bytes 3145736 | tf_op jit(solution)/shard_map/ppermute | solution.py:262
  107.1 46.8 %collective-permute-start.9 = (bf16[256,2048]{1,0:T(8,128)(2,1)}, bf16[256,2048]{1,0:T(8,128)(2,1)}, u32[]{:S(2)}, u32[]{:S(2)}) collective-permute-start(bf16[256,2048]{1,0:T(8,128)(2,1)} %get-tuple-element.92), channel_id=1, source_target_pairs={{0,2},{1,3},{2,0},{3,1},{4,6},{5,7},{6,4},{7,5},{8,10},{9,11},{10,... | collective-permute-start | bytes 3145736 | tf_op jit(solution)/shard_map/ppermute | solution.py:266
  113.3 21.1 %copy-start.21 = (bf16[256,2048]{1,0:T(8,128)(2,1)S(1)}, bf16[256,2048]{1,0:T(8,128)(2,1)}, u32[]{:S(2)}) copy-start(bf16[256,2048]{1,0:T(8,128)(2,1)} %get-tuple-element.89) | copy-start | bytes 3145732
  133.1 39.5 %collective-permute-start.11 = (bf16[256,2048]{1,0:T(8,128)(2,1)}, bf16[256,2048]{1,0:T(8,128)(2,1)}, u32[]{:S(2)}, u32[]{:S(2)}) collective-permute-start(bf16[256,2048]{1,0:T(8,128)(2,1)} %add_convert_fusion.2), channel_id=1, source_target_pairs={{0,1},{1,0},{2,3},{3,2},{4,5},{5,4},{6,7},{7,6},{8,9},{9,8},{10,11... | collective-permute-start | bytes 3145736 | tf_op jit(solution)/shard_map/ppermute | solution.py:262
  137.0 35.6 %collective-permute-start.8 = (bf16[256,2048]{1,0:T(8,128)(2,1)}, bf16[256,2048]{1,0:T(8,128)(2,1)}, u32[]{:S(2)}, u32[]{:S(2)}) collective-permute-start(bf16[256,2048]{1,0:T(8,128)(2,1)} %add_convert_fusion.3), channel_id=1, source_target_pairs={{0,2},{1,3},{2,0},{3,1},{4,6},{5,7},{6,4},{7,5},{8,10},{9,11},{10,... | collective-permute-start | bytes 3145736 | tf_op jit(solution)/shard_map/ppermute | solution.py:266
  140.2 37.9 %copy-start.34 = (f32[256]{0:T(256)}, f32[256]{0:T(256)S(1)}, u32[]{:S(2)}) copy-start(f32[256]{0:T(256)S(1)} %get-tuple-element.177) | copy-start | bytes 3076
  140.2 37.9 %copy-start.36 = (f32[256]{0:T(256)}, f32[256]{0:T(256)S(1)}, u32[]{:S(2)}) copy-start(f32[256]{0:T(256)S(1)} %get-tuple-element.176) | copy-start | bytes 3076
  153.8 18.7 %copy-start.20 = (bf16[256,2048]{1,0:T(8,128)(2,1)}, bf16[256,2048]{1,0:T(8,128)(2,1)S(1)}, u32[]{:S(2)}) copy-start(bf16[256,2048]{1,0:T(8,128)(2,1)S(1)} %collective-permute-done.6) | copy-start | bytes 3145732
  178.2 7.0 copy-start.18
  178.4 40.0 %collective-permute-start.14 = (bf16[256,2048]{1,0:T(8,128)(2,1)S(1)}, bf16[256,2048]{1,0:T(8,128)(2,1)}, u32[]{:S(2)}, u32[]{:S(2)}) collective-permute-start(bf16[256,2048]{1,0:T(8,128)(2,1)S(1)} %multiply_convert_fusion.2.refs_1_), channel_id=1, source_target_pairs={{0,2},{1,3},{2,0},{3,1},{4,6},{5,7},{6,4},{7,5},{8,10},{9,11},{10,... | collective-permute-start | bytes 3145736 | tf_op jit(solution)/shard_map/ppermute | solution.py:266
  179.4 104.3 %collective-permute-start.20 = (bf16[256,2048]{1,0:T(8,128)(2,1)S(1)}, bf16[256,2048]{1,0:T(8,128)(2,1)}, u32[]{:S(2)}, u32[]{:S(2)}) collective-permute-start(bf16[256,2048]{1,0:T(8,128)(2,1)S(1)} %multiply_convert_fusion.2.refs_1_), channel_id=1, source_target_pairs={{0,1},{1,0},{2,3},{3,2},{4,5},{5,4},{6,7},{7,6},{8,9},{9,8},{10,11... | collective-permute-start | bytes 3145736 | tf_op jit(solution)/shard_map/ppermute | solution.py:262
  184.2 43.9 %collective-permute-start.12 = (bf16[256,2048]{1,0:T(8,128)(2,1)}, bf16[256,2048]{1,0:T(8,128)(2,1)}, u32[]{:S(2)}, u32[]{:S(2)}) collective-permute-start(bf16[256,2048]{1,0:T(8,128)(2,1)} %multiply_convert_fusion.3.refs_0_), channel_id=1, source_target_pairs={{0,1},{1,0},{2,3},{3,2},{4,5},{5,4},{6,7},{7,6},{8,9},{9,8},{10,11... | collective-permute-start | bytes 3145736 | tf_op jit(solution)/shard_map/ppermute | solution.py:262
  185.1 65.4 %collective-permute-start.16 = (bf16[256,2048]{1,0:T(8,128)(2,1)S(1)}, bf16[256,2048]{1,0:T(8,128)(2,1)}, u32[]{:S(2)}, u32[]{:S(2)}) collective-permute-start(bf16[256,2048]{1,0:T(8,128)(2,1)S(1)} %get-tuple-element.174.refs_2_), channel_id=1, source_target_pairs={{0,1},{1,0},{2,3},{3,2},{4,5},{5,4},{6,7},{7,6},{8,9},{9,8},{10,11... | collective-permute-start | bytes 3145736 | tf_op jit(solution)/shard_map/ppermute | solution.py:262
  186.2 64.4 %copy-start.19 = (bf16[256,2048]{1,0:T(8,128)(2,1)S(1)}, bf16[256,2048]{1,0:T(8,128)(2,1)}, u32[]{:S(2)}) copy-start(bf16[256,2048]{1,0:T(8,128)(2,1)} %copy-done.18) | copy-start | bytes 3145732
  186.2 65.4 %collective-permute-start.18 = (bf16[256,2048]{1,0:T(8,128)(2,1)}, bf16[256,2048]{1,0:T(8,128)(2,1)}, u32[]{:S(2)}, u32[]{:S(2)}) collective-permute-start(bf16[256,2048]{1,0:T(8,128)(2,1)} %get-tuple-element.175.refs_3_), channel_id=1, source_target_pairs={{0,2},{1,3},{2,0},{3,1},{4,6},{5,7},{6,4},{7,5},{8,10},{9,11},{10,... | collective-permute-start | bytes 3145736 | tf_op jit(solution)/shard_map/ppermute | solution.py:266
  218.4 66.0 %collective-permute-start.21 = (bf16[256,2048]{1,0:T(8,128)(2,1)}, bf16[256,2048]{1,0:T(8,128)(2,1)}, u32[]{:S(2)}, u32[]{:S(2)}) collective-permute-start(bf16[256,2048]{1,0:T(8,128)(2,1)} %multiply_convert_fusion.3.refs_0_), channel_id=1, source_target_pairs={{0,2},{1,3},{2,0},{3,1},{4,6},{5,7},{6,4},{7,5},{8,10},{9,11},{10,... | collective-permute-start | bytes 3145736 | tf_op jit(solution)/shard_map/ppermute | solution.py:266
  228.1 57.8 %collective-permute-start.22 = (bf16[256,2048]{1,0:T(8,128)(2,1)}, bf16[256,2048]{1,0:T(8,128)(2,1)}, u32[]{:S(2)}, u32[]{:S(2)}) collective-permute-start(bf16[256,2048]{1,0:T(8,128)(2,1)} %get-tuple-element.175.refs_3_), channel_id=1, source_target_pairs={{0,1},{1,0},{2,3},{3,2},{4,5},{5,4},{6,7},{7,6},{8,9},{9,8},{10,11... | collective-permute-start | bytes 3145736 | tf_op jit(solution)/shard_map/ppermute | solution.py:262
  250.6 35.8 %collective-permute-start.23 = (bf16[256,2048]{1,0:T(8,128)(2,1)S(1)}, bf16[256,2048]{1,0:T(8,128)(2,1)}, u32[]{:S(2)}, u32[]{:S(2)}) collective-permute-start(bf16[256,2048]{1,0:T(8,128)(2,1)S(1)} %copy-done.19), channel_id=1, source_target_pairs={{0,2},{1,3},{2,0},{3,1},{4,6},{5,7},{6,4},{7,5},{8,10},{9,11},{10,... | collective-permute-start | bytes 3145736 | tf_op jit(solution)/shard_map/ppermute | solution.py:266
  251.6 65.6 %collective-permute-start.15 = (bf16[256,2048]{1,0:T(8,128)(2,1)}, bf16[256,2048]{1,0:T(8,128)(2,1)S(1)}, u32[]{:S(2)}, u32[]{:S(2)}) collective-permute-start(bf16[256,2048]{1,0:T(8,128)(2,1)} %collective-permute-done.14.refs_1_), channel_id=1, source_target_pairs={{0,1},{1,0},{2,3},{3,2},{4,5},{5,4},{6,7},{7,6},{8,9},{9,8},{10,11... | collective-permute-start | bytes 3145736 | tf_op jit(solution)/shard_map/ppermute | solution.py:262
  283.8 33.5 %collective-permute-start.13 = (bf16[256,2048]{1,0:T(8,128)(2,1)}, bf16[256,2048]{1,0:T(8,128)(2,1)S(1)}, u32[]{:S(2)}, u32[]{:S(2)}) collective-permute-start(bf16[256,2048]{1,0:T(8,128)(2,1)} %collective-permute-done.12.refs_0_), channel_id=1, source_target_pairs={{0,2},{1,3},{2,0},{3,1},{4,6},{5,7},{6,4},{7,5},{8,10},{9,11},{10,... | collective-permute-start | bytes 3145736 | tf_op jit(solution)/shard_map/ppermute | solution.py:266
  284.4 36.7 %collective-permute-start.17 = (bf16[256,2048]{1,0:T(8,128)(2,1)}, bf16[256,2048]{1,0:T(8,128)(2,1)}, u32[]{:S(2)}, u32[]{:S(2)}) collective-permute-start(bf16[256,2048]{1,0:T(8,128)(2,1)} %collective-permute-done.16.refs_2_), channel_id=1, source_target_pairs={{0,2},{1,3},{2,0},{3,1},{4,6},{5,7},{6,4},{7,5},{8,10},{9,11},{10,... | collective-permute-start | bytes 3145736 | tf_op jit(solution)/shard_map/ppermute | solution.py:266
  285.9 35.2 %collective-permute-start.19 = (bf16[256,2048]{1,0:T(8,128)(2,1)}, bf16[256,2048]{1,0:T(8,128)(2,1)}, u32[]{:S(2)}, u32[]{:S(2)}) collective-permute-start(bf16[256,2048]{1,0:T(8,128)(2,1)} %collective-permute-done.18.refs_3_), channel_id=1, source_target_pairs={{0,1},{1,0},{2,3},{3,2},{4,5},{5,4},{6,7},{7,6},{8,9},{9,8},{10,11... | collective-permute-start | bytes 3145736 | tf_op jit(solution)/shard_map/ppermute | solution.py:262
  778.4 12.2 %copy-start.3 = (bf16[512,2048]{1,0:T(8,128)(2,1)S(1)}, bf16[512,2048]{1,0:T(8,128)(2,1)}, u32[]{:S(2)}) copy-start(bf16[512,2048]{1,0:T(8,128)(2,1)} %param.10) | copy-start | bytes 6291460
  778.4 12.1 %copy-start.9 = (bf16[256,2048]{1,0:T(8,128)(2,1)S(1)}, bf16[256,2048]{1,0:T(8,128)(2,1)}, u32[]{:S(2)}) copy-start(bf16[256,2048]{1,0:T(8,128)(2,1)} %get-tuple-element.142) | copy-start | bytes 3145732
  778.4 12.1 %copy-start.10 = (bf16[256,2048]{1,0:T(8,128)(2,1)S(1)}, bf16[256,2048]{1,0:T(8,128)(2,1)}, u32[]{:S(2)}) copy-start(bf16[256,2048]{1,0:T(8,128)(2,1)} %get-tuple-element.145) | copy-start | bytes 3145732
  778.4 12.1 %copy-start.11 = (bf16[256,2048]{1,0:T(8,128)(2,1)S(1)}, bf16[256,2048]{1,0:T(8,128)(2,1)}, u32[]{:S(2)}) copy-start(bf16[256,2048]{1,0:T(8,128)(2,1)} %get-tuple-element.143) | copy-start | bytes 3145732
  778.4 12.1 %copy-start.12 = (bf16[256,2048]{1,0:T(8,128)(2,1)S(1)}, bf16[256,2048]{1,0:T(8,128)(2,1)}, u32[]{:S(2)}) copy-start(bf16[256,2048]{1,0:T(8,128)(2,1)} %get-tuple-element.146) | copy-start | bytes 3145732
  778.4 12.1 %copy-start.31 = (f32[256]{0:T(256)S(1)}, f32[256]{0:T(256)}, u32[]{:S(2)}) copy-start(f32[256]{0:T(256)} %copy-done.30) | copy-start | bytes 3076
  778.4 12.1 %copy-start.33 = (f32[256]{0:T(256)S(1)}, f32[256]{0:T(256)}, u32[]{:S(2)}) copy-start(f32[256]{0:T(256)} %copy-done.32) | copy-start | bytes 3076
  796.4 8.8 %slice-start = ((s8[5242880]{0:T(1024)(128)(4,1)}), s8[4194304]{0:T(1024)(128)(4,1)S(1)}, s32[]{:S(2)}) async-start(s8[5242880]{0:T(1024)(128)(4,1)} %bitcast.28), calls=%async_computation | async-start | bytes 8388608
  796.4 8.8 %slice-start.1 = ((s8[5242880]{0:T(1024)(128)(4,1)}), s8[1048576]{0:T(1024)(128)(4,1)S(1)}, s32[]{:S(2)}) async-start(s8[5242880]{0:T(1024)(128)(4,1)} %bitcast.28), calls=%async_computation.1 | async-start | bytes 2097152
  796.4 8.8 %copy-start.17 = (bf16[2048,128]{1,0:T(8,128)(2,1)S(1)}, bf16[2048,128]{1,0:T(8,128)(2,1)}, u32[]{:S(2)}) copy-start(bf16[2048,128]{1,0:T(8,128)(2,1)} %get-tuple-element.164) | copy-start | bytes 1572868
  809.2 9.4 %copy-start.8 = (f32[512,2048]{1,0:T(8,128)S(1)}, f32[512,2048]{1,0:T(8,128)}, u32[]{:S(2)}) copy-start(f32[512,2048]{1,0:T(8,128)} %get-tuple-element.141) | copy-start | bytes 12582916
  809.2 9.4 %copy-start.13 = (bf16[256,2048]{1,0:T(8,128)(2,1)S(1)}, bf16[256,2048]{1,0:T(8,128)(2,1)}, u32[]{:S(2)}) copy-start(bf16[256,2048]{1,0:T(8,128)(2,1)} %get-tuple-element.144) | copy-start | bytes 3145732
  809.3 9.4 %copy-start.14 = (bf16[256,2048]{1,0:T(8,128)(2,1)S(1)}, bf16[256,2048]{1,0:T(8,128)(2,1)}, u32[]{:S(2)}) copy-start(bf16[256,2048]{1,0:T(8,128)(2,1)} %get-tuple-element.147) | copy-start | bytes 3145732
  (21 other events, 59.5 us)

commit v3 on v2

--- a/solution.py
+++ b/solution.py
@@ -541,10 +541,12 @@
     first = [remote(top_d, met.at[0], 0, near_x), remote(low_d, met.at[1], 1, near_y)]
     direct = [remote(top_x, landed[0], 2, near_x), remote(low_y, landed[1], 3, near_y)]
     second = [remote(mid.at[0], landed[2], 4, near_y), remote(mid.at[1], landed[3], 5, near_x)]
-    loads = [
-        pltpu.make_async_copy(top_y, mid.at[0], load_sems.at[0]),
-        pltpu.make_async_copy(low_x, mid.at[1], load_sems.at[1]),
-    ]
+    loads = []
+    if top_y is not None:
+        loads = [
+            pltpu.make_async_copy(top_y, mid.at[0], load_sems.at[0]),
+            pltpu.make_async_copy(low_x, mid.at[1], load_sems.at[1]),
+        ]
 
     def open_sum():
         begin(first)
@@ -568,10 +570,12 @@
         finish(direct)
         finish(second)
 
-    return open_sum, join_sum, close_sum
-
-
-def unit_grads(act, grad_two_all, normed_two_all, grad_parts, back_sums, middle, cotangent, live):
+    return open_sum, join_sum, close_sum, first, direct
+
+
+def unit_grads(
+    act, grad_two_all, normed_two_all, grad_parts, back_sums, middle, cotangent, live, out_weight
+):
     rows, units = act.shape
     width = grad_two_all.shape[1]
     local_rows = middle.shape[0]
@@ -586,12 +590,12 @@
     def body(*refs):
         act_in, two_in, normed_in, parts_in = refs[:4]
         partial = refs[4:12]
-        middle_in, cot_in, live_ref = refs[12:15]
-        out_grad, in_grad, branch_out, middle_out = refs[15:19]
-        act_ref, shared, parts_ref, landed, own_ref, cot_ref, mid_ref, grad_ref, branch = refs[19:28]
-        load_sems, stage_sems, gather_sems = refs[28:31]
-        line = refs[31:40]
-        square = refs[40:44]
+        middle_in, cot_in, weight_in, live_ref = refs[12:16]
+        out_grad, in_grad, branch_out, middle_out, gated_out = refs[16:21]
+        act_ref, shared, parts_ref, landed, own_ref, cot_ref, mid_ref, grad_ref, branch = refs[21:30]
+        gated_ref, load_sems, stage_sems, gather_sems, back_sems = refs[30:35]
+        line = refs[35:44]
+        square = refs[44:48]
         places = neighbours()
         near_x, near_y = places[5:]
         enter(places)
@@ -599,7 +603,7 @@
         load_two = pltpu.make_async_copy(two_in, shared, load_sems.at[1])
         load_parts = pltpu.make_async_copy(parts_in, parts_ref, load_sems.at[2])
         load_normed = pltpu.make_async_copy(normed_in, shared, load_sems.at[3])
-        open_sum, join_sum, close_sum = square_sum(
+        open_sum, join_sum, close_sum, _, _ = square_sum(
             square, places, partial[2:], [landed.at[at] for at in range(4)]
         )
         load_two.start()
@@ -716,7 +720,7 @@
         sends[0].wait_recv()
         sends[1].wait_recv()
         begin(later)
-        lax.fori_loop(33, count + STAGES, step, 0)
+        lax.fori_loop(33, 50, step, 0)
         written.wait()
         finish(keep)
         for copy in sends[:2]:
@@ -724,15 +728,53 @@
         finish(sends[2:])
         finish(later)
 
+        weight_loads = [
+            pltpu.make_async_copy(weight_in.at[block(at)], landed.at[at], back_sems.at[at])
+            for at in range(weight_in.shape[0] // BLK)
+        ]
+        stages = (own_ref, cot_ref)
+
+        def row_load(at):
+            return pltpu.make_async_copy(
+                branch_out.at[block(at)], stages[at % 2], back_sems.at[2 + at % 2]
+            )
+
+        def gated_store(at):
+            return pltpu.make_async_copy(
+                gated_ref.at[at % 2], gated_out.at[block(at)], back_sems.at[4 + at % 2]
+            )
+
+        begin(weight_loads)
+        row_load(0).start()
+        at_step = 50
+        for at in range(rows // BLK):
+            lax.fori_loop(at_step, at_step + 2, step, 0)
+            at_step += 2
+            if at == 0:
+                finish(weight_loads)
+            if at + 1 < rows // BLK:
+                row_load(at + 1).start()
+            row_load(at).wait()
+            if at >= 2:
+                gated_store(at - 2).wait()
+            for part in range(len(weight_loads)):
+                result = across(stages[at % 2][...], landed[part])
+                gated_ref[at % 2, :, part * BLK : (part + 1) * BLK] = result.astype(low)
+            gated_store(at).start()
+        lax.fori_loop(at_step, count + STAGES, step, 0)
+        gated_store(rows // BLK - 2).wait()
+        gated_store(rows // BLK - 1).wait()
+
     return pl.pallas_call(
         body,
-        in_specs=any_specs(14) + [pl.BlockSpec(memory_space=pltpu.VMEM)],
-        out_specs=any_specs(4),
+        in_specs=any_specs(15) + [pl.BlockSpec(memory_space=pltpu.VMEM)],
+        out_specs=any_specs(5),
         out_shape=[
             jax.ShapeDtypeStruct((out_blocks, SUB, width), low),
             jax.ShapeDtypeStruct((in_blocks, SUB, grad_parts.shape[1]), low),
             jax.ShapeDtypeStruct((rows, width), low),
             jax.ShapeDtypeStruct((local_rows, width), jnp.float32),
+            jax.ShapeDtypeStruct((rows, out_weight.shape[0]), low),
         ],
         scratch_shapes=[
             pltpu.VMEM(act.shape, low),
@@ -744,9 +786,11 @@
             pltpu.VMEM((BLK, width), jnp.float32),
             pltpu.VMEM((BLK, width), jnp.float32),
             pltpu.VMEM((2, BLK, width), low),
+            pltpu.VMEM((2, BLK, out_weight.shape[0]), low),
             pltpu.SemaphoreType.DMA((4,)),
             pltpu.SemaphoreType.DMA((6,)),
             pltpu.SemaphoreType.DMA((6, 2)),
+            pltpu.SemaphoreType.DMA((6,)),
         ]
         + line_scratch()
         + square_scratch(),
@@ -755,10 +799,20 @@
         ),
         cost_estimate=cost(2 * 3 * rows * width * units, 60e6),
         name="unit_grads",
-    )(act, grad_two_all, normed_two_all, grad_parts, *back_sums, middle, cotangent, live)
-
-
-def mix_grads(gated, grad_branch_all, normed_all, grad_projected, sums, two_sums):
+    )(
+        act,
+        grad_two_all,
+        normed_two_all,
+        grad_parts,
+        *back_sums,
+        middle,
+        cotangent,
+        out_weight,
+        live,
+    )
+
+
+def mix_grads(gated, grad_branch_all, normed_all, grad_projected, mix_weight, two_sums):
     _, rows, columns = gated.shape
     width = normed_all.shape[1]
     parts = grad_projected.shape[0]
@@ -767,47 +821,71 @@
     per_row = columns // TILE
     per_part = (width // PIECE) * per_row
     count = out_chunks + parts * per_part
+    wide_tile = 1024
 
     def body(*refs):
-        gated_in, branch_in, normed_in, grads_in = refs[:4]
-        partial, two_partial = refs[4:10], refs[10:16]
-        out_grad, mix_grad = refs[16:18]
-        landed, two_landed = refs[18:22], refs[22:26]
-        gated_ref, branch_ref, normed_ref, grads_ref, load_sems = refs[26:31]
-        line = refs[31:40]
-        square, two_square = refs[40:44], refs[44:48]
+        gated_in, branch_in, normed_in, grads_in, weight_in = refs[:5]
+        two_partial = refs[5:11]
+        out_grad, mix_grad = refs[11:13]
+        own_outs = refs[13:15]
+        landed, two_landed = refs[15:19], refs[19:23]
+        gated_ref, branch_ref, normed_ref, grads_ref, weight_ref, far, near, own_ref = refs[23:31]
+        load_sems, branch_sems, grad_sems, weight_sems, own_sems = refs[31:36]
+        line = refs[36:45]
+        square, two_square = refs[45:49], refs[49:53]
+        mid = square[1]
         places = neighbours()
         enter(places)
-        loads = [
-            pltpu.make_async_copy(gated_in.at[0], gated_ref, load_sems.at[0]),
-            pltpu.make_async_copy(branch_in, branch_ref, load_sems.at[1]),
-            pltpu.make_async_copy(normed_in, normed_ref, load_sems.at[2]),
-            pltpu.make_async_copy(grads_in, grads_ref, load_sems.at[3]),
-        ]
-        begin(loads)
-        open_sum, join_sum, close_sum = square_sum(square, places, partial, landed)
-        open_two, join_two, close_two = square_sum(two_square, places, two_partial, two_landed)
-        open_sum()
-        finish(loads[:2])
+
+        def part_columns(c):
+            return pl.ds(c * columns, columns)
+
+        load_gated = pltpu.make_async_copy(gated_in.at[0], gated_ref, load_sems.at[0])
+        load_normed = pltpu.make_async_copy(normed_in, normed_ref, load_sems.at[1])
+
+        def load_branch(k):
+            at = pl.ds(pl.multiple_of(k * TILE, TILE), TILE)
+            slot = k % 2
+            return pltpu.make_async_copy(branch_in.at[:, at], branch_ref.at[slot], branch_sems.at[slot])
+
+        grad_loads = [
+            pltpu.make_async_copy(grads_in.at[c], grads_ref.at[:, part_columns(c)], grad_sems.at[c])
+            for c in range(parts)
+        ]
+        weight_loads = [
+            pltpu.make_async_copy(weight_in.at[c], weight_ref.at[:, part_columns(c)], weight_sems.at[c])
+            for c in range(parts)
+        ]
+        load_gated.start()
+        load_branch(0).start()
+        begin(grad_loads)
+        begin(weight_loads)
+        load_normed.start()
+        _, join_sum, close_sum, first, direct = square_sum(
+            square,
+            places,
+            (near.at[0], near.at[1], None, None, far.at[0], far.at[1]),
+            landed,
+        )
+        open_two, join_two, close_two, _, _ = square_sum(two_square, places, two_partial, two_landed)
+        load_gated.wait()
 
         def product(k, own):
             @pl.when(k < out_chunks)
             def _():
-                wide_at = pl.ds(pl.multiple_of(k * TILE, TILE), TILE)
-                result = down(gated_ref[...], branch_ref[:, wide_at]).astype(low)
+                load_branch(k).wait()
+                pl.when(k + 1 < out_chunks)(lambda: load_branch(k + 1).start())
+                result = down(gated_ref[...], branch_ref[k % 2]).astype(low)
                 for part in range(4):
                     own[part] = result[part * SUB : (part + 1) * SUB]
-
-            @pl.when(k == out_chunks)
-            def _():
-                finish(loads[2:])
 
             @pl.when(k >= out_chunks)
             def _():
                 at = k - out_chunks
                 rows_at = pl.ds(pl.multiple_of(((at // per_row) % 4) * PIECE, PIECE), PIECE)
-                wide_at = pl.ds(pl.multiple_of((at % per_row) * TILE, TILE), TILE)
-                result = down(normed_ref[:, rows_at], grads_ref[at // per_part, :, wide_at]).astype(low)
+                start = (at // per_part) * columns + (at % per_row) * TILE
+                wide_at = pl.ds(pl.multiple_of(start, TILE), TILE)
+                result = down(normed_ref[:, rows_at], grads_ref[:, wide_at]).astype(low)
                 for part in range(4):
                     own[part] = result[part * SUB : (part + 1) * SUB]
 
@@ -821,30 +899,69 @@
             ]
 
         step = line_sum(line, places, count, product, targets)
-        lax.fori_loop(0, 9, step, 0)
+
+        def partial(piece, tile, top, low_part):
+            at = slice(tile * wide_tile, (tile + 1) * wide_tile)
+            acts = grads_ref[piece * PIECE : (piece + 1) * PIECE, :]
+            total = across(acts, weight_ref[at, :])
+            top[:, at] = total[:HALF].astype(low)
+            low_part[:, at] = total[HALF:].astype(low)
+
+        own_stores = [
+            pltpu.make_async_copy(own_ref.at[at], own_outs[at], own_sems.at[at]) for at in range(2)
+        ]
+        places_of = (
+            (3, far.at[0], far.at[1], first),
+            (1, near.at[0], near.at[1], direct),
+            (2, mid.at[1], mid.at[0], []),
+            (0, own_ref.at[0], own_ref.at[1], own_stores),
+        )
+        lax.fori_loop(0, 2, step, 0)
+        finish(grad_loads)
+        finish(weight_loads)
+        at_step = 2
+        for piece, top, low_part, copies in places_of:
+            for tile in range(width // wide_tile):
+                partial(piece, tile, top, low_part)
+                if tile == width // wide_tile - 1:
+                    begin(copies)
+                lax.fori_loop(at_step, at_step + 1, step, 0)
+                at_step += 1
+                if at_step == 8:
+                    load_normed.wait()
+        lax.fori_loop(at_step, 12, step, 0)
         join_sum()
         open_two()
-        lax.fori_loop(9, 33, step, 0)
+        lax.fori_loop(12, 36, step, 0)
         join_two()
-        lax.fori_loop(33, count + STAGES, step, 0)
+        lax.fori_loop(36, count + STAGES, step, 0)
         close_sum()
         close_two()
+        finish(own_stores)
 
     return pl.pallas_call(
         body,
-        in_specs=any_specs(16),
-        out_specs=any_specs(10),
+        in_specs=any_specs(11),
+        out_specs=any_specs(12),
         out_shape=[
             jax.ShapeDtypeStruct((columns // SUB, SUB, width), low),
             jax.ShapeDtypeStruct((parts * width // SUB, SUB, columns), low),
         ]
-        + [jax.ShapeDtypeStruct((BLK, width), low)] * 8,
+        + [jax.ShapeDtypeStruct((BLK, width), low)] * 10,
         scratch_shapes=[
             pltpu.VMEM((rows, columns), low),
+            pltpu.VMEM((2, rows, TILE), low),
             pltpu.VMEM((rows, width), low),
-            pltpu.VMEM((rows, width), low),
-            pltpu.VMEM(grad_projected.shape, low),
-            pltpu.SemaphoreType.DMA((4,)),
+            pltpu.VMEM((rows, parts * columns), low),
+            pltpu.VMEM((width, parts * columns), low),
+            pltpu.VMEM((2, BLK, width), low),
+            pltpu.VMEM((2, BLK, width), low),
+            pltpu.VMEM((2, BLK, width), low),
+            pltpu.SemaphoreType.DMA((2,)),
+            pltpu.SemaphoreType.DMA((2,)),
+            pltpu.SemaphoreType.DMA((parts,)),
+            pltpu.SemaphoreType.DMA((parts,)),
+            pltpu.SemaphoreType.DMA((2,)),
         ]
         + line_scratch()
         + square_scratch()
@@ -852,9 +969,9 @@
         compiler_params=pltpu.CompilerParams(
             vmem_limit_bytes=VMEM, collective_id=2, has_side_effects=True
         ),
-        cost_estimate=cost(2 * 5 * rows * width * columns, 60e6),
+        cost_estimate=cost(2 * 9 * rows * width * columns, 60e6),
         name="mix_grads",
-    )(gated, grad_branch_all, normed_all, grad_projected, *sums, *two_sums)
+    )(gated, grad_branch_all, normed_all, grad_projected, mix_weight, *two_sums)
 
 
 def row_copies(pair, rows, sems, at):
@@ -888,8 +1005,9 @@
             for c in range(parts)
         ]
         begin(row_loads)
-        begin(weight_loads)
+        begin(weight_loads[:joined])
         finish(row_loads)
+        begin(weight_loads[joined:])
         keep = pltpu.make_async_copy(rows, rows_out.at[spot, :], row_sems.at[2])
         keep.start()
         for c in range(0, parts, joined):
@@ -923,7 +1041,7 @@
     )(*pair, weight, *kept)
 
 
-def partial_sums(acts, weight, pieces, transposed):
+def partial_sums(acts, weight, pieces, transposed, after=()):
     parts, _, columns = acts.shape
     width = weight.shape[1] if transposed else weight.shape[2]
     deep = parts * columns
@@ -931,6 +1049,7 @@
     wide_tile = 1024
 
     def body(act_in, weight_in, *refs):
+        refs = refs[len(after) :]
         outs = refs[: 2 * len(pieces)]
         acts_ref, weights, out, act_sems, weight_sems, out_sems = refs[2 * len(pieces) :]
 
@@ -964,16 +1083,17 @@
                 ]
             )
         begin(act_loads[0])
-        for loads in weight_loads:
-            begin(loads)
-        for loads in act_loads[1:]:
-            begin(loads)
+        begin(weight_loads[0])
         stores = []
         for at in range(len(pieces)):
             finish(act_loads[at])
             for j, loads in enumerate(weight_loads):
                 if at == 0:
                     finish(loads)
+                    if j + 1 < len(weight_loads):
+                        begin(weight_loads[j + 1])
+                if j == len(weight_loads) - 1 and at + 1 < len(pieces):
+                    begin(act_loads[at + 1])
                 tile = slice(j * wide_tile, (j + 1) * wide_tile)
                 if transposed:
                     total = across(acts_ref[at], weights[tile, :])
@@ -991,7 +1111,7 @@
 
     return pl.pallas_call(
         body,
-        in_specs=any_specs(2),
+        in_specs=any_specs(2 + len(after)),
         out_specs=any_specs(2 * len(pieces)),
         out_shape=[jax.ShapeDtypeStruct((HALF, width), low)] * (2 * len(pieces)),
         scratch_shapes=[
@@ -1007,7 +1127,7 @@
             2 * len(pieces) * PIECE * parts * width * columns, 2 * parts * width * columns + 8e6
         ),
         name="partial_sums",
-    )(acts, weight)
+    )(acts, weight, *after)
 
 
 def unit_piece(pair, grad_pair, ffn_in, ffn_out, kept, piece):
@@ -1043,11 +1163,11 @@
 
         weights = [weight_loads(at, *cut, cut[0], main + cut[0]) for at, cut in enumerate(cuts)]
         weights.append(weight_loads(2, main, tail, 2 * main, 2 * main + tail))
+        queue = [[copy] for loads_here in weights[:2] for copy in loads_here] + [weights[2]]
+        queue[2] = grad_loads + queue[2]
         begin(loads)
-        begin(weights[0])
-        begin(grad_loads)
-        begin(weights[1])
-        begin(weights[2])
+        begin(queue[0])
+        begin(queue[1])
         finish(loads)
         stores = [
             pltpu.make_async_copy(rows, rows_out.at[spot, :], done_sems.at[0]),
@@ -1059,20 +1179,24 @@
             parts[:, first] = (grad_act * part_b).astype(low)
             parts[:, second] = (grad_act * part_a).astype(low)
 
+        def ready(at):
+            if at + 2 < len(queue):
+                begin(queue[at + 2])
+            finish(queue[at])
+
         for which, (start, size) in enumerate(cuts):
-            finish(weights[which][:1])
             at, second = slice(start, start + size), slice(main + start, main + start + size)
+            ready(3 * which)
             part_a = straight(rows[...], w_in[:, at])
-            finish(weights[which][1:2])
+            ready(3 * which + 1)
             part_b = straight(rows[...], w_in[:, second])
-            finish(weights[which][2:])
+            ready(3 * which + 2)
             if which == 0:
-                finish(grad_loads)
                 begin(stores)
             grad_act = across(grads[...], w_out[at, :])
             products(at, at, second, part_a, part_b, grad_act)
+        finish(weights[2])
         if tail:
-            finish(weights[2])
             both = straight(rows[...], w_in[:, 2 * main :])
             grad_act = across(grads[...], w_out[main:, :])
             products(
@@ -1137,6 +1261,81 @@
         cost_estimate=cost(12 * PIECE * width * units, 6 * width * units + 12e6),
         name="gated_unit",
     )(*pair, *grad_pair, ffn_in, ffn_out, *kept)
+
+
+def live_rows(cotangent, live, after):
+    width = cotangent.shape[1]
+
+    def body(cot_ref, live_ref, *refs):
+        for half, out_ref in enumerate(refs[len(after) :]):
+            rows = pl.ds(half * HALF, HALF)
+            product = cot_ref[rows, :].astype(jnp.float32) * live_ref[rows, :1]
+            out_ref[...] = product.astype(jnp.bfloat16)
+
+    return pl.pallas_call(
+        body,
+        in_specs=[pl.BlockSpec(memory_space=pltpu.VMEM)] * 2 + any_specs(len(after)),
+        out_specs=[pl.BlockSpec(memory_space=pltpu.VMEM)] * 2,
+        out_shape=[jax.ShapeDtypeStruct((HALF, width), jnp.bfloat16)] * 2,
+        compiler_params=pltpu.CompilerParams(vmem_limit_bytes=VMEM),
+        cost_estimate=cost(2e6, 4e6),
+        name="live_rows",
+    )(cotangent, live, *after)
+
+
+def finish_rows(mix_low, out_low, hidden, middle, grad_middle, live, normed_terms, two_terms):
+    parts, width, columns = mix_low.shape
+    local_rows = hidden.shape[0]
+    tile = local_rows // parts
+    out_tile = out_low.shape[0] // parts
+    half_steps = parts // 2
+    terms = len(normed_terms) + len(two_terms)
+
+    def body(mix_ref, out_ref, hidden_ref, middle_ref, grad_ref, live_ref, *refs):
+        term_refs = refs[:terms]
+        mix_out, out_out, layer_ref, input_ref = refs[terms:]
+        mix_out[...] = mix_ref[...].astype(jnp.float32)
+        out_out[...] = out_ref[...].astype(jnp.float32)
+
+        def rows_of(half):
+            normed = add_rows(*(ref[...] for ref in term_refs[3 * half : 3 * half + 3]))
+            two = add_rows(*(ref[...] for ref in term_refs[6 + 3 * half : 9 + 3 * half]))
+            layer = middle_ref[...] + live_ref[...] * two
+            layer_ref[...] = layer.astype(jnp.bfloat16)
+            back = norm_back(hidden_ref[...].astype(jnp.float32), normed)
+            input_ref[...] = (grad_ref[...] + back).astype(jnp.bfloat16)
+
+        first = pl.program_id(0) < half_steps
+        pl.when(first)(lambda: rows_of(0))
+        pl.when(jnp.logical_not(first))(lambda: rows_of(1))
+
+    def rows_spec(size):
+        return pl.BlockSpec((tile, size), lambda i: (i, 0))
+
+    def half_spec(half):
+        if half == 0:
+            return pl.BlockSpec((tile, width), lambda i: (jnp.minimum(i, half_steps - 1), 0))
+        return pl.BlockSpec((tile, width), lambda i: (jnp.maximum(i - half_steps, 0), 0))
+
+    term_specs = ([half_spec(0)] * 3 + [half_spec(1)] * 3) * 2
+    mix_spec = pl.BlockSpec((1, width, columns), lambda i: (i, 0, 0))
+    out_spec = pl.BlockSpec((out_tile, out_low.shape[1]), lambda i: (i, 0))
+    return pl.pallas_call(
+        body,
+        grid=(parts,),
+        in_specs=[mix_spec, out_spec, rows_spec(width), rows_spec(width), rows_spec(width), rows_spec(1)]
+        + term_specs,
+        out_specs=[mix_spec, out_spec, rows_spec(width), rows_spec(width)],
+        out_shape=[
+            jax.ShapeDtypeStruct(mix_low.shape, jnp.float32),
+            jax.ShapeDtypeStruct(out_low.shape, jnp.float32),
+            jax.ShapeDtypeStruct(hidden.shape, jnp.bfloat16),
+            jax.ShapeDtypeStruct(hidden.shape, jnp.bfloat16),
+        ],
+        compiler_params=pltpu.CompilerParams(vmem_limit_bytes=VMEM),
+        cost_estimate=cost(1e8, 60e6),
+        name="finish_rows",
+    )(mix_low, out_low, hidden, middle, grad_middle, live, *normed_terms, *two_terms)
 
 
 def block_decays(rate):
@@ -1199,14 +1398,35 @@
     )(slots, fresh, rates, parts)
 
 
-def mix_backward(slots, fresh, rates, parts, mixing_all, states, grad_gated):
+def mix_backward(slots, fresh, rates, parts, mixing_all, states, grad_gated, in_low, out_low):
     _, group_rows, columns = parts.shape
     heads = columns // HS
     low = jnp.bfloat16
+    width, both_units = in_low.shape
+    units = both_units // 2
+    main = units // TILE * TILE
+    tail = units - main
+    in_rows, out_rows = width // heads, units // heads
 
     def body(
-        slot_ref, fresh_ref, rate_ref, parts_ref, mixing_ref, states_ref, grad_ref, out_ref
+        slot_ref,
+        fresh_ref,
+        rate_ref,
+        parts_ref,
+        mixing_ref,
+        states_ref,
+        grad_ref,
+        in_ref,
+        wide_ref,
+        out_ref,
+        in_out,
+        wide_out,
     ):
+        wide_out[...] = wide_ref[...].astype(jnp.float32)
+        for c in range(2):
+            in_out[c, :, :main] = in_ref[:, c * main : (c + 1) * main].astype(jnp.float32)
+            rest = slice(2 * main + c * tail, 2 * main + (c + 1) * tail)
+            in_out[c, :, main:] = in_ref[:, rest].astype(jnp.float32)
         within, entry, leave, whole = block_decays(rate_ref[pl.program_id(0)])
         later = jnp.zeros((HS, HS), jnp.float32)
         for block in reversed(range(NBLK)):
@@ -1247,14 +1467,24 @@
                 pl.BlockSpec((group_rows, HS), lambda h, *_: (0, h)),
                 pl.BlockSpec((1, NBLK, HS, HS), lambda h, *_: (h, 0, 0, 0)),
                 pl.BlockSpec((group_rows, HS), lambda h, *_: (0, h)),
+                pl.BlockSpec((in_rows, both_units), lambda h, *_: (h, 0)),
+                pl.BlockSpec((out_rows, width), lambda h, *_: (h, 0)),
             ],
-            out_specs=pl.BlockSpec((4, group_rows, HS), lambda h, *_: (0, 0, h)),
+            out_specs=[
+                pl.BlockSpec((4, group_rows, HS), lambda h, *_: (0, 0, h)),
+                pl.BlockSpec((2, in_rows, units), lambda h, *_: (0, h, 0)),
+                pl.BlockSpec((out_rows, width), lambda h, *_: (h, 0)),
+            ],
         ),
-        out_shape=jax.ShapeDtypeStruct(parts.shape, low),
+        out_shape=[
+            jax.ShapeDtypeStruct(parts.shape, low),
+            jax.ShapeDtypeStruct((2, width, units), jnp.float32),
+            jax.ShapeDtypeStruct((units, width), jnp.float32),
+        ],
         compiler_params=pltpu.CompilerParams(vmem_limit_bytes=VMEM),
-        cost_estimate=cost(20e9, 22e6),
+        cost_estimate=cost(20e9, 75e6),
         name="mix_backward",
-    )(slots, fresh, rates, parts, mixing_all, states, grad_gated)
+    )(slots, fresh, rates, parts, mixing_all, states, grad_gated, in_low, out_low)
 
 
 def norm_back(values, grad):
@@ -1284,18 +1514,19 @@
 
     lives = halves(live)
     inputs = [rows.astype(jnp.float32) for rows in halves(hidden)]
-    grads_in = [rows.astype(jnp.float32) for rows in halves(cotangent)]
 
     pieces = gather_pieces(*(row_norm(rows).astype(low) for rows in inputs))
     kept = ()
     for at, pair in enumerate(pieces):
         kept = project_piece(pair, mix_weight, kept, at)
     normed_all, parts = kept
-    grad_pieces = gather_pieces(*((m * g).astype(low) for m, g in zip(lives, grads_in)))
+    grad_pieces = gather_pieces(*live_rows(cotangent, live, pieces[3]))
 
     gated, mixing, states = mix_forward(slots, fresh, rates, parts)
     far_top, far_low, near_top, near_low = partial_sums(gated, out_weight[None], (3, 1), False)
-    side_low, side_top, own_top, own_low = partial_sums(gated, out_weight[None], (2, 0), False)
+    side_low, side_top, own_top, own_low = partial_sums(
+        gated, out_weight[None], (2, 0), False, after=grad_pieces[1] + grad_pieces[2]
+    )
     branch = scatter_pieces(
         (own_top, own_low), (near_top, near_low), (side_low, side_top), (far_top, far_low)
     )
@@ -1311,47 +1542,41 @@
         two_sums += [two_top, two_low]
     normed_two_all, grad_two_all, act, grad_parts = kept
 
-    out_grads, in_grads, grad_branch_all, grad_middle = unit_grads(
-        act, grad_two_all, normed_two_all, grad_parts, back_sums, jnp.concatenate(middle), cotangent, live
-    )
-    main = units // TILE * TILE
-    tail = units - main
-    in_grads = in_grads.reshape(width, 2 * units)
-    grad_ffn_in = jnp.stack(
-        [
-            jnp.concatenate(
-                [
-                    in_grads[:, c * main : (c + 1) * main],
-                    in_grads[:, 2 * main + c * tail : 2 * main + (c + 1) * tail],
-                ],
-                axis=1,
-            )
-            for c in range(2)
-        ]
-    ).astype(jnp.float32)
-    grad_ffn_out = out_grads.reshape(units, width).astype(jnp.float32)
-
-    grad_gated = across(grad_branch_all, out_weight).astype(low)
-    grad_projected = mix_backward(slots, fresh, rates, parts, mixing, states, grad_gated)
-    sums = partial_sums(grad_projected, mix_weight, (0, 1, 2, 3), True)
-    out_grads, mix_grads_low, *terms = mix_grads(
-        gated, grad_branch_all, normed_all, grad_projected, sums[2:], two_sums[2:]
-    )
-    grad_out = out_grads.reshape(out_weight.shape).astype(jnp.float32)
-    grad_mix = mix_grads_low.reshape(mix_weight.shape).astype(jnp.float32)
-    grad_normed = add_rows(sums[0], terms[0], terms[2]), add_rows(sums[1], terms[1], terms[3])
-    branch_two = (
-        add_rows(two_sums[0], terms[4], terms[6]),
-        add_rows(two_sums[1], terms[5], terms[7]),
-    )
-    layer_out = jnp.concatenate(
-        [(v + m * b).astype(low) for v, m, b in zip(middle, lives, branch_two)]
-    )
-    input_grad = jnp.concatenate(
-        [
-            (g + norm_back(x, n)).astype(low)
-            for g, x, n in zip(halves(grad_middle), inputs, grad_normed)
-        ]
+    middle = jnp.concatenate(middle)
+    out_low, in_low, grad_branch_all, grad_middle, grad_gated = unit_grads(
+        act,
+        grad_two_all,
+        normed_two_all,
+        grad_parts,
+        back_sums,
+        middle,
+        cotangent,
+        live,
+        out_weight,
+    )
+    grad_projected, grad_ffn_in, grad_ffn_out = mix_backward(
+        slots,
+        fresh,
+        rates,
+        parts,
+        mixing,
+        states,
+        grad_gated,
+        in_low.reshape(width, 2 * units),
+        out_low.reshape(units, width),
+    )
+    out_low, mix_low, own_top, own_low, *terms = mix_grads(
+        gated, grad_branch_all, normed_all, grad_projected, mix_weight, two_sums[2:]
+    )
+    grad_mix, grad_out, layer_out, input_grad = finish_rows(
+        mix_low.reshape(mix_weight.shape),
+        out_low.reshape(out_weight.shape),
+        hidden,
+        middle,
+        grad_middle,
+        live,
+        (own_top, terms[0], terms[2], own_low, terms[1], terms[3]),
+        (two_sums[0], terms[4], terms[6], two_sums[1], terms[5], terms[7]),
     )
     return (layer_out, input_grad, grad_mix, grad_out, grad_ffn_in, grad_ffn_out)
 

time: 839 us -> 787 us (0.938)
  other arithmetic: 70.3 us -> 17.7 us
  Pallas kernels: 587 us -> 609 us
  local copies, waits for them, and re-layouts: 17.7 us -> 4.62 us
  matrix products: 9.14 us -> 0 us
    convert_element_type x7 -> x0, other arithmetic: 37.2 us -> none  [the longest x1 12.1 us: square_device(): grad_mix = mix_grads_low.reshape(mix_weight.shape).astype(jnp.float32)]
    pallas_call x5 -> x6, Pallas kernels: 399 us -> 417 us  [the longest x1 225 us: unit_grads(): pl.pallas_call(body, in_specs=any_specs(15) + [pl.BlockSpec(memory_space=...]
    pallas_call x4, Pallas kernels: 123 us -> 107 us  [unit_piece(): pl.pallas_call(body, in_specs=any_specs(6 + len(kept)), out_specs=any_spe...]
    ppermute x12, waiting for transfers between devices: 22.1 us -> 36.6 us  [over_y(): return lax.ppermute(rows, 'narrow', [(at, at ^ 2) for at in range(4)])]
    ppermute x12, waiting for transfers between devices: 95.5 us -> 82.2 us  [over_x(): return lax.ppermute(rows, 'narrow', [(at, at ^ 1) for at in range(4)])]
    slice x2 -> x0, local copies, waits for them, and re-layouts: 11.1 us -> none  [the longest x1 8.65 us: square_device(): in_grads[:, c * main:(c + 1) * main]]
    pallas_call x1, Pallas kernels: 18.1 us -> 29 us  [mix_backward(): pl.pallas_call(body, grid_spec=pltpu.PrefetchScalarGridSpec(num_scalar_pr...]
    dot_general x1 -> x0, matrix products: 9.14 us -> none  [across(): lax.dot_general(left, right, (((1,), (1,)), ((), ())), preferred_element_...]
  transfers between devices with their start and end apart: 24 -> 24, of which waited for: 9 -> 10; matrix products, arithmetic and copies ran while one was open for 2% -> 2% of each run, Pallas kernels for 15% -> 19%
where the time goes in v3:
time: 787 us; the launch traced here: 778 us
  Pallas kernels  609 us (77%)
  waiting for transfers between devices  119 us (15%)
  starting transfers between devices  26.8 us (3%)
  other arithmetic  17.7 us (2%)
    pallas_call x1, Pallas kernels, unit_grads(): pl.pallas_call(body, in_specs=any_specs(15) + [pl.BlockSpec(memory_space=...  225 us
    pallas_call x1, Pallas kernels, mix_grads(): pl.pallas_call(body, in_specs=any_specs(11), out_specs=any_specs(12), out...  156 us
    pallas_call x4, Pallas kernels, unit_piece(): pl.pallas_call(body, in_specs=any_specs(6 + len(kept)), out_specs=any_spe...  107 us
    ppermute x12, waiting for transfers between devices, over_x(): return lax.ppermute(rows, 'narrow', [(at, at ^ 1) for at in range(4)])  82.2 us
    pallas_call x4, Pallas kernels, project_piece(): pl.pallas_call(body, in_specs=any_specs(3 + len(kept)), out_specs=any_spe...  45.6 us
    ppermute x12, waiting for transfers between devices, over_y(): return lax.ppermute(rows, 'narrow', [(at, at ^ 2) for at in range(4)])  36.6 us
    pallas_call x1, Pallas kernels, mix_backward(): pl.pallas_call(body, grid_spec=pltpu.PrefetchScalarGridSpec(num_scalar_pr...  29 us
    pallas_call x1, Pallas kernels, finish_rows(): pl.pallas_call(body, grid=(parts,), in_specs=[mix_spec, out_spec, rows_sp...  20.3 us
  transfers between devices with their start and end apart: 24, of which 10 were waited for; matrix products, arithmetic and copies ran while one was open for 2% of the time, Pallas kernels for 19%

profile of v3, /device:TPU:0, one launch (start us, length us, event | category | flops | bytes accessed | tf_op | source)
XLA Modules:
  0.0 778.1 jit_solution(1941098736787487006)
XLA Ops:
  0.6 2.2 fusion.2
  2.9 1.7 fusion.3
  4.6 2.9 collective-permute-start.4
  7.5 1.5 collective-permute-start.2
  10.2 1.3 broadcast_select_fusion
  12.1 1.2 compare_convert_fusion.fresh_ref
  14.0 8.7 %project.4 = (bf16[2048,2048]{1,0:T(8,128)(2,1)}, bf16[4,2048,512]{2,1,0:T(8,128)(2,1)}) custom-call(bf16[256,2048]{1,0:T(8,128)(2,1)} %get-tuple-element.171.refs_0_, bf16[256,2048]{1,0:T(8,128)(2,1)} %get-tuple-element.170.refs_1_, bf16[4,2048,512]{2,1,0:T(8,128)(2,1)} %refs_4_.9), custom_call_target="tpu_custom_call" | custom-call | flops 4294967296 | bytes 16388608 | tf_op jit(solution)/shard_map/project/pallas_call | solution.py:1021
  22.8 11.1 %collective-permute-done.2.refs_1_ = bf16[256,2048]{1,0:T(8,128)(2,1)} collective-permute-done((bf16[256,2048]{1,0:T(8,128)(2,1)}, bf16[256,2048]{1,0:T(8,128)(2,1)}, u32[]{:S(2)}, u32[]{:S(2)}) %collective-permute-start.2) | collective-permute-done | bytes 1048608 | tf_op jit(solution)/shard_map/ppermute | solution.py:266
  33.9 20.3 %collective-permute-done.refs_0_ = bf16[256,2048]{1,0:T(8,128)(2,1)} collective-permute-done((bf16[256,2048]{1,0:T(8,128)(2,1)}, bf16[256,2048]{1,0:T(8,128)(2,1)}, u32[]{:S(2)}, u32[]{:S(2)}) %collective-permute-start) | collective-permute-done | bytes 1048608 | tf_op jit(solution)/shard_map/ppermute | solution.py:262
  54.3 2.1 collective-permute-start.1
  59.7 8.7 %project.5 = (bf16[2048,2048]{1,0:T(8,128)(2,1)}, bf16[4,2048,512]{2,1,0:T(8,128)(2,1)}) custom-call(bf16[256,2048]{1,0:T(8,128)(2,1)} %collective-permute-done.refs_0_, bf16[256,2048]{1,0:T(8,128)(2,1)} %collective-permute-done.2.refs_1_, bf16[4,2048,512]{2,1,0:T(8,128)(2,1)} %refs_4_.9, ...), custom_call_target="tpu_custom_call", output_to_operand_aliasing={{0}: (3, {}), {1}: (4, {})} | custom-call | flops 4294967296 | bytes 16388608 | tf_op jit(solution)/shard_map/project/pallas_call | solution.py:1021
  68.4 8.8 %project.6 = (bf16[2048,2048]{1,0:T(8,128)(2,1)}, bf16[4,2048,512]{2,1,0:T(8,128)(2,1)}) custom-call(bf16[256,2048]{1,0:T(8,128)(2,1)} %collective-permute-done.4.refs_0_, bf16[256,2048]{1,0:T(8,128)(2,1)} %collective-permute-done.5.refs_1_, bf16[4,2048,512]{2,1,0:T(8,128)(2,1)} %refs_4_.9, ...), custom_call_target="tpu_custom_call", output_to_operand_aliasing={{0}: (3, {}), {1}: (4, {})} | custom-call | flops 4294967296 | bytes 16388608 | tf_op jit(solution)/shard_map/project/pallas_call | solution.py:1021
  77.2 0.9 collective-permute-done.1.refs_0_
  78.2 3.2 live_rows.1
  81.4 1.4 collective-permute-start.9
  82.8 1.5 collective-permute-start.6
  85.4 19.4 %project.7 = (bf16[2048,2048]{1,0:T(8,128)(2,1)}, bf16[4,2048,512]{2,1,0:T(8,128)(2,1)}) custom-call(bf16[256,2048]{1,0:T(8,128)(2,1)} %collective-permute-done.1.refs_0_, bf16[256,2048]{1,0:T(8,128)(2,1)} %copy-done.3, bf16[4,2048,512]{2,1,0:T(8,128)(2,1)} %refs_4_.9, ...), custom_call_target="tpu_custom_call", output_to_operand_aliasing={{0}: (3, {}), {1}: (4, {})} | custom-call | flops 4294967296 | bytes 16388608 | tf_op jit(solution)/shard_map/project/pallas_call | solution.py:1021
  104.8 9.8 %mix_forward.1 = (bf16[1,2048,512]{2,1,0:T(8,128)(2,1)}, bf16[2048,512]{1,0:T(8,128)(2,1)}, bf16[4,8,128,128]{3,2,1,0:T(8,128)(2,1)}) custom-call(s32[8]{0:T(128)} %compare_select_fusion.1.slot_ref, s32[8]{0:T(128)} %compare_convert_fusion.fresh_ref, f32[4]{0:T(128)} %multiply_power_fusion.rate_ref, bf16[4,2048,512]{2,1,0:T(8,128)(2,1)} %get-tuple-element.89.parts_ref), custom_call_target="tpu_custom_call" | custom-call | flops 8000000000 | bytes 14000000 | tf_op jit(solution)/shard_map/mix_forward/pallas_call | solution.py:1378
  114.7 6.3 partial_sums.3
  121.0 1.6 collective-permute-start.11
  122.5 1.4 collective-permute-start.16
  124.5 7.2 collective-permute-done.8.refs_2_
  132.3 6.4 partial_sums.2
  138.7 15.5 %collective-permute-done.11 = bf16[256,2048]{1,0:T(8,128)(2,1)} collective-permute-done((bf16[256,2048]{1,0:T(8,128)(2,1)}, bf16[256,2048]{1,0:T(8,128)(2,1)}, u32[]{:S(2)}, u32[]{:S(2)}) %collective-permute-start.11) | collective-permute-done | bytes 1048608 | tf_op jit(solution)/shard_map/ppermute | solution.py:262
  154.1 1.9 add_convert_fusion.1
  156.8 1.6 add_convert_fusion
  158.4 1.6 collective-permute-start.17
  160.0 1.4 collective-permute-start.20
  161.4 15.1 %collective-permute-done.10 = bf16[256,2048]{1,0:T(8,128)(2,1)S(1)} collective-permute-done((bf16[256,2048]{1,0:T(8,128)(2,1)}, bf16[256,2048]{1,0:T(8,128)(2,1)S(1)}, u32[]{:S(2)}, u32[]{:S(2)}) %collective-permute-start.10) | collective-permute-done | bytes 1048608 | tf_op jit(solution)/shard_map/ppermute | solution.py:262
  176.5 1.5 collective-permute-start.21
  178.0 19.6 %collective-permute-done.12 = bf16[256,2048]{1,0:T(8,128)(2,1)S(1)} collective-permute-done((bf16[256,2048]{1,0:T(8,128)(2,1)S(1)}, bf16[256,2048]{1,0:T(8,128)(2,1)S(1)}, u32[]{:S(2)}, u32[]{:S(2)}) %collective-permute-start.12) | collective-permute-done | bytes 1048608 | tf_op jit(solution)/shard_map/ppermute | solution.py:266
  197.6 1.4 collective-permute-done.17
  199.0 2.7 multiply_reduce_fusion
  201.9 1.6 collective-permute-start.22
  204.0 2.3 pad_maximum_fusion.refs_12_.middle_ref
  207.5 26.9 %gated_unit.4 = (bf16[2048,2048]{1,0:T(8,128)(2,1)}, bf16[2048,2048]{1,0:T(8,128)(2,1)}, bf16[2048,1408]{1,0:T(8,128)(2,1)}, bf16[2048,2816]{1,0:T(8,128)(2,1)},...) custom-call(bf16[256,2048]{1,0:T(8,128)(2,1)} %copy-done.8, ...), custom_call_target="tpu_custom_call" | custom-call | flops 17716740096 | bytes 29301504 | tf_op jit(solution)/shard_map/gated_unit/pallas_call | solution.py:1235
  234.5 5.0 collective-permute-done.18.refs_1_
  239.5 1.5 collective-permute-start.23
  240.9 22.7 %collective-permute-done.13.refs_0_ = bf16[256,2048]{1,0:T(8,128)(2,1)} collective-permute-done((bf16[256,2048]{1,0:T(8,128)(2,1)S(1)}, bf16[256,2048]{1,0:T(8,128)(2,1)}, u32[]{:S(2)}, u32[]{:S(2)}) %collective-permute-start.13) | collective-permute-done | bytes 1048608 | tf_op jit(solution)/shard_map/ppermute | solution.py:262
  263.6 1.5 collective-permute-start.19
  265.1 26.9 %gated_unit.5 = (bf16[2048,2048]{1,0:T(8,128)(2,1)}, bf16[2048,2048]{1,0:T(8,128)(2,1)}, bf16[2048,1408]{1,0:T(8,128)(2,1)}, bf16[2048,2816]{1,0:T(8,128)(2,1)},...) custom-call(bf16[256,2048]{1,0:T(8,128)(2,1)} %collective-permute-do, ...), custom_call_target="tpu_custom_call", output_to_operand_aliasing={{0}: (6, {}), {1}: (7, {}), {2}: (8, {}), {3}: (9, {})} | custom-call | flops 17716740096 | bytes 29301504 | tf_op jit(solution)/shard_map/gated_unit/pallas_call | solution.py:1235
  292.7 26.8 %gated_unit.6 = (bf16[2048,2048]{1,0:T(8,128)(2,1)}, bf16[2048,2048]{1,0:T(8,128)(2,1)}, bf16[2048,1408]{1,0:T(8,128)(2,1)}, bf16[2048,2816]{1,0:T(8,128)(2,1)},...) custom-call(bf16[256,2048]{1,0:T(8,128)(2,1)} %collective-permute-do, ...), custom_call_target="tpu_custom_call", output_to_operand_aliasing={{0}: (6, {}), {1}: (7, {}), {2}: (8, {}), {3}: (9, {})} | custom-call | flops 17716740096 | bytes 29301504 | tf_op jit(solution)/shard_map/gated_unit/pallas_call | solution.py:1235
  319.6 1.0 copy-done.13
  320.9 26.8 %gated_unit.7 = (bf16[2048,2048]{1,0:T(8,128)(2,1)}, bf16[2048,2048]{1,0:T(8,128)(2,1)}, bf16[2048,1408]{1,0:T(8,128)(2,1)}, bf16[2048,2816]{1,0:T(8,128)(2,1)},...) custom-call(bf16[256,2048]{1,0:T(8,128)(2,1)} %copy-done.14, ...), custom_call_target="tpu_custom_call", output_to_operand_aliasing={{0}: (6, {}), {1}: (7, {}), {2}: (8, {}), {3}: (9, {})} | custom-call | flops 17716740096 | bytes 29301504 | tf_op jit(solution)/shard_map/gated_unit/pallas_call | solution.py:1235
  347.7 224.7 %unit_grads.1 = (bf16[11,128,2048]{2,1,0:T(8,128)(2,1)}, bf16[16,128,2816]{2,1,0:T(8,128)(2,1)}, bf16[2048,2048]{1,0:T(8,128)(2,1)}, f32[512,2048]{1,0:T(8,128)}, bf16[2048,512]{1,0:T(8,128)(2,1)}) custom-call(bf16[2048,1408]{1,0:T(8,128)(2,1)} %get-tuple-element.113.refs_0_, bf16[2048,2048]{1,0:T(8,128)(2,1)} %get-tuple-element.114.refs_1_, ...), custom_call_target="tpu_custom_call" | custom-call | flops 35433480192 | bytes 60000000 | tf_op jit(solution)/shard_map/unit_grads/pallas_call | solution.py:768
  572.4 29.0 %mix_backward.1 = (bf16[4,2048,512]{2,1,0:T(8,128)(2,1)}, f32[2,2048,1408]{2,1,0:T(8,128)}, f32[1408,2048]{1,0:T(8,128)}) custom-call(s32[8]{0:T(128)} %compare_select_fusion.1.slot_ref, s32[8]{0:T(128)} %compare_convert_fusion.fresh_ref, f32[4]{0:T(128)} %multiply_power_fusion.rate_ref, bf16[4,2048,512]{2,1,0:T(8,128)(2,1)} %get-tuple-element.89.parts_ref, ...), custom_call_target="tpu_custom_call" | custom-call | flops 20000000000 | bytes 75000000 | tf_op jit(solution)/shard_map/mix_backward/pallas_call | solution.py:1460
  601.3 156.2 %mix_grads.1 = (bf16[4,128,2048]{2,1,0:T(8,128)(2,1)}, bf16[64,128,512]{2,1,0:T(8,128)(2,1)}, bf16[256,2048]{1,0:T(8,128)(2,1)}, bf16[256,2048]{1,0:T(8,128)(2,1...) custom-call(bf16[1,2048,512]{2,1,0:T(8,128)(2,1)} %get-tuple-element, ...), custom_call_target="tpu_custom_call" | custom-call | flops 38654705664 | bytes 60000000 | tf_op jit(solution)/shard_map/mix_grads/pallas_call | solution.py:942
  757.6 20.3 %finish_rows.1 = (f32[4,2048,512]{2,1,0:T(8,128)}, f32[512,2048]{1,0:T(8,128)}, bf16[512,2048]{1,0:T(8,128)(2,1)}, bf16[512,2048]{1,0:T(8,128)(2,1)}) custom-call(bf16[4,2048,512]{2,1,0:T(8,128)(2,1)} %bitcast.15, bf16[512,2048]{1,0:T(8,128)(2,1)} %bitcast.16, bf16[512,2048]{1,0:T(8,128)(2,1)} %hidden_ref.1, ...), custom_call_target="tpu_custom_call" | custom-call | flops 100000000 | bytes 60000000 | tf_op jit(solution)/shard_map/finish_rows/pallas_call | solution.py:1323
  (73 shorter events, 11.9 us)
Async XLA Ops:
  0.6 2.2 copy-start.2
  2.9 6.8 copy-start.10
  2.9 7.3 copy-start.11
  4.6 63.8 %collective-permute-start.4 = (bf16[256,2048]{1,0:T(8,128)(2,1)}, bf16[256,2048]{1,0:T(8,128)(2,1)}, u32[]{:S(2)}, u32[]{:S(2)}) collective-permute-start(bf16[256,2048]{1,0:T(8,128)(2,1)} %get-tuple-element.170.refs_1_), channel_id=1, source_target_pairs={{0,1},{1,0},{2,3},{3,2},{4,5},{5,4},{6,7},{7,6},{8,9},{9,8},{10,11... | collective-permute-start | bytes 3145736 | tf_op jit(solution)/shard_map/ppermute | solution.py:262
  7.5 26.4 %collective-permute-start.2 = (bf16[256,2048]{1,0:T(8,128)(2,1)}, bf16[256,2048]{1,0:T(8,128)(2,1)}, u32[]{:S(2)}, u32[]{:S(2)}) collective-permute-start(bf16[256,2048]{1,0:T(8,128)(2,1)} %get-tuple-element.170.refs_1_), channel_id=1, source_target_pairs={{0,2},{1,3},{2,0},{3,1},{4,6},{5,7},{6,4},{7,5},{8,10},{9,11},{10,... | collective-permute-start | bytes 3145736 | tf_op jit(solution)/shard_map/ppermute | solution.py:266
  9.0 59.4 %collective-permute-start.5 = (bf16[256,2048]{1,0:T(8,128)(2,1)}, bf16[256,2048]{1,0:T(8,128)(2,1)}, u32[]{:S(2)}, u32[]{:S(2)}) collective-permute-start(bf16[256,2048]{1,0:T(8,128)(2,1)} %get-tuple-element.171.refs_0_), channel_id=1, source_target_pairs={{0,2},{1,3},{2,0},{3,1},{4,6},{5,7},{6,4},{7,5},{8,10},{9,11},{10,... | collective-permute-start | bytes 3145736 | tf_op jit(solution)/shard_map/ppermute | solution.py:266
  9.5 44.7 %collective-permute-start = (bf16[256,2048]{1,0:T(8,128)(2,1)}, bf16[256,2048]{1,0:T(8,128)(2,1)}, u32[]{:S(2)}, u32[]{:S(2)}) collective-permute-start(bf16[256,2048]{1,0:T(8,128)(2,1)} %get-tuple-element.171.refs_0_), channel_id=1, source_target_pairs={{0,1},{1,0},{2,3},{3,2},{4,5},{5,4},{6,7},{7,6},{8,9},{9,8},{10,11... | collective-permute-start | bytes 3145736 | tf_op jit(solution)/shard_map/ppermute | solution.py:262
  14.0 42.9 %copy-start.1 = (s32[4]{0:T(128)S(1)}, s32[4]{0:T(128)}, u32[]{:S(2)}) copy-start(s32[4]{0:T(128)} %constant.68.clone) | copy-start | bytes 52
  14.0 43.6 %copy-start = (s32[4]{0:T(128)S(1)}, s32[4]{0:T(128)}, u32[]{:S(2)}) copy-start(s32[4]{0:T(128)} %constant.67.clone) | copy-start | bytes 52
  33.9 43.3 %collective-permute-start.3 = (bf16[256,2048]{1,0:T(8,128)(2,1)}, bf16[256,2048]{1,0:T(8,128)(2,1)S(1)}, u32[]{:S(2)}, u32[]{:S(2)}) collective-permute-start(bf16[256,2048]{1,0:T(8,128)(2,1)} %collective-permute-done.2.refs_1_), channel_id=1, source_target_pairs={{0,1},{1,0},{2,3},{3,2},{4,5},{5,4},{6,7},{7,6},{8,9},{9,8},{10,11... | collective-permute-start | bytes 3145736 | tf_op jit(solution)/shard_map/ppermute | solution.py:262
  54.3 23.8 %collective-permute-start.1 = (bf16[256,2048]{1,0:T(8,128)(2,1)}, bf16[256,2048]{1,0:T(8,128)(2,1)}, u32[]{:S(2)}, u32[]{:S(2)}) collective-permute-start(bf16[256,2048]{1,0:T(8,128)(2,1)} %collective-permute-done.refs_0_), channel_id=1, source_target_pairs={{0,2},{1,3},{2,0},{3,1},{4,6},{5,7},{6,4},{7,5},{8,10},{9,11},{10,... | collective-permute-start | bytes 3145736 | tf_op jit(solution)/shard_map/ppermute | solution.py:266
  77.2 1.0 copy-start.3
  81.4 41.1 %collective-permute-start.9 = (bf16[256,2048]{1,0:T(8,128)(2,1)}, bf16[256,2048]{1,0:T(8,128)(2,1)S(1)}, u32[]{:S(2)}, u32[]{:S(2)}) collective-permute-start(bf16[256,2048]{1,0:T(8,128)(2,1)} %get-tuple-element.91.refs_2_), channel_id=1, source_target_pairs={{0,2},{1,3},{2,0},{3,1},{4,6},{5,7},{6,4},{7,5},{8,10},{9,11},{10,... | collective-permute-start | bytes 3145736 | tf_op jit(solution)/shard_map/ppermute | solution.py:266
  82.8 41.1 %collective-permute-start.6 = (bf16[256,2048]{1,0:T(8,128)(2,1)}, bf16[256,2048]{1,0:T(8,128)(2,1)}, u32[]{:S(2)}, u32[]{:S(2)}) collective-permute-start(bf16[256,2048]{1,0:T(8,128)(2,1)} %get-tuple-element.91.refs_2_), channel_id=1, source_target_pairs={{0,1},{1,0},{2,3},{3,2},{4,5},{5,4},{6,7},{7,6},{8,9},{9,8},{10,11... | collective-permute-start | bytes 3145736 | tf_op jit(solution)/shard_map/ppermute | solution.py:262
  84.3 47.4 %collective-permute-start.8 = (bf16[256,2048]{1,0:T(8,128)(2,1)}, bf16[256,2048]{1,0:T(8,128)(2,1)}, u32[]{:S(2)}, u32[]{:S(2)}) collective-permute-start(bf16[256,2048]{1,0:T(8,128)(2,1)} %get-tuple-element.92.refs_3_), channel_id=1, source_target_pairs={{0,1},{1,0},{2,3},{3,2},{4,5},{5,4},{6,7},{7,6},{8,9},{9,8},{10,11... | collective-permute-start | bytes 3145736 | tf_op jit(solution)/shard_map/ppermute | solution.py:262
  84.8 47.5 %collective-permute-start.7 = (bf16[256,2048]{1,0:T(8,128)(2,1)}, bf16[256,2048]{1,0:T(8,128)(2,1)}, u32[]{:S(2)}, u32[]{:S(2)}) collective-permute-start(bf16[256,2048]{1,0:T(8,128)(2,1)} %get-tuple-element.92.refs_3_), channel_id=1, source_target_pairs={{0,2},{1,3},{2,0},{3,1},{4,6},{5,7},{6,4},{7,5},{8,10},{9,11},{10,... | collective-permute-start | bytes 3145736 | tf_op jit(solution)/shard_map/ppermute | solution.py:266
  121.0 33.2 %collective-permute-start.11 = (bf16[256,2048]{1,0:T(8,128)(2,1)}, bf16[256,2048]{1,0:T(8,128)(2,1)}, u32[]{:S(2)}, u32[]{:S(2)}) collective-permute-start(bf16[256,2048]{1,0:T(8,128)(2,1)} %get-tuple-element.96), channel_id=1, source_target_pairs={{0,1},{1,0},{2,3},{3,2},{4,5},{5,4},{6,7},{7,6},{8,9},{9,8},{10,11... | collective-permute-start | bytes 3145736 | tf_op jit(solution)/shard_map/ppermute | solution.py:262
  122.5 1.4 copy-start.9
  122.5 34.3 %collective-permute-start.16 = (bf16[256,2048]{1,0:T(8,128)(2,1)}, bf16[256,2048]{1,0:T(8,128)(2,1)}, u32[]{:S(2)}, u32[]{:S(2)}) collective-permute-start(bf16[256,2048]{1,0:T(8,128)(2,1)} %get-tuple-element.100), channel_id=1, source_target_pairs={{0,2},{1,3},{2,0},{3,1},{4,6},{5,7},{6,4},{7,5},{8,10},{9,11},{10,... | collective-permute-start | bytes 3145736 | tf_op jit(solution)/shard_map/ppermute | solution.py:266
  123.9 52.6 %collective-permute-start.10 = (bf16[256,2048]{1,0:T(8,128)(2,1)}, bf16[256,2048]{1,0:T(8,128)(2,1)S(1)}, u32[]{:S(2)}, u32[]{:S(2)}) collective-permute-start(bf16[256,2048]{1,0:T(8,128)(2,1)} %get-tuple-element.94), channel_id=1, source_target_pairs={{0,1},{1,0},{2,3},{3,2},{4,5},{5,4},{6,7},{7,6},{8,9},{9,8},{10,11... | collective-permute-start | bytes 3145736 | tf_op jit(solution)/shard_map/ppermute | solution.py:262
  131.7 46.3 %collective-permute-start.15 = (bf16[256,2048]{1,0:T(8,128)(2,1)}, bf16[256,2048]{1,0:T(8,128)(2,1)}, u32[]{:S(2)}, u32[]{:S(2)}) collective-permute-start(bf16[256,2048]{1,0:T(8,128)(2,1)} %get-tuple-element.98), channel_id=1, source_target_pairs={{0,2},{1,3},{2,0},{3,1},{4,6},{5,7},{6,4},{7,5},{8,10},{9,11},{10,... | collective-permute-start | bytes 3145736 | tf_op jit(solution)/shard_map/ppermute | solution.py:266
  138.7 18.1 %copy-start.6 = (bf16[256,2048]{1,0:T(8,128)(2,1)S(1)}, bf16[256,2048]{1,0:T(8,128)(2,1)}, u32[]{:S(2)}) copy-start(bf16[256,2048]{1,0:T(8,128)(2,1)} %get-tuple-element.99) | copy-start | bytes 3145732
  156.1 42.9 %copy-start.4 = (bf16[256,2048]{1,0:T(8,128)(2,1)S(1)}, bf16[256,2048]{1,0:T(8,128)(2,1)}, u32[]{:S(2)}) copy-start(bf16[256,2048]{1,0:T(8,128)(2,1)} %get-tuple-element.93) | copy-start | bytes 3145732
  156.1 42.9 %copy-start.5 = (bf16[256,2048]{1,0:T(8,128)(2,1)S(1)}, bf16[256,2048]{1,0:T(8,128)(2,1)}, u32[]{:S(2)}) copy-start(bf16[256,2048]{1,0:T(8,128)(2,1)} %get-tuple-element.97) | copy-start | bytes 3145732
  156.1 41.5 %collective-permute-start.12 = (bf16[256,2048]{1,0:T(8,128)(2,1)S(1)}, bf16[256,2048]{1,0:T(8,128)(2,1)S(1)}, u32[]{:S(2)}, u32[]{:S(2)}) collective-permute-start(bf16[256,2048]{1,0:T(8,128)(2,1)S(1)} %add_convert_fusion.1), channel_id=1, source_target_pairs={{0,2},{1,3},{2,0},{3,1},{4,6},{5,7},{6,4},{7,5},{8,10},{9,11},{10,... | collective-permute-start | bytes 3145736 | tf_op jit(solution)/shard_map/ppermute | solution.py:266
  158.4 40.6 %collective-permute-start.17 = (bf16[256,2048]{1,0:T(8,128)(2,1)S(1)}, bf16[256,2048]{1,0:T(8,128)(2,1)S(1)}, u32[]{:S(2)}, u32[]{:S(2)}) collective-permute-start(bf16[256,2048]{1,0:T(8,128)(2,1)S(1)} %add_convert_fusion), channel_id=1, source_target_pairs={{0,1},{1,0},{2,3},{3,2},{4,5},{5,4},{6,7},{7,6},{8,9},{9,8},{10,11... | collective-permute-start | bytes 3145736 | tf_op jit(solution)/shard_map/ppermute | solution.py:262
  160.0 159.6 %collective-permute-start.20 = (bf16[256,2048]{1,0:T(8,128)(2,1)}, bf16[256,2048]{1,0:T(8,128)(2,1)}, u32[]{:S(2)}, u32[]{:S(2)}) collective-permute-start(bf16[256,2048]{1,0:T(8,128)(2,1)} %collective-permute-done.6.refs_0_.refs_2_), channel_id=1, source_target_pairs={{0,2},{1,3},{2,0},{3,1},{4,6},{5,7},{6,4},{7,5},{8,10},{9,11},{10,... | collective-permute-start | bytes 3145736 | tf_op jit(solution)/shard_map/ppermute | solution.py:266
  176.5 143.1 %collective-permute-start.21 = (bf16[256,2048]{1,0:T(8,128)(2,1)}, bf16[256,2048]{1,0:T(8,128)(2,1)}, u32[]{:S(2)}, u32[]{:S(2)}) collective-permute-start(bf16[256,2048]{1,0:T(8,128)(2,1)} %collective-permute-done.7.refs_1_.refs_3_), channel_id=1, source_target_pairs={{0,1},{1,0},{2,3},{3,2},{4,5},{5,4},{6,7},{7,6},{8,9},{9,8},{10,11... | collective-permute-start | bytes 3145736 | tf_op jit(solution)/shard_map/ppermute | solution.py:262
  201.9 4.5 copy-start.7
  201.9 90.1 %collective-permute-start.22 = (bf16[256,2048]{1,0:T(8,128)(2,1)S(1)}, bf16[256,2048]{1,0:T(8,128)(2,1)}, u32[]{:S(2)}, u32[]{:S(2)}) collective-permute-start(bf16[256,2048]{1,0:T(8,128)(2,1)S(1)} %multiply_convert_fusion.refs_1_), channel_id=1, source_target_pairs={{0,1},{1,0},{2,3},{3,2},{4,5},{5,4},{6,7},{7,6},{8,9},{9,8},{10,11... | collective-permute-start | bytes 3145736 | tf_op jit(solution)/shard_map/ppermute | solution.py:262
  203.4 36.1 %collective-permute-start.18 = (bf16[256,2048]{1,0:T(8,128)(2,1)S(1)}, bf16[256,2048]{1,0:T(8,128)(2,1)S(1)}, u32[]{:S(2)}, u32[]{:S(2)}) collective-permute-start(bf16[256,2048]{1,0:T(8,128)(2,1)S(1)} %multiply_convert_fusion.refs_1_), channel_id=1, source_target_pairs={{0,2},{1,3},{2,0},{3,1},{4,6},{5,7},{6,4},{7,5},{8,10},{9,11},{10,... | collective-permute-start | bytes 3145736 | tf_op jit(solution)/shard_map/ppermute | solution.py:266
  206.5 1.0 copy-start.8
  206.6 57.1 %collective-permute-start.13 = (bf16[256,2048]{1,0:T(8,128)(2,1)S(1)}, bf16[256,2048]{1,0:T(8,128)(2,1)}, u32[]{:S(2)}, u32[]{:S(2)}) collective-permute-start(bf16[256,2048]{1,0:T(8,128)(2,1)S(1)} %multiply_convert_fusion.1.refs_0_), channel_id=1, source_target_pairs={{0,1},{1,0},{2,3},{3,2},{4,5},{5,4},{6,7},{7,6},{8,9},{9,8},{10,11... | collective-permute-start | bytes 3145736 | tf_op jit(solution)/shard_map/ppermute | solution.py:262
  239.5 25.6 %copy-start.12 = (bf16[256,2048]{1,0:T(8,128)(2,1)}, bf16[256,2048]{1,0:T(8,128)(2,1)S(1)}, u32[]{:S(2)}) copy-start(bf16[256,2048]{1,0:T(8,128)(2,1)S(1)} %collective-permute-done.18.refs_1_) | copy-start | bytes 3145732
  239.5 53.2 %collective-permute-start.23 = (bf16[256,2048]{1,0:T(8,128)(2,1)}, bf16[256,2048]{1,0:T(8,128)(2,1)}, u32[]{:S(2)}, u32[]{:S(2)}) collective-permute-start(bf16[256,2048]{1,0:T(8,128)(2,1)} %copy-done.8), channel_id=1, source_target_pairs={{0,2},{1,3},{2,0},{3,1},{4,6},{5,7},{6,4},{7,5},{8,10},{9,11},{10,... | collective-permute-start | bytes 3145736 | tf_op jit(solution)/shard_map/ppermute | solution.py:266
  263.6 56.0 %collective-permute-start.19 = (bf16[256,2048]{1,0:T(8,128)(2,1)S(1)}, bf16[256,2048]{1,0:T(8,128)(2,1)S(1)}, u32[]{:S(2)}, u32[]{:S(2)}) collective-permute-start(bf16[256,2048]{1,0:T(8,128)(2,1)S(1)} %collective-permute-done.18.refs_1_), channel_id=1, source_target_pairs={{0,1},{1,0},{2,3},{3,2},{4,5},{5,4},{6,7},{7,6},{8,9},{9,8},{10,11... | collective-permute-start | bytes 3145736 | tf_op jit(solution)/shard_map/ppermute | solution.py:262
  292.0 27.6 %collective-permute-start.14 = (bf16[256,2048]{1,0:T(8,128)(2,1)}, bf16[256,2048]{1,0:T(8,128)(2,1)S(1)}, u32[]{:S(2)}, u32[]{:S(2)}) collective-permute-start(bf16[256,2048]{1,0:T(8,128)(2,1)} %collective-permute-done.13.refs_0_), channel_id=1, source_target_pairs={{0,2},{1,3},{2,0},{3,1},{4,6},{5,7},{6,4},{7,5},{8,10},{9,11},{10,... | collective-permute-start | bytes 3145736 | tf_op jit(solution)/shard_map/ppermute | solution.py:266
  319.6 1.0 copy-start.13
  319.6 1.3 copy-start.14

commit v4 on v3

--- a/solution.py
+++ b/solution.py
@@ -1,4 +1,5 @@
 import functools
+import math
 
 import jax
 import jax.numpy as jnp
@@ -258,31 +259,8 @@
 VMEM = 60 * 1024 * 1024
 
 
-def over_x(rows):
-    return lax.ppermute(rows, "narrow", [(at, at ^ 1) for at in range(4)])
-
-
-def over_y(rows):
-    return lax.ppermute(rows, "narrow", [(at, at ^ 2) for at in range(4)])
-
-
 def add_low(*terms):
     return sum(term.astype(jnp.float32) for term in terms).astype(jnp.bfloat16)
-
-
-def gather_pieces(top, low):
-    top_x, low_y = over_x(top), over_y(low)
-    low_x, top_y = over_x(low), over_y(top)
-    low_d, top_d = over_x(low_y), over_y(top_x)
-    return ((top, low), (top_x, low_y), (low_x, top_y), (top_d, low_d))
-
-
-def scatter_pieces(own, first, second, third):
-    (top, low), (top_x, low_y), (low_x, top_y), (top_d, low_d) = own, first, second, third
-    to_top_y, to_low_x = over_x(top_d), over_y(low_d)
-    to_top, to_low = over_x(top_x), over_y(low_y)
-    more_top, more_low = over_y(add_low(top_y, to_top_y)), over_x(add_low(low_x, to_low_x))
-    return add_rows(top, to_top, more_top), add_rows(low, to_low, more_low)
 
 
 def add_rows(*terms):
@@ -589,13 +567,13 @@
 
     def body(*refs):
         act_in, two_in, normed_in, parts_in = refs[:4]
-        partial = refs[4:12]
-        middle_in, cot_in, weight_in, live_ref = refs[12:16]
-        out_grad, in_grad, branch_out, middle_out, gated_out = refs[16:21]
-        act_ref, shared, parts_ref, landed, own_ref, cot_ref, mid_ref, grad_ref, branch = refs[21:30]
-        gated_ref, load_sems, stage_sems, gather_sems, back_sems = refs[30:35]
-        line = refs[35:44]
-        square = refs[44:48]
+        partial = [refs[4].at[pl.ds(at * BLK, BLK)] for at in range(8)]
+        middle_in, cot_in, weight_in, live_ref = refs[5:9]
+        out_grad, in_grad, branch_out, middle_out, gated_out = refs[9:14]
+        act_ref, shared, parts_ref, landed, own_ref, cot_ref, mid_ref, grad_ref, branch = refs[14:23]
+        gated_ref, load_sems, stage_sems, gather_sems, back_sems = refs[23:28]
+        line = refs[28:37]
+        square = refs[37:41]
         places = neighbours()
         near_x, near_y = places[5:]
         enter(places)
@@ -767,7 +745,7 @@
 
     return pl.pallas_call(
         body,
-        in_specs=any_specs(15) + [pl.BlockSpec(memory_space=pltpu.VMEM)],
+        in_specs=any_specs(8) + [pl.BlockSpec(memory_space=pltpu.VMEM)],
         out_specs=any_specs(5),
         out_shape=[
             jax.ShapeDtypeStruct((out_blocks, SUB, width), low),
@@ -804,7 +782,7 @@
         grad_two_all,
         normed_two_all,
         grad_parts,
-        *back_sums,
+        back_sums,
         middle,
         cotangent,
         out_weight,
@@ -825,14 +803,14 @@
 
     def body(*refs):
         gated_in, branch_in, normed_in, grads_in, weight_in = refs[:5]
-        two_partial = refs[5:11]
-        out_grad, mix_grad = refs[11:13]
-        own_outs = refs[13:15]
-        landed, two_landed = refs[15:19], refs[19:23]
-        gated_ref, branch_ref, normed_ref, grads_ref, weight_ref, far, near, own_ref = refs[23:31]
-        load_sems, branch_sems, grad_sems, weight_sems, own_sems = refs[31:36]
-        line = refs[36:45]
-        square, two_square = refs[45:49], refs[49:53]
+        two_partial = [refs[5].at[pl.ds(at * BLK, BLK)] for at in range(2, 8)]
+        out_grad, mix_grad = refs[6:8]
+        own_outs = refs[8:10]
+        landed, two_landed = refs[10:14], refs[14:18]
+        gated_ref, branch_ref, normed_ref, grads_ref, weight_ref, far, near, own_ref = refs[18:26]
+        load_sems, branch_sems, grad_sems, weight_sems, own_sems = refs[26:31]
+        line = refs[31:40]
+        square, two_square = refs[40:44], refs[44:48]
         mid = square[1]
         places = neighbours()
         enter(places)
@@ -941,7 +919,7 @@
 
     return pl.pallas_call(
         body,
-        in_specs=any_specs(11),
+        in_specs=any_specs(6),
         out_specs=any_specs(12),
         out_shape=[
             jax.ShapeDtypeStruct((columns // SUB, SUB, width), low),
@@ -971,319 +949,562 @@
         ),
         cost_estimate=cost(2 * 9 * rows * width * columns, 60e6),
         name="mix_grads",
-    )(gated, grad_branch_all, normed_all, grad_projected, mix_weight, *two_sums)
-
-
-def row_copies(pair, rows, sems, at):
-    return [
-        pltpu.make_async_copy(src, rows.at[pl.ds(half * HALF, HALF)], sems.at[at + half])
-        for half, src in enumerate(pair)
-    ]
-
-
-def project_piece(pair, weight, kept, piece):
-    parts, width, columns = weight.shape
+    )(gated, grad_branch_all, normed_all, grad_projected, mix_weight, two_sums)
+
+
+def gated_unit(gated, whole_weight, hidden, live, grads_own, grads_first, ffn_in, ffn_out):
+    _, width, units = ffn_in.shape
+    local_rows = hidden.shape[0]
     group_rows = NBLK * BLK
-    low = jnp.bfloat16
-    spot = pl.ds(piece * PIECE, PIECE)
-    joined = 2
-
-    def body(*refs):
-        weight_in = refs[2]
-        rows_out, parts_out, rows, weights, out, row_sems, weight_sems, out_sems = refs[3 + len(kept) :]
-        row_loads = row_copies(refs[:2], rows, row_sems, 0)
-        weight_loads = [
-            pltpu.make_async_copy(
-                weight_in.at[c], weights.at[:, pl.ds(c * columns, columns)], weight_sems.at[c]
-            )
-            for c in range(parts)
-        ]
-        stores = [
-            pltpu.make_async_copy(
-                out.at[:, pl.ds(c * columns, columns)], parts_out.at[c, spot, :], out_sems.at[c]
-            )
-            for c in range(parts)
-        ]
-        begin(row_loads)
-        begin(weight_loads[:joined])
-        finish(row_loads)
-        begin(weight_loads[joined:])
-        keep = pltpu.make_async_copy(rows, rows_out.at[spot, :], row_sems.at[2])
-        keep.start()
-        for c in range(0, parts, joined):
-            finish(weight_loads[c : c + joined])
-            at = slice(c * columns, (c + joined) * columns)
-            out[:, at] = straight(rows[...], weights[:, at]).astype(low)
-            begin(stores[c : c + joined])
-        finish(stores)
-        keep.wait()
-
-    return pl.pallas_call(
-        body,
-        in_specs=any_specs(3 + len(kept)),
-        out_specs=any_specs(2),
-        out_shape=[
-            jax.ShapeDtypeStruct((group_rows, width), low),
-            jax.ShapeDtypeStruct((parts, group_rows, columns), low),
-        ],
-        scratch_shapes=[
-            pltpu.VMEM((PIECE, width), low),
-            pltpu.VMEM((width, parts * columns), low),
-            pltpu.VMEM((PIECE, parts * columns), low),
-            pltpu.SemaphoreType.DMA((3,)),
-            pltpu.SemaphoreType.DMA((parts,)),
-            pltpu.SemaphoreType.DMA((parts,)),
-        ],
-        input_output_aliases={3 + at: at for at in range(len(kept))},
-        compiler_params=pltpu.CompilerParams(vmem_limit_bytes=VMEM),
-        cost_estimate=cost(2 * PIECE * parts * width * columns, 2 * parts * width * columns + 8e6),
-        name="project",
-    )(*pair, weight, *kept)
-
-
-def partial_sums(acts, weight, pieces, transposed, after=()):
-    parts, _, columns = acts.shape
-    width = weight.shape[1] if transposed else weight.shape[2]
-    deep = parts * columns
-    low = jnp.bfloat16
-    wide_tile = 1024
-
-    def body(act_in, weight_in, *refs):
-        refs = refs[len(after) :]
-        outs = refs[: 2 * len(pieces)]
-        acts_ref, weights, out, act_sems, weight_sems, out_sems = refs[2 * len(pieces) :]
-
-        def place(c):
-            return pl.ds(c * columns, columns)
-
-        act_loads = [
-            [
-                pltpu.make_async_copy(
-                    act_in.at[c, pl.ds(piece * PIECE, PIECE), :],
-                    acts_ref.at[at, :, place(c)],
-                    act_sems.at[at, c],
-                )
-                for c in range(parts)
-            ]
-            for at, piece in enumerate(pieces)
-        ]
-        weight_loads = []
-        for j in range(width // wide_tile):
-            tile = pl.ds(j * wide_tile, wide_tile)
-            weight_loads.append(
-                [
-                    pltpu.make_async_copy(
-                        weight_in.at[c, tile, :], weights.at[tile, place(c)], weight_sems.at[j, c]
-                    )
-                    if transposed
-                    else pltpu.make_async_copy(
-                        weight_in.at[c, :, tile], weights.at[place(c), tile], weight_sems.at[j, c]
-                    )
-                    for c in range(parts)
-                ]
-            )
-        begin(act_loads[0])
-        begin(weight_loads[0])
-        stores = []
-        for at in range(len(pieces)):
-            finish(act_loads[at])
-            for j, loads in enumerate(weight_loads):
-                if at == 0:
-                    finish(loads)
-                    if j + 1 < len(weight_loads):
-                        begin(weight_loads[j + 1])
-                if j == len(weight_loads) - 1 and at + 1 < len(pieces):
-                    begin(act_loads[at + 1])
-                tile = slice(j * wide_tile, (j + 1) * wide_tile)
-                if transposed:
-                    total = across(acts_ref[at], weights[tile, :])
-                else:
-                    total = straight(acts_ref[at], weights[:, tile])
-                out[2 * at, :, tile] = total[:HALF].astype(low)
-                out[2 * at + 1, :, tile] = total[HALF:].astype(low)
-            now = [
-                pltpu.make_async_copy(out.at[at_out], outs[at_out], out_sems.at[at_out])
-                for at_out in (2 * at, 2 * at + 1)
-            ]
-            begin(now)
-            stores += now
-        finish(stores)
-
-    return pl.pallas_call(
-        body,
-        in_specs=any_specs(2 + len(after)),
-        out_specs=any_specs(2 * len(pieces)),
-        out_shape=[jax.ShapeDtypeStruct((HALF, width), low)] * (2 * len(pieces)),
-        scratch_shapes=[
-            pltpu.VMEM((len(pieces), PIECE, deep), low),
-            pltpu.VMEM((width, deep) if transposed else (deep, width), low),
-            pltpu.VMEM((2 * len(pieces), HALF, width), low),
-            pltpu.SemaphoreType.DMA((len(pieces), parts)),
-            pltpu.SemaphoreType.DMA((width // wide_tile, parts)),
-            pltpu.SemaphoreType.DMA((2 * len(pieces),)),
-        ],
-        compiler_params=pltpu.CompilerParams(vmem_limit_bytes=VMEM),
-        cost_estimate=cost(
-            2 * len(pieces) * PIECE * parts * width * columns, 2 * parts * width * columns + 8e6
-        ),
-        name="partial_sums",
-    )(acts, weight, *after)
-
-
-def unit_piece(pair, grad_pair, ffn_in, ffn_out, kept, piece):
-    _, width, units = ffn_in.shape
-    group_rows = NBLK * BLK
+    pieces = group_rows // PIECE
+    deep = gated.shape[2]
+    slices, quarters, slice_rows, _ = whole_weight.shape
     main = units // TILE * TILE
     tail = units - main
     low = jnp.bfloat16
-    spot = pl.ds(piece * PIECE, PIECE)
     cuts = ((0, 2 * TILE), (2 * TILE, main - 2 * TILE))
     wide_tile = 1024
+    first_half, second_half = pl.ds(0, HALF), pl.ds(HALF, HALF)
 
     def body(*refs):
-        in_ref, out_ref = refs[4:6]
-        outs = refs[6 + len(kept) :]
-        rows_out, grads_out, act_out, parts_out = outs[:4]
-        sum_outs = outs[4:8]
-        rows, grads, w_in, w_out, act, parts, sums, row_sems, sems, done_sems, sum_sems = outs[8:]
-        loads = row_copies(refs[:2], rows, row_sems, 0)
-        grad_loads = row_copies(refs[2:4], grads, row_sems, 2)
-
-        def weight_loads(which, start, size, first, second):
+        gated_in, weight_in, hidden_in = refs[:3]
+        grad_in = refs[3:5]
+        in_ref, out_ref, live_ref = refs[5:8]
+        middle_out, rows_out, grads_out, act_out, parts_out, back_out, two_out = refs[8:15]
+        gated_ref, hidden_ref, middle_ref = refs[15:18]
+        rows, grads, sums, w_in, w_out, act, parts = refs[18:25]
+        load_sems, slice_sems, weight_sems, done_sems, sum_sems, gated_sems, gather_sems = refs[25:]
+        wide, narrow, _, _, _, near_x, near_y = neighbours()
+        far = (wide, 3 - narrow)
+        barrier = pltpu.get_barrier_semaphore()
+        for place in (near_x, near_y, far):
+            pl.semaphore_signal(barrier, inc=1, device_id=place, device_id_type=MESH)
+        pl.semaphore_wait(barrier, 3)
+
+        here = pl.ds(pl.multiple_of(narrow * deep, deep), deep)
+
+        def send_gated(slot, to, kind, place):
+            return pltpu.make_async_remote_copy(
+                src_ref=gated_in.at[0, pl.ds(slot * BLK, BLK)],
+                dst_ref=gated_ref.at[(first_half, second_half)[to], here],
+                send_sem=gated_sems.at[kind, 0],
+                recv_sem=gated_sems.at[kind, 1],
+                device_id=place,
+                device_id_type=MESH,
+            )
+
+        gated_sends = [
+            send_gated(6, 0, 0, far),
+            send_gated(7, 1, 1, far),
+            send_gated(2, 0, 2, near_x),
+            send_gated(3, 1, 3, near_y),
+            send_gated(4, 1, 4, near_x),
+            send_gated(5, 0, 5, near_y),
+        ]
+        keep_gated = pltpu.make_async_copy(
+            gated_in.at[0, pl.ds(0, PIECE)], gated_ref.at[:, here], load_sems.at[0]
+        )
+
+        def load_slice(at):
+            part, quarter = at // quarters, at % quarters
+            to = pl.ds(pl.multiple_of(quarter * deep + part * slice_rows, slice_rows), slice_rows)
+            return pltpu.make_async_copy(
+                weight_in.at[part, quarter], w_in.at[to, pl.ds(0, width)], slice_sems.at[at]
+            )
+
+        def start_slice(at, carry):
+            load_slice(at).start()
+            return carry
+
+        def wait_slice(at, carry):
+            load_slice(at).wait()
+            return carry
+
+        load_hidden = pltpu.make_async_copy(hidden_in, hidden_ref, load_sems.at[1])
+        load_grads = [
+            pltpu.make_async_copy(src, grads.at[at], load_sems.at[2 + at])
+            for at, src in enumerate(grad_in)
+        ]
+        weights = []
+        for start, size, first, second in tuple((a, b, a, main + a) for a, b in cuts) + (
+            (main, tail, 2 * main, 2 * main + tail),
+        ):
             at = pl.ds(start, size)
-            return [
-                pltpu.make_async_copy(
-                    in_ref.at[0, :, at], w_in.at[:, pl.ds(first, size)], sems.at[which, 0]
-                ),
-                pltpu.make_async_copy(
-                    in_ref.at[1, :, at], w_in.at[:, pl.ds(second, size)], sems.at[which, 1]
-                ),
-                pltpu.make_async_copy(out_ref.at[at, :], w_out.at[at, :], sems.at[which, 2]),
+            weights += [
+                pltpu.make_async_copy(in_ref.at[0, :, at], w_in.at[:, pl.ds(first, size)], weight_sems.at[len(weights)]),
+                pltpu.make_async_copy(in_ref.at[1, :, at], w_in.at[:, pl.ds(second, size)], weight_sems.at[len(weights) + 1]),
+                pltpu.make_async_copy(out_ref.at[at, :], w_out.at[at, :], weight_sems.at[len(weights) + 2]),
             ]
 
-        weights = [weight_loads(at, *cut, cut[0], main + cut[0]) for at, cut in enumerate(cuts)]
-        weights.append(weight_loads(2, main, tail, 2 * main, 2 * main + tail))
-        queue = [[copy] for loads_here in weights[:2] for copy in loads_here] + [weights[2]]
-        queue[2] = grad_loads + queue[2]
-        begin(loads)
-        begin(queue[0])
-        begin(queue[1])
-        finish(loads)
-        stores = [
-            pltpu.make_async_copy(rows, rows_out.at[spot, :], done_sems.at[0]),
-            pltpu.make_async_copy(grads, grads_out.at[spot, :], done_sems.at[1]),
-        ]
+        def remote(src, dst, sems, kind, place):
+            return pltpu.make_async_remote_copy(
+                src_ref=src,
+                dst_ref=dst,
+                send_sem=sems.at[kind, 0],
+                recv_sem=sems.at[kind, 1],
+                device_id=place,
+                device_id_type=MESH,
+            )
+
+        def half(ref, piece, at):
+            return ref.at[piece, (first_half, second_half)[at]]
+
+        def gather(ref, kind):
+            return (
+                [
+                    remote(half(ref, 0, 0), half(ref, 1, 0), gather_sems, kind, near_x),
+                    remote(half(ref, 0, 1), half(ref, 1, 1), gather_sems, kind + 1, near_y),
+                ],
+                [
+                    remote(half(ref, 0, 1), half(ref, 2, 0), gather_sems, kind + 2, near_x),
+                    remote(half(ref, 0, 0), half(ref, 2, 1), gather_sems, kind + 3, near_y),
+                ],
+                [
+                    remote(half(ref, 1, 1), half(ref, 3, 1), gather_sems, kind + 4, near_x),
+                    remote(half(ref, 1, 0), half(ref, 3, 0), gather_sems, kind + 5, near_y),
+                ],
+            )
+
+        row_sends = gather(rows, 0)
+        grad_sends = gather(grads, 6)
+
+        begin(gated_sends)
+        begin([keep_gated])
+        lax.fori_loop(0, slices * quarters, start_slice, 0)
+        begin(load_grads)
+        begin([load_hidden])
+        finish(load_grads)
+        begin(grad_sends[1])
+        finish([keep_gated, load_hidden])
+        lax.fori_loop(0, slices * quarters, wait_slice, 0)
+        finish(gated_sends)
+        for j in range(width // wide_tile):
+            at = slice(j * wide_tile, (j + 1) * wide_tile)
+            middle_ref[:, at] = straight(gated_ref[...], w_in[:, at])
+        begin(weights)
+
+        def second_norm(i, carry, at):
+            here = pl.ds(pl.multiple_of(at * HALF + i * 32, 32), 32)
+            middle = hidden_ref[here, :].astype(jnp.float32) + live_ref[here, :1] * middle_ref[here, :]
+            middle_ref[here, :] = middle
+            rows[0, here, :] = row_norm(middle).astype(low)
+            return carry
+
+        for at in range(2):
+            lax.fori_loop(0, HALF // 32, functools.partial(second_norm, at=at), 0)
+            row_sends[0][at].start()
+        begin(row_sends[1])
+        begin(grad_sends[2])
+        store_middle = pltpu.make_async_copy(middle_ref, middle_out, done_sems.at[0])
+        store_middle.start()
 
         def products(at, first, second, part_a, part_b, grad_act):
             act[:, at] = (part_a * part_b).astype(low)
             parts[:, first] = (grad_act * part_b).astype(low)
             parts[:, second] = (grad_act * part_a).astype(low)
 
-        def ready(at):
-            if at + 2 < len(queue):
-                begin(queue[at + 2])
-            finish(queue[at])
-
-        for which, (start, size) in enumerate(cuts):
-            at, second = slice(start, start + size), slice(main + start, main + start + size)
-            ready(3 * which)
-            part_a = straight(rows[...], w_in[:, at])
-            ready(3 * which + 1)
-            part_b = straight(rows[...], w_in[:, second])
-            ready(3 * which + 2)
-            if which == 0:
-                begin(stores)
-            grad_act = across(grads[...], w_out[at, :])
-            products(at, at, second, part_a, part_b, grad_act)
-        finish(weights[2])
-        if tail:
-            both = straight(rows[...], w_in[:, 2 * main :])
-            grad_act = across(grads[...], w_out[main:, :])
-            products(
-                slice(main, units),
-                slice(2 * main, 2 * main + tail),
-                slice(2 * main + tail, 2 * units),
-                both[:, :tail],
-                both[:, tail:],
-                grad_act,
-            )
-        more = [
-            pltpu.make_async_copy(act, act_out.at[spot, :], done_sems.at[2]),
-            pltpu.make_async_copy(parts, parts_out.at[spot, :], done_sems.at[3]),
-        ]
-        begin(more)
-        stores += more
+        def sum_stores(piece, j):
+            tile = pl.ds(j * wide_tile, wide_tile)
+            return [
+                pltpu.make_async_copy(
+                    sums.at[at, :, tile],
+                    (back_out, two_out)[at // 2].at[
+                        pl.ds(pl.multiple_of(piece * PIECE + (at % 2) * HALF, HALF), HALF), tile
+                    ],
+                    sum_sems.at[j, at],
+                )
+                for at in range(4)
+            ]
+
+        def work(piece, carry):
+            spot = pl.ds(pl.multiple_of(piece * PIECE, PIECE), PIECE)
+            arrived, arrived_grads = rows.at[piece], grads.at[piece]
+
+            @pl.when(piece == 1)
+            def _():
+                finish(row_sends[0])
+                begin(row_sends[2])
+
+            @pl.when(piece == 2)
+            def _():
+                finish(row_sends[1])
+                finish(grad_sends[1])
+
+            @pl.when(piece == 3)
+            def _():
+                finish(row_sends[2])
+                finish(grad_sends[2])
+
+            stores = [
+                pltpu.make_async_copy(arrived, rows_out.at[spot, :], done_sems.at[1]),
+                pltpu.make_async_copy(arrived_grads, grads_out.at[spot, :], done_sems.at[2]),
+            ]
+            begin(stores)
+            for which, (start, size) in enumerate(cuts):
+                at, second = slice(start, start + size), slice(main + start, main + start + size)
+
+                @pl.when(piece == 0)
+                def _(which=which):
+                    finish(weights[3 * which : 3 * which + 3])
+
+                part_a = straight(arrived[...], w_in[:, at])
+                part_b = straight(arrived[...], w_in[:, second])
+                grad_act = across(arrived_grads[...], w_out[at, :])
+                products(at, at, second, part_a, part_b, grad_act)
+
+            @pl.when(piece == 0)
+            def _():
+                finish(weights[6:])
+
+            if tail:
+                both = straight(arrived[...], w_in[:, 2 * main :])
+                grad_act = across(arrived_grads[...], w_out[main:, :])
+                products(
+                    slice(main, units),
+                    slice(2 * main, 2 * main + tail),
+                    slice(2 * main + tail, 2 * units),
+                    both[:, :tail],
+                    both[:, tail:],
+                    grad_act,
+                )
+            stores += [
+                pltpu.make_async_copy(act, act_out.at[spot, :], done_sems.at[3]),
+                pltpu.make_async_copy(parts, parts_out.at[spot, :], done_sems.at[4]),
+            ]
+            begin(stores[2:])
+            for j in range(width // wide_tile):
+                at = slice(j * wide_tile, (j + 1) * wide_tile)
+
+                @pl.when(piece > 0)
+                def _(j=j):
+                    finish(sum_stores(piece - 1, j))
+
+                back = across(parts[...], w_in[at, :])
+                sums[0, :, at] = back[:HALF].astype(low)
+                sums[1, :, at] = back[HALF:].astype(low)
+                two = straight(act[...], w_out[:, at])
+                sums[2, :, at] = two[:HALF].astype(low)
+                sums[3, :, at] = two[HALF:].astype(low)
+                begin(sum_stores(piece, j))
+            finish(stores)
+            return carry
+
+        lax.fori_loop(0, pieces, work, 0)
         for j in range(width // wide_tile):
-            at = slice(j * wide_tile, (j + 1) * wide_tile)
-            back = across(parts[...], w_in[at, :])
-            sums[0, :, at] = back[:HALF].astype(low)
-            sums[1, :, at] = back[HALF:].astype(low)
-            two = straight(act[...], w_out[:, at])
-            sums[2, :, at] = two[:HALF].astype(low)
-            sums[3, :, at] = two[HALF:].astype(low)
-            tile = pl.ds(j * wide_tile, wide_tile)
-            now = [
-                pltpu.make_async_copy(
-                    sums.at[at_out, :, tile], sum_outs[at_out].at[:, tile], sum_sems.at[j, at_out]
-                )
-                for at_out in range(4)
-            ]
-            begin(now)
-            stores += now
-        finish(stores)
+            finish(sum_stores(pieces - 1, j))
+        store_middle.wait()
 
     return pl.pallas_call(
         body,
-        in_specs=any_specs(6 + len(kept)),
-        out_specs=any_specs(8),
+        in_specs=any_specs(7) + [pl.BlockSpec(memory_space=pltpu.VMEM)],
+        out_specs=any_specs(7),
         out_shape=[
+            jax.ShapeDtypeStruct((local_rows, width), jnp.float32),
             jax.ShapeDtypeStruct((group_rows, width), low),
             jax.ShapeDtypeStruct((group_rows, width), low),
             jax.ShapeDtypeStruct((group_rows, units), low),
             jax.ShapeDtypeStruct((group_rows, 2 * units), low),
-        ]
-        + [jax.ShapeDtypeStruct((HALF, width), low)] * 4,
+            jax.ShapeDtypeStruct((group_rows, width), low),
+            jax.ShapeDtypeStruct((group_rows, width), low),
+        ],
         scratch_shapes=[
-            pltpu.VMEM((PIECE, width), low),
-            pltpu.VMEM((PIECE, width), low),
+            pltpu.VMEM((local_rows, quarters * deep), low),
+            pltpu.VMEM((local_rows, width), low),
+            pltpu.VMEM((local_rows, width), jnp.float32),
+            pltpu.VMEM((pieces, PIECE, width), low),
+            pltpu.VMEM((pieces, PIECE, width), low),
+            pltpu.VMEM((4, HALF, width), low),
             pltpu.VMEM((width, 2 * units), low),
             pltpu.VMEM((units, width), low),
             pltpu.VMEM((PIECE, units), low),
             pltpu.VMEM((PIECE, 2 * units), low),
-            pltpu.VMEM((4, HALF, width), low),
             pltpu.SemaphoreType.DMA((4,)),
-            pltpu.SemaphoreType.DMA((3, 3)),
-            pltpu.SemaphoreType.DMA((4,)),
+            pltpu.SemaphoreType.DMA((slices * quarters,)),
+            pltpu.SemaphoreType.DMA((9,)),
+            pltpu.SemaphoreType.DMA((5,)),
             pltpu.SemaphoreType.DMA((width // wide_tile, 4)),
+            pltpu.SemaphoreType.DMA((6, 2)),
+            pltpu.SemaphoreType.DMA((12, 2)),
         ],
-        input_output_aliases={6 + at: at for at in range(len(kept))},
-        compiler_params=pltpu.CompilerParams(vmem_limit_bytes=VMEM),
-        cost_estimate=cost(12 * PIECE * width * units, 6 * width * units + 12e6),
+        compiler_params=pltpu.CompilerParams(
+            vmem_limit_bytes=VMEM, collective_id=3, has_side_effects=True
+        ),
+        cost_estimate=cost(12 * group_rows * width * units, 90e6),
         name="gated_unit",
-    )(*pair, *grad_pair, ffn_in, ffn_out, *kept)
-
-
-def live_rows(cotangent, live, after):
-    width = cotangent.shape[1]
-
-    def body(cot_ref, live_ref, *refs):
-        for half, out_ref in enumerate(refs[len(after) :]):
-            rows = pl.ds(half * HALF, HALF)
-            product = cot_ref[rows, :].astype(jnp.float32) * live_ref[rows, :1]
-            out_ref[...] = product.astype(jnp.bfloat16)
-
+    )(gated, whole_weight, hidden, grads_own, grads_first, ffn_in, ffn_out, live)
+
+
+def mix_rows(hidden, cotangent, mix_weight, out_weight, live, keep):
+    local_rows, width = hidden.shape
+    parts, _, columns = mix_weight.shape
+    heads = columns // HS
+    group_rows = NBLK * BLK
+    pieces = group_rows // PIECE
+    wide_size = lax.axis_size("wide")
+    slice_rows = columns // wide_size
+    low = jnp.bfloat16
+    joined = 2
+    halves_at = (pl.ds(0, HALF), pl.ds(HALF, HALF))
+
+    def body(*refs):
+        hidden_in, cot_in, mix_in, out_in, live_ref, keep_ref = refs[:6]
+        rows_out, parts_out, gated_out, mixing_out, states_out, grads_out, first_out, whole_out = refs[6:14]
+        hidden_ref, cot_ref, rows, weights, parts_ref, gated_ref, mixing_ref, states_ref = refs[14:22]
+        load_sems, mix_sems, store_sems, parts_sems, gather_sems, slice_sems, line_sems, core_sems = refs[22:]
+        wide, narrow, z, core, mate, near_x, near_y = neighbours()
+        far = (wide, 3 - narrow)
+        above, below = (wide + 2, narrow), (wide - 2, narrow)
+        barrier = pltpu.get_barrier_semaphore()
+
+        def greet(place):
+            pl.semaphore_signal(barrier, inc=1, device_id=place, device_id_type=MESH)
+
+        load_hidden = pltpu.make_async_copy(hidden_in, hidden_ref, load_sems.at[0])
+        load_cot = pltpu.make_async_copy(cot_in, cot_ref, load_sems.at[1])
+        mix_loads = [
+            pltpu.make_async_copy(
+                mix_in.at[c], weights.at[:, pl.ds(c * columns, columns)], mix_sems.at[c]
+            )
+            for c in range(parts)
+        ]
+        load_hidden.start()
+        for place in (near_x, near_y, far, mate):
+            greet(place)
+        pl.when(z < 3)(lambda: greet(above))
+        pl.when(z > 0)(lambda: greet(below))
+        middle = (z == 1) | (z == 2)
+        pl.when(middle)(lambda: pl.semaphore_wait(barrier, 6))
+        pl.when(jnp.logical_not(middle))(lambda: pl.semaphore_wait(barrier, 5))
+
+        def remote(src, dst, sems, kind, place):
+            return pltpu.make_async_remote_copy(
+                src_ref=src,
+                dst_ref=dst,
+                send_sem=sems.at[kind, 0],
+                recv_sem=sems.at[kind, 1],
+                device_id=place,
+                device_id_type=MESH,
+            )
+
+        slice_at = out_in.at[pl.ds(pl.multiple_of(wide * slice_rows, slice_rows), slice_rows)]
+        keep_slice = pltpu.make_async_copy(slice_at, whole_out.at[wide, narrow], load_sems.at[2])
+        slice_sends = [
+            remote(slice_at, whole_out.at[wide, narrow], slice_sems, at, place)
+            for at, place in enumerate((far, near_x, near_y))
+        ]
+
+        def up(hop):
+            return remote(
+                whole_out.at[wide - 2 * (hop - 1)], whole_out.at[wide - 2 * (hop - 1)], line_sems, hop - 1, above
+            )
+
+        def down_line(hop):
+            return remote(
+                whole_out.at[wide + 2 * (hop - 1)], whole_out.at[wide + 2 * (hop - 1)], line_sems, 2 + hop, below
+            )
+
+        def to_mate(hop, sign):
+            at = wide + sign * 2 * hop
+            return remote(whole_out.at[at], whole_out.at[at], core_sems, 3 + sign * hop, mate)
+
+        def send_hop(hop):
+            pl.when((z < 3) & (z >= hop - 1))(lambda: up(hop).start())
+            pl.when((z > 0) & (z + hop - 1 <= 3))(lambda: down_line(hop).start())
+
+        def take_hop(hop):
+            @pl.when(z >= hop)
+            def _():
+                up(hop).wait_recv()
+                to_mate(hop, -1).start()
+
+            @pl.when(z + hop <= 3)
+            def _():
+                down_line(hop).wait_recv()
+                to_mate(hop, 1).start()
+
+        def end_hop(hop):
+            pl.when((z < 3) & (z >= hop - 1))(lambda: up(hop).wait_send())
+            pl.when((z > 0) & (z + hop - 1 <= 3))(lambda: down_line(hop).wait_send())
+            pl.when(z >= hop)(lambda: to_mate(hop, -1).wait())
+            pl.when(z + hop <= 3)(lambda: to_mate(hop, 1).wait())
+
+        begin(slice_sends)
+        keep_slice.start()
+
+        def half(piece, at):
+            return rows.at[piece, halves_at[at]]
+
+        row_sends = (
+            [remote(half(0, 0), half(1, 0), gather_sems, 0, near_x), remote(half(0, 1), half(1, 1), gather_sems, 1, near_y)],
+            [remote(half(0, 1), half(2, 0), gather_sems, 2, near_x), remote(half(0, 0), half(2, 1), gather_sems, 3, near_y)],
+            [remote(half(1, 1), half(3, 1), gather_sems, 4, near_x), remote(half(1, 0), half(3, 0), gather_sems, 5, near_y)],
+        )
+        grad_sends = [
+            remote(cot_ref.at[halves_at[0]], first_out.at[halves_at[0]], gather_sems, 6, near_x),
+            remote(cot_ref.at[halves_at[1]], first_out.at[halves_at[1]], gather_sems, 7, near_y),
+        ]
+        load_hidden.wait()
+        begin(mix_loads)
+        load_cot.start()
+
+        def first_norm(i, carry):
+            at = pl.ds(pl.multiple_of(i * 32, 32), 32)
+            rows[0, at, :] = row_norm(hidden_ref[at, :].astype(jnp.float32)).astype(low)
+            return carry
+
+        for at in range(2):
+            lax.fori_loop(at * HALF // 32, (at + 1) * HALF // 32, first_norm, 0)
+            row_sends[0][at].start()
+        begin(row_sends[1])
+
+        def row_store(piece):
+            at = pl.ds(piece * PIECE, PIECE)
+            return pltpu.make_async_copy(rows.at[piece], rows_out.at[at, :], store_sems.at[piece])
+
+        def part_stores(piece):
+            at = pl.ds(piece * PIECE, PIECE)
+            return [
+                pltpu.make_async_copy(
+                    parts_ref.at[at, pl.ds(c * columns, columns)], parts_out.at[c, at, :], parts_sems.at[piece, c]
+                )
+                for c in range(parts)
+            ]
+
+        def project(piece):
+            row_store(piece).start()
+            for c in range(0, parts, joined):
+                if piece == 0:
+                    finish(mix_loads[c : c + joined])
+                at = slice(c * columns, (c + joined) * columns)
+                result = straight(rows[piece], weights[:, at]).astype(low)
+                parts_ref[piece * PIECE : (piece + 1) * PIECE, at] = result
+            begin(part_stores(piece))
+
+        project(0)
+        load_cot.wait()
+
+        def live_cot(i, carry):
+            at = pl.ds(pl.multiple_of(i * 32, 32), 32)
+            cot_ref[at, :] = (live_ref[at, :1] * cot_ref[at, :].astype(jnp.float32)).astype(low)
+            return carry
+
+        keep_slice.wait()
+        finish(slice_sends)
+        to_mate(0, 1).start()
+        send_hop(1)
+        lax.fori_loop(0, local_rows // 32, live_cot, 0)
+        store_grads = pltpu.make_async_copy(cot_ref, grads_out, load_sems.at[3])
+        store_grads.start()
+        finish(row_sends[0])
+        begin(row_sends[2])
+        begin(grad_sends)
+        project(1)
+        take_hop(1)
+        send_hop(2)
+        finish(row_sends[1])
+        project(2)
+        take_hop(2)
+        send_hop(3)
+        finish(row_sends[2])
+        project(3)
+
+        def slot_of(block):
+            off_x = (block // 2 % 2 + narrow % 2) % 2
+            off_y = (block // 4 + narrow // 2) % 2
+            if block % 2:
+                return 1 + 3 * off_x + 2 * off_y + off_x * off_y
+            return 2 * off_x + 5 * off_y - off_x * off_y
+
+        def attend(head, carry):
+            head_id = (heads * narrow + head).astype(jnp.float32)
+            rate = jnp.exp(jnp.full((1, 1), -0.5 * math.log(2.0), jnp.float32) * (head_id + 1.0))
+            within, entry, leave, whole = block_decays(rate)
+            state = jnp.zeros((HS, HS), jnp.float32)
+
+            def part(c, rows_at):
+                at = pl.ds(pl.multiple_of(c * columns + head * HS, HS), HS)
+                return parts_ref[rows_at, at]
+
+            for block in range(NBLK):
+                rows_at = pl.ds(pl.multiple_of(slot_of(block) * BLK, BLK), BLK)
+                queries = jax.nn.silu(part(0, rows_at).astype(jnp.float32)).astype(low)
+                keys = jax.nn.silu(part(1, rows_at).astype(jnp.float32)).astype(low)
+                values = part(2, rows_at)
+                gate = part(3, rows_at).astype(jnp.float32)
+                state = keep_ref[block : block + 1, :] * state
+                state_low = state.astype(low)
+                states_ref[head, block] = state_low
+                scores = (across(queries, keys) * within).astype(low)
+                mixing = straight(scores, values) + entry * straight(queries, state_low)
+                late_keys = (keys.astype(jnp.float32) * leave).astype(low)
+                state = whole * state + down(late_keys, values)
+                scale = lax.rsqrt(jnp.mean(mixing * mixing, axis=-1, keepdims=True) + head_floor)
+                at = pl.ds(pl.multiple_of(head * HS, HS), HS)
+                gated_ref[rows_at, at] = (mixing * scale * gate).astype(low)
+                mixing_ref[rows_at, at] = mixing.astype(low)
+            return carry
+
+        lax.fori_loop(0, heads // 2, attend, 0)
+        take_hop(3)
+        lax.fori_loop(heads // 2, heads, attend, 0)
+        stores = [
+            pltpu.make_async_copy(gated_ref, gated_out.at[0], load_sems.at[4]),
+            pltpu.make_async_copy(mixing_ref, mixing_out, load_sems.at[5]),
+            pltpu.make_async_copy(states_ref, states_out, load_sems.at[6]),
+        ]
+        begin(stores)
+        to_mate(0, 1).wait()
+        for hop in range(1, 4):
+            end_hop(hop)
+        finish(grad_sends)
+        store_grads.wait()
+        for piece in range(pieces):
+            row_store(piece).wait()
+            finish(part_stores(piece))
+        finish(stores)
+
+    low_shape = functools.partial(jax.ShapeDtypeStruct, dtype=low)
     return pl.pallas_call(
         body,
-        in_specs=[pl.BlockSpec(memory_space=pltpu.VMEM)] * 2 + any_specs(len(after)),
-        out_specs=[pl.BlockSpec(memory_space=pltpu.VMEM)] * 2,
-        out_shape=[jax.ShapeDtypeStruct((HALF, width), jnp.bfloat16)] * 2,
-        compiler_params=pltpu.CompilerParams(vmem_limit_bytes=VMEM),
-        cost_estimate=cost(2e6, 4e6),
-        name="live_rows",
-    )(cotangent, live, *after)
-
-
-def finish_rows(mix_low, out_low, hidden, middle, grad_middle, live, normed_terms, two_terms):
+        in_specs=any_specs(4) + [pl.BlockSpec(memory_space=pltpu.VMEM)] * 2,
+        out_specs=any_specs(8),
+        out_shape=[
+            low_shape((group_rows, width)),
+            low_shape((parts, group_rows, columns)),
+            low_shape((1, group_rows, columns)),
+            low_shape((group_rows, columns)),
+            low_shape((heads, NBLK, HS, HS)),
+            low_shape((local_rows, width)),
+            low_shape((local_rows, width)),
+            low_shape((wide_size, pieces, slice_rows, width)),
+        ],
+        scratch_shapes=[
+            pltpu.VMEM((local_rows, width), low),
+            pltpu.VMEM((local_rows, width), low),
+            pltpu.VMEM((pieces, PIECE, width), low),
+            pltpu.VMEM((width, parts * columns), low),
+            pltpu.VMEM((group_rows, parts * columns), low),
+            pltpu.VMEM((group_rows, columns), low),
+            pltpu.VMEM((group_rows, columns), low),
+            pltpu.VMEM((heads, NBLK, HS, HS), low),
+            pltpu.SemaphoreType.DMA((7,)),
+            pltpu.SemaphoreType.DMA((parts,)),
+            pltpu.SemaphoreType.DMA((pieces,)),
+            pltpu.SemaphoreType.DMA((pieces, parts)),
+            pltpu.SemaphoreType.DMA((8, 2)),
+            pltpu.SemaphoreType.DMA((3, 2)),
+            pltpu.SemaphoreType.DMA((6, 2)),
+            pltpu.SemaphoreType.DMA((7, 2)),
+        ],
+        compiler_params=pltpu.CompilerParams(
+            vmem_limit_bytes=VMEM, collective_id=4, has_side_effects=True
+        ),
+        cost_estimate=cost(2 * group_rows * parts * width * columns, 50e6),
+        name="mix_rows",
+    )(hidden, cotangent, mix_weight, out_weight, live, keep)
+
+
+def finish_rows(mix_low, out_low, hidden, middle, grad_middle, live, normed_terms, two_sums, two_terms):
     parts, width, columns = mix_low.shape
     local_rows = hidden.shape[0]
     tile = local_rows // parts
@@ -1291,7 +1512,7 @@
     half_steps = parts // 2
     terms = len(normed_terms) + len(two_terms)
 
-    def body(mix_ref, out_ref, hidden_ref, middle_ref, grad_ref, live_ref, *refs):
+    def body(mix_ref, out_ref, hidden_ref, middle_ref, grad_ref, live_ref, own_ref, *refs):
         term_refs = refs[:terms]
         mix_out, out_out, layer_ref, input_ref = refs[terms:]
         mix_out[...] = mix_ref[...].astype(jnp.float32)
@@ -1299,7 +1520,7 @@
 
         def rows_of(half):
             normed = add_rows(*(ref[...] for ref in term_refs[3 * half : 3 * half + 3]))
-            two = add_rows(*(ref[...] for ref in term_refs[6 + 3 * half : 9 + 3 * half]))
+            two = add_rows(*(ref[...] for ref in term_refs[6 + 2 * half : 8 + 2 * half]), own_ref[...])
             layer = middle_ref[...] + live_ref[...] * two
             layer_ref[...] = layer.astype(jnp.bfloat16)
             back = norm_back(hidden_ref[...].astype(jnp.float32), normed)
@@ -1317,13 +1538,15 @@
             return pl.BlockSpec((tile, width), lambda i: (jnp.minimum(i, half_steps - 1), 0))
         return pl.BlockSpec((tile, width), lambda i: (jnp.maximum(i - half_steps, 0), 0))
 
-    term_specs = ([half_spec(0)] * 3 + [half_spec(1)] * 3) * 2
+    term_specs = [half_spec(0)] * 3 + [half_spec(1)] * 3 + [half_spec(0)] * 2 + [half_spec(1)] * 2
     mix_spec = pl.BlockSpec((1, width, columns), lambda i: (i, 0, 0))
     out_spec = pl.BlockSpec((out_tile, out_low.shape[1]), lambda i: (i, 0))
     return pl.pallas_call(
         body,
         grid=(parts,),
-        in_specs=[mix_spec, out_spec, rows_spec(width), rows_spec(width), rows_spec(width), rows_spec(1)]
+        in_specs=[mix_spec, out_spec]
+        + [rows_spec(width)] * 3
+        + [rows_spec(1), rows_spec(width)]
         + term_specs,
         out_specs=[mix_spec, out_spec, rows_spec(width), rows_spec(width)],
         out_shape=[
@@ -1335,7 +1558,7 @@
         compiler_params=pltpu.CompilerParams(vmem_limit_bytes=VMEM),
         cost_estimate=cost(1e8, 60e6),
         name="finish_rows",
-    )(mix_low, out_low, hidden, middle, grad_middle, live, *normed_terms, *two_terms)
+    )(mix_low, out_low, hidden, middle, grad_middle, live, two_sums, *normed_terms, *two_terms)
 
 
 def block_decays(rate):
@@ -1346,56 +1569,8 @@
     place = lax.broadcasted_iota(jnp.int32, (BLK, 1), 0).astype(jnp.float32)
     entry = jnp.exp(-rate * (place + 1.0))
     leave = jnp.exp(-rate * (BLK - 1.0 - place))
-    whole = jnp.exp(jnp.full((1, HS), -BLK * rate, jnp.float32))
+    whole = jnp.exp(-BLK * rate * jnp.ones((1, HS), jnp.float32))
     return within, entry, leave, whole
-
-
-def mix_forward(slots, fresh, rates, parts):
-    _, group_rows, columns = parts.shape
-    heads = columns // HS
-    low = jnp.bfloat16
-
-    def body(slot_ref, fresh_ref, rate_ref, parts_ref, gated_ref, mixing_ref, states_ref):
-        within, entry, leave, whole = block_decays(rate_ref[pl.program_id(0)])
-        state = jnp.zeros((HS, HS), jnp.float32)
-        for block in range(NBLK):
-            rows = pl.ds(pl.multiple_of(slot_ref[block] * BLK, BLK), BLK)
-            queries = jax.nn.silu(parts_ref[0, rows, :].astype(jnp.float32)).astype(low)
-            keys = jax.nn.silu(parts_ref[1, rows, :].astype(jnp.float32))
-            values = parts_ref[2, rows, :]
-            gate = parts_ref[3, rows, :].astype(jnp.float32)
-            state = jnp.where(fresh_ref[block] != 0, 0.0, state)
-            state_low = state.astype(low)
-            states_ref[0, block] = state_low
-            weights = (across(queries, keys.astype(low)) * within).astype(low)
-            mixing = straight(weights, values) + entry * straight(queries, state_low)
-            late_keys = (keys.astype(low).astype(jnp.float32) * leave).astype(low)
-            state = whole * state + down(late_keys, values)
-            scale = lax.rsqrt(jnp.mean(mixing * mixing, axis=-1, keepdims=True) + head_floor)
-            gated_ref[0, rows, :] = (mixing * scale * gate).astype(low)
-            mixing_ref[rows, :] = mixing.astype(low)
-
-    return pl.pallas_call(
-        body,
-        grid_spec=pltpu.PrefetchScalarGridSpec(
-            num_scalar_prefetch=3,
-            grid=(heads,),
-            in_specs=[pl.BlockSpec((4, group_rows, HS), lambda h, *_: (0, 0, h))],
-            out_specs=[
-                pl.BlockSpec((1, group_rows, HS), lambda h, *_: (0, 0, h)),
-                pl.BlockSpec((group_rows, HS), lambda h, *_: (0, h)),
-                pl.BlockSpec((1, NBLK, HS, HS), lambda h, *_: (h, 0, 0, 0)),
-            ],
-        ),
-        out_shape=[
-            jax.ShapeDtypeStruct((1, group_rows, columns), low),
-            jax.ShapeDtypeStruct((group_rows, columns), low),
-            jax.ShapeDtypeStruct((heads, NBLK, HS, HS), low),
-        ],
-        compiler_params=pltpu.CompilerParams(vmem_limit_bytes=VMEM),
-        cost_estimate=cost(8e9, 14e6),
-        name="mix_forward",
-    )(slots, fresh, rates, parts)
 
 
 def mix_backward(slots, fresh, rates, parts, mixing_all, states, grad_gated, in_low, out_low):
@@ -1509,40 +1684,20 @@
     slots, fresh = slot_tables(narrow_index, fresh_block)
     low = jnp.bfloat16
 
-    def halves(rows):
-        return rows[:HALF], rows[HALF:]
-
-    lives = halves(live)
-    inputs = [rows.astype(jnp.float32) for rows in halves(hidden)]
-
-    pieces = gather_pieces(*(row_norm(rows).astype(low) for rows in inputs))
-    kept = ()
-    for at, pair in enumerate(pieces):
-        kept = project_piece(pair, mix_weight, kept, at)
-    normed_all, parts = kept
-    grad_pieces = gather_pieces(*live_rows(cotangent, live, pieces[3]))
-
-    gated, mixing, states = mix_forward(slots, fresh, rates, parts)
-    far_top, far_low, near_top, near_low = partial_sums(gated, out_weight[None], (3, 1), False)
-    side_low, side_top, own_top, own_low = partial_sums(
-        gated, out_weight[None], (2, 0), False, after=grad_pieces[1] + grad_pieces[2]
-    )
-    branch = scatter_pieces(
-        (own_top, own_low), (near_top, near_low), (side_low, side_top), (far_top, far_low)
-    )
-    middle = [x + m * b for x, m, b in zip(inputs, lives, branch)]
-
-    pieces = gather_pieces(*(row_norm(rows).astype(low) for rows in middle))
-    kept, back_sums, two_sums = (), [], []
-    for at, (pair, grad_pair) in enumerate(zip(pieces, grad_pieces)):
-        *kept, back_top, back_low, two_top, two_low = unit_piece(
-            pair, grad_pair, ffn_in_weight, ffn_out_weight, kept, at
-        )
-        back_sums += [back_top, back_low]
-        two_sums += [two_top, two_low]
-    normed_two_all, grad_two_all, act, grad_parts = kept
-
-    middle = jnp.concatenate(middle)
+    keep = jnp.broadcast_to(jnp.where(fresh_block, 0.0, 1.0)[:, None], (NBLK, HS))
+    normed_all, parts, gated, mixing, states, grads_own, grads_first, whole_weight = mix_rows(
+        hidden, cotangent, mix_weight, out_weight, live, keep
+    )
+    middle, normed_two_all, grad_two_all, act, grad_parts, back_sums, two_sums = gated_unit(
+        gated,
+        whole_weight,
+        hidden,
+        live,
+        grads_own,
+        grads_first,
+        ffn_in_weight,
+        ffn_out_weight,
+    )
     out_low, in_low, grad_branch_all, grad_middle, grad_gated = unit_grads(
         act,
         grad_two_all,
@@ -1566,7 +1721,7 @@
         out_low.reshape(units, width),
     )
     out_low, mix_low, own_top, own_low, *terms = mix_grads(
-        gated, grad_branch_all, normed_all, grad_projected, mix_weight, two_sums[2:]
+        gated, grad_branch_all, normed_all, grad_projected, mix_weight, two_sums
     )
     grad_mix, grad_out, layer_out, input_grad = finish_rows(
         mix_low.reshape(mix_weight.shape),
@@ -1576,7 +1731,8 @@
         grad_middle,
         live,
         (own_top, terms[0], terms[2], own_low, terms[1], terms[3]),
-        (two_sums[0], terms[4], terms[6], two_sums[1], terms[5], terms[7]),
+        two_sums,
+        (terms[4], terms[6], terms[5], terms[7]),
     )
     return (layer_out, input_grad, grad_mix, grad_out, grad_ffn_in, grad_ffn_out)
 

time: 787 us -> 730 us (0.928)
  waiting for transfers between devices: 119 us -> 0 us
  Pallas kernels: 609 us -> 708 us
  starting transfers between devices: 26.8 us -> 0 us
  other arithmetic: 17.7 us -> 6.9 us
    ppermute x24 -> x0, waiting for transfers between devices: 119 us -> none  [the longest x12 82.2 us: over_x(): return lax.ppermute(rows, 'narrow', [(at, at ^ 1) for at in range(4)])]
    pallas_call x15 -> x5, Pallas kernels: 580 us -> 679 us  [the longest x1 224 us: unit_grads(): pl.pallas_call(body, in_specs=any_specs(8) + [pl.BlockSpec(memory_space=p...]
    ppermute x24 -> x0, starting transfers between devices: 26.8 us -> none  [the longest x12 13.8 us: over_x(): return lax.ppermute(rows, 'narrow', [(at, at ^ 1) for at in range(4)])]
  transfers between devices with their start and end apart: 24 -> 0, of which waited for: 10 -> 0; matrix products, arithmetic and copies ran while one was open for 2% -> 0% of each run, Pallas kernels for 19% -> 0%
where the time goes in v4:
time: 730 us; the launch traced here: 721 us
  Pallas kernels  708 us (97%)
    pallas_call x1, Pallas kernels, unit_grads(): pl.pallas_call(body, in_specs=any_specs(8) + [pl.BlockSpec(memory_space=p...  224 us
    pallas_call x1, Pallas kernels, gated_unit(): pl.pallas_call(body, in_specs=any_specs(7) + [pl.BlockSpec(memory_space=p...  170 us
    pallas_call x1, Pallas kernels, mix_grads(): pl.pallas_call(body, in_specs=any_specs(6), out_specs=any_specs(12), out_...  156 us
    pallas_call x1, Pallas kernels, mix_rows(): pl.pallas_call(body, in_specs=any_specs(4) + [pl.BlockSpec(memory_space=p...  108 us
    pallas_call x1, Pallas kernels, mix_backward(): pl.pallas_call(body, grid_spec=pltpu.PrefetchScalarGridSpec(num_scalar_pr...  29 us
    pallas_call x1, Pallas kernels, finish_rows(): pl.pallas_call(body, grid=(parts,), in_specs=[mix_spec, out_spec] + [rows...  19.4 us

profile of v4, /device:TPU:0, one launch (start us, length us, event | category | flops | bytes accessed | tf_op | source)
XLA Modules:
  0.0 721.1 jit_solution(16016612744694253849)
XLA Ops:
  0.7 0.6 multiply_power_fusion.rate_ref
  1.2 1.3 fusion.4
  2.6 1.9 convert_reduce_fusion
  4.5 1.9 subtract_multiply_fusion
  6.4 1.2 fusion.2.fresh_ref
  7.6 0.6 fusion.3
  8.3 1.3 gather_fusion.1
  9.6 1.3 gather_fusion
  10.9 0.5 compare_select_fusion.1.slot_ref
  11.4 0.7 broadcast_in_dim.40.refs_5_
  12.1 0.1 convert_bitcast_fusion
  12.1 0.1 dynamic_slice.3
  12.2 0.9 copy.16.refs_4_.refs_7_.refs_8_.live_ref
  13.1 108.1 %mix_rows.1 = (bf16[2048,2048]{1,0:T(8,128)(2,1)}, bf16[4,2048,512]{2,1,0:T(8,128)(2,1)}, bf16[1,2048,512]{2,1,0:T(8,128)(2,1)}, bf16[2048,512]{1,0:T(8,128)(2,1...) custom-call(bf16[512,2048]{1,0:T(8,128)(2,1)} %hidden_ref.1, ...), custom_call_target="tpu_custom_call" | custom-call | flops 17179869184 | bytes 50000000 | tf_op jit(solution)/shard_map/mix_rows/pallas_call | solution.py:1467
  121.3 170.2 %gated_unit.1 = (f32[512,2048]{1,0:T(8,128)}, bf16[2048,2048]{1,0:T(8,128)(2,1)}, bf16[2048,2048]{1,0:T(8,128)(2,1)}, bf16[2048,1408]{1,0:T(8,128)(2,1)}, bf16[2...) custom-call(bf16[1,2048,512]{2,1,0:T(8,128)(2,1)} %get-tuple-element.45.refs_0_, ...), custom_call_target="tpu_custom_call" | custom-call | flops 70866960384 | bytes 90000000 | tf_op jit(solution)/shard_map/gated_unit/pallas_call | solution.py:1197
  291.5 224.5 %unit_grads.1 = (bf16[11,128,2048]{2,1,0:T(8,128)(2,1)}, bf16[16,128,2816]{2,1,0:T(8,128)(2,1)}, bf16[2048,2048]{1,0:T(8,128)(2,1)}, f32[512,2048]{1,0:T(8,128)}, bf16[2048,512]{1,0:T(8,128)(2,1)}) custom-call(bf16[2048,1408]{1,0:T(8,128)(2,1)} %get-tuple-element.49.refs_0_, bf16[2048,2048]{1,0:T(8,128)(2,1)} %get-tuple-element.50.refs_1_, ...), custom_call_target="tpu_custom_call" | custom-call | flops 35433480192 | bytes 60000000 | tf_op jit(solution)/shard_map/unit_grads/pallas_call | solution.py:746
  516.0 29.0 %mix_backward.1 = (bf16[4,2048,512]{2,1,0:T(8,128)(2,1)}, f32[2,2048,1408]{2,1,0:T(8,128)}, f32[1408,2048]{1,0:T(8,128)}) custom-call(s32[8]{0:T(128)} %compare_select_fusion.1.slot_ref, s32[8]{0:T(128)} %fusion.2.fresh_ref, f32[4]{0:T(128)} %multiply_power_fusion.rate_ref, bf16[4,2048,512]{2,1,0:T(8,128)(2,1)} %get-tuple-element.57.parts_ref, ...), custom_call_target="tpu_custom_call" | custom-call | flops 20000000000 | bytes 75000000 | tf_op jit(solution)/shard_map/mix_backward/pallas_call | solution.py:1635
  544.9 156.4 %mix_grads.1 = (bf16[4,128,2048]{2,1,0:T(8,128)(2,1)}, bf16[64,128,512]{2,1,0:T(8,128)(2,1)}, bf16[256,2048]{1,0:T(8,128)(2,1)}, bf16[256,2048]{1,0:T(8,128)(2,1...) custom-call(bf16[1,2048,512]{2,1,0:T(8,128)(2,1)} %get-tuple-element, ...), custom_call_target="tpu_custom_call" | custom-call | flops 38654705664 | bytes 60000000 | tf_op jit(solution)/shard_map/mix_grads/pallas_call | solution.py:920
  701.3 19.4 %finish_rows.1 = (f32[4,2048,512]{2,1,0:T(8,128)}, f32[512,2048]{1,0:T(8,128)}, bf16[512,2048]{1,0:T(8,128)(2,1)}, bf16[512,2048]{1,0:T(8,128)(2,1)}) custom-call(bf16[4,2048,512]{2,1,0:T(8,128)(2,1)} %bitcast.14, bf16[512,2048]{1,0:T(8,128)(2,1)} %bitcast.15, bf16[512,2048]{1,0:T(8,128)(2,1)} %hidden_ref.1, ...), custom_call_target="tpu_custom_call" | custom-call | flops 100000000 | bytes 60000000 | tf_op jit(solution)/shard_map/finish_rows/pallas_call | solution.py:1544
  (3 shorter events, 0.0 us)

commit v5 on v4

--- a/solution.py
+++ b/solution.py
@@ -267,14 +267,6 @@
     return sum(term.astype(jnp.float32) for term in terms)
 
 
-def slot_tables(narrow_index, fresh_block):
-    block_ids = jnp.arange(NBLK, dtype=jnp.int32)
-    partner = (block_ids // 2) ^ narrow_index
-    even = jnp.array([0, 2, 5, 6], jnp.int32)[partner]
-    odd = jnp.array([1, 4, 3, 7], jnp.int32)[partner]
-    return jnp.where(block_ids % 2 == 0, even, odd), fresh_block.astype(jnp.int32)
-
-
 def across(left, right):
     return lax.dot_general(left, right, (((1,), (1,)), ((), ())), preferred_element_type=jnp.float32)
 
@@ -319,6 +311,18 @@
     near_x = (wide, narrow + 1 - 2 * (narrow % 2))
     near_y = (wide, (narrow + 2) % 4)
     return wide, narrow, z, core, mate, near_x, near_y
+
+
+def slot_of(block, narrow):
+    off_x = (block // 2 % 2 + narrow % 2) % 2
+    off_y = (block // 4 + narrow // 2) % 2
+    if block % 2:
+        return 1 + 3 * off_x + 2 * off_y + off_x * off_y
+    return 2 * off_x + 5 * off_y - off_x * off_y
+
+
+def head_rate(head):
+    return jnp.exp(jnp.full((1, 1), -8.0 / HEADS * math.log(2.0), jnp.float32) * (head.astype(jnp.float32) + 1.0))
 
 
 def line_scratch():
@@ -468,8 +472,10 @@
             for copy in (cross_one(s), cross_two(s), out_one(s), out_two(s)):
                 copy.wait_send()
 
-        for condition, copy in deliveries(k, s):
-            pl.when(condition)(copy.wait)
+        for t in range(2):
+            for which, src in enumerate((full, other)):
+                ref = targets(k, 0)[0][1]
+                pltpu.make_async_copy(src.at[s, t], ref, out_sems.at[2 * t + which, s]).wait()
 
     stages = (
         (12, clear),
@@ -495,13 +501,12 @@
     return step
 
 
-def square_scratch():
-    low = jnp.bfloat16
-    block = pltpu.VMEM((2, BLK, HEADS * HS), low)
-    return [block, block, pltpu.SemaphoreType.DMA((6, 2)), pltpu.SemaphoreType.DMA((2,))]
-
-
-def square_sum(scratch, places, parts, landed):
+def square_scratch(uses):
+    block = pltpu.VMEM((2, BLK, HEADS * HS), jnp.bfloat16)
+    return [block, block, pltpu.SemaphoreType.DMA((uses, 6, 2)), pltpu.SemaphoreType.DMA((uses, 2))]
+
+
+def square_sum(scratch, places, parts, landed, use):
     met, mid, sems, load_sems = scratch
     top_x, low_y, low_x, top_y, top_d, low_d = parts
     near_x, near_y = places[5:]
@@ -510,8 +515,8 @@
         return pltpu.make_async_remote_copy(
             src_ref=src,
             dst_ref=dst,
-            send_sem=sems.at[kind, 0],
-            recv_sem=sems.at[kind, 1],
+            send_sem=sems.at[use, kind, 0],
+            recv_sem=sems.at[use, kind, 1],
             device_id=place,
             device_id_type=MESH,
         )
@@ -522,8 +527,8 @@
     loads = []
     if top_y is not None:
         loads = [
-            pltpu.make_async_copy(top_y, mid.at[0], load_sems.at[0]),
-            pltpu.make_async_copy(low_x, mid.at[1], load_sems.at[1]),
+            pltpu.make_async_copy(top_y, mid.at[0], load_sems.at[use, 0]),
+            pltpu.make_async_copy(low_x, mid.at[1], load_sems.at[use, 1]),
         ]
 
     def open_sum():
@@ -542,93 +547,214 @@
                 return carry
 
             lax.fori_loop(0, BLK // 64, tile, 0)
-            second[at].start()
+        begin(second)
 
     def close_sum():
         finish(direct)
         finish(second)
 
-    return open_sum, join_sum, close_sum, first, direct
-
-
-def unit_grads(
-    act, grad_two_all, normed_two_all, grad_parts, back_sums, middle, cotangent, live, out_weight
+    return open_sum, join_sum, close_sum
+
+
+def weight_grads(
+    act,
+    grad_two_all,
+    normed_two_all,
+    grad_parts,
+    back_sums,
+    two_sums,
+    middle,
+    cotangent,
+    out_weight,
+    mix_weight,
+    parts_all,
+    mixing_all,
+    states_all,
+    gated,
+    normed_all,
+    live,
+    keep,
 ):
     rows, units = act.shape
     width = grad_two_all.shape[1]
     local_rows = middle.shape[0]
+    parts, _, columns = parts_all.shape
+    heads = columns // HS
     low = jnp.bfloat16
-    out_blocks, in_blocks = units // SUB, width // SUB
+    in_columns = grad_parts.shape[1] // TILE
+    in_rows = width // PIECE
+    out_blocks = units // SUB
     halves = width // 1024
-    out_chunks = out_blocks * halves
-    columns = grad_parts.shape[1] // TILE
-    in_chunks = (width // PIECE) * columns
-    count = out_chunks + in_chunks
+    first_out = in_rows * in_columns
+    first_branch = first_out + halves * out_blocks
+    first_mix = first_branch + width // TILE
+    per_row = columns // TILE
+    per_part = in_rows * per_row
+    count = first_mix + parts * per_part
 
     def body(*refs):
-        act_in, two_in, normed_in, parts_in = refs[:4]
-        partial = [refs[4].at[pl.ds(at * BLK, BLK)] for at in range(8)]
-        middle_in, cot_in, weight_in, live_ref = refs[5:9]
-        out_grad, in_grad, branch_out, middle_out, gated_out = refs[9:14]
-        act_ref, shared, parts_ref, landed, own_ref, cot_ref, mid_ref, grad_ref, branch = refs[14:23]
-        gated_ref, load_sems, stage_sems, gather_sems, back_sems = refs[23:28]
-        line = refs[28:37]
-        square = refs[37:41]
+        act_in, two_in, normed_two_in, parts_in, back_in, two_sums_in = refs[:6]
+        middle_in, cot_in, weight_in, mix_in = refs[6:10]
+        all_in, mixing_in, states_in, gated_in, normed_in, live_ref, keep_ref = refs[10:17]
+        in_grad, out_grad, branch_grad, mix_grad, branch_out, middle_out = refs[17:23]
+        own_outs, last_landed, two_landed = refs[23:25], refs[25:29], refs[29:33]
+        shared, wide_ref, act_ref, landed, stage_ref, mid_ref, grad_ref, branch = refs[33:41]
+        near, gated_grad, states_ref = refs[41:44]
+        normed_sems, parts_sems, load_sems, stage_sems, gather_sems, back_sems, head_sems, mix_sems = refs[44:52]
+        tile_sems, own_sems = refs[52:54]
+        line, square = refs[54:63], refs[63:67]
+        mid = square[1]
         places = neighbours()
-        near_x, near_y = places[5:]
+        narrow, near_x, near_y = places[1], places[5], places[6]
         enter(places)
+
+        def block(at):
+            return pl.ds(at * BLK, BLK)
+
+        def cols(at, size):
+            return pl.ds(pl.multiple_of(at, 128), size)
+
+        def load_normed_two(at):
+            here = cols(at * PIECE, PIECE)
+            return pltpu.make_async_copy(normed_two_in.at[:, here], shared.at[:, here], normed_sems.at[at])
+
+        def load_parts(at):
+            here = cols(at * TILE, TILE)
+            return pltpu.make_async_copy(parts_in.at[:, here], wide_ref.at[:, here], parts_sems.at[at])
+
+        def load_half(src, half, sem):
+            here = pl.ds(half * 1024, 1024)
+            return pltpu.make_async_copy(src.at[:, here], shared.at[:, here], load_sems.at[sem])
+
         load_act = pltpu.make_async_copy(act_in, act_ref, load_sems.at[0])
-        load_two = pltpu.make_async_copy(two_in, shared, load_sems.at[1])
-        load_parts = pltpu.make_async_copy(parts_in, parts_ref, load_sems.at[2])
-        load_normed = pltpu.make_async_copy(normed_in, shared, load_sems.at[3])
-        open_sum, join_sum, close_sum, _, _ = square_sum(
-            square, places, partial[2:], [landed.at[at] for at in range(4)]
-        )
-        load_two.start()
-        load_act.start()
-        open_sum()
-        load_parts.start()
-        load_two.wait()
-        load_act.wait()
+        load_two = [load_half(two_in, half, 1 + half) for half in range(halves)]
+        load_normed = [load_half(normed_in, half, 3 + half) for half in range(halves)]
+        load_gated = pltpu.make_async_copy(gated_in.at[0], act_ref.at[:, pl.ds(0, columns)], load_sems.at[5])
+
+        def load_branch(at):
+            slot = at % 2
+            return pltpu.make_async_copy(
+                branch_out.at[:, cols(at * TILE, TILE)],
+                act_ref.at[:, cols(columns + slot * TILE, TILE)],
+                tile_sems.at[slot],
+            )
 
         def product(k, own):
-            @pl.when(k < out_chunks)
+            def split_rows(result):
+                for part in range(4):
+                    own[part] = result[part * SUB : (part + 1) * SUB]
+
+            @pl.when(k < first_out)
             def _():
-                rows_at = pl.ds(pl.multiple_of((k // halves) * SUB, SUB), SUB)
-                wide_at = pl.ds(pl.multiple_of((k % halves) * 1024, 1024), 1024)
-                result = down(act_ref[:, rows_at], shared[:, wide_at]).astype(low)
+                row, column = k // in_columns, k % in_columns
+
+                @pl.when(column == 0)
+                def _():
+                    load_normed_two(row).wait()
+
+                @pl.when(row == 0)
+                def _():
+                    load_parts(column).wait()
+
+                here, there = cols(row * PIECE, PIECE), cols(column * TILE, TILE)
+                split_rows(down(shared[:, here], wide_ref[:, there]).astype(low))
+
+                @pl.when(k == first_out - in_columns)
+                def _():
+                    load_two[0].start()
+
+            @pl.when(k == first_out)
+            def _():
+                begin(load_two[1:])
+                load_act.wait()
+                load_two[0].wait()
+
+            @pl.when(k == first_out + out_blocks)
+            def _():
+                finish(load_two[1:])
+                load_normed[0].start()
+
+            @pl.when((k >= first_out) & (k < first_branch))
+            def _():
+                at = k - first_out
+                here = cols((at % out_blocks) * SUB, SUB)
+                there = cols((at // out_blocks) * 1024, 1024)
+                result = down(act_ref[:, here], shared[:, there]).astype(low)
                 for part in range(4):
                     own[part] = result[:, part * TILE : (part + 1) * TILE]
 
-            @pl.when(k == out_chunks)
+            @pl.when(k == first_branch)
             def _():
-                load_normed.start()
-                load_parts.wait()
-                load_normed.wait()
-
-            @pl.when(k >= out_chunks)
+                load_branch(0).start()
+                load_gated.start()
+                begin(load_normed[1:])
+                load_gated.wait()
+
+            @pl.when((k >= first_branch) & (k < first_mix))
             def _():
-                at = k - out_chunks
-                rows_at = pl.ds(pl.multiple_of((at // columns) * PIECE, PIECE), PIECE)
-                wide_at = pl.ds(pl.multiple_of((at % columns) * TILE, TILE), TILE)
-                result = down(shared[:, rows_at], parts_ref[:, wide_at]).astype(low)
-                for part in range(4):
-                    own[part] = result[part * SUB : (part + 1) * SUB]
+                at = k - first_branch
+                load_branch(at).wait()
+                pl.when(k + 1 < first_mix)(lambda: load_branch(at + 1).start())
+                there = cols(columns + (at % 2) * TILE, TILE)
+                split_rows(down(act_ref[:, :columns], act_ref[:, there]).astype(low))
+
+            @pl.when(k == first_mix)
+            def _():
+                finish(load_normed)
+
+            @pl.when(k >= first_mix)
+            def _():
+                at = k - first_mix
+                here = cols(((at // per_row) % in_rows) * PIECE, PIECE)
+                there = cols((at // per_part) * columns + (at % per_row) * TILE, TILE)
+                split_rows(down(shared[:, here], wide_ref[:, there]).astype(low))
 
         def targets(k, part):
-            wide_at = pl.ds(pl.multiple_of((k % halves) * 1024 + part * TILE, TILE), TILE)
-            at = jnp.maximum(k - out_chunks, 0)
-            in_at = pl.ds(pl.multiple_of((at % columns) * TILE, TILE), TILE)
-            first = jnp.minimum(k, out_chunks - 1) // halves
+            one = jnp.minimum(k, first_out - 1)
+            two = jnp.clip(k - first_out, 0, first_branch - first_out - 1)
+            three = jnp.clip(k - first_branch, 0, first_mix - first_branch - 1)
+            four = jnp.maximum(k - first_mix, 0)
             return [
-                (k < out_chunks, out_grad.at[first, :, wide_at]),
-                (k >= out_chunks, in_grad.at[(at // columns) * 4 + part, :, in_at]),
+                (
+                    k < first_out,
+                    in_grad.at[(one // in_columns) * 4 + part, :, cols((one % in_columns) * TILE, TILE)],
+                ),
+                (
+                    (k >= first_out) & (k < first_branch),
+                    out_grad.at[two % out_blocks, :, cols((two // out_blocks) * 1024 + part * TILE, TILE)],
+                ),
+                (
+                    (k >= first_branch) & (k < first_mix),
+                    branch_grad.at[part, :, cols(three * TILE, TILE)],
+                ),
+                (
+                    k >= first_mix,
+                    mix_grad.at[(four // per_row) * 4 + part, :, cols((four % per_row) * TILE, TILE)],
+                ),
             ]
 
         step = line_sum(line, places, count, product, targets)
-
-        def block(at):
-            return pl.ds(at * BLK, BLK)
+        now = [0]
+
+        def run(steps):
+            lax.fori_loop(now[0], now[0] + steps, step, 0)
+            now[0] += steps
+
+        open_sum, join_sum, close_sum = square_sum(
+            square,
+            places,
+            [back_in.at[block(at)] for at in range(2, 8)],
+            [landed.at[at] for at in range(4)],
+            0,
+        )
+        load_normed_two(0).start()
+        load_parts(0).start()
+        open_sum()
+        for at in range(1, in_columns):
+            load_parts(at).start()
+        for at in range(1, in_rows):
+            load_normed_two(at).start()
+        load_act.start()
 
         def spread(src, slot, kind, place):
             return pltpu.make_async_remote_copy(
@@ -642,12 +768,12 @@
 
         def stage(half):
             return [
-                pltpu.make_async_copy(partial[half], own_ref, stage_sems.at[0]),
-                pltpu.make_async_copy(cot_in.at[block(half)], cot_ref, stage_sems.at[1]),
+                pltpu.make_async_copy(back_in.at[block(half)], stage_ref.at[0], stage_sems.at[0]),
+                pltpu.make_async_copy(cot_in.at[block(half)], stage_ref.at[1], stage_sems.at[1]),
                 pltpu.make_async_copy(middle_in.at[block(half)], mid_ref, stage_sems.at[2]),
             ]
 
-        keep = [
+        keep_branch = [
             pltpu.make_async_copy(branch.at[at], branch_out.at[block(at)], stage_sems.at[3 + at])
             for at in range(2)
         ]
@@ -655,10 +781,8 @@
         def rows_back(half):
             def tile(i, carry):
                 at = pl.ds(pl.multiple_of(i * 32, 32), 32)
-                grad = own_ref[at, :].astype(jnp.float32)
-                grad += landed[half, at, :].astype(jnp.float32)
-                grad += landed[2 + half, at, :].astype(jnp.float32)
-                result = cot_ref[at, :].astype(jnp.float32) + norm_back(mid_ref[at, :], grad)
+                grad = add_rows(stage_ref[0, at, :], landed[half, at, :], landed[2 + half, at, :])
+                result = stage_ref[1, at, :].astype(jnp.float32) + norm_back(mid_ref[at, :], grad)
                 grad_ref[at, :] = result
                 live_at = pl.ds(pl.multiple_of(half * BLK + i * 32, 32), 32)
                 branch[half, at, :] = (live_ref[live_at, :1] * result).astype(low)
@@ -679,11 +803,10 @@
             spread(branch_out.at[block(3)], 7, 4, near_x),
             spread(branch_out.at[block(2)], 6, 5, near_y),
         ]
-
-        lax.fori_loop(0, 9, step, 0)
+        run(9)
         join_sum()
         begin(stage(0))
-        lax.fori_loop(9, 25, step, 0)
+        run(16)
         close_sum()
         finish(stage(0))
         written = rows_back(0)
@@ -692,264 +815,240 @@
         finish(stage(1))
         written.wait()
         written = rows_back(1)
-        begin([sends[1], sends[2], sends[3]])
-        begin(keep)
-        lax.fori_loop(25, 33, step, 0)
+        begin(sends[1:])
+        begin(keep_branch)
+        run(8)
         sends[0].wait_recv()
         sends[1].wait_recv()
         begin(later)
-        lax.fori_loop(33, 50, step, 0)
+        run(17)
         written.wait()
-        finish(keep)
+        finish(keep_branch)
         for copy in sends[:2]:
             copy.wait_send()
         finish(sends[2:])
         finish(later)
 
+        open_two, join_two, close_two = square_sum(
+            square, places, [two_sums_in.at[block(at)] for at in range(2, 8)], two_landed, 1
+        )
+        open_two()
+
+        def head_loads(head):
+            here = cols(head * HS, HS)
+            loads = [
+                pltpu.make_async_copy(
+                    all_in.at[c, :, here],
+                    wide_ref.at[:, pl.ds(parts * columns + c * HS, HS)],
+                    head_sems.at[c],
+                )
+                for c in range(parts)
+            ]
+            loads.append(
+                pltpu.make_async_copy(
+                    mixing_in.at[:, here],
+                    wide_ref.at[:, pl.ds(parts * columns + parts * HS, HS)],
+                    head_sems.at[parts],
+                )
+            )
+            loads.append(pltpu.make_async_copy(states_in.at[head], states_ref, head_sems.at[parts + 1]))
+            return loads
+
         weight_loads = [
             pltpu.make_async_copy(weight_in.at[block(at)], landed.at[at], back_sems.at[at])
-            for at in range(weight_in.shape[0] // BLK)
+            for at in range(columns // BLK)
         ]
-        stages = (own_ref, cot_ref)
 
         def row_load(at):
-            return pltpu.make_async_copy(
-                branch_out.at[block(at)], stages[at % 2], back_sems.at[2 + at % 2]
-            )
-
-        def gated_store(at):
-            return pltpu.make_async_copy(
-                gated_ref.at[at % 2], gated_out.at[block(at)], back_sems.at[4 + at % 2]
-            )
+            here = pl.ds(pl.multiple_of(at * BLK, BLK), BLK)
+            return pltpu.make_async_copy(branch_out.at[here], stage_ref.at[at % 2], back_sems.at[2 + at % 2])
 
         begin(weight_loads)
         row_load(0).start()
-        at_step = 50
-        for at in range(rows // BLK):
-            lax.fori_loop(at_step, at_step + 2, step, 0)
-            at_step += 2
-            if at == 0:
-                finish(weight_loads)
-            if at + 1 < rows // BLK:
-                row_load(at + 1).start()
+        begin(head_loads(0))
+        finish(weight_loads)
+        back_from = now[0]
+
+        def back_block(at, carry):
+            step(back_from + at, 0)
             row_load(at).wait()
-            if at >= 2:
-                gated_store(at - 2).wait()
+            pl.when(at + 1 < rows // BLK)(lambda: row_load(at + 1).start())
+            here = pl.ds(pl.multiple_of(at * BLK, BLK), BLK)
             for part in range(len(weight_loads)):
-                result = across(stages[at % 2][...], landed[part])
-                gated_ref[at % 2, :, part * BLK : (part + 1) * BLK] = result.astype(low)
-            gated_store(at).start()
-        lax.fori_loop(at_step, count + STAGES, step, 0)
-        gated_store(rows // BLK - 2).wait()
-        gated_store(rows // BLK - 1).wait()
-
+                result = across(stage_ref[at % 2], landed[part])
+                gated_grad[here, part * BLK : (part + 1) * BLK] = result.astype(low)
+            return carry
+
+        lax.fori_loop(0, rows // BLK, back_block, 0)
+        now[0] += rows // BLK
+        join_two()
+
+        def load_mix(at):
+            here = pl.ds(pl.multiple_of(at * BLK, BLK), BLK)
+            slot = at % 4
+            return [
+                pltpu.make_async_copy(
+                    mix_in.at[c, here, :], landed.at[slot, :, pl.ds(c * columns, columns)], mix_sems.at[slot, c]
+                )
+                for c in range(parts)
+            ]
+
+        for at in range(4):
+            begin(load_mix(at))
+        attend_from = now[0]
+
+        def attend(head, carry):
+            rate = head_rate(heads * narrow + head)
+            within, entry, leave, whole = block_decays(rate)
+            finish(head_loads(head))
+            later_grad = jnp.zeros((HS, HS), jnp.float32)
+            base = parts * columns
+            for at in range(NBLK):
+                block_at = NBLK - 1 - at
+                here = pl.ds(pl.multiple_of(slot_of(block_at, narrow) * BLK, BLK), BLK)
+
+                def load(c, here=here):
+                    return wide_ref[here, base + c * HS : base + (c + 1) * HS]
+
+                def store(c, value, here=here):
+                    wide_ref[here, cols(c * columns + head * HS, HS)] = value.astype(low)
+
+                raw_queries = load(0).astype(jnp.float32)
+                raw_keys = load(1).astype(jnp.float32)
+                queries, keys = jax.nn.silu(raw_queries).astype(low), jax.nn.silu(raw_keys).astype(low)
+                values = load(2)
+                gate = load(3).astype(jnp.float32)
+                mixing = load(4).astype(jnp.float32)
+                grad_rows = gated_grad[here, cols(head * HS, HS)].astype(jnp.float32)
+                scale = lax.rsqrt(jnp.mean(mixing * mixing, axis=-1, keepdims=True) + head_floor)
+                headed = mixing * scale
+                store(3, grad_rows * headed)
+                grad_headed = grad_rows * gate
+                inner = jnp.mean(grad_headed * headed, axis=-1, keepdims=True)
+                grad = (scale * (grad_headed - headed * inner)).astype(low)
+                scores = (across(queries, keys) * within).astype(low)
+                grad_scores = (across(grad, values) * within).astype(low)
+                later_low = later_grad.astype(low)
+                grad_queries = straight(grad_scores, keys) + entry * across(grad, states_ref[block_at])
+                grad_keys = down(grad_scores, queries) + leave * across(values, later_low)
+                grad_values = down(scores, grad) + leave * straight(keys, later_low)
+                early_queries = (queries.astype(jnp.float32) * entry).astype(low)
+                later_grad = keep_ref[block_at : block_at + 1, :1] * (
+                    whole * later_grad + down(early_queries, grad)
+                )
+                store(0, grad_queries * silu_slope(raw_queries))
+                store(1, grad_keys * silu_slope(raw_keys))
+                store(2, grad_values)
+                if at % 2:
+                    step(attend_from + head * (NBLK // 2) + at // 2, 0)
+            pl.when(head + 1 < heads)(lambda: begin(head_loads(head + 1)))
+            return carry
+
+        lax.fori_loop(0, heads, attend, 0)
+        now[0] += heads * (NBLK // 2)
+
+        sum_from = now[0]
+        outs = ((3, branch, False), (1, near, False), (2, mid, True), (0, stage_ref, False))
+
+        def sum_tile(at, carry):
+            finish(load_mix(at))
+            here = cols(at * BLK, BLK)
+            for piece, out, swapped in outs:
+                acts = wide_ref[piece * PIECE : (piece + 1) * PIECE, : parts * columns]
+                total = across(acts, landed[at % 4]).astype(low)
+                out[int(swapped), :, here] = total[:HALF]
+                out[1 - int(swapped), :, here] = total[HALF:]
+            pl.when(at + 4 < width // BLK)(lambda: begin(load_mix(at + 4)))
+            step(sum_from + at, 0)
+            return carry
+
+        close_two()
+        lax.fori_loop(0, width // BLK, sum_tile, 0)
+        now[0] += width // BLK
+        open_last, join_last, close_last = square_sum(
+            square,
+            places,
+            (near.at[0], near.at[1], None, None, branch.at[0], branch.at[1]),
+            last_landed,
+            2,
+        )
+        own_stores = [
+            pltpu.make_async_copy(stage_ref.at[at], own_outs[at], own_sems.at[at]) for at in range(2)
+        ]
+        open_last()
+        begin(own_stores)
+        run(9)
+        join_last()
+        run(count + STAGES - now[0])
+        close_last()
+        finish(own_stores)
+
+    def low_shape(*shape):
+        return jax.ShapeDtypeStruct(shape, low)
+
+    sem = pltpu.SemaphoreType.DMA
     return pl.pallas_call(
         body,
-        in_specs=any_specs(8) + [pl.BlockSpec(memory_space=pltpu.VMEM)],
-        out_specs=any_specs(5),
+        in_specs=any_specs(15) + [pl.BlockSpec(memory_space=pltpu.VMEM)] * 2,
+        out_specs=any_specs(16),
         out_shape=[
-            jax.ShapeDtypeStruct((out_blocks, SUB, width), low),
-            jax.ShapeDtypeStruct((in_blocks, SUB, grad_parts.shape[1]), low),
-            jax.ShapeDtypeStruct((rows, width), low),
+            low_shape(width // SUB, SUB, grad_parts.shape[1]),
+            low_shape(out_blocks, SUB, width),
+            low_shape(columns // SUB, SUB, width),
+            low_shape(parts * width // SUB, SUB, columns),
+            low_shape(rows, width),
             jax.ShapeDtypeStruct((local_rows, width), jnp.float32),
-            jax.ShapeDtypeStruct((rows, out_weight.shape[0]), low),
-        ],
+        ]
+        + [low_shape(BLK, width)] * 10,
         scratch_shapes=[
-            pltpu.VMEM(act.shape, low),
             pltpu.VMEM((rows, width), low),
             pltpu.VMEM(grad_parts.shape, low),
+            pltpu.VMEM(act.shape, low),
             pltpu.VMEM((4, BLK, width), low),
-            pltpu.VMEM((BLK, width), low),
-            pltpu.VMEM((BLK, width), low),
+            pltpu.VMEM((2, BLK, width), low),
             pltpu.VMEM((BLK, width), jnp.float32),
             pltpu.VMEM((BLK, width), jnp.float32),
             pltpu.VMEM((2, BLK, width), low),
-            pltpu.VMEM((2, BLK, out_weight.shape[0]), low),
-            pltpu.SemaphoreType.DMA((4,)),
-            pltpu.SemaphoreType.DMA((6,)),
-            pltpu.SemaphoreType.DMA((6, 2)),
-            pltpu.SemaphoreType.DMA((6,)),
+            pltpu.VMEM((2, BLK, width), low),
+            pltpu.VMEM((rows, columns), low),
+            pltpu.VMEM((NBLK, HS, HS), low),
+            sem((in_rows,)),
+            sem((in_columns,)),
+            sem((6,)),
+            sem((6,)),
+            sem((6, 2)),
+            sem((4,)),
+            sem((parts + 2,)),
+            sem((4, parts)),
+            sem((2,)),
+            sem((2,)),
         ]
         + line_scratch()
-        + square_scratch(),
+        + square_scratch(3),
         compiler_params=pltpu.CompilerParams(
             vmem_limit_bytes=VMEM, collective_id=1, has_side_effects=True
         ),
-        cost_estimate=cost(2 * 3 * rows * width * units, 60e6),
-        name="unit_grads",
+        cost_estimate=cost(2 * rows * width * (3 * units + 9 * columns), 120e6),
+        name="weight_grads",
     )(
         act,
         grad_two_all,
         normed_two_all,
         grad_parts,
         back_sums,
+        two_sums,
         middle,
         cotangent,
         out_weight,
+        mix_weight,
+        parts_all,
+        mixing_all,
+        states_all,
+        gated,
+        normed_all,
         live,
-    )
-
-
-def mix_grads(gated, grad_branch_all, normed_all, grad_projected, mix_weight, two_sums):
-    _, rows, columns = gated.shape
-    width = normed_all.shape[1]
-    parts = grad_projected.shape[0]
-    low = jnp.bfloat16
-    out_chunks = width // TILE
-    per_row = columns // TILE
-    per_part = (width // PIECE) * per_row
-    count = out_chunks + parts * per_part
-    wide_tile = 1024
-
-    def body(*refs):
-        gated_in, branch_in, normed_in, grads_in, weight_in = refs[:5]
-        two_partial = [refs[5].at[pl.ds(at * BLK, BLK)] for at in range(2, 8)]
-        out_grad, mix_grad = refs[6:8]
-        own_outs = refs[8:10]
-        landed, two_landed = refs[10:14], refs[14:18]
-        gated_ref, branch_ref, normed_ref, grads_ref, weight_ref, far, near, own_ref = refs[18:26]
-        load_sems, branch_sems, grad_sems, weight_sems, own_sems = refs[26:31]
-        line = refs[31:40]
-        square, two_square = refs[40:44], refs[44:48]
-        mid = square[1]
-        places = neighbours()
-        enter(places)
-
-        def part_columns(c):
-            return pl.ds(c * columns, columns)
-
-        load_gated = pltpu.make_async_copy(gated_in.at[0], gated_ref, load_sems.at[0])
-        load_normed = pltpu.make_async_copy(normed_in, normed_ref, load_sems.at[1])
-
-        def load_branch(k):
-            at = pl.ds(pl.multiple_of(k * TILE, TILE), TILE)
-            slot = k % 2
-            return pltpu.make_async_copy(branch_in.at[:, at], branch_ref.at[slot], branch_sems.at[slot])
-
-        grad_loads = [
-            pltpu.make_async_copy(grads_in.at[c], grads_ref.at[:, part_columns(c)], grad_sems.at[c])
-            for c in range(parts)
-        ]
-        weight_loads = [
-            pltpu.make_async_copy(weight_in.at[c], weight_ref.at[:, part_columns(c)], weight_sems.at[c])
-            for c in range(parts)
-        ]
-        load_gated.start()
-        load_branch(0).start()
-        begin(grad_loads)
-        begin(weight_loads)
-        load_normed.start()
-        _, join_sum, close_sum, first, direct = square_sum(
-            square,
-            places,
-            (near.at[0], near.at[1], None, None, far.at[0], far.at[1]),
-            landed,
-        )
-        open_two, join_two, close_two, _, _ = square_sum(two_square, places, two_partial, two_landed)
-        load_gated.wait()
-
-        def product(k, own):
-            @pl.when(k < out_chunks)
-            def _():
-                load_branch(k).wait()
-                pl.when(k + 1 < out_chunks)(lambda: load_branch(k + 1).start())
-                result = down(gated_ref[...], branch_ref[k % 2]).astype(low)
-                for part in range(4):
-                    own[part] = result[part * SUB : (part + 1) * SUB]
-
-            @pl.when(k >= out_chunks)
-            def _():
-                at = k - out_chunks
-                rows_at = pl.ds(pl.multiple_of(((at // per_row) % 4) * PIECE, PIECE), PIECE)
-                start = (at // per_part) * columns + (at % per_row) * TILE
-                wide_at = pl.ds(pl.multiple_of(start, TILE), TILE)
-                result = down(normed_ref[:, rows_at], grads_ref[:, wide_at]).astype(low)
-                for part in range(4):
-                    own[part] = result[part * SUB : (part + 1) * SUB]
-
-        def targets(k, part):
-            first_at = pl.ds(pl.multiple_of(jnp.minimum(k, out_chunks - 1) * TILE, TILE), TILE)
-            at = jnp.maximum(k - out_chunks, 0)
-            wide_at = pl.ds(pl.multiple_of((at % per_row) * TILE, TILE), TILE)
-            return [
-                (k < out_chunks, out_grad.at[part, :, first_at]),
-                (k >= out_chunks, mix_grad.at[(at // per_row) * 4 + part, :, wide_at]),
-            ]
-
-        step = line_sum(line, places, count, product, targets)
-
-        def partial(piece, tile, top, low_part):
-            at = slice(tile * wide_tile, (tile + 1) * wide_tile)
-            acts = grads_ref[piece * PIECE : (piece + 1) * PIECE, :]
-            total = across(acts, weight_ref[at, :])
-            top[:, at] = total[:HALF].astype(low)
-            low_part[:, at] = total[HALF:].astype(low)
-
-        own_stores = [
-            pltpu.make_async_copy(own_ref.at[at], own_outs[at], own_sems.at[at]) for at in range(2)
-        ]
-        places_of = (
-            (3, far.at[0], far.at[1], first),
-            (1, near.at[0], near.at[1], direct),
-            (2, mid.at[1], mid.at[0], []),
-            (0, own_ref.at[0], own_ref.at[1], own_stores),
-        )
-        lax.fori_loop(0, 2, step, 0)
-        finish(grad_loads)
-        finish(weight_loads)
-        at_step = 2
-        for piece, top, low_part, copies in places_of:
-            for tile in range(width // wide_tile):
-                partial(piece, tile, top, low_part)
-                if tile == width // wide_tile - 1:
-                    begin(copies)
-                lax.fori_loop(at_step, at_step + 1, step, 0)
-                at_step += 1
-                if at_step == 8:
-                    load_normed.wait()
-        lax.fori_loop(at_step, 12, step, 0)
-        join_sum()
-        open_two()
-        lax.fori_loop(12, 36, step, 0)
-        join_two()
-        lax.fori_loop(36, count + STAGES, step, 0)
-        close_sum()
-        close_two()
-        finish(own_stores)
-
-    return pl.pallas_call(
-        body,
-        in_specs=any_specs(6),
-        out_specs=any_specs(12),
-        out_shape=[
-            jax.ShapeDtypeStruct((columns // SUB, SUB, width), low),
-            jax.ShapeDtypeStruct((parts * width // SUB, SUB, columns), low),
-        ]
-        + [jax.ShapeDtypeStruct((BLK, width), low)] * 10,
-        scratch_shapes=[
-            pltpu.VMEM((rows, columns), low),
-            pltpu.VMEM((2, rows, TILE), low),
-            pltpu.VMEM((rows, width), low),
-            pltpu.VMEM((rows, parts * columns), low),
-            pltpu.VMEM((width, parts * columns), low),
-            pltpu.VMEM((2, BLK, width), low),
-            pltpu.VMEM((2, BLK, width), low),
-            pltpu.VMEM((2, BLK, width), low),
-            pltpu.SemaphoreType.DMA((2,)),
-            pltpu.SemaphoreType.DMA((2,)),
-            pltpu.SemaphoreType.DMA((parts,)),
-            pltpu.SemaphoreType.DMA((parts,)),
-            pltpu.SemaphoreType.DMA((2,)),
-        ]
-        + line_scratch()
-        + square_scratch()
-        + square_scratch(),
-        compiler_params=pltpu.CompilerParams(
-            vmem_limit_bytes=VMEM, collective_id=2, has_side_effects=True
-        ),
-        cost_estimate=cost(2 * 9 * rows * width * columns, 60e6),
-        name="mix_grads",
-    )(gated, grad_branch_all, normed_all, grad_projected, mix_weight, two_sums)
+        keep,
+    )
 
 
 def gated_unit(gated, whole_weight, hidden, live, grads_own, grads_first, ffn_in, ffn_out):
@@ -1408,17 +1507,8 @@
         finish(row_sends[2])
         project(3)
 
-        def slot_of(block):
-            off_x = (block // 2 % 2 + narrow % 2) % 2
-            off_y = (block // 4 + narrow // 2) % 2
-            if block % 2:
-                return 1 + 3 * off_x + 2 * off_y + off_x * off_y
-            return 2 * off_x + 5 * off_y - off_x * off_y
-
         def attend(head, carry):
-            head_id = (heads * narrow + head).astype(jnp.float32)
-            rate = jnp.exp(jnp.full((1, 1), -0.5 * math.log(2.0), jnp.float32) * (head_id + 1.0))
-            within, entry, leave, whole = block_decays(rate)
+            within, entry, leave, whole = block_decays(head_rate(heads * narrow + head))
             state = jnp.zeros((HS, HS), jnp.float32)
 
             def part(c, rows_at):
@@ -1426,7 +1516,7 @@
                 return parts_ref[rows_at, at]
 
             for block in range(NBLK):
-                rows_at = pl.ds(pl.multiple_of(slot_of(block) * BLK, BLK), BLK)
+                rows_at = pl.ds(pl.multiple_of(slot_of(block, narrow) * BLK, BLK), BLK)
                 queries = jax.nn.silu(part(0, rows_at).astype(jnp.float32)).astype(low)
                 keys = jax.nn.silu(part(1, rows_at).astype(jnp.float32)).astype(low)
                 values = part(2, rows_at)
@@ -1504,24 +1594,37 @@
     )(hidden, cotangent, mix_weight, out_weight, live, keep)
 
 
-def finish_rows(mix_low, out_low, hidden, middle, grad_middle, live, normed_terms, two_sums, two_terms):
+def finish_rows(
+    mix_low, out_low, in_low, wide_low, hidden, middle, grad_middle, live, normed_terms, two_sums, two_terms
+):
     parts, width, columns = mix_low.shape
     local_rows = hidden.shape[0]
-    tile = local_rows // parts
-    out_tile = out_low.shape[0] // parts
-    half_steps = parts // 2
+    units = wide_low.shape[0]
+    main = units // TILE * TILE
+    tail = units - main
+    steps = 2 * parts
+    tile, out_tile = local_rows // steps, out_low.shape[0] // steps
+    in_tile, unit_tile, mix_tile = width // steps, units // steps, width // 2
+    half_steps = steps // 2
     terms = len(normed_terms) + len(two_terms)
 
-    def body(mix_ref, out_ref, hidden_ref, middle_ref, grad_ref, live_ref, own_ref, *refs):
+    def body(
+        mix_ref, out_ref, in_ref, wide_ref, hidden_ref, middle_ref, grad_ref, live_ref, own_ref, *refs
+    ):
         term_refs = refs[:terms]
-        mix_out, out_out, layer_ref, input_ref = refs[terms:]
+        mix_out, out_out, in_out, wide_out, layer_ref, input_ref = refs[terms:]
         mix_out[...] = mix_ref[...].astype(jnp.float32)
         out_out[...] = out_ref[...].astype(jnp.float32)
+        wide_out[...] = wide_ref[...].astype(jnp.float32)
+        for c in range(2):
+            in_out[c, :, :main] = in_ref[:, c * main : (c + 1) * main].astype(jnp.float32)
+            rest = slice(2 * main + c * tail, 2 * main + (c + 1) * tail)
+            in_out[c, :, main:] = in_ref[:, rest].astype(jnp.float32)
 
         def rows_of(half):
             normed = add_rows(*(ref[...] for ref in term_refs[3 * half : 3 * half + 3]))
             two = add_rows(*(ref[...] for ref in term_refs[6 + 2 * half : 8 + 2 * half]), own_ref[...])
-            layer = middle_ref[...] + live_ref[...] * two
+            layer = middle_ref[...] + live_ref[:, :1] * two
             layer_ref[...] = layer.astype(jnp.bfloat16)
             back = norm_back(hidden_ref[...].astype(jnp.float32), normed)
             input_ref[...] = (grad_ref[...] + back).astype(jnp.bfloat16)
@@ -1530,8 +1633,8 @@
         pl.when(first)(lambda: rows_of(0))
         pl.when(jnp.logical_not(first))(lambda: rows_of(1))
 
-    def rows_spec(size):
-        return pl.BlockSpec((tile, size), lambda i: (i, 0))
+    def rows_spec(size, height=tile):
+        return pl.BlockSpec((height, size), lambda i: (i, 0))
 
     def half_spec(half):
         if half == 0:
@@ -1539,26 +1642,49 @@
         return pl.BlockSpec((tile, width), lambda i: (jnp.maximum(i - half_steps, 0), 0))
 
     term_specs = [half_spec(0)] * 3 + [half_spec(1)] * 3 + [half_spec(0)] * 2 + [half_spec(1)] * 2
-    mix_spec = pl.BlockSpec((1, width, columns), lambda i: (i, 0, 0))
-    out_spec = pl.BlockSpec((out_tile, out_low.shape[1]), lambda i: (i, 0))
+    mix_spec = pl.BlockSpec((1, mix_tile, columns), lambda i: (i // 2, i % 2, 0))
+    out_spec = rows_spec(width, out_tile)
+    wide_spec = rows_spec(width, unit_tile)
+    wide_float = jnp.float32
     return pl.pallas_call(
         body,
-        grid=(parts,),
-        in_specs=[mix_spec, out_spec]
+        grid=(steps,),
+        in_specs=[mix_spec, out_spec, rows_spec(2 * units, in_tile), wide_spec]
         + [rows_spec(width)] * 3
-        + [rows_spec(1), rows_spec(width)]
+        + [rows_spec(live.shape[1]), rows_spec(width)]
         + term_specs,
-        out_specs=[mix_spec, out_spec, rows_spec(width), rows_spec(width)],
+        out_specs=[
+            mix_spec,
+            out_spec,
+            pl.BlockSpec((2, in_tile, units), lambda i: (0, i, 0)),
+            wide_spec,
+            rows_spec(width),
+            rows_spec(width),
+        ],
         out_shape=[
-            jax.ShapeDtypeStruct(mix_low.shape, jnp.float32),
-            jax.ShapeDtypeStruct(out_low.shape, jnp.float32),
+            jax.ShapeDtypeStruct(mix_low.shape, wide_float),
+            jax.ShapeDtypeStruct(out_low.shape, wide_float),
+            jax.ShapeDtypeStruct((2, width, units), wide_float),
+            jax.ShapeDtypeStruct(wide_low.shape, wide_float),
             jax.ShapeDtypeStruct(hidden.shape, jnp.bfloat16),
             jax.ShapeDtypeStruct(hidden.shape, jnp.bfloat16),
         ],
         compiler_params=pltpu.CompilerParams(vmem_limit_bytes=VMEM),
-        cost_estimate=cost(1e8, 60e6),
+        cost_estimate=cost(1e8, 110e6),
         name="finish_rows",
-    )(mix_low, out_low, hidden, middle, grad_middle, live, two_sums, *normed_terms, *two_terms)
+    )(
+        mix_low,
+        out_low,
+        in_low,
+        wide_low,
+        hidden,
+        middle,
+        grad_middle,
+        live,
+        two_sums,
+        *normed_terms,
+        *two_terms,
+    )
 
 
 def block_decays(rate):
@@ -1573,95 +1699,6 @@
     return within, entry, leave, whole
 
 
-def mix_backward(slots, fresh, rates, parts, mixing_all, states, grad_gated, in_low, out_low):
-    _, group_rows, columns = parts.shape
-    heads = columns // HS
-    low = jnp.bfloat16
-    width, both_units = in_low.shape
-    units = both_units // 2
-    main = units // TILE * TILE
-    tail = units - main
-    in_rows, out_rows = width // heads, units // heads
-
-    def body(
-        slot_ref,
-        fresh_ref,
-        rate_ref,
-        parts_ref,
-        mixing_ref,
-        states_ref,
-        grad_ref,
-        in_ref,
-        wide_ref,
-        out_ref,
-        in_out,
-        wide_out,
-    ):
-        wide_out[...] = wide_ref[...].astype(jnp.float32)
-        for c in range(2):
-            in_out[c, :, :main] = in_ref[:, c * main : (c + 1) * main].astype(jnp.float32)
-            rest = slice(2 * main + c * tail, 2 * main + (c + 1) * tail)
-            in_out[c, :, main:] = in_ref[:, rest].astype(jnp.float32)
-        within, entry, leave, whole = block_decays(rate_ref[pl.program_id(0)])
-        later = jnp.zeros((HS, HS), jnp.float32)
-        for block in reversed(range(NBLK)):
-            rows = pl.ds(pl.multiple_of(slot_ref[block] * BLK, BLK), BLK)
-            raw_queries = parts_ref[0, rows, :].astype(jnp.float32)
-            raw_keys = parts_ref[1, rows, :].astype(jnp.float32)
-            queries_float = jax.nn.silu(raw_queries).astype(low).astype(jnp.float32)
-            queries, keys = queries_float.astype(low), jax.nn.silu(raw_keys).astype(low)
-            values = parts_ref[2, rows, :]
-            gate = parts_ref[3, rows, :].astype(jnp.float32)
-            mixing = mixing_ref[rows, :].astype(jnp.float32)
-            grad_gated_rows = grad_ref[rows, :].astype(jnp.float32)
-            scale = lax.rsqrt(jnp.mean(mixing * mixing, axis=-1, keepdims=True) + head_floor)
-            headed = mixing * scale
-            out_ref[3, rows, :] = (grad_gated_rows * headed).astype(low)
-            grad_headed = grad_gated_rows * gate
-            inner = jnp.mean(grad_headed * headed, axis=-1, keepdims=True)
-            grad = (scale * (grad_headed - headed * inner)).astype(low)
-            weights = (across(queries, keys) * within).astype(low)
-            grad_scores = (across(grad, values) * within).astype(low)
-            later_low = later.astype(low)
-            grad_queries = straight(grad_scores, keys) + entry * across(grad, states_ref[0, block])
-            grad_keys = down(grad_scores, queries) + leave * across(values, later_low)
-            grad_values = down(weights, grad) + leave * straight(keys, later_low)
-            early_queries = (queries_float * entry).astype(low)
-            later = jnp.where(fresh_ref[block] != 0, 0.0, whole * later + down(early_queries, grad))
-            out_ref[0, rows, :] = (grad_queries * silu_slope(raw_queries)).astype(low)
-            out_ref[1, rows, :] = (grad_keys * silu_slope(raw_keys)).astype(low)
-            out_ref[2, rows, :] = grad_values.astype(low)
-
-    return pl.pallas_call(
-        body,
-        grid_spec=pltpu.PrefetchScalarGridSpec(
-            num_scalar_prefetch=3,
-            grid=(heads,),
-            in_specs=[
-                pl.BlockSpec((4, group_rows, HS), lambda h, *_: (0, 0, h)),
-                pl.BlockSpec((group_rows, HS), lambda h, *_: (0, h)),
-                pl.BlockSpec((1, NBLK, HS, HS), lambda h, *_: (h, 0, 0, 0)),
-                pl.BlockSpec((group_rows, HS), lambda h, *_: (0, h)),
-                pl.BlockSpec((in_rows, both_units), lambda h, *_: (h, 0)),
-                pl.BlockSpec((out_rows, width), lambda h, *_: (h, 0)),
-            ],
-            out_specs=[
-                pl.BlockSpec((4, group_rows, HS), lambda h, *_: (0, 0, h)),
-                pl.BlockSpec((2, in_rows, units), lambda h, *_: (0, h, 0)),
-                pl.BlockSpec((out_rows, width), lambda h, *_: (h, 0)),
-            ],
-        ),
-        out_shape=[
-            jax.ShapeDtypeStruct(parts.shape, low),
-            jax.ShapeDtypeStruct((2, width, units), jnp.float32),
-            jax.ShapeDtypeStruct((units, width), jnp.float32),
-        ],
-        compiler_params=pltpu.CompilerParams(vmem_limit_bytes=VMEM),
-        cost_estimate=cost(20e9, 75e6),
-        name="mix_backward",
-    )(slots, fresh, rates, parts, mixing_all, states, grad_gated, in_low, out_low)
-
-
 def norm_back(values, grad):
     scale = lax.rsqrt(jnp.mean(values * values, axis=-1, keepdims=True) + epsilon)
     unit = values * scale
@@ -1673,16 +1710,11 @@
 ):
     local_rows, width = hidden.shape
     units = ffn_out_weight.shape[0]
-    head_count = mix_weight.shape[2] // HS
     narrow_index = lax.axis_index("narrow")
     valid_all, fresh_block = group_masks(seq_lengths, block_seq)
     live = lax.dynamic_slice_in_dim(
         valid_all.astype(jnp.float32), narrow_index * local_rows, local_rows
     )[:, None]
-    head_ids = narrow_index * head_count + jnp.arange(head_count, dtype=jnp.int32)
-    rates = 2.0 ** (-8.0 * (head_ids.astype(jnp.float32) + 1.0) / HEADS)
-    slots, fresh = slot_tables(narrow_index, fresh_block)
-    low = jnp.bfloat16
 
     keep = jnp.broadcast_to(jnp.where(fresh_block, 0.0, 1.0)[:, None], (NBLK, HS))
     normed_all, parts, gated, mixing, states, grads_own, grads_first, whole_weight = mix_rows(
@@ -1698,34 +1730,30 @@
         ffn_in_weight,
         ffn_out_weight,
     )
-    out_low, in_low, grad_branch_all, grad_middle, grad_gated = unit_grads(
+    in_low, wide_low, out_low, mix_low, _, grad_middle, own_top, own_low, *terms = weight_grads(
         act,
         grad_two_all,
         normed_two_all,
         grad_parts,
         back_sums,
+        two_sums,
         middle,
         cotangent,
-        live,
         out_weight,
-    )
-    grad_projected, grad_ffn_in, grad_ffn_out = mix_backward(
-        slots,
-        fresh,
-        rates,
+        mix_weight,
         parts,
         mixing,
         states,
-        grad_gated,
-        in_low.reshape(width, 2 * units),
-        out_low.reshape(units, width),
-    )
-    out_low, mix_low, own_top, own_low, *terms = mix_grads(
-        gated, grad_branch_all, normed_all, grad_projected, mix_weight, two_sums
-    )
-    grad_mix, grad_out, layer_out, input_grad = finish_rows(
+        gated,
+        normed_all,
+        live,
+        keep,
+    )
+    grad_mix, grad_out, grad_ffn_in, grad_ffn_out, layer_out, input_grad = finish_rows(
         mix_low.reshape(mix_weight.shape),
         out_low.reshape(out_weight.shape),
+        in_low.reshape(width, 2 * units),
+        wide_low.reshape(units, width),
         hidden,
         middle,
         grad_middle,

time: 730 us -> 668 us (0.915)
  Pallas kernels: 708 us -> 651 us
    pallas_call x4 -> x2, Pallas kernels: 429 us -> 381 us  [the longest x1 345 us: weight_grads(): pl.pallas_call(body, in_specs=any_specs(15) + [pl.BlockSpec(memory_space=...]
    pallas_call x1, Pallas kernels: 170 us -> 163 us  [gated_unit(): pl.pallas_call(body, in_specs=any_specs(7) + [pl.BlockSpec(memory_space=p...]
where the time goes in v5:
time: 668 us; the launch traced here: 660 us
  Pallas kernels  651 us (97%)
    pallas_call x1, Pallas kernels, weight_grads(): pl.pallas_call(body, in_specs=any_specs(15) + [pl.BlockSpec(memory_space=...  345 us
    pallas_call x1, Pallas kernels, gated_unit(): pl.pallas_call(body, in_specs=any_specs(7) + [pl.BlockSpec(memory_space=p...  163 us
    pallas_call x1, Pallas kernels, mix_rows(): pl.pallas_call(body, in_specs=any_specs(4) + [pl.BlockSpec(memory_space=p...  108 us
    pallas_call x1, Pallas kernels, finish_rows(): pl.pallas_call(body, grid=(steps,), in_specs=[mix_spec, out_spec, rows_sp...  35.8 us

profile of v5, /device:TPU:0, one launch (start us, length us, event | category | flops | bytes accessed | tf_op | source)
XLA Modules:
  0.0 659.8 jit_solution(3316439708341005572)
XLA Ops:
  0.6 1.3 fusion
  1.9 1.9 convert_reduce_fusion
  3.9 1.9 subtract_multiply_fusion
  5.8 0.7 compare_select_fusion
  6.5 0.7 broadcast_in_dim.38.refs_5_.refs_16_
  7.2 0.1 convert_bitcast_fusion
  7.2 0.1 dynamic_slice.3
  7.3 0.9 copy.14.refs_4_.refs_7_.refs_15_.live_ref
  8.2 108.1 %mix_rows.1 = (bf16[2048,2048]{1,0:T(8,128)(2,1)}, bf16[4,2048,512]{2,1,0:T(8,128)(2,1)}, bf16[1,2048,512]{2,1,0:T(8,128)(2,1)}, bf16[2048,512]{1,0:T(8,128)(2,1...) custom-call(bf16[512,2048]{1,0:T(8,128)(2,1)} %hidden_ref.1, ...), custom_call_target="tpu_custom_call" | custom-call | flops 17179869184 | bytes 50000000 | tf_op jit(solution)/shard_map/mix_rows/pallas_call | solution.py:1557
  116.4 162.6 %gated_unit.1 = (f32[512,2048]{1,0:T(8,128)}, bf16[2048,2048]{1,0:T(8,128)(2,1)}, bf16[2048,2048]{1,0:T(8,128)(2,1)}, bf16[2048,1408]{1,0:T(8,128)(2,1)}, bf16[2...) custom-call(bf16[1,2048,512]{2,1,0:T(8,128)(2,1)} %get-tuple-element.42.refs_0_.refs_13_, ...), custom_call_target="tpu_custom_call" | custom-call | flops 70866960384 | bytes 90000000 | tf_op jit(solution)/shard_map/gated_unit/pallas_call | solution.py:1296
  279.0 344.8 %weight_grads.1 = (bf16[16,128,2816]{2,1,0:T(8,128)(2,1)}, bf16[11,128,2048]{2,1,0:T(8,128)(2,1)}, bf16[4,128,2048]{2,1,0:T(8,128)(2,1)}, bf16[64,128,512]{2,1,0...) custom-call(bf16[2048,1408]{1,0:T(8,128)(2,1)} %get-tuple-element.46, ...), custom_call_target="tpu_custom_call" | custom-call | flops 74088185856 | bytes 120000000 | tf_op jit(solution)/shard_map/weight_grads/pallas_call | solution.py:990
  623.8 35.8 %finish_rows.1 = (f32[4,2048,512]{2,1,0:T(8,128)}, f32[512,2048]{1,0:T(8,128)}, f32[2,2048,1408]{2,1,0:T(8,128)}, f32[1408,2048]{1,0:T(8,128)}, bf16[512,2048]{1,0:T(8,128)(2,1)}, /*index=5*/bf16[512,2048]{1,0:T(8,128)(2,1)}) custom-call(bf16[4,2048,512]{2,1,0:T(8,128)(2,1)} %bitcast.13, bf16[512,2048]{1,0:T(8,128)(2,1)} %bitcast.15, ...), custom_call_target="tpu_custom_call" | custom-call | flops 100000000 | bytes 110000000 | tf_op jit(solution)/shard_map/finish_rows/pallas_call | solution.py:1649
  (1 shorter events, 0.0 us)

commit v6 on v5

--- a/solution.py
+++ b/solution.py
@@ -288,8 +288,8 @@
 
 
 MESH = pl.DeviceIdType.MESH
-SLOTS = 13
-STAGES = 12
+SLOTS = 12
+STAGES = 11
 SUB = 128
 TILE = 256
 
@@ -478,7 +478,7 @@
                 pltpu.make_async_copy(src.at[s, t], ref, out_sems.at[2 * t + which, s]).wait()
 
     stages = (
-        (12, clear),
+        (11, clear),
         (10, deliver),
         (9, back),
         (7, pass_on),
@@ -1072,7 +1072,7 @@
         middle_out, rows_out, grads_out, act_out, parts_out, back_out, two_out = refs[8:15]
         gated_ref, hidden_ref, middle_ref = refs[15:18]
         rows, grads, sums, w_in, w_out, act, parts = refs[18:25]
-        load_sems, slice_sems, weight_sems, done_sems, sum_sems, gated_sems, gather_sems = refs[25:]
+        load_sems, slice_sems, weight_sems, done_sems, sum_sems, last_sems, gated_sems, gather_sems = refs[25:]
         wide, narrow, _, _, _, near_x, near_y = neighbours()
         far = (wide, 3 - narrow)
         barrier = pltpu.get_barrier_semaphore()
@@ -1148,6 +1148,9 @@
         def half(ref, piece, at):
             return ref.at[piece, (first_half, second_half)[at]]
 
+        def quarter(ref, piece, at):
+            return ref.at[piece, pl.ds(at * SUB, SUB)]
+
         def gather(ref, kind):
             return (
                 [
@@ -1159,13 +1162,17 @@
                     remote(half(ref, 0, 0), half(ref, 2, 1), gather_sems, kind + 3, near_y),
                 ],
                 [
-                    remote(half(ref, 1, 1), half(ref, 3, 1), gather_sems, kind + 4, near_x),
-                    remote(half(ref, 1, 0), half(ref, 3, 0), gather_sems, kind + 5, near_y),
+                    remote(quarter(ref, 1, 2), quarter(ref, 3, 1), gather_sems, kind + 4, near_x),
+                    remote(quarter(ref, 1, 0), quarter(ref, 3, 0), gather_sems, kind + 5, near_y),
+                ],
+                [
+                    remote(quarter(ref, 1, 3), quarter(ref, 3, 3), gather_sems, kind + 6, near_x),
+                    remote(quarter(ref, 1, 1), quarter(ref, 3, 2), gather_sems, kind + 7, near_y),
                 ],
             )
 
         row_sends = gather(rows, 0)
-        grad_sends = gather(grads, 6)
+        grad_sends = gather(grads, 8)
 
         begin(gated_sends)
         begin([keep_gated])
@@ -1193,14 +1200,48 @@
             lax.fori_loop(0, HALF // 32, functools.partial(second_norm, at=at), 0)
             row_sends[0][at].start()
         begin(row_sends[1])
-        begin(grad_sends[2])
         store_middle = pltpu.make_async_copy(middle_ref, middle_out, done_sems.at[0])
         store_middle.start()
 
-        def products(at, first, second, part_a, part_b, grad_act):
-            act[:, at] = (part_a * part_b).astype(low)
-            parts[:, first] = (grad_act * part_b).astype(low)
-            parts[:, second] = (grad_act * part_a).astype(low)
+        def products(size, at, first, second, part_a, part_b, grad_act):
+            act[:size, at] = (part_a * part_b).astype(low)
+            parts[:size, first] = (grad_act * part_b).astype(low)
+            parts[:size, second] = (grad_act * part_a).astype(low)
+
+        def unit(arrived, arrived_grads, size, weights_wait):
+            for which, (start, count) in enumerate(cuts):
+                at, second = slice(start, start + count), slice(main + start, main + start + count)
+                weights_wait(3 * which, 3 * which + 3)
+                part_a = straight(arrived[...], w_in[:, at])
+                part_b = straight(arrived[...], w_in[:, second])
+                grad_act = across(arrived_grads[...], w_out[at, :])
+                products(size, at, at, second, part_a, part_b, grad_act)
+            weights_wait(6, 9)
+            if tail:
+                both = straight(arrived[...], w_in[:, 2 * main :])
+                grad_act = across(arrived_grads[...], w_out[main:, :])
+                products(
+                    size,
+                    slice(main, units),
+                    slice(2 * main, 2 * main + tail),
+                    slice(2 * main + tail, 2 * units),
+                    both[:, :tail],
+                    both[:, tail:],
+                    grad_act,
+                )
+
+        def row_stores(arrived, arrived_grads, at):
+            return [
+                pltpu.make_async_copy(arrived, rows_out.at[at, :], done_sems.at[1]),
+                pltpu.make_async_copy(arrived_grads, grads_out.at[at, :], done_sems.at[2]),
+            ]
+
+        def unit_stores(size, at):
+            here = pl.ds(0, size)
+            return [
+                pltpu.make_async_copy(act.at[here], act_out.at[at, :], done_sems.at[3]),
+                pltpu.make_async_copy(parts.at[here], parts_out.at[at, :], done_sems.at[4]),
+            ]
 
         def sum_stores(piece, j):
             tile = pl.ds(j * wide_tile, wide_tile)
@@ -1216,81 +1257,96 @@
             ]
 
         def work(piece, carry):
-            spot = pl.ds(pl.multiple_of(piece * PIECE, PIECE), PIECE)
+            at = pl.ds(pl.multiple_of(piece * PIECE, PIECE), PIECE)
             arrived, arrived_grads = rows.at[piece], grads.at[piece]
 
             @pl.when(piece == 1)
             def _():
                 finish(row_sends[0])
-                begin(row_sends[2])
+                for step in (2, 3):
+                    begin(row_sends[step])
+                    begin(grad_sends[step])
 
             @pl.when(piece == 2)
             def _():
                 finish(row_sends[1])
                 finish(grad_sends[1])
 
-            @pl.when(piece == 3)
+            stores = row_stores(arrived, arrived_grads, at)
+            begin(stores)
+
+            def weights_wait(start, stop):
+                pl.when(piece == 0)(lambda: finish(weights[start:stop]))
+
+            unit(arrived, arrived_grads, PIECE, weights_wait)
+            more = unit_stores(PIECE, at)
+            begin(more)
+            for j in range(width // wide_tile):
+                tile = slice(j * wide_tile, (j + 1) * wide_tile)
+
+                @pl.when(piece > 0)
+                def _(j=j):
+                    finish(sum_stores(piece - 1, j))
+
+                back = across(parts[...], w_in[tile, :])
+                sums[0, :, tile] = back[:HALF].astype(low)
+                sums[1, :, tile] = back[HALF:].astype(low)
+                two = straight(act[...], w_out[:, tile])
+                sums[2, :, tile] = two[:HALF].astype(low)
+                sums[3, :, tile] = two[HALF:].astype(low)
+                begin(sum_stores(piece, j))
+            finish(stores)
+            finish(more)
+            return carry
+
+        lax.fori_loop(0, pieces - 1, work, 0)
+        for j in range(width // wide_tile):
+            finish(sum_stores(pieces - 2, j))
+
+        def last_stores(which):
+            return [
+                pltpu.make_async_copy(
+                    sums.at[2 * total + which, pl.ds(part * SUB, SUB)],
+                    (back_out, two_out)[total].at[
+                        pl.ds(pl.multiple_of((pieces - 1) * PIECE + part * HALF + which * SUB, SUB), SUB)
+                    ],
+                    last_sems.at[which, 2 * total + part],
+                )
+                for total in range(2)
+                for part in range(2)
+            ]
+
+        def last_work(which, carry):
+            @pl.when(which == 0)
             def _():
                 finish(row_sends[2])
                 finish(grad_sends[2])
 
-            stores = [
-                pltpu.make_async_copy(arrived, rows_out.at[spot, :], done_sems.at[1]),
-                pltpu.make_async_copy(arrived_grads, grads_out.at[spot, :], done_sems.at[2]),
-            ]
+            @pl.when(which == 1)
+            def _():
+                finish(row_sends[3])
+                finish(grad_sends[3])
+
+            here = pl.ds(pl.multiple_of(which * HALF, HALF), HALF)
+            at = pl.ds(pl.multiple_of((pieces - 1) * PIECE + which * HALF, HALF), HALF)
+            arrived, arrived_grads = rows.at[pieces - 1, here], grads.at[pieces - 1, here]
+            stores = row_stores(arrived, arrived_grads, at)
             begin(stores)
-            for which, (start, size) in enumerate(cuts):
-                at, second = slice(start, start + size), slice(main + start, main + start + size)
-
-                @pl.when(piece == 0)
-                def _(which=which):
-                    finish(weights[3 * which : 3 * which + 3])
-
-                part_a = straight(arrived[...], w_in[:, at])
-                part_b = straight(arrived[...], w_in[:, second])
-                grad_act = across(arrived_grads[...], w_out[at, :])
-                products(at, at, second, part_a, part_b, grad_act)
-
-            @pl.when(piece == 0)
-            def _():
-                finish(weights[6:])
-
-            if tail:
-                both = straight(arrived[...], w_in[:, 2 * main :])
-                grad_act = across(arrived_grads[...], w_out[main:, :])
-                products(
-                    slice(main, units),
-                    slice(2 * main, 2 * main + tail),
-                    slice(2 * main + tail, 2 * units),
-                    both[:, :tail],
-                    both[:, tail:],
-                    grad_act,
-                )
-            stores += [
-                pltpu.make_async_copy(act, act_out.at[spot, :], done_sems.at[3]),
-                pltpu.make_async_copy(parts, parts_out.at[spot, :], done_sems.at[4]),
-            ]
-            begin(stores[2:])
+            unit(arrived, arrived_grads, HALF, lambda start, stop: None)
+            more = unit_stores(HALF, at)
+            begin(more)
             for j in range(width // wide_tile):
-                at = slice(j * wide_tile, (j + 1) * wide_tile)
-
-                @pl.when(piece > 0)
-                def _(j=j):
-                    finish(sum_stores(piece - 1, j))
-
-                back = across(parts[...], w_in[at, :])
-                sums[0, :, at] = back[:HALF].astype(low)
-                sums[1, :, at] = back[HALF:].astype(low)
-                two = straight(act[...], w_out[:, at])
-                sums[2, :, at] = two[:HALF].astype(low)
-                sums[3, :, at] = two[HALF:].astype(low)
-                begin(sum_stores(piece, j))
+                tile = slice(j * wide_tile, (j + 1) * wide_tile)
+                sums[which, :, tile] = across(parts[:HALF], w_in[tile, :]).astype(low)
+                sums[2 + which, :, tile] = straight(act[:HALF], w_out[:, tile]).astype(low)
+            begin(last_stores(which))
             finish(stores)
+            finish(more)
             return carry
 
-        lax.fori_loop(0, pieces, work, 0)
-        for j in range(width // wide_tile):
-            finish(sum_stores(pieces - 1, j))
+        lax.fori_loop(0, 2, last_work, 0)
+        for which in range(2):
+            finish(last_stores(which))
         store_middle.wait()
 
     return pl.pallas_call(
@@ -1322,8 +1378,9 @@
             pltpu.SemaphoreType.DMA((9,)),
             pltpu.SemaphoreType.DMA((5,)),
             pltpu.SemaphoreType.DMA((width // wide_tile, 4)),
+            pltpu.SemaphoreType.DMA((2, 4)),
             pltpu.SemaphoreType.DMA((6, 2)),
-            pltpu.SemaphoreType.DMA((12, 2)),
+            pltpu.SemaphoreType.DMA((16, 2)),
         ],
         compiler_params=pltpu.CompilerParams(
             vmem_limit_bytes=VMEM, collective_id=3, has_side_effects=True
@@ -1333,7 +1390,7 @@
     )(gated, whole_weight, hidden, grads_own, grads_first, ffn_in, ffn_out, live)
 
 
-def mix_rows(hidden, cotangent, mix_weight, out_weight, live, keep):
+def mix_rows(hidden, cotangent, mix_weight, out_weight, seq_lengths, block_seq):
     local_rows, width = hidden.shape
     parts, _, columns = mix_weight.shape
     heads = columns // HS
@@ -1346,10 +1403,11 @@
     halves_at = (pl.ds(0, HALF), pl.ds(HALF, HALF))
 
     def body(*refs):
-        hidden_in, cot_in, mix_in, out_in, live_ref, keep_ref = refs[:6]
+        hidden_in, cot_in, mix_in, out_in, length_ref, owner_ref = refs[:6]
         rows_out, parts_out, gated_out, mixing_out, states_out, grads_out, first_out, whole_out = refs[6:14]
-        hidden_ref, cot_ref, rows, weights, parts_ref, gated_ref, mixing_ref, states_ref = refs[14:22]
-        load_sems, mix_sems, store_sems, parts_sems, gather_sems, slice_sems, line_sems, core_sems = refs[22:]
+        live_ref, keep_ref = refs[14:16]
+        hidden_ref, cot_ref, rows, weights, parts_ref, gated_ref, mixing_ref, states_ref = refs[16:24]
+        load_sems, mix_sems, store_sems, parts_sems, gather_sems, slice_sems, line_sems, core_sems = refs[24:]
         wide, narrow, z, core, mate, near_x, near_y = neighbours()
         far = (wide, 3 - narrow)
         above, below = (wide + 2, narrow), (wide - 2, narrow)
@@ -1479,6 +1537,22 @@
                 parts_ref[piece * PIECE : (piece + 1) * PIECE, at] = result
             begin(part_stores(piece))
 
+        def same_slot(block):
+            return owner_ref[block] == owner_ref[0]
+
+        first_count = sum(jnp.where(same_slot(block), 1, 0) for block in range(NBLK))
+
+        def start_of(block):
+            return jnp.where(same_slot(block), 0, first_count)
+
+        for block in range(NBLK):
+            entering = jnp.where(start_of(block) == block, 0.0, 1.0)
+            keep_ref[block : block + 1, :] = jnp.full((1, HS), entering, jnp.float32)
+        for at in range(local_rows // BLK):
+            block = narrow * (local_rows // BLK) + at
+            limit = jnp.where(same_slot(block), length_ref[0], length_ref[1])
+            place = lax.broadcasted_iota(jnp.int32, (BLK, HS), 0) + (block - start_of(block)) * BLK
+            live_ref[at * BLK : (at + 1) * BLK, :] = jnp.where(place < limit, 1.0, 0.0)
         project(0)
         load_cot.wait()
 
@@ -1556,8 +1630,8 @@
     low_shape = functools.partial(jax.ShapeDtypeStruct, dtype=low)
     return pl.pallas_call(
         body,
-        in_specs=any_specs(4) + [pl.BlockSpec(memory_space=pltpu.VMEM)] * 2,
-        out_specs=any_specs(8),
+        in_specs=any_specs(4) + [pl.BlockSpec(memory_space=pltpu.SMEM)] * 2,
+        out_specs=any_specs(8) + [pl.BlockSpec(memory_space=pltpu.VMEM)] * 2,
         out_shape=[
             low_shape((group_rows, width)),
             low_shape((parts, group_rows, columns)),
@@ -1567,6 +1641,8 @@
             low_shape((local_rows, width)),
             low_shape((local_rows, width)),
             low_shape((wide_size, pieces, slice_rows, width)),
+            jax.ShapeDtypeStruct((local_rows, HS), jnp.float32),
+            jax.ShapeDtypeStruct((NBLK, HS), jnp.float32),
         ],
         scratch_shapes=[
             pltpu.VMEM((local_rows, width), low),
@@ -1591,7 +1667,7 @@
         ),
         cost_estimate=cost(2 * group_rows * parts * width * columns, 50e6),
         name="mix_rows",
-    )(hidden, cotangent, mix_weight, out_weight, live, keep)
+    )(hidden, cotangent, mix_weight, out_weight, seq_lengths, block_seq)
 
 
 def finish_rows(
@@ -1708,17 +1784,10 @@
 def square_device(
     hidden, mix_weight, out_weight, ffn_in_weight, ffn_out_weight, seq_lengths, block_seq, cotangent
 ):
-    local_rows, width = hidden.shape
+    width = hidden.shape[1]
     units = ffn_out_weight.shape[0]
-    narrow_index = lax.axis_index("narrow")
-    valid_all, fresh_block = group_masks(seq_lengths, block_seq)
-    live = lax.dynamic_slice_in_dim(
-        valid_all.astype(jnp.float32), narrow_index * local_rows, local_rows
-    )[:, None]
-
-    keep = jnp.broadcast_to(jnp.where(fresh_block, 0.0, 1.0)[:, None], (NBLK, HS))
-    normed_all, parts, gated, mixing, states, grads_own, grads_first, whole_weight = mix_rows(
-        hidden, cotangent, mix_weight, out_weight, live, keep
+    normed_all, parts, gated, mixing, states, grads_own, grads_first, whole_weight, live, keep = mix_rows(
+        hidden, cotangent, mix_weight, out_weight, seq_lengths, block_seq
     )
     middle, normed_two_all, grad_two_all, act, grad_parts, back_sums, two_sums = gated_unit(
         gated,

time: 668 us -> 650 us (0.973)
  Pallas kernels: 651 us -> 640 us
    pallas_call x1, Pallas kernels: 163 us -> 151 us  [gated_unit(): pl.pallas_call(body, in_specs=any_specs(7) + [pl.BlockSpec(memory_space=p...]
where the time goes in v6:
time: 650 us; the launch traced here: 641 us
  Pallas kernels  640 us (98%)
    pallas_call x1, Pallas kernels, weight_grads(): pl.pallas_call(body, in_specs=any_specs(15) + [pl.BlockSpec(memory_space=...  344 us
    pallas_call x1, Pallas kernels, gated_unit(): pl.pallas_call(body, in_specs=any_specs(7) + [pl.BlockSpec(memory_space=p...  151 us
    pallas_call x1, Pallas kernels, mix_rows(): pl.pallas_call(body, in_specs=any_specs(4) + [pl.BlockSpec(memory_space=p...  109 us
    pallas_call x1, Pallas kernels, finish_rows(): pl.pallas_call(body, grid=(steps,), in_specs=[mix_spec, out_spec, rows_sp...  35.8 us

profile of v6, /device:TPU:0, one launch (start us, length us, event | category | flops | bytes accessed | tf_op | source)
XLA Modules:
  0.0 641.3 jit_solution(3238742937062593352)
XLA Ops:
  0.6 108.7 %mix_rows.1 = (bf16[2048,2048]{1,0:T(8,128)(2,1)}, bf16[4,2048,512]{2,1,0:T(8,128)(2,1)}, bf16[1,2048,512]{2,1,0:T(8,128)(2,1)}, bf16[2048,512]{1,0:T(8,128)(2,1...) custom-call(bf16[512,2048]{1,0:T(8,128)(2,1)} %hidden_ref.1, ...), custom_call_target="tpu_custom_call" | custom-call | flops 17179869184 | bytes 50000000 | tf_op jit(solution)/shard_map/mix_rows/pallas_call | solution.py:1631
  109.3 151.3 %gated_unit.1 = (f32[512,2048]{1,0:T(8,128)}, bf16[2048,2048]{1,0:T(8,128)(2,1)}, bf16[2048,2048]{1,0:T(8,128)(2,1)}, bf16[2048,1408]{1,0:T(8,128)(2,1)}, bf16[2...) custom-call(bf16[1,2048,512]{2,1,0:T(8,128)(2,1)} %get-tuple-element.44.refs_0_.refs_13_, ...), custom_call_target="tpu_custom_call" | custom-call | flops 70866960384 | bytes 90000000 | tf_op jit(solution)/shard_map/gated_unit/pallas_call | solution.py:1352
  260.7 344.4 %weight_grads.1 = (bf16[16,128,2816]{2,1,0:T(8,128)(2,1)}, bf16[11,128,2048]{2,1,0:T(8,128)(2,1)}, bf16[4,128,2048]{2,1,0:T(8,128)(2,1)}, bf16[64,128,512]{2,1,0...) custom-call(bf16[2048,1408]{1,0:T(8,128)(2,1)} %get-tuple-element.49, ...), custom_call_target="tpu_custom_call" | custom-call | flops 74088185856 | bytes 120000000 | tf_op jit(solution)/shard_map/weight_grads/pallas_call | solution.py:990
  605.1 35.8 %finish_rows.1 = (f32[4,2048,512]{2,1,0:T(8,128)}, f32[512,2048]{1,0:T(8,128)}, f32[2,2048,1408]{2,1,0:T(8,128)}, f32[1408,2048]{1,0:T(8,128)}, bf16[512,2048]{1,0:T(8,128)(2,1)}, /*index=5*/bf16[512,2048]{1,0:T(8,128)(2,1)}) custom-call(bf16[4,2048,512]{2,1,0:T(8,128)(2,1)} %bitcast.5, bf16[512,2048]{1,0:T(8,128)(2,1)} %bitcast.7, ...), custom_call_target="tpu_custom_call" | custom-call | flops 100000000 | bytes 110000000 | tf_op jit(solution)/shard_map/finish_rows/pallas_call | solution.py:1725

commit v7 on v6

--- a/solution.py
+++ b/solution.py
@@ -506,7 +506,7 @@
     return [block, block, pltpu.SemaphoreType.DMA((uses, 6, 2)), pltpu.SemaphoreType.DMA((uses, 2))]
 
 
-def square_sum(scratch, places, parts, landed, use):
+def square_sum(scratch, places, parts, landed, use, side=None):
     met, mid, sems, load_sems = scratch
     top_x, low_y, low_x, top_y, top_d, low_d = parts
     near_x, near_y = places[5:]
@@ -543,7 +543,8 @@
 
             def tile(i, carry, at=at):
                 rows = pl.ds(pl.multiple_of(i * 64, 64), 64)
-                mid[at, rows, :] = add_low(mid[at, rows, :], met[at, rows, :])
+                mine = mid[at, rows, :] if side is None else side[at][rows, :]
+                mid[at, rows, :] = add_low(mine, met[at, rows, :])
                 return carry
 
             lax.fori_loop(0, BLK // 64, tile, 0)
@@ -572,6 +573,7 @@
     states_all,
     gated,
     normed_all,
+    hidden,
     live,
     keep,
 ):
@@ -595,18 +597,16 @@
     def body(*refs):
         act_in, two_in, normed_two_in, parts_in, back_in, two_sums_in = refs[:6]
         middle_in, cot_in, weight_in, mix_in = refs[6:10]
-        all_in, mixing_in, states_in, gated_in, normed_in, live_ref, keep_ref = refs[10:17]
-        in_grad, out_grad, branch_grad, mix_grad, branch_out, middle_out = refs[17:23]
-        own_outs, last_landed, two_landed = refs[23:25], refs[25:29], refs[29:33]
-        shared, wide_ref, act_ref, landed, stage_ref, mid_ref, grad_ref, branch = refs[33:41]
-        near, gated_grad, states_ref = refs[41:44]
-        normed_sems, parts_sems, load_sems, stage_sems, gather_sems, back_sems, head_sems, mix_sems = refs[44:52]
-        tile_sems, own_sems = refs[52:54]
-        line, square = refs[54:63], refs[63:67]
-        mid = square[1]
+        all_in, mixing_in, states_in, gated_in, normed_in, hidden_in, live_ref, keep_ref = refs[10:18]
+        in_grad, out_grad, branch_grad, mix_grad, branch_out, middle_out, layer_out, input_out = refs[18:26]
+        last_landed, two_landed = refs[26:30], refs[30:34]
+        shared, wide_ref, act_ref, landed, stage_ref, mid_ref, grad_ref, branch = refs[34:42]
+        near, gated_grad, states_ref = refs[42:45]
+        normed_sems, parts_sems, load_sems, stage_sems, gather_sems, back_sems, head_sems, mix_sems = refs[45:53]
+        tile_sems, last_sems = refs[53:55]
+        line, square = refs[55:64], refs[64:68]
         places = neighbours()
         narrow, near_x, near_y = places[1], places[5], places[6]
-        enter(places)
 
         def block(at):
             return pl.ds(at * BLK, BLK)
@@ -683,10 +683,11 @@
                 for part in range(4):
                     own[part] = result[:, part * TILE : (part + 1) * TILE]
 
+            pl.when(k == first_branch - out_blocks + columns // SUB)(lambda: load_gated.start())
+            pl.when(k == first_branch - out_blocks + (columns + TILE) // SUB)(lambda: load_branch(0).start())
+
             @pl.when(k == first_branch)
             def _():
-                load_branch(0).start()
-                load_gated.start()
                 begin(load_normed[1:])
                 load_gated.wait()
 
@@ -749,6 +750,7 @@
         )
         load_normed_two(0).start()
         load_parts(0).start()
+        enter(places)
         open_sum()
         for at in range(1, in_columns):
             load_parts(at).start()
@@ -803,36 +805,22 @@
             spread(branch_out.at[block(3)], 7, 4, near_x),
             spread(branch_out.at[block(2)], 6, 5, near_y),
         ]
-        run(9)
-        join_sum()
-        begin(stage(0))
-        run(16)
-        close_sum()
-        finish(stage(0))
-        written = rows_back(0)
-        sends[0].start()
-        begin(stage(1))
-        finish(stage(1))
-        written.wait()
-        written = rows_back(1)
-        begin(sends[1:])
-        begin(keep_branch)
-        run(8)
-        sends[0].wait_recv()
-        sends[1].wait_recv()
-        begin(later)
-        run(17)
-        written.wait()
-        finish(keep_branch)
-        for copy in sends[:2]:
-            copy.wait_send()
-        finish(sends[2:])
-        finish(later)
-
-        open_two, join_two, close_two = square_sum(
-            square, places, [two_sums_in.at[block(at)] for at in range(2, 8)], two_landed, 1
-        )
-        open_two()
+        weight_loads = [
+            pltpu.make_async_copy(weight_in.at[block(at)], landed.at[at], back_sems.at[at])
+            for at in range(columns // BLK)
+        ]
+
+        def row_loads(slot):
+            return [
+                pltpu.make_async_copy(branch_out.at[block(slot + at)], stage_ref.at[at], back_sems.at[2 + at])
+                for at in range(2)
+            ]
+
+        def back_rows(slot, rows_ref):
+            for at in range(2):
+                for part in range(len(weight_loads)):
+                    result = across(rows_ref[at], landed[part]).astype(low)
+                    gated_grad[(slot + at) * BLK : (slot + at + 1) * BLK, part * BLK : (part + 1) * BLK] = result
 
         def head_loads(head):
             here = cols(head * HS, HS)
@@ -854,34 +842,56 @@
             loads.append(pltpu.make_async_copy(states_in.at[head], states_ref, head_sems.at[parts + 1]))
             return loads
 
-        weight_loads = [
-            pltpu.make_async_copy(weight_in.at[block(at)], landed.at[at], back_sems.at[at])
-            for at in range(columns // BLK)
-        ]
-
-        def row_load(at):
-            here = pl.ds(pl.multiple_of(at * BLK, BLK), BLK)
-            return pltpu.make_async_copy(branch_out.at[here], stage_ref.at[at % 2], back_sems.at[2 + at % 2])
-
+        open_two, join_two, close_two = square_sum(
+            square, places, [two_sums_in.at[block(at)] for at in range(2, 8)], two_landed, 1
+        )
+        run(9)
+        join_sum()
+        begin(stage(0))
+        run(16)
+        close_sum()
+        finish(stage(0))
+        written = rows_back(0)
+        sends[0].start()
+        begin(stage(1))
+        run(1)
+        finish(stage(1))
+        written.wait()
+        written = rows_back(1)
+        begin(sends[1:])
+        begin(keep_branch)
         begin(weight_loads)
-        row_load(0).start()
+        run(2)
+        finish(weight_loads)
+        back_rows(0, branch)
+        run(6)
+        for copy in sends[:2]:
+            copy.wait_recv()
+        begin(later)
+        begin(row_loads(2))
+        run(1)
+        finish(row_loads(2))
+        back_rows(2, stage_ref)
+        run(7)
+        for copy in sends[2:]:
+            copy.wait_recv()
+        begin(row_loads(4))
+        run(1)
+        finish(row_loads(4))
+        back_rows(4, stage_ref)
+        run(8)
         begin(head_loads(0))
-        finish(weight_loads)
-        back_from = now[0]
-
-        def back_block(at, carry):
-            step(back_from + at, 0)
-            row_load(at).wait()
-            pl.when(at + 1 < rows // BLK)(lambda: row_load(at + 1).start())
-            here = pl.ds(pl.multiple_of(at * BLK, BLK), BLK)
-            for part in range(len(weight_loads)):
-                result = across(stage_ref[at % 2], landed[part])
-                gated_grad[here, part * BLK : (part + 1) * BLK] = result.astype(low)
-            return carry
-
-        lax.fori_loop(0, rows // BLK, back_block, 0)
-        now[0] += rows // BLK
-        join_two()
+        for copy in later:
+            copy.wait_recv()
+        begin(row_loads(6))
+        run(1)
+        finish(row_loads(6))
+        back_rows(6, stage_ref)
+        written.wait()
+        finish(keep_branch)
+        for copy in sends + later:
+            copy.wait_send()
+        open_two()
 
         def load_mix(at):
             here = pl.ds(pl.multiple_of(at * BLK, BLK), BLK)
@@ -896,11 +906,13 @@
         for at in range(4):
             begin(load_mix(at))
         attend_from = now[0]
+        breaks = (2, 5, NBLK - 1)
 
         def attend(head, carry):
             rate = head_rate(heads * narrow + head)
             within, entry, leave, whole = block_decays(rate)
             finish(head_loads(head))
+            pl.when(head == heads - 1)(join_two)
             later_grad = jnp.zeros((HS, HS), jnp.float32)
             base = parts * columns
             for at in range(NBLK):
@@ -939,49 +951,117 @@
                 store(0, grad_queries * silu_slope(raw_queries))
                 store(1, grad_keys * silu_slope(raw_keys))
                 store(2, grad_values)
-                if at % 2:
-                    step(attend_from + head * (NBLK // 2) + at // 2, 0)
-            pl.when(head + 1 < heads)(lambda: begin(head_loads(head + 1)))
+                if at == NBLK - 1:
+                    pl.when(head + 1 < heads)(lambda: begin(head_loads(head + 1)))
+                if at in breaks:
+                    step(attend_from + head * len(breaks) + breaks.index(at), 0)
             return carry
 
         lax.fori_loop(0, heads, attend, 0)
-        now[0] += heads * (NBLK // 2)
+        now[0] += heads * len(breaks)
 
         sum_from = now[0]
-        outs = ((3, branch, False), (1, near, False), (2, mid, True), (0, stage_ref, False))
+        side = (mid_ref, grad_ref)
+
+        def put(pair):
+            def store(at, here, value):
+                pair[at, :, here] = value
+
+            return store
+
+        def put_side(at, here, value):
+            side[1 - at][:, here] = value.astype(jnp.float32)
+
+        outs = ((3, put(branch)), (1, put(near)), (2, put_side), (0, put(stage_ref)))
 
         def sum_tile(at, carry):
             finish(load_mix(at))
             here = cols(at * BLK, BLK)
-            for piece, out, swapped in outs:
+            for which, (piece, store) in enumerate(outs):
                 acts = wide_ref[piece * PIECE : (piece + 1) * PIECE, : parts * columns]
                 total = across(acts, landed[at % 4]).astype(low)
-                out[int(swapped), :, here] = total[:HALF]
-                out[1 - int(swapped), :, here] = total[HALF:]
-            pl.when(at + 4 < width // BLK)(lambda: begin(load_mix(at + 4)))
-            step(sum_from + at, 0)
+                store(0, here, total[:HALF])
+                store(1, here, total[HALF:])
+                if which == 3:
+                    pl.when(at + 4 < width // BLK)(lambda: begin(load_mix(at + 4)))
+                if which % 2:
+                    step(sum_from + 2 * at + which // 2, 0)
             return carry
 
-        close_two()
         lax.fori_loop(0, width // BLK, sum_tile, 0)
-        now[0] += width // BLK
+        now[0] += 2 * (width // BLK)
         open_last, join_last, close_last = square_sum(
             square,
             places,
             (near.at[0], near.at[1], None, None, branch.at[0], branch.at[1]),
             last_landed,
             2,
+            side,
         )
-        own_stores = [
-            pltpu.make_async_copy(stage_ref.at[at], own_outs[at], own_sems.at[at]) for at in range(2)
-        ]
+        close_two()
         open_last()
-        begin(own_stores)
         run(9)
         join_last()
+
+        def block_loads(half, terms, floats):
+            loads = [
+                pltpu.make_async_copy(src, landed.at[at], last_sems.at[at]) for at, src in enumerate(terms)
+            ]
+            loads.append(pltpu.make_async_copy(floats.at[block(half)], mid_ref, last_sems.at[3]))
+            return loads
+
+        def block_store(half, out):
+            return pltpu.make_async_copy(landed.at[3], out.at[block(half)], last_sems.at[4])
+
+        def layer_loads(half):
+            terms = (two_sums_in.at[block(half)], two_landed[half], two_landed[2 + half])
+            return block_loads(half, terms, middle_in)
+
+        def input_loads(half):
+            terms = (last_landed[half], last_landed[2 + half], hidden_in.at[block(half)])
+            return block_loads(half, terms, middle_out)
+
+        def layer_tile(i, carry, half):
+            at = pl.ds(pl.multiple_of(i * 32, 32), 32)
+            live_at = pl.ds(pl.multiple_of(half * BLK + i * 32, 32), 32)
+            branch_two = add_rows(landed[0, at, :], landed[1, at, :], landed[2, at, :])
+            landed[3, at, :] = (mid_ref[at, :] + live_ref[live_at, :1] * branch_two).astype(low)
+            return carry
+
+        def input_tile(i, carry, half):
+            at = pl.ds(pl.multiple_of(i * 32, 32), 32)
+            grad_normed = add_rows(stage_ref[half, at, :], landed[0, at, :], landed[1, at, :])
+            back = norm_back(landed[2, at, :].astype(jnp.float32), grad_normed)
+            landed[3, at, :] = (mid_ref[at, :] + back).astype(low)
+            return carry
+
+        def rows_out(loads, tile, out):
+            tiles = BLK // 32 // 4
+            for half in range(2):
+                begin(loads(half))
+                run(1)
+                finish(loads(half))
+                if half:
+                    block_store(0, out).wait()
+                base = now[0]
+
+                def part(at, carry, half=half, base=base):
+                    for one in range(tiles):
+                        tile(tiles * at + one, 0, half)
+                    step(base + at, 0)
+                    return carry
+
+                lax.fori_loop(0, 4, part, 0)
+                now[0] += 4
+                block_store(half, out).start()
+
+        rows_out(layer_loads, layer_tile, layer_out)
+        run(first_mix + 31 - now[0])
+        block_store(1, layer_out).wait()
+        close_last()
+        rows_out(input_loads, input_tile, input_out)
         run(count + STAGES - now[0])
-        close_last()
-        finish(own_stores)
+        block_store(1, input_out).wait()
 
     def low_shape(*shape):
         return jax.ShapeDtypeStruct(shape, low)
@@ -989,7 +1069,7 @@
     sem = pltpu.SemaphoreType.DMA
     return pl.pallas_call(
         body,
-        in_specs=any_specs(15) + [pl.BlockSpec(memory_space=pltpu.VMEM)] * 2,
+        in_specs=any_specs(16) + [pl.BlockSpec(memory_space=pltpu.VMEM)] * 2,
         out_specs=any_specs(16),
         out_shape=[
             low_shape(width // SUB, SUB, grad_parts.shape[1]),
@@ -998,8 +1078,10 @@
             low_shape(parts * width // SUB, SUB, columns),
             low_shape(rows, width),
             jax.ShapeDtypeStruct((local_rows, width), jnp.float32),
+            low_shape(local_rows, width),
+            low_shape(local_rows, width),
         ]
-        + [low_shape(BLK, width)] * 10,
+        + [low_shape(BLK, width)] * 8,
         scratch_shapes=[
             pltpu.VMEM((rows, width), low),
             pltpu.VMEM(grad_parts.shape, low),
@@ -1021,7 +1103,7 @@
             sem((parts + 2,)),
             sem((4, parts)),
             sem((2,)),
-            sem((2,)),
+            sem((5,)),
         ]
         + line_scratch()
         + square_scratch(3),
@@ -1046,6 +1128,7 @@
         states_all,
         gated,
         normed_all,
+        hidden,
         live,
         keep,
     )
@@ -1075,11 +1158,6 @@
         load_sems, slice_sems, weight_sems, done_sems, sum_sems, last_sems, gated_sems, gather_sems = refs[25:]
         wide, narrow, _, _, _, near_x, near_y = neighbours()
         far = (wide, 3 - narrow)
-        barrier = pltpu.get_barrier_semaphore()
-        for place in (near_x, near_y, far):
-            pl.semaphore_signal(barrier, inc=1, device_id=place, device_id_type=MESH)
-        pl.semaphore_wait(barrier, 3)
-
         here = pl.ds(pl.multiple_of(narrow * deep, deep), deep)
 
         def send_gated(slot, to, kind, place):
@@ -1174,11 +1252,14 @@
         row_sends = gather(rows, 0)
         grad_sends = gather(grads, 8)
 
+        begin(load_grads)
+        begin([keep_gated, load_hidden])
+        barrier = pltpu.get_barrier_semaphore()
+        for place in (near_x, near_y, far):
+            pl.semaphore_signal(barrier, inc=1, device_id=place, device_id_type=MESH)
+        pl.semaphore_wait(barrier, 3)
         begin(gated_sends)
-        begin([keep_gated])
         lax.fori_loop(0, slices * quarters, start_slice, 0)
-        begin(load_grads)
-        begin([load_hidden])
         finish(load_grads)
         begin(grad_sends[1])
         finish([keep_gated, load_hidden])
@@ -1670,25 +1751,16 @@
     )(hidden, cotangent, mix_weight, out_weight, seq_lengths, block_seq)
 
 
-def finish_rows(
-    mix_low, out_low, in_low, wide_low, hidden, middle, grad_middle, live, normed_terms, two_sums, two_terms
-):
+def widen(mix_low, out_low, in_low, wide_low, rows):
     parts, width, columns = mix_low.shape
-    local_rows = hidden.shape[0]
     units = wide_low.shape[0]
     main = units // TILE * TILE
     tail = units - main
     steps = 2 * parts
-    tile, out_tile = local_rows // steps, out_low.shape[0] // steps
-    in_tile, unit_tile, mix_tile = width // steps, units // steps, width // 2
-    half_steps = steps // 2
-    terms = len(normed_terms) + len(two_terms)
-
-    def body(
-        mix_ref, out_ref, in_ref, wide_ref, hidden_ref, middle_ref, grad_ref, live_ref, own_ref, *refs
-    ):
-        term_refs = refs[:terms]
-        mix_out, out_out, in_out, wide_out, layer_ref, input_ref = refs[terms:]
+
+    def body(mix_ref, out_ref, in_ref, wide_ref, one_ref, two_ref, mix_out, out_out, in_out, wide_out, one_out, two_out):
+        one_out[...] = one_ref[...]
+        two_out[...] = two_ref[...]
         mix_out[...] = mix_ref[...].astype(jnp.float32)
         out_out[...] = out_ref[...].astype(jnp.float32)
         wide_out[...] = wide_ref[...].astype(jnp.float32)
@@ -1697,70 +1769,28 @@
             rest = slice(2 * main + c * tail, 2 * main + (c + 1) * tail)
             in_out[c, :, main:] = in_ref[:, rest].astype(jnp.float32)
 
-        def rows_of(half):
-            normed = add_rows(*(ref[...] for ref in term_refs[3 * half : 3 * half + 3]))
-            two = add_rows(*(ref[...] for ref in term_refs[6 + 2 * half : 8 + 2 * half]), own_ref[...])
-            layer = middle_ref[...] + live_ref[:, :1] * two
-            layer_ref[...] = layer.astype(jnp.bfloat16)
-            back = norm_back(hidden_ref[...].astype(jnp.float32), normed)
-            input_ref[...] = (grad_ref[...] + back).astype(jnp.bfloat16)
-
-        first = pl.program_id(0) < half_steps
-        pl.when(first)(lambda: rows_of(0))
-        pl.when(jnp.logical_not(first))(lambda: rows_of(1))
-
-    def rows_spec(size, height=tile):
-        return pl.BlockSpec((height, size), lambda i: (i, 0))
-
-    def half_spec(half):
-        if half == 0:
-            return pl.BlockSpec((tile, width), lambda i: (jnp.minimum(i, half_steps - 1), 0))
-        return pl.BlockSpec((tile, width), lambda i: (jnp.maximum(i - half_steps, 0), 0))
-
-    term_specs = [half_spec(0)] * 3 + [half_spec(1)] * 3 + [half_spec(0)] * 2 + [half_spec(1)] * 2
-    mix_spec = pl.BlockSpec((1, mix_tile, columns), lambda i: (i // 2, i % 2, 0))
-    out_spec = rows_spec(width, out_tile)
-    wide_spec = rows_spec(width, unit_tile)
-    wide_float = jnp.float32
+    def rows_spec(array):
+        return pl.BlockSpec((array.shape[0] // steps, array.shape[1]), lambda i: (i, 0))
+
+    mix_spec = pl.BlockSpec((1, width // 2, columns), lambda i: (i // 2, i % 2, 0))
+    shapes = (mix_low.shape, out_low.shape, (2, width, units), wide_low.shape)
     return pl.pallas_call(
         body,
         grid=(steps,),
-        in_specs=[mix_spec, out_spec, rows_spec(2 * units, in_tile), wide_spec]
-        + [rows_spec(width)] * 3
-        + [rows_spec(live.shape[1]), rows_spec(width)]
-        + term_specs,
+        in_specs=[mix_spec] + [rows_spec(array) for array in (out_low, in_low, wide_low, *rows)],
         out_specs=[
             mix_spec,
-            out_spec,
-            pl.BlockSpec((2, in_tile, units), lambda i: (0, i, 0)),
-            wide_spec,
-            rows_spec(width),
-            rows_spec(width),
+            rows_spec(out_low),
+            pl.BlockSpec((2, width // steps, units), lambda i: (0, i, 0)),
+            rows_spec(wide_low),
+            *(rows_spec(array) for array in rows),
         ],
-        out_shape=[
-            jax.ShapeDtypeStruct(mix_low.shape, wide_float),
-            jax.ShapeDtypeStruct(out_low.shape, wide_float),
-            jax.ShapeDtypeStruct((2, width, units), wide_float),
-            jax.ShapeDtypeStruct(wide_low.shape, wide_float),
-            jax.ShapeDtypeStruct(hidden.shape, jnp.bfloat16),
-            jax.ShapeDtypeStruct(hidden.shape, jnp.bfloat16),
-        ],
+        out_shape=[jax.ShapeDtypeStruct(shape, jnp.float32) for shape in shapes]
+        + [jax.ShapeDtypeStruct(array.shape, array.dtype) for array in rows],
         compiler_params=pltpu.CompilerParams(vmem_limit_bytes=VMEM),
-        cost_estimate=cost(1e8, 110e6),
-        name="finish_rows",
-    )(
-        mix_low,
-        out_low,
-        in_low,
-        wide_low,
-        hidden,
-        middle,
-        grad_middle,
-        live,
-        two_sums,
-        *normed_terms,
-        *two_terms,
-    )
+        cost_estimate=cost(1e8, 84e6),
+        name="widen",
+    )(mix_low, out_low, in_low, wide_low, *rows)
 
 
 def block_decays(rate):
@@ -1799,7 +1829,7 @@
         ffn_in_weight,
         ffn_out_weight,
     )
-    in_low, wide_low, out_low, mix_low, _, grad_middle, own_top, own_low, *terms = weight_grads(
+    in_low, wide_low, out_low, mix_low, _, _, layer_out, input_grad, *_ = weight_grads(
         act,
         grad_two_all,
         normed_two_all,
@@ -1815,21 +1845,16 @@
         states,
         gated,
         normed_all,
+        hidden,
         live,
         keep,
     )
-    grad_mix, grad_out, grad_ffn_in, grad_ffn_out, layer_out, input_grad = finish_rows(
+    grad_mix, grad_out, grad_ffn_in, grad_ffn_out, layer_out, input_grad = widen(
         mix_low.reshape(mix_weight.shape),
         out_low.reshape(out_weight.shape),
         in_low.reshape(width, 2 * units),
         wide_low.reshape(units, width),
-        hidden,
-        middle,
-        grad_middle,
-        live,
-        (own_top, terms[0], terms[2], own_low, terms[1], terms[3]),
-        two_sums,
-        (terms[4], terms[6], terms[5], terms[7]),
+        (layer_out, input_grad),
     )
     return (layer_out, input_grad, grad_mix, grad_out, grad_ffn_in, grad_ffn_out)
 

time: 650 us -> 637 us (0.980)
  Pallas kernels: 640 us -> 628 us
    pallas_call x2, Pallas kernels: 380 us -> 368 us  [the longest x1 337 us: weight_grads(): pl.pallas_call(body, in_specs=any_specs(16) + [pl.BlockSpec(memory_space=...]
where the time goes in v7:
time: 637 us; the launch traced here: 629 us
  Pallas kernels  628 us (99%)
    pallas_call x1, Pallas kernels, weight_grads(): pl.pallas_call(body, in_specs=any_specs(16) + [pl.BlockSpec(memory_space=...  337 us
    pallas_call x1, Pallas kernels, gated_unit(): pl.pallas_call(body, in_specs=any_specs(7) + [pl.BlockSpec(memory_space=p...  151 us
    pallas_call x1, Pallas kernels, mix_rows(): pl.pallas_call(body, in_specs=any_specs(4) + [pl.BlockSpec(memory_space=p...  109 us
    pallas_call x1, Pallas kernels, widen(): pl.pallas_call(body, grid=(steps,), in_specs=[mix_spec] + [rows_spec(arra...  30.8 us

profile of v7, /device:TPU:0, one launch (start us, length us, event | category | flops | bytes accessed | tf_op | source)
XLA Modules:
  0.0 628.9 jit_solution(12912539174623026980)
XLA Ops:
  0.6 108.7 %mix_rows.1 = (bf16[2048,2048]{1,0:T(8,128)(2,1)}, bf16[4,2048,512]{2,1,0:T(8,128)(2,1)}, bf16[1,2048,512]{2,1,0:T(8,128)(2,1)}, bf16[2048,512]{1,0:T(8,128)(2,1...) custom-call(bf16[512,2048]{1,0:T(8,128)(2,1)} %refs_15_.1, ...), custom_call_target="tpu_custom_call" | custom-call | flops 17179869184 | bytes 50000000 | tf_op jit(solution)/shard_map/mix_rows/pallas_call | solution.py:1712
  109.3 151.3 %gated_unit.1 = (f32[512,2048]{1,0:T(8,128)}, bf16[2048,2048]{1,0:T(8,128)(2,1)}, bf16[2048,2048]{1,0:T(8,128)(2,1)}, bf16[2048,1408]{1,0:T(8,128)(2,1)}, bf16[2...) custom-call(bf16[1,2048,512]{2,1,0:T(8,128)(2,1)} %get-tuple-element.35.refs_0_.refs_13_, ...), custom_call_target="tpu_custom_call" | custom-call | flops 70866960384 | bytes 90000000 | tf_op jit(solution)/shard_map/gated_unit/pallas_call | solution.py:1433
  260.6 337.3 %weight_grads.1 = (bf16[16,128,2816]{2,1,0:T(8,128)(2,1)}, bf16[11,128,2048]{2,1,0:T(8,128)(2,1)}, bf16[4,128,2048]{2,1,0:T(8,128)(2,1)}, bf16[64,128,512]{2,1,0...) custom-call(bf16[2048,1408]{1,0:T(8,128)(2,1)} %get-tuple-element.40, ...), custom_call_target="tpu_custom_call" | custom-call | flops 74088185856 | bytes 120000000 | tf_op jit(solution)/shard_map/weight_grads/pallas_call | solution.py:1070
  597.9 30.8 %widen.1 = (f32[4,2048,512]{2,1,0:T(8,128)}, f32[512,2048]{1,0:T(8,128)}, f32[2,2048,1408]{2,1,0:T(8,128)}, f32[1408,2048]{1,0:T(8,128)}, bf16[512,2048]{1,0:T(8,128)(2,1)}, /*index=5*/bf16[512,2048]{1,0:T(8,128)(2,1)}) custom-call(bf16[4,2048,512]{2,1,0:T(8,128)(2,1)} %bitcast.5, bf16[512,2048]{1,0:T(8,128)(2,1)} %bitcast.7, bf16[2048,2816]{1,0:T(8,128)(2,1)} %bitcast.4, ...), custom_call_target="tpu_custom_call" | custom-call | flops 100000000 | bytes 84000000 | tf_op jit(solution)/shard_map/widen/pallas_call | solution.py:1777

commit v8 on v7

--- a/solution.py
+++ b/solution.py
@@ -405,6 +405,9 @@
     def core_two(s):
         return remote(full.at[s], other.at[s], 6, s, mate)
 
+    def landing(ref, kind, slot):
+        return remote(ref, ref, kind, slot, mate)
+
     def add(left, right):
         return (left.astype(jnp.float32) + right.astype(jnp.float32)).astype(jnp.bfloat16)
 
@@ -428,7 +431,7 @@
     def ends(k, s):
         @pl.when(middle)
         def _():
-            line_one(s).wait_recv()
+            landing(ended.at[s], 1, s).wait_recv()
             both[s] = add(both[s], ended[s])
             cross_one(s).start()
 
@@ -449,8 +452,8 @@
     def back(k, s):
         @pl.when(end)
         def _():
-            out_one(s).wait_recv()
-            out_two(s).wait_recv()
+            landing(full.at[s, region], 4, s).wait_recv()
+            landing(full.at[s, 1 - region], 5, s).wait_recv()
 
         core_two(s).start()
 
@@ -1154,8 +1157,8 @@
         in_ref, out_ref, live_ref = refs[5:8]
         middle_out, rows_out, grads_out, act_out, parts_out, back_out, two_out = refs[8:15]
         gated_ref, hidden_ref, middle_ref = refs[15:18]
-        rows, grads, sums, w_in, w_out, act, parts = refs[18:25]
-        load_sems, slice_sems, weight_sems, done_sems, sum_sems, last_sems, gated_sems, gather_sems = refs[25:]
+        rows, grads, sums, w_in, w_out, act, parts, held = refs[18:26]
+        load_sems, slice_sems, weight_sems, done_sems, sum_sems, last_sems, gated_sems, gather_sems = refs[26:]
         wide, narrow, _, _, _, near_x, near_y = neighbours()
         far = (wide, 3 - narrow)
         here = pl.ds(pl.multiple_of(narrow * deep, deep), deep)
@@ -1398,28 +1401,40 @@
             ]
 
         def last_work(which, carry):
-            @pl.when(which == 0)
-            def _():
-                finish(row_sends[2])
-                finish(grad_sends[2])
-
-            @pl.when(which == 1)
-            def _():
-                finish(row_sends[3])
-                finish(grad_sends[3])
-
             here = pl.ds(pl.multiple_of(which * HALF, HALF), HALF)
             at = pl.ds(pl.multiple_of((pieces - 1) * PIECE + which * HALF, HALF), HALF)
             arrived, arrived_grads = rows.at[pieces - 1, here], grads.at[pieces - 1, here]
+            pl.when(which == 0)(lambda: finish(row_sends[2]))
+            pl.when(which == 1)(lambda: finish(row_sends[3]))
+            held[...] = straight(arrived[...], w_in[...])
+
+            def columns_of(start, stop):
+                first, second = slice(start, stop), slice(main + start, main + stop)
+                if start == main:
+                    first, second = slice(2 * main, 2 * main + tail), slice(2 * main + tail, 2 * units)
+                return first, second
+
+            ranges = ((0, main), (main, units)) if tail else ((0, main),)
+            for start, stop in ranges:
+                first, second = columns_of(start, stop)
+                act[:HALF, start:stop] = (held[:, first] * held[:, second]).astype(low)
+            for j in range(width // wide_tile):
+                tile = slice(j * wide_tile, (j + 1) * wide_tile)
+                sums[2 + which, :, tile] = straight(act[:HALF], w_out[:, tile]).astype(low)
+            pl.when(which == 0)(lambda: finish(grad_sends[2]))
+            pl.when(which == 1)(lambda: finish(grad_sends[3]))
             stores = row_stores(arrived, arrived_grads, at)
             begin(stores)
-            unit(arrived, arrived_grads, HALF, lambda start, stop: None)
+            for start, stop in ranges:
+                first, second = columns_of(start, stop)
+                grad_act = across(arrived_grads[...], w_out[start:stop, :])
+                parts[:HALF, first] = (grad_act * held[:, second]).astype(low)
+                parts[:HALF, second] = (grad_act * held[:, first]).astype(low)
             more = unit_stores(HALF, at)
             begin(more)
             for j in range(width // wide_tile):
                 tile = slice(j * wide_tile, (j + 1) * wide_tile)
                 sums[which, :, tile] = across(parts[:HALF], w_in[tile, :]).astype(low)
-                sums[2 + which, :, tile] = straight(act[:HALF], w_out[:, tile]).astype(low)
             begin(last_stores(which))
             finish(stores)
             finish(more)
@@ -1454,6 +1469,7 @@
             pltpu.VMEM((units, width), low),
             pltpu.VMEM((PIECE, units), low),
             pltpu.VMEM((PIECE, 2 * units), low),
+            pltpu.VMEM((HALF, 2 * units), jnp.float32),
             pltpu.SemaphoreType.DMA((4,)),
             pltpu.SemaphoreType.DMA((slices * quarters,)),
             pltpu.SemaphoreType.DMA((9,)),
@@ -1552,12 +1568,14 @@
         def take_hop(hop):
             @pl.when(z >= hop)
             def _():
-                up(hop).wait_recv()
+                arrived = whole_out.at[wide - 2 * hop]
+                remote(arrived, arrived, line_sems, hop - 1, mate).wait_recv()
                 to_mate(hop, -1).start()
 
             @pl.when(z + hop <= 3)
             def _():
-                down_line(hop).wait_recv()
+                arrived = whole_out.at[wide + 2 * hop]
+                remote(arrived, arrived, line_sems, 2 + hop, mate).wait_recv()
                 to_mate(hop, 1).start()
 
         def end_hop(hop):

time: 637 us -> 634 us (level)
  no operation moved by 1% of the time
where the time goes in v8:
time: 634 us; the launch traced here: 627 us
  Pallas kernels  626 us (99%)
    pallas_call x1, Pallas kernels, weight_grads(): pl.pallas_call(body, in_specs=any_specs(16) + [pl.BlockSpec(memory_space=...  337 us
    pallas_call x1, Pallas kernels, gated_unit(): pl.pallas_call(body, in_specs=any_specs(7) + [pl.BlockSpec(memory_space=p...  150 us
    pallas_call x1, Pallas kernels, mix_rows(): pl.pallas_call(body, in_specs=any_specs(4) + [pl.BlockSpec(memory_space=p...  109 us
    pallas_call x1, Pallas kernels, widen(): pl.pallas_call(body, grid=(steps,), in_specs=[mix_spec] + [rows_spec(arra...  30.8 us

profile of v8, /device:TPU:0, one launch (start us, length us, event | category | flops | bytes accessed | tf_op | source)
XLA Modules:
  0.0 627.3 jit_solution(2593314529461003284)
XLA Ops:
  0.6 108.7 %mix_rows.1 = (bf16[2048,2048]{1,0:T(8,128)(2,1)}, bf16[4,2048,512]{2,1,0:T(8,128)(2,1)}, bf16[1,2048,512]{2,1,0:T(8,128)(2,1)}, bf16[2048,512]{1,0:T(8,128)(2,1...) custom-call(bf16[512,2048]{1,0:T(8,128)(2,1)} %refs_15_.1, ...), custom_call_target="tpu_custom_call" | custom-call | flops 17179869184 | bytes 50000000 | tf_op jit(solution)/shard_map/mix_rows/pallas_call | solution.py:1730
  109.3 150.4 %gated_unit.1 = (f32[512,2048]{1,0:T(8,128)}, bf16[2048,2048]{1,0:T(8,128)(2,1)}, bf16[2048,2048]{1,0:T(8,128)(2,1)}, bf16[2048,1408]{1,0:T(8,128)(2,1)}, bf16[2...) custom-call(bf16[1,2048,512]{2,1,0:T(8,128)(2,1)} %get-tuple-element.35.refs_0_.refs_13_, ...), custom_call_target="tpu_custom_call" | custom-call | flops 70866960384 | bytes 90000000 | tf_op jit(solution)/shard_map/gated_unit/pallas_call | solution.py:1448
  259.7 336.6 %weight_grads.1 = (bf16[16,128,2816]{2,1,0:T(8,128)(2,1)}, bf16[11,128,2048]{2,1,0:T(8,128)(2,1)}, bf16[4,128,2048]{2,1,0:T(8,128)(2,1)}, bf16[64,128,512]{2,1,0...) custom-call(bf16[2048,1408]{1,0:T(8,128)(2,1)} %get-tuple-element.40, ...), custom_call_target="tpu_custom_call" | custom-call | flops 74088185856 | bytes 120000000 | tf_op jit(solution)/shard_map/weight_grads/pallas_call | solution.py:1073
  596.3 30.8 %widen.1 = (f32[4,2048,512]{2,1,0:T(8,128)}, f32[512,2048]{1,0:T(8,128)}, f32[2,2048,1408]{2,1,0:T(8,128)}, f32[1408,2048]{1,0:T(8,128)}, bf16[512,2048]{1,0:T(8,128)(2,1)}, /*index=5*/bf16[512,2048]{1,0:T(8,128)(2,1)}) custom-call(bf16[4,2048,512]{2,1,0:T(8,128)(2,1)} %bitcast.5, bf16[512,2048]{1,0:T(8,128)(2,1)} %bitcast.7, bf16[2048,2816]{1,0:T(8,128)(2,1)} %bitcast.4, ...), custom_call_target="tpu_custom_call" | custom-call | flops 100000000 | bytes 84000000 | tf_op jit(solution)/shard_map/widen/pallas_call | solution.py:1795

commit v9 on v8

--- a/solution.py
+++ b/solution.py
@@ -1774,7 +1774,7 @@
     units = wide_low.shape[0]
     main = units // TILE * TILE
     tail = units - main
-    steps = 2 * parts
+    steps = parts
 
     def body(mix_ref, out_ref, in_ref, wide_ref, one_ref, two_ref, mix_out, out_out, in_out, wide_out, one_out, two_out):
         one_out[...] = one_ref[...]
@@ -1790,7 +1790,7 @@
     def rows_spec(array):
         return pl.BlockSpec((array.shape[0] // steps, array.shape[1]), lambda i: (i, 0))
 
-    mix_spec = pl.BlockSpec((1, width // 2, columns), lambda i: (i // 2, i % 2, 0))
+    mix_spec = pl.BlockSpec((1, width, columns), lambda i: (i, 0, 0))
     shapes = (mix_low.shape, out_low.shape, (2, width, units), wide_low.shape)
     return pl.pallas_call(
         body,

time: 634 us -> 632 us (level)
  no operation moved by 1% of the time
where the time goes in v9:
time: 632 us; the launch traced here: 625 us
  Pallas kernels  624 us (99%)
    pallas_call x1, Pallas kernels, weight_grads(): pl.pallas_call(body, in_specs=any_specs(16) + [pl.BlockSpec(memory_space=...  337 us
    pallas_call x1, Pallas kernels, gated_unit(): pl.pallas_call(body, in_specs=any_specs(7) + [pl.BlockSpec(memory_space=p...  150 us
    pallas_call x1, Pallas kernels, mix_rows(): pl.pallas_call(body, in_specs=any_specs(4) + [pl.BlockSpec(memory_space=p...  109 us
    pallas_call x1, Pallas kernels, widen(): pl.pallas_call(body, grid=(steps,), in_specs=[mix_spec] + [rows_spec(arra...  28.4 us

profile of v9, /device:TPU:0, one launch (start us, length us, event | category | flops | bytes accessed | tf_op | source)
XLA Modules:
  0.0 624.9 jit_solution(2455792239096168165)
XLA Ops:
  0.6 108.7 %mix_rows.1 = (bf16[2048,2048]{1,0:T(8,128)(2,1)}, bf16[4,2048,512]{2,1,0:T(8,128)(2,1)}, bf16[1,2048,512]{2,1,0:T(8,128)(2,1)}, bf16[2048,512]{1,0:T(8,128)(2,1...) custom-call(bf16[512,2048]{1,0:T(8,128)(2,1)} %refs_15_.1, ...), custom_call_target="tpu_custom_call" | custom-call | flops 17179869184 | bytes 50000000 | tf_op jit(solution)/shard_map/mix_rows/pallas_call | solution.py:1730
  109.3 150.4 %gated_unit.1 = (f32[512,2048]{1,0:T(8,128)}, bf16[2048,2048]{1,0:T(8,128)(2,1)}, bf16[2048,2048]{1,0:T(8,128)(2,1)}, bf16[2048,1408]{1,0:T(8,128)(2,1)}, bf16[2...) custom-call(bf16[1,2048,512]{2,1,0:T(8,128)(2,1)} %get-tuple-element.35.refs_0_.refs_13_, ...), custom_call_target="tpu_custom_call" | custom-call | flops 70866960384 | bytes 90000000 | tf_op jit(solution)/shard_map/gated_unit/pallas_call | solution.py:1448
  259.7 336.6 %weight_grads.1 = (bf16[16,128,2816]{2,1,0:T(8,128)(2,1)}, bf16[11,128,2048]{2,1,0:T(8,128)(2,1)}, bf16[4,128,2048]{2,1,0:T(8,128)(2,1)}, bf16[64,128,512]{2,1,0...) custom-call(bf16[2048,1408]{1,0:T(8,128)(2,1)} %get-tuple-element.40, ...), custom_call_target="tpu_custom_call" | custom-call | flops 74088185856 | bytes 120000000 | tf_op jit(solution)/shard_map/weight_grads/pallas_call | solution.py:1073
  596.3 28.4 %widen.1 = (f32[4,2048,512]{2,1,0:T(8,128)}, f32[512,2048]{1,0:T(8,128)}, f32[2,2048,1408]{2,1,0:T(8,128)}, f32[1408,2048]{1,0:T(8,128)}, bf16[512,2048]{1,0:T(8,128)(2,1)}, /*index=5*/bf16[512,2048]{1,0:T(8,128)(2,1)}) custom-call(bf16[4,2048,512]{2,1,0:T(8,128)(2,1)} %bitcast.5, bf16[512,2048]{1,0:T(8,128)(2,1)} %bitcast.7, bf16[2048,2816]{1,0:T(8,128)(2,1)} %bitcast.4, ...), custom_call_target="tpu_custom_call" | custom-call | flops 100000000 | bytes 84000000 | tf_op jit(solution)/shard_map/widen/pallas_call | solution.py:1795

commit v10 on v9

--- a/solution.py
+++ b/solution.py
@@ -751,11 +751,14 @@
             [landed.at[at] for at in range(4)],
             0,
         )
+        ahead = min(3, in_columns)
         load_normed_two(0).start()
-        load_parts(0).start()
+        for at in range(ahead):
+            load_parts(at).start()
         enter(places)
+        run(1)
         open_sum()
-        for at in range(1, in_columns):
+        for at in range(ahead, in_columns):
             load_parts(at).start()
         for at in range(1, in_rows):
             load_normed_two(at).start()
@@ -1059,7 +1062,7 @@
                 block_store(half, out).start()
 
         rows_out(layer_loads, layer_tile, layer_out)
-        run(first_mix + 31 - now[0])
+        run(first_mix + 32 - now[0])
         block_store(1, layer_out).wait()
         close_last()
         rows_out(input_loads, input_tile, input_out)
@@ -1387,16 +1390,16 @@
         for j in range(width // wide_tile):
             finish(sum_stores(pieces - 2, j))
 
-        def last_stores(which):
+        def last_stores(which, total, j):
+            tile = pl.ds(j * wide_tile, wide_tile)
             return [
                 pltpu.make_async_copy(
-                    sums.at[2 * total + which, pl.ds(part * SUB, SUB)],
+                    sums.at[2 * total + which, pl.ds(part * SUB, SUB), tile],
                     (back_out, two_out)[total].at[
-                        pl.ds(pl.multiple_of((pieces - 1) * PIECE + part * HALF + which * SUB, SUB), SUB)
+                        pl.ds(pl.multiple_of((pieces - 1) * PIECE + part * HALF + which * SUB, SUB), SUB), tile
                     ],
-                    last_sems.at[which, 2 * total + part],
+                    last_sems.at[which, 2 * total + part, j],
                 )
-                for total in range(2)
                 for part in range(2)
             ]
 
@@ -1421,6 +1424,7 @@
             for j in range(width // wide_tile):
                 tile = slice(j * wide_tile, (j + 1) * wide_tile)
                 sums[2 + which, :, tile] = straight(act[:HALF], w_out[:, tile]).astype(low)
+                begin(last_stores(which, 1, j))
             pl.when(which == 0)(lambda: finish(grad_sends[2]))
             pl.when(which == 1)(lambda: finish(grad_sends[3]))
             stores = row_stores(arrived, arrived_grads, at)
@@ -1435,14 +1439,16 @@
             for j in range(width // wide_tile):
                 tile = slice(j * wide_tile, (j + 1) * wide_tile)
                 sums[which, :, tile] = across(parts[:HALF], w_in[tile, :]).astype(low)
-            begin(last_stores(which))
+                begin(last_stores(which, 0, j))
             finish(stores)
             finish(more)
             return carry
 
         lax.fori_loop(0, 2, last_work, 0)
         for which in range(2):
-            finish(last_stores(which))
+            for total in range(2):
+                for j in range(width // wide_tile):
+                    finish(last_stores(which, total, j))
         store_middle.wait()
 
     return pl.pallas_call(
@@ -1475,7 +1481,7 @@
             pltpu.SemaphoreType.DMA((9,)),
             pltpu.SemaphoreType.DMA((5,)),
             pltpu.SemaphoreType.DMA((width // wide_tile, 4)),
-            pltpu.SemaphoreType.DMA((2, 4)),
+            pltpu.SemaphoreType.DMA((2, 4, width // wide_tile)),
             pltpu.SemaphoreType.DMA((6, 2)),
             pltpu.SemaphoreType.DMA((16, 2)),
         ],

time: 632 us -> 633 us (level)
  no operation moved by 1% of the time
where the time goes in v10:
time: 633 us; the launch traced here: 625 us
  Pallas kernels  624 us (99%)
    pallas_call x1, Pallas kernels, weight_grads(): pl.pallas_call(body, in_specs=any_specs(16) + [pl.BlockSpec(memory_space=...  336 us
    pallas_call x1, Pallas kernels, gated_unit(): pl.pallas_call(body, in_specs=any_specs(7) + [pl.BlockSpec(memory_space=p...  145 us
    pallas_call x1, Pallas kernels, mix_rows(): pl.pallas_call(body, in_specs=any_specs(4) + [pl.BlockSpec(memory_space=p...  114 us
    pallas_call x1, Pallas kernels, widen(): pl.pallas_call(body, grid=(steps,), in_specs=[mix_spec] + [rows_spec(arra...  28.4 us

profile of v10, /device:TPU:0, one launch (start us, length us, event | category | flops | bytes accessed | tf_op | source)
XLA Modules:
  0.0 625.1 jit_solution(14122371588332483296)
XLA Ops:
  0.6 114.4 %mix_rows.1 = (bf16[2048,2048]{1,0:T(8,128)(2,1)}, bf16[4,2048,512]{2,1,0:T(8,128)(2,1)}, bf16[1,2048,512]{2,1,0:T(8,128)(2,1)}, bf16[2048,512]{1,0:T(8,128)(2,1...) custom-call(bf16[512,2048]{1,0:T(8,128)(2,1)} %refs_15_.1, ...), custom_call_target="tpu_custom_call" | custom-call | flops 17179869184 | bytes 50000000 | tf_op jit(solution)/shard_map/mix_rows/pallas_call | solution.py:1736
  115.1 145.2 %gated_unit.1 = (f32[512,2048]{1,0:T(8,128)}, bf16[2048,2048]{1,0:T(8,128)(2,1)}, bf16[2048,2048]{1,0:T(8,128)(2,1)}, bf16[2048,1408]{1,0:T(8,128)(2,1)}, bf16[2...) custom-call(bf16[1,2048,512]{2,1,0:T(8,128)(2,1)} %get-tuple-element.35.refs_0_.refs_13_, ...), custom_call_target="tpu_custom_call" | custom-call | flops 70866960384 | bytes 90000000 | tf_op jit(solution)/shard_map/gated_unit/pallas_call | solution.py:1454
  260.3 336.1 %weight_grads.1 = (bf16[16,128,2816]{2,1,0:T(8,128)(2,1)}, bf16[11,128,2048]{2,1,0:T(8,128)(2,1)}, bf16[4,128,2048]{2,1,0:T(8,128)(2,1)}, bf16[64,128,512]{2,1,0...) custom-call(bf16[2048,1408]{1,0:T(8,128)(2,1)} %get-tuple-element.40, ...), custom_call_target="tpu_custom_call" | custom-call | flops 74088185856 | bytes 120000000 | tf_op jit(solution)/shard_map/weight_grads/pallas_call | solution.py:1076
  596.4 28.4 %widen.1 = (f32[4,2048,512]{2,1,0:T(8,128)}, f32[512,2048]{1,0:T(8,128)}, f32[2,2048,1408]{2,1,0:T(8,128)}, f32[1408,2048]{1,0:T(8,128)}, bf16[512,2048]{1,0:T(8,128)(2,1)}, /*index=5*/bf16[512,2048]{1,0:T(8,128)(2,1)}) custom-call(bf16[4,2048,512]{2,1,0:T(8,128)(2,1)} %bitcast.5, bf16[512,2048]{1,0:T(8,128)(2,1)} %bitcast.7, bf16[2048,2816]{1,0:T(8,128)(2,1)} %bitcast.4, ...), custom_call_target="tpu_custom_call" | custom-call | flops 100000000 | bytes 84000000 | tf_op jit(solution)/shard_map/widen/pallas_call | solution.py:1801
